TPU v7x, 32 devices: a whole 2x2x4 slice. The times are simulated.
32 devices in a mesh: seq: 16 (over z, y, x), head: 2 (over core), dp: 1.
Axes of the slice: x: 2, y: 2, z: 4, core: 2. Of those that a mesh axis runs over, the one named last changes fastest.
Arguments:
- queries: bfloat16 [4096, 2048], P(('dp', 'seq'), 'head'), may hold values from -32 to 32
- keys: bfloat16 [4096, 2048], P(('dp', 'seq'), 'head'), may hold values from -32 to 32
- values: bfloat16 [4096, 2048], P(('dp', 'seq'), 'head'), may hold values from -6 to 6
- out_grad: bfloat16 [4096, 4096], P(('dp', 'seq')), may hold values from -6 to 6
- proj_weight: bfloat16 [4096, 2048], P(None, 'head'), may hold values from -0.09375 to 0.09375
- layout: int32 [32, 10], replicated, may hold values from -1 to 31, as said below
Outputs:
- query_grad: bfloat16 [4096, 2048], P(('dp', 'seq'), 'head')
- key_grad: bfloat16 [4096, 2048], P(('dp', 'seq'), 'head')
- value_grad: bfloat16 [4096, 2048], P(('dp', 'seq'), 'head')
- proj_grad: float32 [4096, 2048], P(('dp', 'seq'), 'head')
Inputs may be any that keep to these rules, and one draw needn't show every extreme that they name: `layout`: row i lists, in increasing order, some of the blocks j < i - 7 whose remainder modulo 16 equals one offset, below 8 and shared by all rows (the last row lists all of them), then the blocks max(0, i - w + 1) to i for a window w of its own between 1 and 8, and ends with -1 in the unused entries; a row whose block follows a block of that remainder has w = 8.
All inputs are finite; a program needn't handle non-finite values.
Results may differ from a plain program's by a relative error of at most 0.03.
Values may be sent and summed in bfloat16 or wider, within the bound.
No kernel may reach another device: no remote copies, remote signals or barrier semaphores. Data moves between devices by JAX's collectives and lax.ppermute only.
A program may use at most 192 MiB of HBM per device.

v0:
```python
import jax
import jax.numpy as jnp
from jax import lax
from jax.sharding import PartitionSpec as P

HD = 128
BLK = 128
LOCAL = 8
STRIDE = 16


def passed_along(block, axis, distance):
    devices = range(lax.axis_size(axis))
    route = [(i - distance, i) for i in devices if i - distance in devices]
    return lax.ppermute(block, axis, route)


def broadcast(array, axis, root):
    mine = lax.axis_index(axis) == root
    return lax.psum(jnp.where(mine, array, jnp.zeros_like(array)), axis)


def listed(table_row, block_ids):
    return jnp.any(table_row[None, :] == block_ids[:, None], axis=1) & (block_ids >= 0)


def local(queries, keys, values, out_grad, proj_weight, layout):
    tok_dev = queries.shape[0]
    width = queries.shape[1]
    heads_here = width // HD
    blocks_dev = tok_dev // BLK
    block_count = layout.shape[0]
    summary_count = block_count // STRIDE
    score_scale = HD ** (-0.5)
    first_block = lax.axis_index("seq") * blocks_dev
    offset_block = layout[block_count - 1, 0] % STRIDE
    reach_back = (LOCAL - 2) // blocks_dev + 1
    span_blocks = [
        min(blocks_dev, LOCAL - 1 - hop_index * blocks_dev) for hop_index in range(reach_back)
    ]
    attn_grad = jnp.dot(out_grad, proj_weight, preferred_element_type=jnp.float32).astype(
        jnp.bfloat16
    )
    near_keys = []
    near_values = []
    for distance in range(reach_back, 0, -1):
        rows_needed = span_blocks[distance - 1] * BLK
        moved_keys, moved_values = passed_along(
            (keys[tok_dev - rows_needed :], values[tok_dev - rows_needed :]), "seq", distance
        )
        near_keys.append(moved_keys)
        near_values.append(moved_values)
    pool_keys = jnp.concatenate(near_keys + [keys], axis=0).reshape(-1, heads_here, HD)
    pool_values = jnp.concatenate(near_values + [values], axis=0).reshape(-1, heads_here, HD)

    def fetch_summary(scan_state, summary_index):
        block_id = summary_index * STRIDE + offset_block
        start_row = block_id % blocks_dev * BLK
        owner_rank = block_id // blocks_dev
        piece_keys = lax.dynamic_slice_in_dim(keys, start_row, BLK, 0)
        piece_values = lax.dynamic_slice_in_dim(values, start_row, BLK, 0)
        received = (
            broadcast(piece_keys, "seq", owner_rank),
            broadcast(piece_values, "seq", owner_rank),
        )
        return (scan_state, received)

    ignored, fetched = lax.scan(fetch_summary, None, jnp.arange(summary_count, dtype=jnp.int32))
    far_keys = fetched[0].reshape(summary_count * BLK, heads_here, HD)
    far_values = fetched[1].reshape(summary_count * BLK, heads_here, HD)
    far_ids = jnp.arange(summary_count, dtype=jnp.int32) * STRIDE + offset_block
    query_blocks = queries.reshape(blocks_dev, BLK, heads_here, HD)
    grad_blocks = attn_grad.reshape(blocks_dev, BLK, heads_here, HD)
    window_offsets = jnp.arange(LOCAL, dtype=jnp.int32)
    causal_local = jnp.arange(LOCAL * BLK)[None, :] <= (LOCAL - 1) * BLK + jnp.arange(BLK)[:, None]

    def query_step(scan_state, local_block):
        query_rows = query_blocks[local_block]
        grad_rows = grad_blocks[local_block]
        block_id = first_block + local_block
        table_row = layout[block_id]
        window_key_rows = lax.dynamic_slice_in_dim(pool_keys, local_block * BLK, LOCAL * BLK, 0)
        window_value_rows = lax.dynamic_slice_in_dim(pool_values, local_block * BLK, LOCAL * BLK, 0)
        window_ids = block_id - (LOCAL - 1) + window_offsets
        plain_window = (window_ids % STRIDE != offset_block) | (window_ids == block_id)
        local_allowed = (
            causal_local & jnp.repeat(listed(table_row, window_ids) & plain_window, BLK)[None, :]
        )
        far_allowed = jnp.repeat(listed(table_row, far_ids) & (far_ids < block_id), BLK)[None, :]
        near_scores = (
            jnp.einsum(
                "ahd,chd->hac", query_rows, window_key_rows, preferred_element_type=jnp.float32
            )
            * score_scale
        )
        far_scores = (
            jnp.einsum("ahd,chd->hac", query_rows, far_keys, preferred_element_type=jnp.float32)
            * score_scale
        )
        near_scores = jnp.where(local_allowed[None], near_scores, -jnp.inf)
        far_scores = jnp.where(far_allowed[None], far_scores, -jnp.inf)
        row_top = jnp.maximum(jnp.max(near_scores, axis=-1), jnp.max(far_scores, axis=-1))[
            ..., None
        ]
        row_total = jnp.sum(jnp.exp(near_scores - row_top), axis=-1, keepdims=True) + jnp.sum(
            jnp.exp(far_scores - row_top), axis=-1, keepdims=True
        )
        log_total = row_top + jnp.log(row_total)
        near_probs = jnp.exp(near_scores - log_total)
        far_probs = jnp.exp(far_scores - log_total)
        near_low = near_probs.astype(jnp.bfloat16)
        far_low = far_probs.astype(jnp.bfloat16)
        out_rows = (
            jnp.einsum(
                "hac,chd->ahd", near_low, window_value_rows, preferred_element_type=jnp.float32
            )
            + jnp.einsum("hac,chd->ahd", far_low, far_values, preferred_element_type=jnp.float32)
        ).astype(jnp.bfloat16)
        delta_rows = jnp.transpose(
            jnp.sum(out_rows.astype(jnp.float32) * grad_rows.astype(jnp.float32), axis=-1)
        )[..., None]
        near_dprob = jnp.einsum(
            "ahd,chd->hac", grad_rows, window_value_rows, preferred_element_type=jnp.float32
        )
        far_dprob = jnp.einsum(
            "ahd,chd->hac", grad_rows, far_values, preferred_element_type=jnp.float32
        )
        near_dscore = (score_scale * near_probs * (near_dprob - delta_rows)).astype(jnp.bfloat16)
        far_dscore = (score_scale * far_probs * (far_dprob - delta_rows)).astype(jnp.bfloat16)
        query_grad_rows = (
            jnp.einsum(
                "hac,chd->ahd", near_dscore, window_key_rows, preferred_element_type=jnp.float32
            )
            + jnp.einsum("hac,chd->ahd", far_dscore, far_keys, preferred_element_type=jnp.float32)
        ).astype(jnp.bfloat16)
        far_key_grad = scan_state[0] + jnp.einsum(
            "hac,ahd->chd", far_dscore, query_rows, preferred_element_type=jnp.float32
        )
        far_value_grad = scan_state[1] + jnp.einsum(
            "hac,ahd->chd", far_low, grad_rows, preferred_element_type=jnp.float32
        )
        start_row = local_block * BLK
        old_keys = lax.dynamic_slice_in_dim(scan_state[2], start_row, LOCAL * BLK, 0)
        old_values = lax.dynamic_slice_in_dim(scan_state[3], start_row, LOCAL * BLK, 0)
        new_keys = old_keys + jnp.einsum(
            "hac,ahd->chd", near_dscore, query_rows, preferred_element_type=jnp.float32
        )
        new_values = old_values + jnp.einsum(
            "hac,ahd->chd", near_low, grad_rows, preferred_element_type=jnp.float32
        )
        pool_key_grad = lax.dynamic_update_slice_in_dim(scan_state[2], new_keys, start_row, 0)
        pool_value_grad = lax.dynamic_update_slice_in_dim(scan_state[3], new_values, start_row, 0)
        new_state = (far_key_grad, far_value_grad, pool_key_grad, pool_value_grad)
        return (new_state, (out_rows, query_grad_rows, log_total[..., 0], delta_rows[..., 0]))

    far_zeros = jnp.zeros((summary_count * BLK, heads_here, HD), jnp.float32)
    pool_zeros = jnp.zeros((pool_keys.shape[0], heads_here, HD), jnp.float32)
    init_state = (far_zeros, far_zeros, pool_zeros, pool_zeros)
    state_out, scanned = lax.scan(query_step, init_state, jnp.arange(blocks_dev, dtype=jnp.int32))
    out_blocks, query_parts, log_blocks, delta_blocks = scanned
    attn_out = out_blocks.reshape(tok_dev, width)
    query_grad = query_parts.reshape(tok_dev, width)
    own_ids = first_block + jnp.arange(blocks_dev, dtype=jnp.int32)
    is_summary = own_ids % STRIDE == offset_block
    summary_slot = jnp.minimum(own_ids // STRIDE, summary_count - 1)
    summed = lax.psum((state_out[0], state_out[1]), "seq")
    far_key_sum = summed[0].reshape(summary_count, BLK, width)
    far_value_sum = summed[1].reshape(summary_count, BLK, width)
    far_key_add = jnp.take(far_key_sum, summary_slot, axis=0)
    far_value_add = jnp.take(far_value_sum, summary_slot, axis=0)
    own_start = (LOCAL - 1) * BLK
    key_grad = state_out[2][own_start:]
    value_grad = state_out[3][own_start:]
    pool_start = 0
    for distance in range(reach_back, 0, -1):
        rows_needed = span_blocks[distance - 1] * BLK
        back_keys, back_values = passed_along(
            (
                state_out[2][pool_start : pool_start + rows_needed],
                state_out[3][pool_start : pool_start + rows_needed],
            ),
            "seq",
            -distance,
        )
        key_grad = key_grad.at[tok_dev - rows_needed :].add(back_keys)
        value_grad = value_grad.at[tok_dev - rows_needed :].add(back_values)
        pool_start = pool_start + rows_needed
    key_total = key_grad.reshape(blocks_dev, BLK, width) + jnp.where(
        is_summary[:, None, None], far_key_add, 0.0
    )
    value_total = value_grad.reshape(blocks_dev, BLK, width) + jnp.where(
        is_summary[:, None, None], far_value_add, 0.0
    )
    proj_grad = lax.psum_scatter(
        lax.dot_general(
            out_grad, attn_out, (((0,), (0,)), ((), ())), preferred_element_type=jnp.float32
        ),
        "seq",
        scatter_dimension=0,
        tiled=True,
    )
    key_out = key_total.reshape(tok_dev, width).astype(jnp.bfloat16)
    value_out = value_total.reshape(tok_dev, width).astype(jnp.bfloat16)
    return (query_grad, key_out, value_out, proj_grad)


def solution(mesh):
    return jax.shard_map(
        local,
        mesh=mesh,
        in_specs=(
            P(("dp", "seq"), "head"),
            P(("dp", "seq"), "head"),
            P(("dp", "seq"), "head"),
            P(("dp", "seq"), None),
            P(None, "head"),
            P(),
        ),
        out_specs=(
            P(("dp", "seq"), "head"),
            P(("dp", "seq"), "head"),
            P(("dp", "seq"), "head"),
            P(("dp", "seq"), "head"),
        ),
        check_vma=False,
    )
```

profile of v0, /device:TPU:0, one launch (start us, length us, event | category | flops | bytes accessed | tf_op | source)
XLA Modules:
  0.0 1010.7 jit_solution(17089847465544552807)
XLA Ops:
  10.2 6.6 collective-permute-start.1
  16.8 4.2 collective-permute-start.2
  25.2 2.6 collective-permute-start
  29.5 2.8 collective-permute-start.4
  38.3 6.6 fusion.55
  44.9 235.3 %while.53 = (s32[]{:T(128)}, bf16[2,128,1024]{2,1,0:T(8,128)(2,1)}, bf16[2,128,1024]{2,1,0:T(8,128)(2,1)}, s32[2]{0:T(128)S(1)}, s32[]{:T(128)}, /*index=5*/bf16...) while((s32[]{:T(128)}, bf16[2,128,1024]{2,1,0:T(8,128)(2,1)}, ...), condition=%wide.region_3.4_spmd, body=%wide.region_0.3_spmd.sunk | while | flops 524319 | bytes 5243400 | solution.py:68
  47.3 111.9 %all-reduce.9.cloned.1.call-done = (bf16[1,128,1024]{2,1,0:T(8,128)(2,1)}, bf16[1,128,1024]{2,1,0:T(8,128)(2,1)}) async-done(((bf16[1,128,1024]{2,1,0:T(8,128)(2,1)}, bf16[1,128,1024]{2,1,0:T(8,128)(2,1)}), (bf16[1,128,1024]{2,1,0:T(8,128)(2,1)}, bf16[1,128,1024]{2,1,0:T(8,128)(2,1)})) %all-reduce.9.cloned.1.call-update) | async-done | bytes 524304 | tf_op jit(solution)/shard_map/while/body/eval_jaxpr/psum | solution.py:20
  164.8 112.0 %all-reduce.9.cloned.1.call-done = (bf16[1,128,1024]{2,1,0:T(8,128)(2,1)}, bf16[1,128,1024]{2,1,0:T(8,128)(2,1)}) async-done(((bf16[1,128,1024]{2,1,0:T(8,128)(2,1)}, bf16[1,128,1024]{2,1,0:T(8,128)(2,1)}), (bf16[1,128,1024]{2,1,0:T(8,128)(2,1)}, bf16[1,128,1024]{2,1,0:T(8,128)(2,1)})) %all-reduce.9.cloned.1.call-update) | async-done | bytes 524304 | tf_op jit(solution)/shard_map/while/body/eval_jaxpr/psum | solution.py:20
  286.5 3.5 collective-permute-start.5
  291.7 3.4 collective-permute-start.6
  306.8 8.9 collective-permute-done.6
  318.4 4.3 copy.75
  327.9 81.6 %while.54 = (s32[]{:T(128)}, f32[256,8,128]{0,2,1:T(8,128)}, f32[256,8,128]{0,2,1:T(8,128)}, f32[1152,8,128]{0,2,1:T(8,128)}, f32[1152,8,128]{0,2,1:T(8,128)}, /...) while((s32[]{:T(128)}, f32[256,8,128]{0,2,1:T(8,128)}, ...), condition=%wide.region_12.13_spmd.clone.clone.clone, body=%wide.region_4.12_spmd.clone.clone.clone.sunk | while | flops 2044459392 | bytes 163682480 | solution.py:159
  336.5 2.6 fusion.116
  350.8 3.7 multiply_convert_fusion.2
  354.5 5.1 fusion.120
  376.8 2.6 fusion.116
  386.2 2.8 fusion.118
  389.0 2.8 fusion.119
  391.8 3.7 multiply_convert_fusion.2
  395.5 5.2 fusion.120
  409.4 2.8 reshape.422
  418.4 8.2 convolution_bitcast_fusion.4
  426.7 2.7 fusion.64
  440.1 45.4 %collective-permute-done.12 = f32[128,8,128]{0,2,1:T(8,128)S(1)} collective-permute-done((f32[128,8,128]{0,2,1:T(8,128)S(1)}, f32[128,8,128]{0,2,1:T(8,128)S(1)}, u32[]{:S(2)}, u32[]{:S(2)}) %collective-permute-start.12) | collective-permute-done | bytes 524320 | tf_op jit(solution)/shard_map/ppermute | solution.py:15
  486.8 12.4 %collective-permute-done.8 = f32[128,8,128]{0,2,1:T(8,128)S(1)} collective-permute-done((f32[128,8,128]{0,2,1:T(8,128)S(1)}, f32[128,8,128]{0,2,1:T(8,128)S(1)}, u32[]{:S(2)}, u32[]{:S(2)}) %collective-permute-start.8) | collective-permute-done | bytes 524320 | tf_op jit(solution)/shard_map/ppermute | solution.py:15
  508.9 18.8 %collective-permute-done.11 = f32[256,8,128]{0,2,1:T(8,128)} collective-permute-done((f32[256,8,128]{0,2,1:T(8,128)}, f32[256,8,128]{0,2,1:T(8,128)}, u32[]{:S(2)}, u32[]{:S(2)}) %collective-permute-start.11) | collective-permute-done | bytes 1048608 | tf_op jit(solution)/shard_map/ppermute | solution.py:15
  527.7 21.5 %collective-permute-done.10 = f32[256,8,128]{0,2,1:T(8,128)} collective-permute-done((f32[256,8,128]{0,2,1:T(8,128)}, f32[256,8,128]{0,2,1:T(8,128)}, u32[]{:S(2)}, u32[]{:S(2)}) %collective-permute-start.10) | collective-permute-done | bytes 1048608 | tf_op jit(solution)/shard_map/ppermute | solution.py:15
  555.4 78.4 %all-reduce.7.cloned.1.call-done = (f32[2,128,1024]{2,1,0:T(8,128)}, f32[2,128,1024]{2,1,0:T(8,128)}) async-done(((f32[2,128,1024]{2,1,0:T(8,128)}, f32[2,128,1024]{2,1,0:T(8,128)}), (f32[2,128,1024]{2,1,0:T(8,128)}, f32[2,128,1024]{2,1,0:T(8,128)})) %all-reduce.7.cloned.1.call-update) | async-done | bytes 2097168 | tf_op jit(solution)/shard_map/psum | solution.py:166
  635.7 2.8 gather_fusion
  638.5 3.4 fusion.57
  641.9 358.9 %reduce-scatter.2.cloned.1.call-done = f32[256,1024]{0,1:T(8,128)} async-done(((f32[4096,1024]{0,1:T(8,128)}), f32[256,1024]{0,1:T(8,128)}) %reduce-scatter.2.cloned.1.call-update) | async-done | bytes 1048592 | tf_op jit(solution)/shard_map/reduce_scatter | solution.py:194
  (228 shorter events, 134.0 us)
Async XLA Ops:
  8.0 30.3 %copy-start = (bf16[256,4096]{1,0:T(8,128)(2,1)S(1)}, bf16[256,4096]{1,0:T(8,128)(2,1)}, u32[]{:S(2)}) copy-start(bf16[256,4096]{1,0:T(8,128)(2,1)} %param.43) | copy-start | bytes 6291460
  10.2 285.6 %collective-permute-start.1 = (bf16[256,1024]{0,1:T(8,128)(2,1)}, bf16[256,1024]{0,1:T(8,128)(2,1)}, u32[]{:S(2)}, u32[]{:S(2)}) collective-permute-start(bf16[256,1024]{0,1:T(8,128)(2,1)} %copy.69), channel_id=1, source_target_pairs={{0,6},{2,8},{4,10},{6,12},{8,14},{10,16},{12,18},{14,20},{16,22},{... | collective-permute-start | bytes 1572872 | tf_op jit(solution)/shard_map/ppermute | solution.py:15
  16.8 283.4 %collective-permute-start.2 = (bf16[256,1024]{0,1:T(8,128)(2,1)}, bf16[256,1024]{0,1:T(8,128)(2,1)}, u32[]{:S(2)}, u32[]{:S(2)}) collective-permute-start(bf16[256,1024]{0,1:T(8,128)(2,1)} %copy.69), channel_id=1, source_target_pairs={{0,4},{2,6},{4,8},{6,10},{8,12},{10,14},{12,16},{14,18},{16,20},{1... | collective-permute-start | bytes 1572872 | tf_op jit(solution)/shard_map/ppermute | solution.py:15
  21.0 281.1 %collective-permute-start.3 = (bf16[256,1024]{0,1:T(8,128)(2,1)}, bf16[256,1024]{0,1:T(8,128)(2,1)}, u32[]{:S(2)}, u32[]{:S(2)}) collective-permute-start(bf16[256,1024]{0,1:T(8,128)(2,1)} %copy.69), channel_id=1, source_target_pairs={{0,2},{2,4},{4,6},{6,8},{8,10},{10,12},{12,14},{14,16},{16,18},{18... | collective-permute-start | bytes 1572872 | tf_op jit(solution)/shard_map/ppermute | solution.py:15
  25.2 261.2 %collective-permute-start = (bf16[128,1024]{0,1:T(8,128)(2,1)}, bf16[128,1024]{0,1:T(8,128)(2,1)}, u32[]{:S(2)}, u32[]{:S(2)}) collective-permute-start(bf16[128,1024]{0,1:T(8,128)(2,1)} %slice.222), channel_id=1, source_target_pairs={{0,8},{2,10},{4,12},{6,14},{8,16},{10,18},{12,20},{14,22},{16,24},... | collective-permute-start | bytes 786440 | tf_op jit(solution)/shard_map/ppermute | solution.py:15
  29.5 262.2 %collective-permute-start.4 = (bf16[128,1024]{1,0:T(8,128)(2,1)}, bf16[128,1024]{1,0:T(8,128)(2,1)S(1)}, u32[]{:S(2)}, u32[]{:S(2)}) collective-permute-start(bf16[128,1024]{1,0:T(8,128)(2,1)} %slice.205), channel_id=1, source_target_pairs={{0,8},{2,10},{4,12},{6,14},{8,16},{10,18},{12,20},{14,22},{16,24},... | collective-permute-start | bytes 786440 | tf_op jit(solution)/shard_map/ppermute | solution.py:15
  38.3 6.6 copy-start.10
  38.3 6.6 copy-start.12
  44.9 114.3 %all-reduce.9.cloned.1.call-start = ((), (), s32[]{:S(2)}) async-start(), calls=%async_computation.3 | async-start | bytes 1048576 | tf_op jit(solution)/shard_map/while/body/eval_jaxpr/psum | solution.py:20
  162.5 114.3 %all-reduce.9.cloned.1.call-start = ((), (), s32[]{:S(2)}) async-start(), calls=%async_computation.3 | async-start | bytes 1048576 | tf_op jit(solution)/shard_map/while/body/eval_jaxpr/psum | solution.py:20
  280.2 353.6 %all-reduce.7.cloned.1.call-start = ((), (), s32[]{:S(2)}) async-start(), calls=%async_computation.2 | async-start | bytes 4194304 | tf_op jit(solution)/shard_map/psum | solution.py:166
  286.5 19.5 %collective-permute-start.5 = (bf16[256,1024]{1,0:T(8,128)(2,1)S(1)}, bf16[256,1024]{1,0:T(8,128)(2,1)S(1)}, u32[]{:S(2)}, u32[]{:S(2)}) collective-permute-start(bf16[256,1024]{1,0:T(8,128)(2,1)S(1)} %get-tuple-element.1109), channel_id=1, source_target_pairs={{0,6},{2,8},{4,10},{6,12},{8,14},{10,16},{12,18},{14,20},{16,22},{... | collective-permute-start | bytes 1572872 | tf_op jit(solution)/shard_map/ppermute | solution.py:15
  291.7 24.0 %collective-permute-start.6 = (bf16[256,1024]{1,0:T(8,128)(2,1)S(1)}, bf16[256,1024]{1,0:T(8,128)(2,1)S(1)}, u32[]{:S(2)}, u32[]{:S(2)}) collective-permute-start(bf16[256,1024]{1,0:T(8,128)(2,1)S(1)} %get-tuple-element.1109), channel_id=1, source_target_pairs={{0,4},{2,6},{4,8},{6,10},{8,12},{10,14},{12,16},{14,18},{16,20},{1... | collective-permute-start | bytes 1572872 | tf_op jit(solution)/shard_map/ppermute | solution.py:15
  295.8 20.8 %collective-permute-start.7 = (bf16[256,1024]{1,0:T(8,128)(2,1)S(1)}, bf16[256,1024]{1,0:T(8,128)(2,1)S(1)}, u32[]{:S(2)}, u32[]{:S(2)}) collective-permute-start(bf16[256,1024]{1,0:T(8,128)(2,1)S(1)} %get-tuple-element.1109), channel_id=1, source_target_pairs={{0,2},{2,4},{4,6},{6,8},{8,10},{10,12},{12,14},{14,16},{16,18},{18... | collective-permute-start | bytes 1572872 | tf_op jit(solution)/shard_map/ppermute | solution.py:15
  327.9 7.7 copy-start.19
  350.8 8.8 slice-start
  368.2 7.7 copy-start.19
  386.2 5.6 copy-start.2
  386.2 5.6 copy-start.6
  391.8 8.9 slice-start
  418.3 582.4 %reduce-scatter.2.cloned.1.call-start = ((), (), s32[]{:S(2)}) async-start(), calls=%async_computation.1 | async-start | bytes 17825792 | tf_op jit(solution)/shard_map/reduce_scatter | solution.py:194
  426.7 11.6 %slice-start.2 = ((s8[4718592]{0:T(1024)(128)(4,1)}), s8[4194304]{0:T(1024)(128)(4,1)S(1)}, s32[]{:S(2)}) async-start(s8[4718592]{0:T(1024)(128)(4,1)} %bitcast.185), calls=%async_computation.6 | async-start | bytes 8388608
  426.7 11.6 %slice-start.3 = ((s8[4718592]{0:T(1024)(128)(4,1)}), s8[524288]{0:T(1024)(128)(4,1)S(1)}, s32[]{:S(2)}) async-start(s8[4718592]{0:T(1024)(128)(4,1)} %bitcast.185), calls=%async_computation.7 | async-start | bytes 1048576
  429.4 71.1 %collective-permute-start.15 = (f32[256,8,128]{0,2,1:T(8,128)S(1)}, f32[256,8,128]{0,2,1:T(8,128)S(1)}, u32[]{:S(2)}, u32[]{:S(2)}) collective-permute-start(f32[256,8,128]{0,2,1:T(8,128)S(1)} %get-tuple-element.786), channel_id=1, source_target_pairs={{2,0},{4,2},{6,4},{8,6},{10,8},{12,10},{14,12},{16,14},{18,16},{20... | collective-permute-start | bytes 3145736 | tf_op jit(solution)/shard_map/ppermute | solution.py:15
  431.8 53.7 %collective-permute-start.12 = (f32[128,8,128]{0,2,1:T(8,128)S(1)}, f32[128,8,128]{0,2,1:T(8,128)S(1)}, u32[]{:S(2)}, u32[]{:S(2)}) collective-permute-start(f32[128,8,128]{0,2,1:T(8,128)S(1)} %slice.214), channel_id=1, source_target_pairs={{8,0},{10,2},{12,4},{14,6},{16,8},{18,10},{20,12},{22,14},{24,16},... | collective-permute-start | bytes 1572872 | tf_op jit(solution)/shard_map/ppermute | solution.py:15
  434.2 65.0 %collective-permute-start.8 = (f32[128,8,128]{0,2,1:T(8,128)S(1)}, f32[128,8,128]{0,2,1:T(8,128)S(1)}, u32[]{:S(2)}, u32[]{:S(2)}) collective-permute-start(f32[128,8,128]{0,2,1:T(8,128)S(1)} %slice.208), channel_id=1, source_target_pairs={{8,0},{10,2},{12,4},{14,6},{16,8},{18,10},{20,12},{22,14},{24,16},... | collective-permute-start | bytes 1572872 | tf_op jit(solution)/shard_map/ppermute | solution.py:15
  435.5 68.4 %collective-permute-start.14 = (f32[256,8,128]{0,2,1:T(8,128)S(1)}, f32[256,8,128]{0,2,1:T(8,128)S(1)}, u32[]{:S(2)}, u32[]{:S(2)}) collective-permute-start(f32[256,8,128]{0,2,1:T(8,128)S(1)} %get-tuple-element.787), channel_id=1, source_target_pairs={{4,0},{6,2},{8,4},{10,6},{12,8},{14,10},{16,12},{18,14},{20,16},{2... | collective-permute-start | bytes 3145736 | tf_op jit(solution)/shard_map/ppermute | solution.py:15
  436.8 65.0 %copy-start.18 = (bf16[2,128,8,128]{3,2,1,0:T(8,128)(2,1)S(1)}, bf16[2,128,8,128]{3,2,1,0:T(8,128)(2,1)}, u32[]{:S(2)}) copy-start(bf16[2,128,8,128]{3,2,1,0:T(8,128)(2,1)} %get-tuple-element.496) | copy-start | bytes 1572868
  436.8 68.0 %collective-permute-start.13 = (f32[256,8,128]{0,2,1:T(8,128)S(1)}, f32[256,8,128]{0,2,1:T(8,128)S(1)}, u32[]{:S(2)}, u32[]{:S(2)}) collective-permute-start(f32[256,8,128]{0,2,1:T(8,128)S(1)} %get-tuple-element.784), channel_id=1, source_target_pairs={{6,0},{8,2},{10,4},{12,6},{14,8},{16,10},{18,12},{20,14},{22,16},{... | collective-permute-start | bytes 3145736 | tf_op jit(solution)/shard_map/ppermute | solution.py:15
  485.5 42.2 %collective-permute-start.11 = (f32[256,8,128]{0,2,1:T(8,128)}, f32[256,8,128]{0,2,1:T(8,128)}, u32[]{:S(2)}, u32[]{:S(2)}) collective-permute-start(f32[256,8,128]{0,2,1:T(8,128)} %get-tuple-element.790), channel_id=1, source_target_pairs={{2,0},{4,2},{6,4},{8,6},{10,8},{12,10},{14,12},{16,14},{18,16},{20... | collective-permute-start | bytes 3145736 | tf_op jit(solution)/shard_map/ppermute | solution.py:15
  499.2 50.0 %collective-permute-start.10 = (f32[256,8,128]{0,2,1:T(8,128)}, f32[256,8,128]{0,2,1:T(8,128)}, u32[]{:S(2)}, u32[]{:S(2)}) collective-permute-start(f32[256,8,128]{0,2,1:T(8,128)} %get-tuple-element.791), channel_id=1, source_target_pairs={{4,0},{6,2},{8,4},{10,6},{12,8},{14,10},{16,12},{18,14},{20,16},{2... | collective-permute-start | bytes 3145736 | tf_op jit(solution)/shard_map/ppermute | solution.py:15
  500.5 48.7 %collective-permute-start.9 = (f32[256,8,128]{0,2,1:T(8,128)}, f32[256,8,128]{0,2,1:T(8,128)}, u32[]{:S(2)}, u32[]{:S(2)}) collective-permute-start(f32[256,8,128]{0,2,1:T(8,128)} %get-tuple-element.788), channel_id=1, source_target_pairs={{6,0},{8,2},{10,4},{12,6},{14,8},{16,10},{18,12},{20,14},{22,16},{... | collective-permute-start | bytes 3145736 | tf_op jit(solution)/shard_map/ppermute | solution.py:15
  (29 other events, 96.4 us)
Sparse Core Ops, SparseCore 0:
  51.7 107.4 all-reduce.8
  169.4 107.4 all-reduce.8
Sparse Core Ops, SparseCore 1:
  418.4 215.4 all-reduce.6
  636.1 364.6 reduce-scatter.1
where the time goes:
time: 1010 us
  waiting for transfers between devices  768 us (76%)
  local copies, waits for them, and re-layouts  97.2 us (10%)
  matrix products  67.4 us (7%)
  starting transfers between devices  38.5 us (4%)
  between operations  17.8 us (2%)
  other arithmetic  13.3 us (1%)
    reduce_scatter x1, waiting for transfers between devices, local(): lax.psum_scatter(lax.dot_general(out_grad, attn_out, (((0,), (0,)), ((),...  359 us
    psum x2, waiting for transfers between devices, broadcast(): return lax.psum(jnp.where(mine, array, jnp.zeros_like(array)), axis)  224 us
    ppermute x16, waiting for transfers between devices, passed_along(): return lax.ppermute(block, axis, route)  107 us
    psum x1, waiting for transfers between devices, local(): summed = lax.psum((state_out[0], state_out[1]), 'seq')  78.4 us
    ppermute x16, starting transfers between devices, passed_along(): return lax.ppermute(block, axis, route)  38.4 us
    unnamed x35, local copies, waits for them, and re-layouts  25.3 us
  transfers between devices with their start and end apart: 20, of which 9 were waited for; matrix products, arithmetic and copies ran while one was open for 8% of the time, Pallas kernels for 0%

commit v1 on v0

v1 whole, which is shorter than its diff:
```python
import functools

import jax
import jax.numpy as jnp
from jax import lax
from jax.experimental import pallas as pl
from jax.experimental.pallas import tpu as pltpu
from jax.sharding import PartitionSpec as P

HD = 128
BLK = 128
LOCAL = 8
STRIDE = 16
PAIR = 2 * BLK
SPAN = LOCAL + 1
SCALE = HD ** (-0.5)
VMEM_LIMIT = 48 * 1024 * 1024

NT = (((1,), (1,)), ((), ()))
NN = (((1,), (0,)), ((), ()))
TN = (((0,), (0,)), ((), ()))
SMEM = pl.BlockSpec(memory_space=pltpu.SMEM)
VMEM = pl.BlockSpec(memory_space=pltpu.VMEM)


def shape(dims, dtype=jnp.bfloat16):
    return jax.ShapeDtypeStruct(dims, dtype)


def dot(a, b, dims):
    return lax.dot_general(a, b, dims, preferred_element_type=jnp.float32)


def params():
    return pltpu.CompilerParams(vmem_limit_bytes=VMEM_LIMIT)


def cost(flops, size, exps=0):
    return pl.CostEstimate(flops=flops, bytes_accessed=size, transcendentals=exps)


def call(body, scalars, arrays, outs, scratch, estimate, name):
    return pl.pallas_call(
        body,
        out_shape=outs,
        in_specs=[SMEM] * len(scalars) + [VMEM] * len(arrays),
        out_specs=[VMEM] * len(outs),
        scratch_shapes=scratch,
        compiler_params=params(),
        cost_estimate=estimate,
        name=name,
    )(*scalars, *arrays)


def pack_kv(keys, values, meta, group, width):
    rows = keys.shape[0]

    def body(meta_ref, k_ref, v_ref, *outs):
        me = meta_ref[0]
        for k in range(group):
            at = pl.multiple_of((me ^ k) * width, width)
            outs[k][0] = k_ref[:, pl.ds(at, width)]
            outs[k][1] = v_ref[:, pl.ds(at, width)]

    return call(
        body, (meta,), (keys, values), [shape((2, rows, width))] * group, [],
        cost(0, 4 * keys.size * 2), "pack_kv",
    )


def grads_packed(queries, out_grad, proj_weight, meta, group, width):
    rows, depth = out_grad.shape

    def body(meta_ref, q_ref, og_ref, w_ref, *outs):
        step = pl.program_id(0)
        got = dot(og_ref[...], w_ref[...], NN).astype(jnp.bfloat16)
        for k in range(group):

            @pl.when(step == k)
            def _():
                outs[k][0] = q_ref[...]
                outs[k][1] = got

    return pl.pallas_call(
        body,
        out_shape=[shape((2, rows, width))] * group,
        grid_spec=pltpu.PrefetchScalarGridSpec(
            num_scalar_prefetch=1,
            grid=(group,),
            in_specs=[
                pl.BlockSpec((rows, width), lambda i, m: (0, m[0] ^ i)),
                pl.BlockSpec((rows, depth), lambda i, m: (0, 0)),
                pl.BlockSpec((depth, width), lambda i, m: (0, m[0] ^ i)),
            ],
            out_specs=[pl.BlockSpec((2, rows, width), lambda i, m: (0, 0, 0))] * group,
        ),
        compiler_params=params(),
        cost_estimate=cost(2 * rows * depth * width * group, 12 * 1024 * 1024),
        name="attn_grad",
    )(meta, queries, out_grad, proj_weight)


def pack_out_grad(out_grad, meta, group, parts):
    rows, depth = out_grad.shape
    each = depth // (group * parts)

    def body(meta_ref, og_ref, *outs):
        me = meta_ref[0]
        for k in range(group):
            for part in range(parts):
                at = pl.multiple_of((part * group + (me ^ k)) * each, each)
                outs[k][part * each : (part + 1) * each, :] = og_ref[:, pl.ds(at, each)].T

    return call(
        body, (meta,), (out_grad,), [shape((parts * each, rows))] * group, [],
        cost(0, 4 * out_grad.size), "pack_out_grad",
    )


def pick_summary(pieces, meta, group):
    rows, width = pieces[0].shape[1:]

    def body(meta_ref, *refs):
        me, at = meta_ref[0], meta_ref[2] * BLK
        out = refs[group]
        for k in range(group):

            @pl.when(at // rows == (me ^ k))
            def _():
                start = pl.multiple_of(at % rows, BLK)
                out[...] = refs[k][:, pl.ds(start, BLK), :]

    return call(
        body, (meta,), tuple(pieces), [shape((2, BLK, width))], [],
        cost(0, 2 * 1024 * 1024), "pick_summary",
    )[0]


def fill_pools(meta_ref, own, prev, far, k_pool, v_pool, group, rows, slots):
    me, at_group, offset = meta_ref[0], meta_ref[1], meta_ref[2]
    whole = group * rows
    for k in range(group):
        at = pl.multiple_of((me ^ k) * rows, rows)
        k_pool[pl.ds(at, rows), :] = prev[k][0]
        v_pool[pl.ds(at, rows), :] = prev[k][1]
        k_pool[pl.ds(whole + at, rows), :] = own[k][0]
        v_pool[pl.ds(whole + at, rows), :] = own[k][1]
    tail = jnp.zeros((slots * BLK, k_pool.shape[1]), k_pool.dtype)
    k_pool[2 * whole :, :] = tail
    v_pool[2 * whole :, :] = tail

    @pl.when(at_group % 2 == 1)
    def _():
        to = pl.multiple_of(2 * whole + (at_group // 2) * BLK, BLK)
        start = pl.multiple_of(offset * BLK, BLK)
        k_pool[pl.ds(to, BLK), :] = k_pool[pl.ds(start, BLK), :]
        v_pool[pl.ds(to, BLK), :] = v_pool[pl.ds(start, BLK), :]

    for index, ref in enumerate(far):
        distance = index + 2

        @pl.when((at_group >= distance) & ((at_group - distance) % 2 == 0))
        def _():
            to = pl.multiple_of(2 * whole + ((at_group - distance) // 2) * BLK, BLK)
            k_pool[pl.ds(to, BLK), :] = ref[0]
            v_pool[pl.ds(to, BLK), :] = ref[1]


def causal_masks():
    key_at = lax.broadcasted_iota(jnp.int32, (BLK, PAIR), 0)
    query_at = lax.broadcasted_iota(jnp.int32, (BLK, PAIR), 1)
    first = (key_at <= query_at) | (query_at >= BLK)
    second = key_at <= query_at - BLK
    return first, second


def masked_scores(keys, query, bias, masks):
    raw = dot(keys, query, NT) * SCALE
    tiles = []
    for j in range(keys.shape[0] // BLK):
        tile = raw[j * BLK : (j + 1) * BLK] + bias[j : j + 1]
        if j in (LOCAL - 1, LOCAL):
            tile = jnp.where(masks[j - LOCAL + 1], tile, -jnp.inf)
        tiles.append(tile)
    return jnp.concatenate(tiles, axis=0)


def forward(qd, own, prev, far, bias, meta, group, slots):
    rows, width = qd[0].shape[1:]
    heads = width // HD
    whole = group * rows
    pairs = whole // PAIR
    counts = (group, group, group, len(far))

    def body(meta_ref, bias_ref, *refs):
        refs = list(refs)
        taken = []
        for count in counts:
            taken.append(refs[:count])
            refs = refs[count:]
        qd_refs, own_refs, prev_refs, far_refs = taken
        out_ref, lse_ref, k_pool, v_pool, q_pool = refs
        me = meta_ref[0]
        fill_pools(meta_ref, own_refs, prev_refs, far_refs, k_pool, v_pool, group, rows, slots)
        for k in range(group):
            at = pl.multiple_of((me ^ k) * rows, rows)
            q_pool[pl.ds(at, rows), :] = qd_refs[k][0]
        masks = causal_masks()

        def step(t, carry):
            at = pl.multiple_of(t * PAIR, PAIR)
            window = pl.ds(pl.multiple_of(t * PAIR + BLK, BLK), SPAN * BLK)
            bias_here = bias_ref[t]
            for h in range(heads):
                lanes = slice(h * HD, (h + 1) * HD)
                keys = jnp.concatenate([k_pool[window, lanes], k_pool[2 * whole :, lanes]], axis=0)
                vals = jnp.concatenate([v_pool[window, lanes], v_pool[2 * whole :, lanes]], axis=0)
                s = masked_scores(keys, q_pool[pl.ds(at, PAIR), lanes], bias_here, masks)
                top = jnp.max(s, axis=0, keepdims=True)
                e = jnp.exp(s - top)
                total = jnp.sum(e, axis=0, keepdims=True)
                low = (e * (1.0 / total)).astype(jnp.bfloat16)
                out_ref[pl.ds(at, PAIR), lanes] = dot(low, vals, TN).astype(jnp.bfloat16)
                lse_ref[t, h : h + 1, :] = top + jnp.log(total)
            return carry

        lax.fori_loop(0, pairs, step, 0)

    span = (SPAN + slots) * BLK
    return call(
        body, (meta,), (bias, *qd, *own, *prev, *far),
        [shape((whole, width)), shape((pairs, heads, PAIR), jnp.float32)],
        [
            pltpu.VMEM((2 * whole + slots * BLK, width), jnp.bfloat16),
            pltpu.VMEM((2 * whole + slots * BLK, width), jnp.bfloat16),
            pltpu.VMEM((whole, width), jnp.bfloat16),
        ],
        cost(4 * whole * span * width * 2, 5 * 1024 * 1024, whole * span * heads),
        "attention",
    )


def backward(qd, own, prev, far, attn, lse, bias, meta, group, slots):
    rows, width = qd[0].shape[1:]
    heads = width // HD
    whole = group * rows
    pairs = whole // PAIR
    counts = (group, group, group, len(far))
    out_counts = (group, 1, 1, len(far))
    everything = 2 * whole + slots * BLK

    def body(meta_ref, bias_ref, attn_ref, lse_ref, *refs):
        refs = list(refs)
        taken = []
        for count in counts + out_counts:
            taken.append(refs[:count])
            refs = refs[count:]
        qd_refs, own_refs, prev_refs, far_refs, dq_refs, own_out, prev_out, far_outs = taken
        own_out, prev_out = own_out[0], prev_out[0]
        k_pool, v_pool, q_pool, g_pool, dk, dv, dq = refs
        me, at_group, offset = meta_ref[0], meta_ref[1], meta_ref[2]
        fill_pools(meta_ref, own_refs, prev_refs, far_refs, k_pool, v_pool, group, rows, slots)
        for k in range(group):
            at = pl.multiple_of((me ^ k) * rows, rows)
            q_pool[pl.ds(at, rows), :] = qd_refs[k][0]
            g_pool[pl.ds(at, rows), :] = qd_refs[k][1]
        dk[...] = jnp.zeros_like(dk)
        dv[...] = jnp.zeros_like(dv)
        masks = causal_masks()

        def step(t, carry):
            at = pl.multiple_of(t * PAIR, PAIR)
            here = pl.ds(at, PAIR)
            window = pl.ds(pl.multiple_of(t * PAIR + BLK, BLK), SPAN * BLK)
            bias_here = bias_ref[t]
            for h in range(heads):
                lanes = slice(h * HD, (h + 1) * HD)
                keys = jnp.concatenate([k_pool[window, lanes], k_pool[2 * whole :, lanes]], axis=0)
                vals = jnp.concatenate([v_pool[window, lanes], v_pool[2 * whole :, lanes]], axis=0)
                query, grad = q_pool[here, lanes], g_pool[here, lanes]
                s = masked_scores(keys, query, bias_here, masks)
                probs = jnp.exp(s - lse_ref[t, h : h + 1, :])
                product = attn_ref[here, lanes].astype(jnp.float32) * grad.astype(jnp.float32)
                delta = jnp.sum(product.T, axis=0, keepdims=True)
                dprobs = dot(vals, grad, NT)
                ds = (SCALE * probs * (dprobs - delta)).astype(jnp.bfloat16)
                low = probs.astype(jnp.bfloat16)
                dq[here, lanes] = dot(ds, keys, TN).astype(jnp.bfloat16)
                dk_here = dot(ds, query, NN)
                dv_here = dot(low, grad, NN)
                dk[window, lanes] += dk_here[: SPAN * BLK]
                dv[window, lanes] += dv_here[: SPAN * BLK]
                dk[2 * whole :, lanes] += dk_here[SPAN * BLK :]
                dv[2 * whole :, lanes] += dv_here[SPAN * BLK :]
            return carry

        lax.fori_loop(0, pairs, step, 0)

        @pl.when(at_group % 2 == 1)
        def _():
            start = pl.multiple_of(2 * whole + (at_group // 2) * BLK, BLK)
            to = pl.multiple_of(offset * BLK, BLK)
            dk[pl.ds(to, BLK), :] += dk[pl.ds(start, BLK), :]
            dv[pl.ds(to, BLK), :] += dv[pl.ds(start, BLK), :]

        prev_out[0] = dk[:whole, :].astype(jnp.bfloat16)
        prev_out[1] = dv[:whole, :].astype(jnp.bfloat16)
        own_out[0] = dk[whole : 2 * whole, :]
        own_out[1] = dv[whole : 2 * whole, :]
        for k in range(group):
            at = pl.multiple_of((me ^ k) * rows, rows)
            dq_refs[k][...] = dq[pl.ds(at, rows), :]
        for index, ref in enumerate(far_outs):
            slot = jnp.maximum(at_group - index - 2, 0) // 2
            start = pl.multiple_of(2 * whole + slot * BLK, BLK)
            ref[0] = dk[pl.ds(start, BLK), :].astype(jnp.bfloat16)
            ref[1] = dv[pl.ds(start, BLK), :].astype(jnp.bfloat16)

    span = (SPAN + slots) * BLK
    outs = call(
        body, (meta,), (bias, attn, lse, *qd, *own, *prev, *far),
        [shape((rows, width))] * group
        + [shape((2, whole, width), jnp.float32), shape((2, whole, width))]
        + [shape((2, BLK, width))] * len(far),
        [
            pltpu.VMEM((everything, width), jnp.bfloat16),
            pltpu.VMEM((everything, width), jnp.bfloat16),
            pltpu.VMEM((whole, width), jnp.bfloat16),
            pltpu.VMEM((whole, width), jnp.bfloat16),
            pltpu.VMEM((everything, width), jnp.float32),
            pltpu.VMEM((everything, width), jnp.float32),
            pltpu.VMEM((whole, width), jnp.bfloat16),
        ],
        cost(10 * whole * span * width * 2, 9 * 1024 * 1024, whole * span * heads),
        "attention_back",
    )
    return outs[:group], outs[group], outs[group + 1], outs[group + 2 :]


def combine(own, returned, far, meta, group, rows):
    whole, width = own.shape[1:]

    def body(meta_ref, own_ref, ret_ref, *refs):
        far_refs, outs, acc = refs[: len(far)], refs[len(far) : -1], refs[-1]
        me, offset = meta_ref[0], meta_ref[2]
        acc[...] = own_ref[...] + ret_ref[...].astype(jnp.float32)
        at = pl.multiple_of(offset * BLK, BLK)
        for ref in far_refs:
            acc[:, pl.ds(at, BLK), :] += ref[...].astype(jnp.float32)
        for k in range(group):
            at = pl.multiple_of((me ^ k) * rows, rows)
            outs[k][...] = acc[:, pl.ds(at, rows), :].astype(jnp.bfloat16)

    return call(
        body, (meta,), (own, returned, *far), [shape((2, rows, width))] * group,
        [pltpu.VMEM((2, whole, width), jnp.float32)],
        cost(0, 4 * 1024 * 1024), "combine",
    )


def project(og, attn, meta, group, parts):
    each, rows = og[0].shape[0] // parts, og[0].shape[1]
    whole, width = attn[0].shape

    def body(meta_ref, *refs):
        og_refs, attn_refs = refs[:group], refs[group : 2 * group]
        outs, cotangent, total = refs[2 * group : -2], refs[-2], refs[-1]
        me, at_group = meta_ref[0], meta_ref[1]
        for k in range(group):
            at = pl.multiple_of((me ^ k) * rows, rows)
            cotangent[:, pl.ds(at, rows)] = og_refs[k][...]
        for k in range(group):
            at = pl.multiple_of((me ^ k) * width, width)
            total[:, pl.ds(at, width)] = dot(cotangent[...], attn_refs[k][...], NN)
        for part in range(parts):
            at = pl.multiple_of(lax.rem(at_group + part, parts) * each, each)
            outs[part][...] = total[pl.ds(at, each), :].astype(outs[part].dtype)

    full = group * width
    return call(
        body, (meta,), (*og, *attn),
        [shape((each, full), jnp.float32)] + [shape((each, full))] * (parts - 1),
        [
            pltpu.VMEM((parts * each, whole), jnp.bfloat16),
            pltpu.VMEM((parts * each, full), jnp.float32),
        ],
        cost(2 * parts * each * whole * full, 8 * 1024 * 1024), "project",
    )


def unpack(dq, dkv, meta, group):
    rows, width = dq[0].shape

    def body(meta_ref, *refs):
        q_out, k_out, v_out = refs[2 * group :]
        me = meta_ref[0]
        for k in range(group):
            at = pl.ds(pl.multiple_of((me ^ k) * width, width), width)
            q_out[:, at] = refs[k][...]
            k_out[:, at] = refs[group + k][0]
            v_out[:, at] = refs[group + k][1]

    return call(
        body, (meta,), (*dq, *dkv), [shape((rows, group * width))] * 3, [],
        cost(0, 3 * 1024 * 1024), "unpack",
    )


def listed(table, ids):
    return jnp.any(table[:, None, :] == ids[:, :, None], axis=2) & (ids >= 0)


def local(devices, queries, keys, values, out_grad, proj_weight, layout):
    rows, columns = queries.shape
    group = LOCAL * BLK // rows
    parts = devices // group
    width = columns // group
    blocks = layout.shape[0]
    slots = blocks // STRIDE
    position = lax.axis_index("seq")
    me, at_group = position % group, position // group
    offset = layout[blocks - 1, 0] % STRIDE
    meta = jnp.stack([me, at_group, offset]).astype(jnp.int32)

    def swap(piece, k):
        route = [(i, (i // group) * group + ((i % group) ^ k)) for i in range(devices)]
        return lax.ppermute(piece, "seq", route)

    def shifted(piece, distance):
        route = [
            (i, i + distance * group)
            for i in range(devices)
            if 0 <= i + distance * group < devices
        ]
        return lax.ppermute(piece, "seq", route)

    def around(piece, distance):
        return lax.ppermute(
            piece, "seq", [(i, (i + distance * group) % devices) for i in range(devices)]
        )

    def summary_route(distance, back):
        route = [
            (i, i + distance * group)
            for i in range(devices - distance * group)
            if (i // group) % 2 == 0
        ]
        return [(b, a) for a, b in route] if back else route

    def exchange(pieces):
        return [pieces[0]] + [swap(pieces[k], k) for k in range(1, group)]

    ids = at_group * LOCAL + jnp.arange(LOCAL, dtype=jnp.int32)
    table = lax.dynamic_slice_in_dim(layout, at_group * LOCAL, LOCAL, 0)
    base = ids - jnp.arange(LOCAL, dtype=jnp.int32) % 2 - (LOCAL - 1)
    near_ids = base[:, None] + jnp.arange(SPAN, dtype=jnp.int32)[None, :]
    near = listed(table, near_ids) & (near_ids >= ids[:, None] - (LOCAL - 1))
    far_ids = jnp.broadcast_to(
        jnp.arange(slots, dtype=jnp.int32)[None, :] * STRIDE + offset, (LOCAL, slots)
    )
    distant = listed(table, far_ids) & (far_ids < ids[:, None] - (LOCAL - 1))
    reads = jnp.concatenate([near, distant], axis=1)
    bias = jnp.where(reads, 0.0, -jnp.inf).astype(jnp.float32)
    bias = bias.reshape(LOCAL // 2, 2, SPAN + slots).transpose(0, 2, 1)
    bias = jnp.repeat(bias, BLK, axis=2)

    kv = pack_kv(keys, values, meta, group, width)
    own_kv = exchange(kv)
    prev_kv = [shifted(kv[0], 1)]
    qd = exchange(grads_packed(queries, out_grad, proj_weight, meta, group, width))
    prev_kv += [shifted(own_kv[k], 1) for k in range(1, group)]
    strided = pick_summary(own_kv, meta, group)
    far = [
        lax.ppermute(strided, "seq", summary_route(distance, False))
        for distance in range(2, parts)
    ]
    og = exchange(pack_out_grad(out_grad, meta, group, parts))

    attn, lse = forward(qd, own_kv, prev_kv, far, bias, meta, group, slots)
    attn_pieces = [attn] + [swap(attn, k) for k in range(1, group)]
    dq, own_grad, prev_grad, far_grad = backward(
        qd, own_kv, prev_kv, far, attn, lse, bias, meta, group, slots
    )
    returned = shifted(prev_grad, -1)
    far_back = [
        lax.ppermute(piece, "seq", summary_route(index + 2, True))
        for index, piece in enumerate(far_grad)
    ]
    dq = exchange(dq)
    partial = project(og, attn_pieces, meta, group, parts)
    arrived = [around(partial[d], d) for d in range(1, parts)]
    dkv = exchange(combine(own_grad, returned, far_back, meta, group, rows))
    query_grad, key_grad, value_grad = unpack(dq, dkv, meta, group)
    proj_grad = partial[0]
    for piece in arrived:
        proj_grad = proj_grad + piece.astype(jnp.float32)
    return (query_grad, key_grad, value_grad, proj_grad)


def solution(mesh):
    split = P(("dp", "seq"), "head")
    return jax.shard_map(
        functools.partial(local, mesh.shape["seq"]),
        mesh=mesh,
        in_specs=(split, split, split, P(("dp", "seq"), None), P(None, "head"), P()),
        out_specs=(split, split, split, split),
        check_vma=False,
    )
```

time: 1010 us -> 197 us (0.20)
  waiting for transfers between devices: 768 us -> 92.7 us
  local copies, waits for them, and re-layouts: 97.2 us -> 8.43 us
  matrix products: 67.4 us -> 0 us
  Pallas kernels: 0 us -> 42.1 us
  between operations: 17.8 us -> 2.88 us
  other arithmetic: 13.3 us -> 2.66 us
    reduce_scatter x1 -> x0, waiting for transfers between devices: 359 us -> none  [local(): lax.psum_scatter(lax.dot_general(out_grad, attn_out, (((0,), (0,)), ((),...]
    psum x3 -> x0, waiting for transfers between devices: 302 us -> none  [the longest x2 224 us: broadcast(): return lax.psum(jnp.where(mine, array, jnp.zeros_like(array)), axis)]
    dot_general x26 -> x0, matrix products: 67.4 us -> none  [the longest x2 10.2 us: query_step(): jnp.einsum('hac,ahd->chd', near_dscore, query_rows, preferred_element_typ...]
    pallas_call x0 -> x9, Pallas kernels: none -> 42.1 us  [the longest x8 35 us: call(): pl.pallas_call(body, out_shape=outs, in_specs=[SMEM] * len(scalars) + [VM...]
    unnamed x35 -> x32, local copies, waits for them, and re-layouts: 25.3 us -> 5.83 us
    reshape x9 -> x2, local copies, waits for them, and re-layouts: 17.6 us -> 0.06 us  [local(): bias = jnp.repeat(bias, BLK, axis=2)]
    ppermute x16 -> x30, waiting for transfers between devices: 107 us -> 92.7 us  [the longest x2 62.8 us: local(): lax.ppermute(piece, 'seq', summary_route(index + 2, True))]
    ppermute x16 -> x30, starting transfers between devices: 38.4 us -> 47.3 us  [the longest x18 22.9 us: swap(): return lax.ppermute(piece, 'seq', route)]
  transfers between devices with their start and end apart: 20 -> 30, of which waited for: 9 -> 12; matrix products, arithmetic and copies ran while one was open for 8% -> 2% of each run, Pallas kernels for 0% -> 17%
where the time goes in v1:
time: 197 us; the launch traced here: 196 us
  waiting for transfers between devices  92.7 us (47%)
  starting transfers between devices  47.3 us (24%)
  Pallas kernels  42.1 us (21%)
  local copies, waits for them, and re-layouts  8.43 us (4%)
  between operations  2.88 us (1%)
  other arithmetic  2.66 us (1%)
    ppermute x2, waiting for transfers between devices, local(): lax.ppermute(piece, 'seq', summary_route(index + 2, True))  62.8 us
    pallas_call x8, Pallas kernels, call(): pl.pallas_call(body, out_shape=outs, in_specs=[SMEM] * len(scalars) + [VM...  35 us
    ppermute x18, waiting for transfers between devices, swap(): return lax.ppermute(piece, 'seq', route)  26 us
    ppermute x18, starting transfers between devices, swap(): return lax.ppermute(piece, 'seq', route)  22.9 us
    ppermute x5, starting transfers between devices, shifted(): return lax.ppermute(piece, 'seq', route)  11.1 us
    pallas_call x1, Pallas kernels, grads_packed(): pl.pallas_call(body, out_shape=[shape((2, rows, width))] * group, grid_sp...  7.09 us
    unnamed x32, local copies, waits for them, and re-layouts  5.83 us
    ppermute x3, starting transfers between devices, around(): lax.ppermute(piece, 'seq', [(i, (i + distance * group) % devices) for i i...  5.53 us
  transfers between devices with their start and end apart: 30, of which 12 were waited for; matrix products, arithmetic and copies ran while one was open for 2% of the time, Pallas kernels for 17%

profile of v1, /device:TPU:0, one launch (start us, length us, event | category | flops | bytes accessed | tf_op | source)
XLA Modules:
  0.0 196.0 jit_solution(10133605500524427905)
XLA Ops:
  4.0 1.6 copy-done
  6.6 7.1 %attn_grad.1 = (bf16[2,256,256]{2,1,0:T(8,128)(2,1)S(1)}, bf16[2,256,256]{2,1,0:T(8,128)(2,1)}, bf16[2,256,256]{2,1,0:T(8,128)(2,1)}, bf16[2,256,256]{2,1,0:T(8,128)(2,1)S(1)}) custom-call(s32[3]{0:T(128)S(1)} %pad_add_fusion.meta_ref, bf16[256,1024]{1,0:T(8,128)(2,1)S(1)} %copy-done.3, bf16[256,4096]{1,0:T(8,128)(2,1)S(1)} %copy-done, bf16[4096,1024]{1,0:T(8,128)(2,1)} %w_ref.1), custom_call_target="tpu_custom_call" | custom-call | flops 2147483648 | bytes 12582912 | tf_op jit(solution)/shard_map/attn_grad/pallas_call | solution.py:84
  13.7 2.9 %collective-permute-start = (bf16[2,256,256]{2,1,0:T(8,128)(2,1)}, bf16[2,256,256]{2,1,0:T(8,128)(2,1)}, u32[]{:S(2)}, u32[]{:S(2)}) collective-permute-start(bf16[2,256,256]{2,1,0:T(8,128)(2,1)} %get-tuple-element.38), channel_id=1, source_target_pairs={{0,2},{2,0},{4,6},{6,4},{8,10},{10,8},{12,14},{14,12},{16,18},{18,... | collective-permute-start | bytes 786440 | tf_op jit(solution)/shard_map/ppermute | solution.py:427
  16.6 1.5 collective-permute-start.1
  18.2 1.5 pack_kv.1
  20.3 2.9 %collective-permute-start.5 = (bf16[2,256,256]{2,1,0:T(8,128)(2,1)}, bf16[2,256,256]{2,1,0:T(8,128)(2,1)S(1)}, u32[]{:S(2)}, u32[]{:S(2)}) collective-permute-start(bf16[2,256,256]{2,1,0:T(8,128)(2,1)} %get-tuple-element.44), channel_id=1, source_target_pairs={{0,6},{2,4},{4,2},{6,0},{8,14},{10,12},{12,10},{14,8},{16,22},{18,... | collective-permute-start | bytes 786440 | tf_op jit(solution)/shard_map/ppermute | solution.py:427
  23.9 5.7 %collective-permute-done.3.refs_1_.refs_5_ = bf16[2,256,256]{2,1,0:T(8,128)(2,1)S(1)} collective-permute-done((bf16[2,256,256]{2,1,0:T(8,128)(2,1)}, bf16[2,256,256]{2,1,0:T(8,128)(2,1)S(1)}, u32[]{:S(2)}, u32[]{:S(2)}) %collective-permute-start.3) | collective-permute-done | bytes 262176 | tf_op jit(solution)/shard_map/ppermute | solution.py:427
  29.6 3.0 %collective-permute-start.2 = (bf16[2,256,256]{2,1,0:T(8,128)(2,1)}, bf16[2,256,256]{2,1,0:T(8,128)(2,1)}, u32[]{:S(2)}, u32[]{:S(2)}) collective-permute-start(bf16[2,256,256]{2,1,0:T(8,128)(2,1)} %copy-done.11), channel_id=1, source_target_pairs={{0,6},{2,4},{4,2},{6,0},{8,14},{10,12},{12,10},{14,8},{16,22},{18,... | collective-permute-start | bytes 786440 | tf_op jit(solution)/shard_map/ppermute | solution.py:427
  32.6 8.8 %collective-permute-done.4.refs_2_.refs_6_ = bf16[2,256,256]{2,1,0:T(8,128)(2,1)S(1)} collective-permute-done((bf16[2,256,256]{2,1,0:T(8,128)(2,1)}, bf16[2,256,256]{2,1,0:T(8,128)(2,1)S(1)}, u32[]{:S(2)}, u32[]{:S(2)}) %collective-permute-start.4) | collective-permute-done | bytes 262176 | tf_op jit(solution)/shard_map/ppermute | solution.py:427
  41.5 4.2 %collective-permute-start.6 = (bf16[2,256,256]{2,1,0:T(8,128)(2,1)S(1)}, bf16[2,256,256]{2,1,0:T(8,128)(2,1)}, u32[]{:S(2)}, u32[]{:S(2)}) collective-permute-start(bf16[2,256,256]{2,1,0:T(8,128)(2,1)S(1)} %get-tuple-element.41.refs_0_.refs_4_), channel_id=1, source_target_pairs={{0,8},{2,10},{4,12},{6,14},{8,16},{10,18},{12,20},{14,22},{16,24},... | collective-permute-start | bytes 786440 | tf_op jit(solution)/shard_map/ppermute | solution.py:435
  46.2 3.3 %collective-permute-start.11 = (bf16[2,128,256]{2,1,0:T(8,128)(2,1)S(1)}, bf16[2,128,256]{2,1,0:T(8,128)(2,1)}, u32[]{:S(2)}, u32[]{:S(2)}) collective-permute-start(bf16[2,128,256]{2,1,0:T(8,128)(2,1)S(1)} %pick_summary.1), channel_id=1, source_target_pairs={{0,24},{2,26},{4,28},{6,30},{1,25},{3,27},{5,29},{7,31}} | collective-permute-start | bytes 393224 | tf_op jit(solution)/shard_map/ppermute | solution.py:474
  55.5 1.8 collective-permute-start.10
  58.6 2.5 %collective-permute-start.8 = (bf16[2,256,256]{2,1,0:T(8,128)(2,1)S(1)}, bf16[2,256,256]{2,1,0:T(8,128)(2,1)S(1)}, u32[]{:S(2)}, u32[]{:S(2)}) collective-permute-start(bf16[2,256,256]{2,1,0:T(8,128)(2,1)S(1)} %collective-permute-done.4.refs_2_.refs_6_), channel_id=1, source_target_pairs={{0,8},{2,10},{4,12},{6,14},{8,16},{10,18},{12,20},{14,22},{16,24},... | collective-permute-start | bytes 786440 | tf_op jit(solution)/shard_map/ppermute | solution.py:435
  61.1 1.9 collective-permute-start.9
  63.5 2.1 %collective-permute-start.22 = (bf16[1024,256]{1,0:T(8,128)(2,1)}, bf16[1024,256]{1,0:T(8,128)(2,1)S(1)}, u32[]{:S(2)}, u32[]{:S(2)}) collective-permute-start(bf16[1024,256]{1,0:T(8,128)(2,1)} %copy-done.9), channel_id=1, source_target_pairs={{0,4},{2,6},{4,0},{6,2},{8,12},{10,14},{12,8},{14,10},{16,20},{18,... | collective-permute-start | bytes 1572872 | tf_op jit(solution)/shard_map/ppermute | solution.py:427
  65.6 1.4 collective-permute-start.23
  68.1 2.8 %collective-permute-done.9.refs_11_ = bf16[2,256,256]{2,1,0:T(8,128)(2,1)S(1)} collective-permute-done((bf16[2,256,256]{2,1,0:T(8,128)(2,1)S(1)}, bf16[2,256,256]{2,1,0:T(8,128)(2,1)S(1)}, u32[]{:S(2)}, u32[]{:S(2)}) %collective-permute-start.9) | collective-permute-done | bytes 262176 | tf_op jit(solution)/shard_map/ppermute | solution.py:435
  70.9 12.0 %attention.1 = (bf16[1024,256]{1,0:T(8,128)(2,1)S(1)}, f32[4,2,256]{2,1,0:T(2,128)S(1)}) custom-call(s32[3]{0:T(128)S(1)} %pad_add_fusion.meta_ref, f32[4,11,256]{2,1,0:T(8,128)S(1)} %copy.26.bias_ref, bf16[2,256,256]{2,1,0:T(8,128)(2,1)S(1)} %get-tuple-element.37.refs_0_, bf16[2,256,256]{2,1,0:T(8,128)(2,1)} %collective-permute-done.refs_1_, ...), custom_call_target="tpu_custom_call" | custom-call | flops 2952790016 | bytes 5242880 | tf_op jit(solution)/shard_map/attention/pallas_call | solution.py:43
  84.3 2.1 %collective-permute-start.24 = (bf16[1024,256]{1,0:T(8,128)(2,1)S(1)}, bf16[1024,256]{1,0:T(8,128)(2,1)S(1)}, u32[]{:S(2)}, u32[]{:S(2)}) collective-permute-start(bf16[1024,256]{1,0:T(8,128)(2,1)S(1)} %get-tuple-element.45.attn_ref.refs_4_), channel_id=1, source_target_pairs={{0,2},{2,0},{4,6},{6,4},{8,10},{10,8},{12,14},{14,12},{16,18},{18,... | collective-permute-start | bytes 1572872 | tf_op jit(solution)/shard_map/ppermute | solution.py:427
  86.5 12.4 %attention_back.1 = (bf16[256,256]{1,0:T(8,128)(2,1)S(1)}, bf16[256,256]{1,0:T(8,128)(2,1)S(1)}, bf16[256,256]{1,0:T(8,128)(2,1)S(1)}, bf16[256,256]{1,0:T(8,128...) custom-call(s32[3]{0:T(128)S(1)} %pad_add_fusion.meta_ref, ...), custom_call_target="tpu_custom_call" | custom-call | flops 7381975040 | bytes 9437184 | tf_op jit(solution)/shard_map/attention_back/pallas_call | solution.py:43
  100.2 2.0 %collective-permute-done.25.refs_6_ = bf16[1024,256]{1,0:T(8,128)(2,1)S(1)} collective-permute-done((bf16[1024,256]{1,0:T(8,128)(2,1)S(1)}, bf16[1024,256]{1,0:T(8,128)(2,1)S(1)}, u32[]{:S(2)}, u32[]{:S(2)}) %collective-permute-start.25) | collective-permute-done | bytes 524320 | tf_op jit(solution)/shard_map/ppermute | solution.py:427
  102.2 4.5 %project.1 = (f32[256,1024]{1,0:T(8,128)}, bf16[256,1024]{1,0:T(8,128)(2,1)S(1)}, bf16[256,1024]{1,0:T(8,128)(2,1)S(1)}, bf16[256,1024]{1,0:T(8,128)(2,1)S(1)}) custom-call(s32[3]{0:T(128)S(1)} %pad_add_fusion.meta_ref, bf16[1024,256]{1,0:T(8,128)(2,1)S(1)} %copy-done.7, bf16[1024,256]{1,0:T(8,128)(2,1)S(1)} %collective-permute-done.21.refs_1_, ...), custom_call_target="tpu_custom_call" | custom-call | flops 2147483648 | bytes 8388608 | tf_op jit(solution)/shard_map/project/pallas_call | solution.py:43
  106.7 1.6 collective-permute-start.27
  108.3 1.6 collective-permute-start.28
  109.9 2.3 %collective-permute-start.29 = (bf16[256,1024]{1,0:T(8,128)(2,1)S(1)}, bf16[256,1024]{1,0:T(8,128)(2,1)S(1)}, u32[]{:S(2)}, u32[]{:S(2)}) collective-permute-start(bf16[256,1024]{1,0:T(8,128)(2,1)S(1)} %get-tuple-element.69), channel_id=1, source_target_pairs={{0,24},{2,26},{4,28},{6,30},{8,0},{10,2},{12,4},{14,6},{16,8},{18,... | collective-permute-start | bytes 1572872 | tf_op jit(solution)/shard_map/ppermute | solution.py:438
  113.6 55.5 %collective-permute-done.16.refs_0_ = bf16[2,128,256]{2,1,0:T(8,128)(2,1)S(1)} collective-permute-done((bf16[2,128,256]{2,1,0:T(8,128)(2,1)S(1)}, bf16[2,128,256]{2,1,0:T(8,128)(2,1)S(1)}, u32[]{:S(2)}, u32[]{:S(2)}) %collective-permute-start.16) | collective-permute-done | bytes 131104 | tf_op jit(solution)/shard_map/ppermute | solution.py:486
  170.3 7.4 %collective-permute-done.17.refs_1_ = bf16[2,128,256]{2,1,0:T(8,128)(2,1)S(1)} collective-permute-done((bf16[2,128,256]{2,1,0:T(8,128)(2,1)S(1)}, bf16[2,128,256]{2,1,0:T(8,128)(2,1)S(1)}, u32[]{:S(2)}, u32[]{:S(2)}) %collective-permute-start.17) | collective-permute-done | bytes 131104 | tf_op jit(solution)/shard_map/ppermute | solution.py:486
  179.6 3.1 %collective-permute-done.12.refs_1_ = bf16[256,256]{1,0:T(8,128)(2,1)S(1)} collective-permute-done((bf16[256,256]{1,0:T(8,128)(2,1)S(1)}, bf16[256,256]{1,0:T(8,128)(2,1)S(1)}, u32[]{:S(2)}, u32[]{:S(2)}) %collective-permute-start.12) | collective-permute-done | bytes 131104 | tf_op jit(solution)/shard_map/ppermute | solution.py:427
  184.4 1.7 collective-permute-start.19
  188.6 1.6 collective-permute-done.18.refs_5_
  190.1 2.7 %collective-permute-done.19.refs_6_ = bf16[2,256,256]{2,1,0:T(8,128)(2,1)S(1)} collective-permute-done((bf16[2,256,256]{2,1,0:T(8,128)(2,1)S(1)}, bf16[2,256,256]{2,1,0:T(8,128)(2,1)S(1)}, u32[]{:S(2)}, u32[]{:S(2)}) %collective-permute-start.19) | collective-permute-done | bytes 262176 | tf_op jit(solution)/shard_map/ppermute | solution.py:427
  194.1 1.9 unpack.1
  (92 shorter events, 25.5 us)
Async XLA Ops:
  13.7 41.7 %collective-permute-start = (bf16[2,256,256]{2,1,0:T(8,128)(2,1)}, bf16[2,256,256]{2,1,0:T(8,128)(2,1)}, u32[]{:S(2)}, u32[]{:S(2)}) collective-permute-start(bf16[2,256,256]{2,1,0:T(8,128)(2,1)} %get-tuple-element.38), channel_id=1, source_target_pairs={{0,2},{2,0},{4,6},{6,4},{8,10},{10,8},{12,14},{14,12},{16,18},{18,... | collective-permute-start | bytes 786440 | tf_op jit(solution)/shard_map/ppermute | solution.py:427
  16.6 38.8 %collective-permute-start.1 = (bf16[2,256,256]{2,1,0:T(8,128)(2,1)}, bf16[2,256,256]{2,1,0:T(8,128)(2,1)}, u32[]{:S(2)}, u32[]{:S(2)}) collective-permute-start(bf16[2,256,256]{2,1,0:T(8,128)(2,1)} %get-tuple-element.39), channel_id=1, source_target_pairs={{0,4},{2,6},{4,0},{6,2},{8,12},{10,14},{12,8},{14,10},{16,20},{18,... | collective-permute-start | bytes 786440 | tf_op jit(solution)/shard_map/ppermute | solution.py:427
  19.7 9.9 %collective-permute-start.3 = (bf16[2,256,256]{2,1,0:T(8,128)(2,1)}, bf16[2,256,256]{2,1,0:T(8,128)(2,1)S(1)}, u32[]{:S(2)}, u32[]{:S(2)}) collective-permute-start(bf16[2,256,256]{2,1,0:T(8,128)(2,1)} %get-tuple-element.42), channel_id=1, source_target_pairs={{0,2},{2,0},{4,6},{6,4},{8,10},{10,8},{12,14},{14,12},{16,18},{18,... | collective-permute-start | bytes 786440 | tf_op jit(solution)/shard_map/ppermute | solution.py:427
  20.2 21.2 %collective-permute-start.4 = (bf16[2,256,256]{2,1,0:T(8,128)(2,1)}, bf16[2,256,256]{2,1,0:T(8,128)(2,1)S(1)}, u32[]{:S(2)}, u32[]{:S(2)}) collective-permute-start(bf16[2,256,256]{2,1,0:T(8,128)(2,1)} %get-tuple-element.43), channel_id=1, source_target_pairs={{0,4},{2,6},{4,0},{6,2},{8,12},{10,14},{12,8},{14,10},{16,20},{18,... | collective-permute-start | bytes 786440 | tf_op jit(solution)/shard_map/ppermute | solution.py:427
  20.3 25.4 %collective-permute-start.5 = (bf16[2,256,256]{2,1,0:T(8,128)(2,1)}, bf16[2,256,256]{2,1,0:T(8,128)(2,1)S(1)}, u32[]{:S(2)}, u32[]{:S(2)}) collective-permute-start(bf16[2,256,256]{2,1,0:T(8,128)(2,1)} %get-tuple-element.44), channel_id=1, source_target_pairs={{0,6},{2,4},{4,2},{6,0},{8,14},{10,12},{12,10},{14,8},{16,22},{18,... | collective-permute-start | bytes 786440 | tf_op jit(solution)/shard_map/ppermute | solution.py:427
  29.6 27.7 %collective-permute-start.2 = (bf16[2,256,256]{2,1,0:T(8,128)(2,1)}, bf16[2,256,256]{2,1,0:T(8,128)(2,1)}, u32[]{:S(2)}, u32[]{:S(2)}) collective-permute-start(bf16[2,256,256]{2,1,0:T(8,128)(2,1)} %copy-done.11), channel_id=1, source_target_pairs={{0,6},{2,4},{4,2},{6,0},{8,14},{10,12},{12,10},{14,8},{16,22},{18,... | collective-permute-start | bytes 786440 | tf_op jit(solution)/shard_map/ppermute | solution.py:427
  41.5 17.2 %collective-permute-start.6 = (bf16[2,256,256]{2,1,0:T(8,128)(2,1)S(1)}, bf16[2,256,256]{2,1,0:T(8,128)(2,1)}, u32[]{:S(2)}, u32[]{:S(2)}) collective-permute-start(bf16[2,256,256]{2,1,0:T(8,128)(2,1)S(1)} %get-tuple-element.41.refs_0_.refs_4_), channel_id=1, source_target_pairs={{0,8},{2,10},{4,12},{6,14},{8,16},{10,18},{12,20},{14,22},{16,24},... | collective-permute-start | bytes 786440 | tf_op jit(solution)/shard_map/ppermute | solution.py:435
  46.2 14.9 %collective-permute-start.11 = (bf16[2,128,256]{2,1,0:T(8,128)(2,1)S(1)}, bf16[2,128,256]{2,1,0:T(8,128)(2,1)}, u32[]{:S(2)}, u32[]{:S(2)}) collective-permute-start(bf16[2,128,256]{2,1,0:T(8,128)(2,1)S(1)} %pick_summary.1), channel_id=1, source_target_pairs={{0,24},{2,26},{4,28},{6,30},{1,25},{3,27},{5,29},{7,31}} | collective-permute-start | bytes 393224 | tf_op jit(solution)/shard_map/ppermute | solution.py:474
  55.4 28.9 %collective-permute-start.21 = (bf16[1024,256]{1,0:T(8,128)(2,1)}, bf16[1024,256]{1,0:T(8,128)(2,1)S(1)}, u32[]{:S(2)}, u32[]{:S(2)}) collective-permute-start(bf16[1024,256]{1,0:T(8,128)(2,1)} %copy-done.10), channel_id=1, source_target_pairs={{0,2},{2,0},{4,6},{6,4},{8,10},{10,8},{12,14},{14,12},{16,18},{18,... | collective-permute-start | bytes 1572872 | tf_op jit(solution)/shard_map/ppermute | solution.py:427
  55.5 8.1 %collective-permute-start.10 = (bf16[2,128,256]{2,1,0:T(8,128)(2,1)S(1)}, bf16[2,128,256]{2,1,0:T(8,128)(2,1)S(1)}, u32[]{:S(2)}, u32[]{:S(2)}) collective-permute-start(bf16[2,128,256]{2,1,0:T(8,128)(2,1)S(1)} %pick_summary.1), channel_id=1, source_target_pairs={{0,16},{2,18},{4,20},{6,22},{1,17},{3,19},{5,21},{7,23}} | collective-permute-start | bytes 393224 | tf_op jit(solution)/shard_map/ppermute | solution.py:474
  57.3 8.3 %collective-permute-start.7 = (bf16[2,256,256]{2,1,0:T(8,128)(2,1)S(1)}, bf16[2,256,256]{2,1,0:T(8,128)(2,1)S(1)}, u32[]{:S(2)}, u32[]{:S(2)}) collective-permute-start(bf16[2,256,256]{2,1,0:T(8,128)(2,1)S(1)} %collective-permute-done.3.refs_1_.refs_5_), channel_id=1, source_target_pairs={{0,8},{2,10},{4,12},{6,14},{8,16},{10,18},{12,20},{14,22},{16,24},... | collective-permute-start | bytes 786440 | tf_op jit(solution)/shard_map/ppermute | solution.py:435
  58.6 9.4 %collective-permute-start.8 = (bf16[2,256,256]{2,1,0:T(8,128)(2,1)S(1)}, bf16[2,256,256]{2,1,0:T(8,128)(2,1)S(1)}, u32[]{:S(2)}, u32[]{:S(2)}) collective-permute-start(bf16[2,256,256]{2,1,0:T(8,128)(2,1)S(1)} %collective-permute-done.4.refs_2_.refs_6_), channel_id=1, source_target_pairs={{0,8},{2,10},{4,12},{6,14},{8,16},{10,18},{12,20},{14,22},{16,24},... | collective-permute-start | bytes 786440 | tf_op jit(solution)/shard_map/ppermute | solution.py:435
  61.1 9.8 %collective-permute-start.9 = (bf16[2,256,256]{2,1,0:T(8,128)(2,1)S(1)}, bf16[2,256,256]{2,1,0:T(8,128)(2,1)S(1)}, u32[]{:S(2)}, u32[]{:S(2)}) collective-permute-start(bf16[2,256,256]{2,1,0:T(8,128)(2,1)S(1)} %collective-permute-done.5.refs_3_.refs_7_), channel_id=1, source_target_pairs={{0,8},{2,10},{4,12},{6,14},{8,16},{10,18},{12,20},{14,22},{16,24},... | collective-permute-start | bytes 786440 | tf_op jit(solution)/shard_map/ppermute | solution.py:435
  63.5 35.3 %collective-permute-start.22 = (bf16[1024,256]{1,0:T(8,128)(2,1)}, bf16[1024,256]{1,0:T(8,128)(2,1)S(1)}, u32[]{:S(2)}, u32[]{:S(2)}) collective-permute-start(bf16[1024,256]{1,0:T(8,128)(2,1)} %copy-done.9), channel_id=1, source_target_pairs={{0,4},{2,6},{4,0},{6,2},{8,12},{10,14},{12,8},{14,10},{16,20},{18,... | collective-permute-start | bytes 1572872 | tf_op jit(solution)/shard_map/ppermute | solution.py:427
  65.6 34.5 %collective-permute-start.23 = (bf16[1024,256]{1,0:T(8,128)(2,1)}, bf16[1024,256]{1,0:T(8,128)(2,1)S(1)}, u32[]{:S(2)}, u32[]{:S(2)}) collective-permute-start(bf16[1024,256]{1,0:T(8,128)(2,1)} %copy-done.8), channel_id=1, source_target_pairs={{0,6},{2,4},{4,2},{6,0},{8,14},{10,12},{12,10},{14,8},{16,22},{18,... | collective-permute-start | bytes 1572872 | tf_op jit(solution)/shard_map/ppermute | solution.py:427
  82.9 17.3 %collective-permute-start.26 = (bf16[1024,256]{1,0:T(8,128)(2,1)S(1)}, bf16[1024,256]{1,0:T(8,128)(2,1)S(1)}, u32[]{:S(2)}, u32[]{:S(2)}) collective-permute-start(bf16[1024,256]{1,0:T(8,128)(2,1)S(1)} %get-tuple-element.45.attn_ref.refs_4_), channel_id=1, source_target_pairs={{0,6},{2,4},{4,2},{6,0},{8,14},{10,12},{12,10},{14,8},{16,22},{18,... | collective-permute-start | bytes 1572872 | tf_op jit(solution)/shard_map/ppermute | solution.py:427
  83.5 18.7 %collective-permute-start.25 = (bf16[1024,256]{1,0:T(8,128)(2,1)S(1)}, bf16[1024,256]{1,0:T(8,128)(2,1)S(1)}, u32[]{:S(2)}, u32[]{:S(2)}) collective-permute-start(bf16[1024,256]{1,0:T(8,128)(2,1)S(1)} %get-tuple-element.45.attn_ref.refs_4_), channel_id=1, source_target_pairs={{0,4},{2,6},{4,0},{6,2},{8,12},{10,14},{12,8},{14,10},{16,20},{18,... | collective-permute-start | bytes 1572872 | tf_op jit(solution)/shard_map/ppermute | solution.py:427
  84.3 17.9 %collective-permute-start.24 = (bf16[1024,256]{1,0:T(8,128)(2,1)S(1)}, bf16[1024,256]{1,0:T(8,128)(2,1)S(1)}, u32[]{:S(2)}, u32[]{:S(2)}) collective-permute-start(bf16[1024,256]{1,0:T(8,128)(2,1)S(1)} %get-tuple-element.45.attn_ref.refs_4_), channel_id=1, source_target_pairs={{0,2},{2,0},{4,6},{6,4},{8,10},{10,8},{12,14},{14,12},{16,18},{18,... | collective-permute-start | bytes 1572872 | tf_op jit(solution)/shard_map/ppermute | solution.py:427
  98.9 79.1 %collective-permute-start.15 = (bf16[2,1024,256]{2,1,0:T(8,128)(2,1)S(1)}, bf16[2,1024,256]{2,1,0:T(8,128)(2,1)S(1)}, u32[]{:S(2)}, u32[]{:S(2)}) collective-permute-start(bf16[2,1024,256]{2,1,0:T(8,128)(2,1)S(1)} %get-tuple-element.52), channel_id=1, source_target_pairs={{8,0},{10,2},{12,4},{14,6},{16,8},{18,10},{20,12},{22,14},{24,16},... | collective-permute-start | bytes 3145736 | tf_op jit(solution)/shard_map/ppermute | solution.py:435
  102.2 76.4 %copy-start.2 = (f32[2,1024,256]{2,1,0:T(8,128)S(1)}, f32[2,1024,256]{2,1,0:T(8,128)}, u32[]{:S(2)}) copy-start(f32[2,1024,256]{2,1,0:T(8,128)} %get-tuple-element.51.own_ref) | copy-start | bytes 6291460
  106.7 79.8 %copy-start.12 = (f32[256,1024]{1,0:T(8,128)S(1)}, f32[256,1024]{1,0:T(8,128)}, u32[]{:S(2)}) copy-start(f32[256,1024]{1,0:T(8,128)} %get-tuple-element.66) | copy-start | bytes 3145732
  106.7 76.3 %collective-permute-start.27 = (bf16[256,1024]{1,0:T(8,128)(2,1)S(1)}, bf16[256,1024]{1,0:T(8,128)(2,1)S(1)}, u32[]{:S(2)}, u32[]{:S(2)}) collective-permute-start(bf16[256,1024]{1,0:T(8,128)(2,1)S(1)} %get-tuple-element.67), channel_id=1, source_target_pairs={{0,8},{2,10},{4,12},{6,14},{8,16},{10,18},{12,20},{14,22},{16,24},... | collective-permute-start | bytes 1572872 | tf_op jit(solution)/shard_map/ppermute | solution.py:438
  108.3 76.1 %collective-permute-start.28 = (bf16[256,1024]{1,0:T(8,128)(2,1)S(1)}, bf16[256,1024]{1,0:T(8,128)(2,1)S(1)}, u32[]{:S(2)}, u32[]{:S(2)}) collective-permute-start(bf16[256,1024]{1,0:T(8,128)(2,1)S(1)} %get-tuple-element.68), channel_id=1, source_target_pairs={{0,16},{2,18},{4,20},{6,22},{8,24},{10,26},{12,28},{14,30},{16,0},... | collective-permute-start | bytes 1572872 | tf_op jit(solution)/shard_map/ppermute | solution.py:438
  109.9 76.2 %collective-permute-start.29 = (bf16[256,1024]{1,0:T(8,128)(2,1)S(1)}, bf16[256,1024]{1,0:T(8,128)(2,1)S(1)}, u32[]{:S(2)}, u32[]{:S(2)}) collective-permute-start(bf16[256,1024]{1,0:T(8,128)(2,1)S(1)} %get-tuple-element.69), channel_id=1, source_target_pairs={{0,24},{2,26},{4,28},{6,30},{8,0},{10,2},{12,4},{14,6},{16,8},{18,... | collective-permute-start | bytes 1572872 | tf_op jit(solution)/shard_map/ppermute | solution.py:438
  112.3 56.8 %collective-permute-start.16 = (bf16[2,128,256]{2,1,0:T(8,128)(2,1)S(1)}, bf16[2,128,256]{2,1,0:T(8,128)(2,1)S(1)}, u32[]{:S(2)}, u32[]{:S(2)}) collective-permute-start(bf16[2,128,256]{2,1,0:T(8,128)(2,1)S(1)} %get-tuple-element.53), channel_id=1, source_target_pairs={{16,0},{18,2},{20,4},{22,6},{17,1},{19,3},{21,5},{23,7}} | collective-permute-start | bytes 393224 | tf_op jit(solution)/shard_map/ppermute | solution.py:486
  169.0 8.6 %collective-permute-start.17 = (bf16[2,128,256]{2,1,0:T(8,128)(2,1)S(1)}, bf16[2,128,256]{2,1,0:T(8,128)(2,1)S(1)}, u32[]{:S(2)}, u32[]{:S(2)}) collective-permute-start(bf16[2,128,256]{2,1,0:T(8,128)(2,1)S(1)} %get-tuple-element.54), channel_id=1, source_target_pairs={{24,0},{26,2},{28,4},{30,6},{25,1},{27,3},{29,5},{31,7}} | collective-permute-start | bytes 393224 | tf_op jit(solution)/shard_map/ppermute | solution.py:486
  177.7 5.0 %collective-permute-start.12 = (bf16[256,256]{1,0:T(8,128)(2,1)S(1)}, bf16[256,256]{1,0:T(8,128)(2,1)S(1)}, u32[]{:S(2)}, u32[]{:S(2)}) collective-permute-start(bf16[256,256]{1,0:T(8,128)(2,1)S(1)} %get-tuple-element.48), channel_id=1, source_target_pairs={{0,2},{2,0},{4,6},{6,4},{8,10},{10,8},{12,14},{14,12},{16,18},{18,... | collective-permute-start | bytes 393224 | tf_op jit(solution)/shard_map/ppermute | solution.py:427
  178.0 9.8 %collective-permute-start.13 = (bf16[256,256]{1,0:T(8,128)(2,1)S(1)}, bf16[256,256]{1,0:T(8,128)(2,1)S(1)}, u32[]{:S(2)}, u32[]{:S(2)}) collective-permute-start(bf16[256,256]{1,0:T(8,128)(2,1)S(1)} %get-tuple-element.49), channel_id=1, source_target_pairs={{0,4},{2,6},{4,0},{6,2},{8,12},{10,14},{12,8},{14,10},{16,20},{18,... | collective-permute-start | bytes 393224 | tf_op jit(solution)/shard_map/ppermute | solution.py:427
  182.6 5.9 %collective-permute-start.14 = (bf16[256,256]{1,0:T(8,128)(2,1)S(1)}, bf16[256,256]{1,0:T(8,128)(2,1)S(1)}, u32[]{:S(2)}, u32[]{:S(2)}) collective-permute-start(bf16[256,256]{1,0:T(8,128)(2,1)S(1)} %get-tuple-element.50), channel_id=1, source_target_pairs={{0,6},{2,4},{4,2},{6,0},{8,14},{10,12},{12,10},{14,8},{16,22},{18,... | collective-permute-start | bytes 393224 | tf_op jit(solution)/shard_map/ppermute | solution.py:427
  183.0 7.1 %collective-permute-start.18 = (bf16[2,256,256]{2,1,0:T(8,128)(2,1)S(1)}, bf16[2,256,256]{2,1,0:T(8,128)(2,1)S(1)}, u32[]{:S(2)}, u32[]{:S(2)}) collective-permute-start(bf16[2,256,256]{2,1,0:T(8,128)(2,1)S(1)} %get-tuple-element.56), channel_id=1, source_target_pairs={{0,2},{2,0},{4,6},{6,4},{8,10},{10,8},{12,14},{14,12},{16,18},{18,... | collective-permute-start | bytes 786440 | tf_op jit(solution)/shard_map/ppermute | solution.py:427
  184.4 8.4 %collective-permute-start.19 = (bf16[2,256,256]{2,1,0:T(8,128)(2,1)S(1)}, bf16[2,256,256]{2,1,0:T(8,128)(2,1)S(1)}, u32[]{:S(2)}, u32[]{:S(2)}) collective-permute-start(bf16[2,256,256]{2,1,0:T(8,128)(2,1)S(1)} %get-tuple-element.57), channel_id=1, source_target_pairs={{0,4},{2,6},{4,0},{6,2},{8,12},{10,14},{12,8},{14,10},{16,20},{18,... | collective-permute-start | bytes 786440 | tf_op jit(solution)/shard_map/ppermute | solution.py:427
  186.1 8.0 %collective-permute-start.20 = (bf16[2,256,256]{2,1,0:T(8,128)(2,1)S(1)}, bf16[2,256,256]{2,1,0:T(8,128)(2,1)S(1)}, u32[]{:S(2)}, u32[]{:S(2)}) collective-permute-start(bf16[2,256,256]{2,1,0:T(8,128)(2,1)S(1)} %get-tuple-element.58), channel_id=1, source_target_pairs={{0,6},{2,4},{4,2},{6,0},{8,14},{10,12},{12,10},{14,8},{16,22},{18,... | collective-permute-start | bytes 786440 | tf_op jit(solution)/shard_map/ppermute | solution.py:427
  (14 other events, 121.1 us)

commit v2 on v1

v2 whole, which is shorter than its diff:
```python
import functools
import math

import jax
import jax.numpy as jnp
from jax import lax
from jax.experimental import pallas as pl
from jax.experimental.pallas import tpu as pltpu
from jax.sharding import PartitionSpec as P

HD = 128
BLK = 128
LOCAL = 8
STRIDE = 16
PAIR = 2 * BLK
SPAN = LOCAL + 1
SCALE = HD ** (-0.5)
SCALE2 = SCALE * math.log2(math.e)
VMEM_LIMIT = 48 * 1024 * 1024

NT = (((1,), (1,)), ((), ()))
NN = (((1,), (0,)), ((), ()))
TN = (((0,), (0,)), ((), ()))
SMEM = pl.BlockSpec(memory_space=pltpu.SMEM)
VMEM = pl.BlockSpec(memory_space=pltpu.VMEM)


def shape(dims, dtype=jnp.bfloat16):
    return jax.ShapeDtypeStruct(dims, dtype)


def dot(a, b, dims):
    return lax.dot_general(a, b, dims, preferred_element_type=jnp.float32)


def params():
    return pltpu.CompilerParams(vmem_limit_bytes=VMEM_LIMIT)


def cost(flops, size, exps=0):
    return pl.CostEstimate(flops=flops, bytes_accessed=size, transcendentals=exps)


def call(body, scalars, arrays, outs, scratch, estimate, name, lanes=None):
    specs = [SMEM] * len(scalars)
    for index, array in enumerate(arrays):
        block = None if lanes is None else lanes[index]
        if block is None:
            specs.append(pl.BlockSpec(array.shape, functools.partial(corner, array.ndim, 0)))
        else:
            specs.append(
                pl.BlockSpec(array.shape[:-1] + (HD,), functools.partial(corner, array.ndim, block))
            )
    return pl.pallas_call(
        body,
        grid=(1,),
        out_shape=outs,
        in_specs=specs,
        out_specs=[pl.BlockSpec(o.shape, functools.partial(corner, len(o.shape), 0)) for o in outs],
        scratch_shapes=scratch,
        compiler_params=params(),
        cost_estimate=estimate,
        name=name,
    )(*scalars, *arrays)


def corner(ndim, last, step):
    return (0,) * (ndim - 1) + (last,)


def split_refs(refs, counts):
    refs, taken = list(refs), []
    for count in counts:
        taken.append(refs[:count])
        refs = refs[count:]
    return taken, refs


def pack_kv(keys, values, meta, group, width):
    rows = keys.shape[0]

    def body(meta_ref, k_ref, v_ref, *outs):
        me = meta_ref[0]
        for k in range(group):
            at = pl.multiple_of((me ^ k) * width, width)
            outs[k][0] = k_ref[:, pl.ds(at, width)]
            outs[k][1] = v_ref[:, pl.ds(at, width)]

    return call(
        body, (meta,), (keys, values), [shape((2, rows, width))] * group, [],
        cost(0, 4 * keys.size * 2), "pack_kv",
    )


def grads_packed(queries, out_grad, proj_weight, meta, group, width):
    rows, depth = out_grad.shape

    def body(meta_ref, q_ref, og_ref, w_ref, *outs):
        step = pl.program_id(0)
        got = dot(og_ref[...], w_ref[...], NN).astype(jnp.bfloat16)
        for k in range(group):

            @pl.when(step == k)
            def _():
                outs[k][0] = q_ref[...]
                outs[k][1] = got

    return pl.pallas_call(
        body,
        out_shape=[shape((2, rows, width))] * group,
        grid_spec=pltpu.PrefetchScalarGridSpec(
            num_scalar_prefetch=1,
            grid=(group,),
            in_specs=[
                pl.BlockSpec((rows, width), lambda i, m: (0, m[0] ^ i)),
                pl.BlockSpec((rows, depth), lambda i, m: (0, 0)),
                pl.BlockSpec((depth, width), lambda i, m: (0, m[0] ^ i)),
            ],
            out_specs=[pl.BlockSpec((2, rows, width), lambda i, m: (0, 0, 0))] * group,
        ),
        compiler_params=params(),
        cost_estimate=cost(2 * rows * depth * width * group, 12 * 1024 * 1024),
        name="attn_grad",
    )(meta, queries, out_grad, proj_weight)


def pack_out_grad(out_grad, meta, group, parts):
    rows, depth = out_grad.shape
    each = depth // (group * parts)
    half = parts // 2

    def body(meta_ref, og_ref, *outs):
        me, core = meta_ref[0], meta_ref[3]
        for k in range(group):
            for part in range(half):
                at = ((core * half + part) * group + (me ^ k)) * each
                at = pl.multiple_of(at, each)
                outs[k][part * each : (part + 1) * each, :] = og_ref[:, pl.ds(at, each)].T

    return call(
        body, (meta,), (out_grad,), [shape((half * each, rows))] * group, [],
        cost(0, 3 * out_grad.size), "pack_out_grad",
    )


def join_columns(pieces, meta, group):
    height, rows = pieces[0].shape

    def body(meta_ref, *refs):
        me = meta_ref[0]
        for k in range(group):
            at = pl.multiple_of((me ^ k) * rows, rows)
            refs[group][:, pl.ds(at, rows)] = refs[k][...]

    return call(
        body, (meta,), tuple(pieces), [shape((height, group * rows))], [],
        cost(0, 2 * 1024 * 1024), "join_columns",
    )[0]


def pick_summary(pieces, meta, group):
    rows, width = pieces[0].shape[1:]

    def body(meta_ref, *refs):
        me, at = meta_ref[0], meta_ref[2] * BLK
        out = refs[group]
        for k in range(group):

            @pl.when(at // rows == (me ^ k))
            def _():
                start = pl.multiple_of(at % rows, BLK)
                out[...] = refs[k][:, pl.ds(start, BLK), :]

    return call(
        body, (meta,), tuple(pieces), [shape((2, BLK, width))], [],
        cost(0, 2 * 1024 * 1024), "pick_summary",
    )[0]


def fill_pools(meta_ref, own, prev, far, k_pool, v_pool, group, rows, slots):
    me, at_group, offset = meta_ref[0], meta_ref[1], meta_ref[2]
    whole = group * rows
    for k in range(group):
        at = pl.multiple_of((me ^ k) * rows, rows)
        k_pool[pl.ds(at, rows), :] = prev[k][0]
        v_pool[pl.ds(at, rows), :] = prev[k][1]
        k_pool[pl.ds(whole + at, rows), :] = own[k][0]
        v_pool[pl.ds(whole + at, rows), :] = own[k][1]
    tail = jnp.zeros((slots * BLK, k_pool.shape[1]), k_pool.dtype)
    k_pool[2 * whole :, :] = tail
    v_pool[2 * whole :, :] = tail

    @pl.when(at_group % 2 == 1)
    def _():
        to = pl.multiple_of(2 * whole + (at_group // 2) * BLK, BLK)
        start = pl.multiple_of(offset * BLK, BLK)
        k_pool[pl.ds(to, BLK), :] = k_pool[pl.ds(start, BLK), :]
        v_pool[pl.ds(to, BLK), :] = v_pool[pl.ds(start, BLK), :]

    for index, ref in enumerate(far):
        distance = index + 2

        @pl.when((at_group >= distance) & ((at_group - distance) % 2 == 0))
        def _():
            to = pl.multiple_of(2 * whole + ((at_group - distance) // 2) * BLK, BLK)
            k_pool[pl.ds(to, BLK), :] = ref[0]
            v_pool[pl.ds(to, BLK), :] = ref[1]


def fill_queries(meta_ref, qd, q_pool, g_pool, group, rows):
    me = meta_ref[0]
    for k in range(group):
        at = pl.multiple_of((me ^ k) * rows, rows)
        q_pool[pl.ds(at, rows), :] = qd[k][0]
        g_pool[pl.ds(at, rows), :] = qd[k][1]


def causal_masks():
    key_at = lax.broadcasted_iota(jnp.int32, (BLK, PAIR), 0)
    query_at = lax.broadcasted_iota(jnp.int32, (BLK, PAIR), 1)
    first = (key_at <= query_at) | (query_at >= BLK)
    second = key_at <= query_at - BLK
    return first, second


def masked_scores(keys, query, bias, masks):
    raw = dot(keys, query, NT) * SCALE2
    tiles = []
    for j in range(keys.shape[0] // BLK):
        tile = raw[j * BLK : (j + 1) * BLK] + bias[j]
        if masks is not None and j in (LOCAL - 1, LOCAL):
            tile = jnp.where(masks[j - LOCAL + 1], tile, -jnp.inf)
        tiles.append(tile)
    return jnp.concatenate(tiles, axis=0)


def bias_rows(bias_ref, t, picked):
    return [bias_ref[t, j : j + 1, :] for j in picked]


def forward(head, qd, own, prev, far, bias, stats, meta, group, slots):
    rows = qd[0].shape[1]
    whole = group * rows
    pairs = whole // PAIR
    counts = (group, group, group, len(far))

    def body(meta_ref, bias_ref, before_ref, *refs):
        (qd_refs, own_refs, prev_refs, far_refs), refs = split_refs(refs, counts)
        out_ref, stats_ref, k_pool, v_pool, q_pool, g_pool = refs
        fill_pools(meta_ref, own_refs, prev_refs, far_refs, k_pool, v_pool, group, rows, slots)
        fill_queries(meta_ref, qd_refs, q_pool, g_pool, group, rows)
        stats_ref[...] = before_ref[...]
        masks = causal_masks()
        for t in range(pairs):
            here = slice(t * PAIR, (t + 1) * PAIR)
            window = slice(t * PAIR + BLK, t * PAIR + BLK + SPAN * BLK)
            keys = jnp.concatenate([k_pool[window, :], k_pool[2 * whole :, :]], axis=0)
            vals = jnp.concatenate([v_pool[window, :], v_pool[2 * whole :, :]], axis=0)
            s = masked_scores(keys, q_pool[here, :], bias_rows(bias_ref, t, range(SPAN + slots)), masks)
            top = jnp.max(s, axis=0, keepdims=True)
            e = jnp.exp2(s - top)
            total = jnp.sum(e, axis=0, keepdims=True)
            low = (e * (1.0 / total)).astype(jnp.bfloat16)
            out = dot(low, vals, TN).astype(jnp.bfloat16)
            out_ref[here, :] = out
            product = out.astype(jnp.float32) * g_pool[here, :].astype(jnp.float32)
            stats_ref[t, 2 * head : 2 * head + 1, :] = top + jnp.log2(total)
            stats_ref[t, 2 * head + 1 : 2 * head + 2, :] = jnp.sum(product.T, axis=0, keepdims=True)

    span = (SPAN + slots) * BLK
    lanes = [None, None] + [head] * sum(counts)
    return call(
        body, (meta,), (bias, stats, *qd, *own, *prev, *far),
        [shape((whole, HD)), shape(stats.shape, jnp.float32)],
        [
            pltpu.VMEM((2 * whole + slots * BLK, HD), jnp.bfloat16),
            pltpu.VMEM((2 * whole + slots * BLK, HD), jnp.bfloat16),
            pltpu.VMEM((whole, HD), jnp.bfloat16),
            pltpu.VMEM((whole, HD), jnp.bfloat16),
        ],
        cost(4 * whole * span * HD * 2, 3 * 1024 * 1024, whole * span),
        f"attention_{head}", lanes,
    )


def backward(head, qd, own, prev, far, bias, stats, meta, group, slots):
    rows = qd[0].shape[1]
    whole = group * rows
    pairs = whole // PAIR
    counts = (group, group, group, len(far))
    everything = 2 * whole + slots * BLK

    def body(meta_ref, bias_ref, stats_ref, *refs):
        (qd_refs, own_refs, prev_refs, far_refs), refs = split_refs(refs, counts)
        ((dq_ref, grad_ref), far_outs), refs = split_refs(refs, (2, len(far)))
        k_pool, v_pool, q_pool, g_pool, far_sum = refs
        at_group = meta_ref[1]
        fill_pools(meta_ref, own_refs, prev_refs, far_refs, k_pool, v_pool, group, rows, slots)
        fill_queries(meta_ref, qd_refs, q_pool, g_pool, group, rows)
        masks = causal_masks()
        grad_ref[...] = jnp.zeros_like(grad_ref)
        far_sum[...] = jnp.zeros_like(far_sum)
        for t in range(pairs):
            here = slice(t * PAIR, (t + 1) * PAIR)
            window = slice(t * PAIR + BLK, t * PAIR + BLK + SPAN * BLK)
            before = max(whole - (t * PAIR + BLK), 0)
            end = SPAN * BLK
            mine = slice(t * PAIR + BLK + before - whole, t * PAIR + BLK + end - whole)
            keys = jnp.concatenate([k_pool[window, :], k_pool[2 * whole :, :]], axis=0)
            vals = jnp.concatenate([v_pool[window, :], v_pool[2 * whole :, :]], axis=0)
            query, grad = q_pool[here, :], g_pool[here, :]
            s = masked_scores(keys, query, bias_rows(bias_ref, t, range(SPAN + slots)), masks)
            probs = jnp.exp2(s - stats_ref[t, 2 * head : 2 * head + 1, :])
            delta = stats_ref[t, 2 * head + 1 : 2 * head + 2, :]
            ds = (probs * (dot(vals, grad, NT) - delta)).astype(jnp.bfloat16)
            low = probs.astype(jnp.bfloat16)
            dq_ref[here, :] = (dot(ds, keys, TN) * SCALE).astype(jnp.bfloat16)
            grad_ref[0, mine, :] += dot(ds[before:end], query, NN)
            grad_ref[1, mine, :] += dot(low[before:end], grad, NN)
            far_sum[0] += dot(ds[end:], query, NN)
            far_sum[1] += dot(low[end:], grad, NN)
        for index, ref in enumerate(far_outs):
            slot = jnp.maximum(at_group - index - 2, 0) // 2
            start = pl.multiple_of(slot * BLK, BLK)
            ref[0] = (far_sum[0, pl.ds(start, BLK), :] * SCALE).astype(jnp.bfloat16)
            ref[1] = far_sum[1, pl.ds(start, BLK), :].astype(jnp.bfloat16)

    span = (SPAN + slots) * BLK
    lanes = [None, None] + [head] * sum(counts)
    outs = call(
        body, (meta,), (bias, stats, *qd, *own, *prev, *far),
        [shape((whole, HD)), shape((2, whole, HD), jnp.float32)]
        + [shape((2, BLK, HD))] * len(far),
        [
            pltpu.VMEM((everything, HD), jnp.bfloat16),
            pltpu.VMEM((everything, HD), jnp.bfloat16),
            pltpu.VMEM((whole, HD), jnp.bfloat16),
            pltpu.VMEM((whole, HD), jnp.bfloat16),
            pltpu.VMEM((2, slots * BLK, HD), jnp.float32),
        ],
        cost(8 * whole * span * HD * 2, 4 * 1024 * 1024, whole * span),
        f"attention_back_{head}", lanes,
    )
    return outs[0], outs[1], outs[2:]


def backward_next(grads, qd, own, bias, stats, meta, group):
    rows, width = qd[0].shape[1:]
    heads = width // HD
    whole = group * rows
    pairs = whole // PAIR

    def body(meta_ref, bias_ref, stats_ref, *refs):
        (grad_refs, qd_refs, own_refs, (out,)), refs = split_refs(refs, (heads, group, group, 1))
        k_pool, v_pool, q_pool, g_pool = refs
        me = meta_ref[0]
        strided = pl.ds(pl.multiple_of(meta_ref[2] * BLK, BLK), BLK)
        for k in range(group):
            at = pl.multiple_of((me ^ k) * rows, rows)
            k_pool[pl.ds(at, rows), :] = own_refs[k][0]
            v_pool[pl.ds(at, rows), :] = own_refs[k][1]
        fill_queries(meta_ref, qd_refs, q_pool, g_pool, group, rows)
        for h in range(heads):
            lanes = slice(h * HD, (h + 1) * HD)
            out[0, :, lanes] = grad_refs[h][0]
            out[1, :, lanes] = grad_refs[h][1]
            for t in range(pairs):
                here = slice(t * PAIR, (t + 1) * PAIR)
                window = slice(t * PAIR + BLK, whole)
                near = (whole - BLK) // BLK - t * (PAIR // BLK)
                keys = jnp.concatenate([k_pool[window, lanes], k_pool[strided, lanes]], axis=0)
                vals = jnp.concatenate([v_pool[window, lanes], v_pool[strided, lanes]], axis=0)
                query, grad = q_pool[here, lanes], g_pool[here, lanes]
                rows_here = bias_rows(bias_ref, t, list(range(near)) + [SPAN])
                s = masked_scores(keys, query, rows_here, None)
                probs = jnp.exp2(s - stats_ref[t, 2 * h : 2 * h + 1, :])
                delta = stats_ref[t, 2 * h + 1 : 2 * h + 2, :]
                ds = (probs * (dot(vals, grad, NT) - delta)).astype(jnp.bfloat16)
                dk = dot(ds, query, NN)
                dv = dot(probs.astype(jnp.bfloat16), grad, NN)
                out[0, window, lanes] += dk[: near * BLK]
                out[1, window, lanes] += dv[: near * BLK]
                out[0, strided, lanes] += dk[near * BLK :]
                out[1, strided, lanes] += dv[near * BLK :]
        out[0] = out[0] * SCALE

    return call(
        body, (meta,), (bias, stats, *grads, *qd, *own),
        [shape((2, whole, width), jnp.float32)],
        [pltpu.VMEM((whole, width), jnp.bfloat16)] * 4,
        cost(8 * whole * 5 * BLK * width, 7 * 1024 * 1024, whole * 5 * BLK * heads),
        "attention_back_next",
    )[0]


def combine(dq, own, far, meta, group, rows):
    whole, width = own.shape[1:]

    def body(meta_ref, own_ref, *refs):
        (dq_refs, far_refs, outs, (acc,)), refs = split_refs(refs, (len(dq), len(far), group, 1))
        me, offset = meta_ref[0], meta_ref[2]
        acc[...] = own_ref[...]
        at = pl.multiple_of(offset * BLK, BLK)
        for ref in far_refs:
            acc[:, pl.ds(at, BLK), :] += ref[...].astype(jnp.float32)
        for k in range(group):
            here = pl.ds(pl.multiple_of((me ^ k) * rows, rows), rows)
            for h in range(len(dq)):
                outs[k][0, :, h * HD : (h + 1) * HD] = dq_refs[h][here, :]
            outs[k][1] = acc[0, here, :].astype(jnp.bfloat16)
            outs[k][2] = acc[1, here, :].astype(jnp.bfloat16)

    return call(
        body, (meta,), (own, *dq, *far), [shape((3, rows, width))] * group,
        [pltpu.VMEM((2, whole, width), jnp.float32)],
        cost(0, 4 * 1024 * 1024), "combine",
    )


def project(head, mine, theirs, attn, meta, group, parts):
    height, whole = mine.shape
    each = 2 * height // parts
    full = group * HD

    def body(meta_ref, mine_ref, theirs_ref, *refs):
        (attn_refs, (keep, send, pool, total)), refs = split_refs(refs, (group, 4))
        me, at_group, core = meta_ref[0], meta_ref[1], meta_ref[3]
        for k in range(group):
            at = pl.multiple_of((me ^ k) * HD, HD)
            pool[:, pl.ds(at, HD)] = attn_refs[k][...]
        first = pl.ds(pl.multiple_of(core * height, height), height)
        second = pl.ds(pl.multiple_of((1 - core) * height, height), height)
        total[first, :] = dot(mine_ref[...], pool[...], NN)
        total[second, :] = dot(theirs_ref[...], pool[...], NN)
        for m in range(parts):
            at = pl.multiple_of((at_group ^ m) * each, each)
            if m % 2 == 0:
                keep[m // 2] = total[pl.ds(at, each), :]
            else:
                send[m // 2] = total[pl.ds(at, each), :].astype(jnp.bfloat16)

    return call(
        body, (meta,), (mine, theirs, *attn),
        [shape((parts // 2, each, full), jnp.float32), shape((parts // 2, each, full))],
        [pltpu.VMEM((whole, full), jnp.bfloat16), pltpu.VMEM((2 * height, full), jnp.float32)],
        cost(4 * height * whole * full, 6 * 1024 * 1024), f"project_{head}",
    )


def halve(head, keep, arrived):
    parts, each, full = keep.shape

    def body(keep_ref, arrived_ref, stay, send):
        for m in range(parts):
            summed = keep_ref[m] + arrived_ref[m].astype(jnp.float32)
            if m % 2 == 0:
                stay[m // 2] = summed
            else:
                send[m // 2] = summed.astype(jnp.bfloat16)

    return call(
        body, (), (keep, arrived),
        [shape((parts // 2, each, full), jnp.float32), shape((parts // 2, each, full))], [],
        cost(0, 3 * 1024 * 1024), f"halve_{head}",
    )


def finish(keep, arrived, group):
    heads = len(keep)
    each = keep[0].shape[1]

    def body(*refs):
        out = refs[2 * heads]
        for h in range(heads):
            total = refs[h][0] + refs[heads + h][0].astype(jnp.float32)
            for j in range(group):
                at = (j * heads + h) * HD
                out[:, at : at + HD] = total[:, j * HD : (j + 1) * HD]

    return call(
        body, (), (*keep, *arrived), [shape((each, group * heads * HD), jnp.float32)], [],
        cost(0, 3 * 1024 * 1024), "finish",
    )[0]


def unpack(pieces, meta, group):
    rows, width = pieces[0].shape[1:]

    def body(meta_ref, *refs):
        me = meta_ref[0]
        for k in range(group):
            at = pl.ds(pl.multiple_of((me ^ k) * width, width), width)
            for which in range(3):
                refs[group + which][:, at] = refs[k][which]

    return call(
        body, (meta,), tuple(pieces), [shape((rows, group * width))] * 3, [],
        cost(0, 3 * 1024 * 1024), "unpack",
    )


def listed(table, ids):
    return jnp.any(table[:, None, :] == ids[:, :, None], axis=2) & (ids >= 0)


def after(value, *others):
    return lax.optimization_barrier((value, *others))[0]


def reading(layout, at_group, offset, slots):
    ids = at_group * LOCAL + jnp.arange(LOCAL, dtype=jnp.int32)
    table = lax.dynamic_slice_in_dim(layout, at_group * LOCAL, LOCAL, 0)
    base = ids - jnp.arange(LOCAL, dtype=jnp.int32) % 2 - (LOCAL - 1)
    near_ids = base[:, None] + jnp.arange(SPAN, dtype=jnp.int32)[None, :]
    near = listed(table, near_ids) & (near_ids >= ids[:, None] - (LOCAL - 1))
    far_ids = jnp.broadcast_to(
        jnp.arange(slots, dtype=jnp.int32)[None, :] * STRIDE + offset, (LOCAL, slots)
    )
    distant = listed(table, far_ids) & (far_ids < ids[:, None] - (LOCAL - 1))
    return near, distant


def as_bias(reads):
    bias = jnp.where(reads, 0.0, -jnp.inf).astype(jnp.float32)
    bias = bias.reshape(LOCAL // 2, 2, reads.shape[1]).transpose(0, 2, 1)
    return jnp.repeat(bias, BLK, axis=2)


def local(devices, queries, keys, values, out_grad, proj_weight, layout):
    rows, columns = queries.shape
    group = LOCAL * BLK // rows
    parts = devices // group
    width = columns // group
    heads = width // HD
    blocks = layout.shape[0]
    slots = blocks // STRIDE
    position = lax.axis_index("seq")
    me, at_group = position % group, position // group
    core = lax.axis_index("head")
    offset = layout[blocks - 1, 0] % STRIDE
    place = jnp.stack([me, at_group]).astype(jnp.int32)
    meta = jnp.stack([me, at_group, offset, core]).astype(jnp.int32)

    def swap(piece, k):
        route = [(i, (i // group) * group + ((i % group) ^ k)) for i in range(devices)]
        return lax.ppermute(piece, "seq", route)

    def shifted(piece, distance):
        route = [
            (i, i + distance * group)
            for i in range(devices)
            if 0 <= i + distance * group < devices
        ]
        return lax.ppermute(piece, "seq", route)

    def swap_groups(piece, bit):
        route = [(i, ((i // group) ^ bit) * group + i % group) for i in range(devices)]
        return lax.ppermute(piece, "seq", route)

    def summary_route(distance, back):
        route = [
            (i, i + distance * group)
            for i in range(devices - distance * group)
            if (i // group) % 2 == 0
        ]
        return [(b, a) for a, b in route] if back else route

    def exchange(pieces):
        return [pieces[0]] + [swap(pieces[k], k) for k in range(1, group)]

    kv = pack_kv(keys, values, place, group, width)
    own_kv = exchange(kv)
    prev_kv = [shifted(kv[0], 1)]
    prev_kv += [shifted(own_kv[k], 1) for k in range(1, group)]
    qd_cut = grads_packed(queries, out_grad, proj_weight, after(place, kv[0]), group, width)
    qd = exchange(qd_cut)
    next_qd = [shifted(piece, -1) for piece in qd]
    strided = pick_summary(own_kv, meta, group)
    far = [
        lax.ppermute(strided, "seq", summary_route(distance, False))
        for distance in range(2, parts)
    ]
    og = exchange(pack_out_grad(out_grad, after(meta, qd[1], qd[2]), group, parts))
    mine = join_columns(og, meta, group)
    theirs = lax.ppermute(mine, "head", [(0, 1), (1, 0)])

    near, distant = reading(layout, at_group, offset, slots)
    bias = as_bias(jnp.concatenate([near, distant], axis=1))
    follows = at_group + 1 < parts
    near, distant = reading(layout, at_group + 1, offset, slots)
    hers = jnp.any(distant & (jnp.arange(slots)[None, :] * 2 == at_group), axis=1, keepdims=True)
    bias_next = as_bias(jnp.concatenate([near, hers], axis=1) & follows)

    stats = jnp.zeros((LOCAL // 2, 2 * heads, PAIR), jnp.float32)
    attn = []
    for h in range(heads):
        got, stats = forward(h, qd, own_kv, prev_kv, far, bias, stats, meta, group, slots)
        attn.append([got] + [swap(got, k) for k in range(1, group)])
    next_stats = shifted(stats, -1)

    dq, grads, far_grads, keep, arrived = [], [], [], [], []
    for h in range(heads):
        got = backward(h, qd, own_kv, prev_kv, far, bias, stats, meta, group, slots)
        dq.append(got[0])
        grads.append(got[1])
        far_grads.append(got[2])
        kept, sent = project(h, mine, theirs, attn[h], meta, group, parts)
        bit = 1
        arrival = swap_groups(sent, bit)
        while kept.shape[0] > 1:
            bit *= 2
            kept, sent = halve(h, kept, arrival)
            arrival = swap_groups(sent, bit)
        keep.append(kept)
        arrived.append(arrival)
    far_back = [
        lax.ppermute(jnp.concatenate(pieces, axis=2), "seq", summary_route(index + 2, True))
        for index, pieces in enumerate(zip(*far_grads))
    ]
    own_grad = backward_next(grads, next_qd, own_kv, bias_next, next_stats, meta, group)
    final = exchange(combine(dq, own_grad, far_back, meta, group, rows))
    query_grad, key_grad, value_grad = unpack(final, meta, group)
    proj_grad = finish(keep, arrived, group)
    return (query_grad, key_grad, value_grad, proj_grad)


def solution(mesh):
    split = P(("dp", "seq"), "head")
    return jax.shard_map(
        functools.partial(local, mesh.shape["seq"]),
        mesh=mesh,
        in_specs=(split, split, split, P(("dp", "seq"), None), P(None, "head"), P()),
        out_specs=(split, split, split, split),
        check_vma=False,
    )
```

time: 197 us -> 196 us (level)
  waiting for transfers between devices: 92.7 us -> 52.3 us
  local copies, waits for them, and re-layouts: 8.43 us -> 27.7 us
  starting transfers between devices: 47.3 us -> 59 us
  Pallas kernels: 42.1 us -> 49.7 us
    ppermute x5 -> x7, waiting for transfers between devices: 62.8 us -> 6.05 us  [the longest x4 6.04 us: swap_groups(): return lax.ppermute(piece, 'seq', route)]
    ppermute x5 -> x9, waiting for transfers between devices: 3.84 us -> 20.3 us  [shifted(): return lax.ppermute(piece, 'seq', route)]
    unnamed x32 -> x80, local copies, waits for them, and re-layouts: 5.83 us -> 21.7 us
    ppermute x18, waiting for transfers between devices: 26 us -> 18.2 us  [swap(): return lax.ppermute(piece, 'seq', route)]
    ppermute x2, waiting for transfers between devices: 0.01 us -> 7.77 us  [local(): lax.ppermute(strided, 'seq', summary_route(distance, False))]
    pallas_call x8 -> x16, Pallas kernels: 35 us -> 42.4 us  [call(): pl.pallas_call(body, grid=(1,), out_shape=outs, in_specs=specs, out_specs...]
    ppermute x5 -> x9, starting transfers between devices: 11.1 us -> 18.4 us  [shifted(): return lax.ppermute(piece, 'seq', route)]
    ppermute x5 -> x7, starting transfers between devices: 8.09 us -> 10.3 us  [the longest x4 7.7 us: swap_groups(): return lax.ppermute(piece, 'seq', route)]
  transfers between devices with their start and end apart: 30 -> 36, of which waited for: 12 -> 9; matrix products, arithmetic and copies ran while one was open for 2% -> 5% of each run, Pallas kernels for 17% -> 20%
where the time goes in v2:
time: 196 us; the launch traced here: 195 us
  starting transfers between devices  59 us (30%)
  waiting for transfers between devices  52.3 us (27%)
  Pallas kernels  49.7 us (25%)
  local copies, waits for them, and re-layouts  27.7 us (14%)
  between operations  2.92 us (1%)
  other arithmetic  2.9 us (1%)
    pallas_call x16, Pallas kernels, call(): pl.pallas_call(body, grid=(1,), out_shape=outs, in_specs=specs, out_specs...  42.4 us
    ppermute x18, starting transfers between devices, swap(): return lax.ppermute(piece, 'seq', route)  24.5 us
    unnamed x80, local copies, waits for them, and re-layouts  21.7 us
    ppermute x9, waiting for transfers between devices, shifted(): return lax.ppermute(piece, 'seq', route)  20.3 us
    ppermute x9, starting transfers between devices, shifted(): return lax.ppermute(piece, 'seq', route)  18.4 us
    ppermute x18, waiting for transfers between devices, swap(): return lax.ppermute(piece, 'seq', route)  18.2 us
    ppermute x2, waiting for transfers between devices, local(): lax.ppermute(strided, 'seq', summary_route(distance, False))  7.77 us
    ppermute x4, starting transfers between devices, swap_groups(): return lax.ppermute(piece, 'seq', route)  7.7 us
  transfers between devices with their start and end apart: 36, of which 9 were waited for; matrix products, arithmetic and copies ran while one was open for 5% of the time, Pallas kernels for 20%

profile of v2, /device:TPU:0, one launch (start us, length us, event | category | flops | bytes accessed | tf_op | source)
XLA Modules:
  0.0 194.5 jit_solution(2050250022584656031)
XLA Ops:
  2.8 1.6 pack_kv.1
  4.4 1.6 copy-done.1
  7.0 7.2 %attn_grad.1 = (bf16[2,256,256]{2,1,0:T(8,128)(2,1)}, bf16[2,256,256]{2,1,0:T(8,128)(2,1)}, bf16[2,256,256]{2,1,0:T(8,128)(2,1)}, bf16[2,256,256]{2,1,0:T(8,128)(2,1)S(1)}) custom-call(s32[2]{0:T(128)S(1)} %pad_add_fusion.1.meta_ref, bf16[256,1024]{1,0:T(8,128)(2,1)S(1)} %copy-done.11, bf16[256,4096]{1,0:T(8,128)(2,1)S(1)} %copy-done.1, bf16[4096,1024]{1,0:T(8,128)(2,1)} %w_ref.1), custom_call_target="tpu_custom_call" | custom-call | flops 2147483648 | bytes 12582912 | tf_op jit(solution)/shard_map/attn_grad/pallas_call | solution.py:108
  14.3 2.9 %collective-permute-start = (bf16[2,256,256]{2,1,0:T(8,128)(2,1)}, bf16[2,256,256]{2,1,0:T(8,128)(2,1)}, u32[]{:S(2)}, u32[]{:S(2)}) collective-permute-start(bf16[2,256,256]{2,1,0:T(8,128)(2,1)} %get-tuple-element.48), channel_id=1, source_target_pairs={{0,2},{2,0},{4,6},{6,4},{8,10},{10,8},{12,14},{14,12},{16,18},{18,... | collective-permute-start | bytes 786440 | tf_op jit(solution)/shard_map/ppermute | solution.py:546
  19.4 2.8 %collective-permute-start.5 = (bf16[2,256,256]{2,1,0:T(8,128)(2,1)}, bf16[2,256,256]{2,1,0:T(8,128)(2,1)S(1)}, u32[]{:S(2)}, u32[]{:S(2)}) collective-permute-start(bf16[2,256,256]{2,1,0:T(8,128)(2,1)} %get-tuple-element.53), channel_id=1, source_target_pairs={{0,6},{2,4},{4,2},{6,0},{8,14},{10,12},{12,10},{14,8},{16,22},{18,... | collective-permute-start | bytes 786440 | tf_op jit(solution)/shard_map/ppermute | solution.py:546
  25.8 1.8 collective-permute-start.2
  30.2 2.1 %collective-permute-start.23 = (bf16[512,256]{1,0:T(8,128)(2,1)S(1)}, bf16[512,256]{1,0:T(8,128)(2,1)S(1)}, u32[]{:S(2)}, u32[]{:S(2)}) collective-permute-start(bf16[512,256]{1,0:T(8,128)(2,1)S(1)} %get-tuple-element.74), channel_id=1, source_target_pairs={{0,4},{2,6},{4,0},{6,2},{8,12},{10,14},{12,8},{14,10},{16,20},{18,... | collective-permute-start | bytes 786440 | tf_op jit(solution)/shard_map/ppermute | solution.py:546
  32.2 10.3 %collective-permute-done.4.refs_2_.refs_6_.refs_8_ = bf16[2,256,256]{2,1,0:T(8,128)(2,1)S(1)} collective-permute-done((bf16[2,256,256]{2,1,0:T(8,128)(2,1)}, bf16[2,256,256]{2,1,0:T(8,128)(2,1)S(1)}, u32[]{:S(2)}, u32[]{:S(2)}) %collective-permute-start.4) | collective-permute-done | bytes 262176 | tf_op jit(solution)/shard_map/ppermute | solution.py:546
  43.0 3.5 %collective-permute-start.6 = (bf16[2,256,256]{2,1,0:T(8,128)(2,1)S(1)}, bf16[2,256,256]{2,1,0:T(8,128)(2,1)S(1)}, u32[]{:S(2)}, u32[]{:S(2)}) collective-permute-start(bf16[2,256,256]{2,1,0:T(8,128)(2,1)S(1)} %get-tuple-element.45.refs_0_.refs_4_.refs_6_), channel_id=1, source_target_pairs={{0,8},{2,10},{4,12},{6,14},{8,16},{10,18},{12,20},{14,22},{16,24},... | collective-permute-start | bytes 786440 | tf_op jit(solution)/shard_map/ppermute | solution.py:554
  48.1 4.5 %collective-permute-start.10 = (bf16[2,128,256]{2,1,0:T(8,128)(2,1)S(1)}, bf16[2,128,256]{2,1,0:T(8,128)(2,1)S(1)}, u32[]{:S(2)}, u32[]{:S(2)}) collective-permute-start(bf16[2,128,256]{2,1,0:T(8,128)(2,1)S(1)} %pick_summary.1), channel_id=1, source_target_pairs={{0,16},{2,18},{4,20},{6,22},{1,17},{3,19},{5,21},{7,23}} | collective-permute-start | bytes 393224 | tf_op jit(solution)/shard_map/ppermute | solution.py:580
  54.1 3.3 %collective-permute-start.8 = (bf16[2,256,256]{2,1,0:T(8,128)(2,1)S(1)}, bf16[2,256,256]{2,1,0:T(8,128)(2,1)}, u32[]{:S(2)}, u32[]{:S(2)}) collective-permute-start(bf16[2,256,256]{2,1,0:T(8,128)(2,1)S(1)} %collective-permute-done.4.refs_2_.refs_6_.refs_8_), channel_id=1, source_target_pairs={{0,8},{2,10},{4,12},{6,14},{8,16},{10,18},{12,20},{14,22},{16,24},... | collective-permute-start | bytes 786440 | tf_op jit(solution)/shard_map/ppermute | solution.py:554
  57.5 3.5 %collective-permute-start.9 = (bf16[2,256,256]{2,1,0:T(8,128)(2,1)S(1)}, bf16[2,256,256]{2,1,0:T(8,128)(2,1)}, u32[]{:S(2)}, u32[]{:S(2)}) collective-permute-start(bf16[2,256,256]{2,1,0:T(8,128)(2,1)S(1)} %collective-permute-done.5.refs_3_.refs_7_.refs_9_), channel_id=1, source_target_pairs={{0,8},{2,10},{4,12},{6,14},{8,16},{10,18},{12,20},{14,22},{16,24},... | collective-permute-start | bytes 786440 | tf_op jit(solution)/shard_map/ppermute | solution.py:554
  63.7 7.8 %collective-permute-done.11.refs_13_ = bf16[2,128,256]{2,1,0:T(8,128)(2,1)S(1)} collective-permute-done((bf16[2,128,256]{2,1,0:T(8,128)(2,1)S(1)}, bf16[2,128,256]{2,1,0:T(8,128)(2,1)S(1)}, u32[]{:S(2)}, u32[]{:S(2)}) %collective-permute-start.11) | collective-permute-done | bytes 131104 | tf_op jit(solution)/shard_map/ppermute | solution.py:580
  72.8 5.1 %attention_0.1 = (bf16[1024,128]{1,0:T(8,128)(2,1)S(1)}, f32[4,4,256]{2,1,0:T(4,128)S(1)}) custom-call(s32[4]{0:T(128)S(1)} %pad_add_fusion.meta_ref, f32[4,11,256]{2,1,0:T(8,128)S(1)} %copy.42.bias_ref, f32[4,4,256]{2,1,0:T(4,128)S(1)} %broadcast_in_dim.67.before_ref, bf16[2,256,256]{2,1,0:T(8,128)(2,1)} %get-tuple-element.47.refs_0_, ...), custom_call_target="tpu_custom_call" | custom-call | flops 1476395008 | bytes 3145728 | tf_op jit(solution)/shard_map/attention_0/pallas_call | solution.py:54
  77.9 3.0 %collective-permute-start.26 = (bf16[1024,128]{1,0:T(8,128)(2,1)S(1)}, bf16[1024,128]{1,0:T(8,128)(2,1)S(1)}, u32[]{:S(2)}, u32[]{:S(2)}) collective-permute-start(bf16[1024,128]{1,0:T(8,128)(2,1)S(1)} %get-tuple-element.76.refs_0_), channel_id=1, source_target_pairs={{0,2},{2,0},{4,6},{6,4},{8,10},{10,8},{12,14},{14,12},{16,18},{18,... | collective-permute-start | bytes 786440 | tf_op jit(solution)/shard_map/ppermute | solution.py:546
  82.5 5.9 %attention_1.1 = (bf16[1024,128]{1,0:T(8,128)(2,1)S(1)}, f32[4,4,256]{2,1,0:T(4,128)}) custom-call(s32[4]{0:T(128)S(1)} %pad_add_fusion.meta_ref, f32[4,11,256]{2,1,0:T(8,128)S(1)} %copy.42.bias_ref, f32[4,4,256]{2,1,0:T(4,128)S(1)} %get-tuple-element.54.before_ref, bf16[2,256,256]{2,1,0:T(8,128)(2,1)} %get-tuple-element.47.refs_0_, ...), custom_call_target="tpu_custom_call" | custom-call | flops 1476395008 | bytes 3145728 | tf_op jit(solution)/shard_map/attention_1/pallas_call | solution.py:54
  89.3 5.0 %attention_back_0.1 = (bf16[1024,128]{1,0:T(8,128)(2,1)S(1)}, f32[2,1024,128]{2,1,0:T(8,128)S(1)}, bf16[2,128,128]{2,1,0:T(8,128)(2,1)S(1)}, bf16[2,128,128]{2,1,0:T(8,128)(2,1)S(1)}) custom-call(s32[4]{0:T(128)S(1)} %pad_add_fusion.meta_ref, f32[4,11,256]{2,1,0:T(8,128)S(1)} %copy.42.bias_ref, f32[4,4,256]{2,1,0:T(4,128)} %get-tuple-element.55.stats_ref, ...), custom_call_target="tpu_custom_call" | custom-call | flops 2952790016 | bytes 4194304 | tf_op jit(solution)/shard_map/attention_back_0/pallas_call | solution.py:54
  94.3 2.0 %collective-permute-start.30 = (bf16[1024,128]{1,0:T(8,128)(2,1)S(1)}, bf16[1024,128]{1,0:T(8,128)(2,1)S(1)}, u32[]{:S(2)}, u32[]{:S(2)}) collective-permute-start(bf16[1024,128]{1,0:T(8,128)(2,1)S(1)} %get-tuple-element.80.refs_0_), channel_id=1, source_target_pairs={{0,2},{2,0},{4,6},{6,4},{8,10},{10,8},{12,14},{14,12},{16,18},{18,... | collective-permute-start | bytes 786440 | tf_op jit(solution)/shard_map/ppermute | solution.py:546
  99.8 4.8 %attention_back_1.1 = (bf16[1024,128]{1,0:T(8,128)(2,1)S(1)}, f32[2,1024,128]{2,1,0:T(8,128)S(1)}, bf16[2,128,128]{2,1,0:T(8,128)(2,1)S(1)}, bf16[2,128,128]{2,1,0:T(8,128)(2,1)S(1)}) custom-call(s32[4]{0:T(128)S(1)} %pad_add_fusion.meta_ref, f32[4,11,256]{2,1,0:T(8,128)S(1)} %copy.42.bias_ref, f32[4,4,256]{2,1,0:T(4,128)} %get-tuple-element.55.stats_ref, ...), custom_call_target="tpu_custom_call" | custom-call | flops 2952790016 | bytes 4194304 | tf_op jit(solution)/shard_map/attention_back_1/pallas_call | solution.py:54
  106.8 3.0 %project_0.1 = (f32[2,256,512]{2,1,0:T(8,128)S(1)}, bf16[2,256,512]{2,1,0:T(8,128)(2,1)}) custom-call(s32[4]{0:T(128)S(1)} %pad_add_fusion.meta_ref, bf16[512,1024]{1,0:T(8,128)(2,1)S(1)} %join_columns.1.mine_ref, bf16[512,1024]{1,0:T(8,128)(2,1)S(1)} %collective-permute-done.25.theirs_ref, bf16[1024,128]{1,0:T(8,128)(2,1)S(1)} %get-tuple-element.76.refs_0_, ...), custom_call_target="tpu_custom_call" | custom-call | flops 1073741824 | bytes 6291456 | tf_op jit(solution)/shard_map/project_0/pallas_call | solution.py:54
  112.4 4.7 %collective-permute-start.29 = (bf16[2,256,512]{2,1,0:T(8,128)(2,1)}, bf16[2,256,512]{2,1,0:T(8,128)(2,1)}, u32[]{:S(2)}, u32[]{:S(2)}) collective-permute-start(bf16[2,256,512]{2,1,0:T(8,128)(2,1)} %get-tuple-element.78), channel_id=1, source_target_pairs={{0,8},{2,10},{4,12},{6,14},{8,0},{10,2},{12,4},{14,6},{16,24},{18,... | collective-permute-start | bytes 1572872 | tf_op jit(solution)/shard_map/ppermute | solution.py:558
  117.1 3.0 %project_1.1 = (f32[2,256,512]{2,1,0:T(8,128)S(1)}, bf16[2,256,512]{2,1,0:T(8,128)(2,1)}) custom-call(s32[4]{0:T(128)S(1)} %pad_add_fusion.meta_ref, bf16[512,1024]{1,0:T(8,128)(2,1)S(1)} %join_columns.1.mine_ref, bf16[512,1024]{1,0:T(8,128)(2,1)S(1)} %collective-permute-done.25.theirs_ref, bf16[1024,128]{1,0:T(8,128)(2,1)S(1)} %get-tuple-element.80.refs_0_, ...), custom_call_target="tpu_custom_call" | custom-call | flops 1073741824 | bytes 6291456 | tf_op jit(solution)/shard_map/project_1/pallas_call | solution.py:54
  127.1 2.7 %collective-permute-done.16.refs_5_ = bf16[2,256,256]{2,1,0:T(8,128)(2,1)S(1)} collective-permute-done((bf16[2,256,256]{2,1,0:T(8,128)(2,1)S(1)}, bf16[2,256,256]{2,1,0:T(8,128)(2,1)S(1)}, u32[]{:S(2)}, u32[]{:S(2)}) %collective-permute-start.16) | collective-permute-done | bytes 262176 | tf_op jit(solution)/shard_map/ppermute | solution.py:554
  136.3 17.5 %collective-permute-done.12.stats_ref = f32[4,4,256]{2,1,0:T(4,128)} collective-permute-done((f32[4,4,256]{2,1,0:T(4,128)}, f32[4,4,256]{2,1,0:T(4,128)}, u32[]{:S(2)}, u32[]{:S(2)}) %collective-permute-start.12) | collective-permute-done | bytes 16416 | tf_op jit(solution)/shard_map/ppermute | solution.py:554
  160.5 5.4 %attention_back_next.1.own_ref = f32[2,1024,256]{2,1,0:T(8,128)} custom-call(s32[4]{0:T(128)S(1)} %pad_add_fusion.meta_ref, f32[4,10,256]{2,1,0:T(8,128)S(1)} %copy.45.bias_ref, f32[4,4,256]{2,1,0:T(4,128)} %collective-permute-done.12.stats_ref, f32[2,1024,128]{2,1,0:T(8,128)S(1)} %get-tuple-element.56.refs_0_, ...), custom_call_target="tpu_custom_call" | custom-call | flops 1342177280 | bytes 7340032 | tf_op jit(solution)/shard_map/attention_back_next/pallas_call | solution.py:54
  165.9 1.6 copy-done
  168.9 1.6 collective-permute-start.19
  174.8 3.0 %collective-permute-start.35 = (bf16[1,256,512]{2,1,0:T(8,128)(2,1)S(1)}, bf16[1,256,512]{2,1,0:T(8,128)(2,1)S(1)}, u32[]{:S(2)}, u32[]{:S(2)}) collective-permute-start(bf16[1,256,512]{2,1,0:T(8,128)(2,1)S(1)} %get-tuple-element.85), channel_id=1, source_target_pairs={{0,16},{2,18},{4,20},{6,22},{8,24},{10,26},{12,28},{14,30},{16,0},... | collective-permute-start | bytes 786440 | tf_op jit(solution)/shard_map/ppermute | solution.py:558
  177.8 2.0 %collective-permute-done.19.refs_1_ = bf16[3,256,256]{2,1,0:T(8,128)(2,1)S(1)} collective-permute-done((bf16[3,256,256]{2,1,0:T(8,128)(2,1)S(1)}, bf16[3,256,256]{2,1,0:T(8,128)(2,1)S(1)}, u32[]{:S(2)}, u32[]{:S(2)}) %collective-permute-start.19) | collective-permute-done | bytes 393248 | tf_op jit(solution)/shard_map/ppermute | solution.py:546
  179.8 5.7 %collective-permute-done.20.refs_2_ = bf16[3,256,256]{2,1,0:T(8,128)(2,1)S(1)} collective-permute-done((bf16[3,256,256]{2,1,0:T(8,128)(2,1)S(1)}, bf16[3,256,256]{2,1,0:T(8,128)(2,1)S(1)}, u32[]{:S(2)}, u32[]{:S(2)}) %collective-permute-start.20) | collective-permute-done | bytes 393248 | tf_op jit(solution)/shard_map/ppermute | solution.py:546
  185.5 1.9 unpack.1
  188.3 5.2 %collective-permute-done.35.refs_3_ = bf16[1,256,512]{2,1,0:T(8,128)(2,1)S(1)} collective-permute-done((bf16[1,256,512]{2,1,0:T(8,128)(2,1)S(1)}, bf16[1,256,512]{2,1,0:T(8,128)(2,1)S(1)}, u32[]{:S(2)}, u32[]{:S(2)}) %collective-permute-start.35) | collective-permute-done | bytes 262176 | tf_op jit(solution)/shard_map/ppermute | solution.py:558
  (178 shorter events, 55.9 us)
Async XLA Ops:
  14.3 11.6 %collective-permute-start = (bf16[2,256,256]{2,1,0:T(8,128)(2,1)}, bf16[2,256,256]{2,1,0:T(8,128)(2,1)}, u32[]{:S(2)}, u32[]{:S(2)}) collective-permute-start(bf16[2,256,256]{2,1,0:T(8,128)(2,1)} %get-tuple-element.48), channel_id=1, source_target_pairs={{0,2},{2,0},{4,6},{6,4},{8,10},{10,8},{12,14},{14,12},{16,18},{18,... | collective-permute-start | bytes 786440 | tf_op jit(solution)/shard_map/ppermute | solution.py:546
  19.3 23.3 %collective-permute-start.4 = (bf16[2,256,256]{2,1,0:T(8,128)(2,1)}, bf16[2,256,256]{2,1,0:T(8,128)(2,1)S(1)}, u32[]{:S(2)}, u32[]{:S(2)}) collective-permute-start(bf16[2,256,256]{2,1,0:T(8,128)(2,1)} %get-tuple-element.52), channel_id=1, source_target_pairs={{0,4},{2,6},{4,0},{6,2},{8,12},{10,14},{12,8},{14,10},{16,20},{18,... | collective-permute-start | bytes 786440 | tf_op jit(solution)/shard_map/ppermute | solution.py:546
  19.4 23.6 %collective-permute-start.5 = (bf16[2,256,256]{2,1,0:T(8,128)(2,1)}, bf16[2,256,256]{2,1,0:T(8,128)(2,1)S(1)}, u32[]{:S(2)}, u32[]{:S(2)}) collective-permute-start(bf16[2,256,256]{2,1,0:T(8,128)(2,1)} %get-tuple-element.53), channel_id=1, source_target_pairs={{0,6},{2,4},{4,2},{6,0},{8,14},{10,12},{12,10},{14,8},{16,22},{18,... | collective-permute-start | bytes 786440 | tf_op jit(solution)/shard_map/ppermute | solution.py:546
  25.8 21.6 %collective-permute-start.2 = (bf16[2,256,256]{2,1,0:T(8,128)(2,1)}, bf16[2,256,256]{2,1,0:T(8,128)(2,1)S(1)}, u32[]{:S(2)}, u32[]{:S(2)}) collective-permute-start(bf16[2,256,256]{2,1,0:T(8,128)(2,1)} %copy-done.32), channel_id=1, source_target_pairs={{0,6},{2,4},{4,2},{6,0},{8,14},{10,12},{12,10},{14,8},{16,22},{18,... | collective-permute-start | bytes 786440 | tf_op jit(solution)/shard_map/ppermute | solution.py:546
  29.3 23.4 %collective-permute-start.22 = (bf16[512,256]{1,0:T(8,128)(2,1)S(1)}, bf16[512,256]{1,0:T(8,128)(2,1)S(1)}, u32[]{:S(2)}, u32[]{:S(2)}) collective-permute-start(bf16[512,256]{1,0:T(8,128)(2,1)S(1)} %get-tuple-element.73), channel_id=1, source_target_pairs={{0,2},{2,0},{4,6},{6,4},{8,10},{10,8},{12,14},{14,12},{16,18},{18,... | collective-permute-start | bytes 786440 | tf_op jit(solution)/shard_map/ppermute | solution.py:546
  30.2 24.0 %collective-permute-start.23 = (bf16[512,256]{1,0:T(8,128)(2,1)S(1)}, bf16[512,256]{1,0:T(8,128)(2,1)S(1)}, u32[]{:S(2)}, u32[]{:S(2)}) collective-permute-start(bf16[512,256]{1,0:T(8,128)(2,1)S(1)} %get-tuple-element.74), channel_id=1, source_target_pairs={{0,4},{2,6},{4,0},{6,2},{8,12},{10,14},{12,8},{14,10},{16,20},{18,... | collective-permute-start | bytes 786440 | tf_op jit(solution)/shard_map/ppermute | solution.py:546
  42.5 14.9 %collective-permute-start.24 = (bf16[512,256]{1,0:T(8,128)(2,1)S(1)}, bf16[512,256]{1,0:T(8,128)(2,1)S(1)}, u32[]{:S(2)}, u32[]{:S(2)}) collective-permute-start(bf16[512,256]{1,0:T(8,128)(2,1)S(1)} %get-tuple-element.75), channel_id=1, source_target_pairs={{0,6},{2,4},{4,2},{6,0},{8,14},{10,12},{12,10},{14,8},{16,22},{18,... | collective-permute-start | bytes 786440 | tf_op jit(solution)/shard_map/ppermute | solution.py:546
  43.0 19.2 %collective-permute-start.6 = (bf16[2,256,256]{2,1,0:T(8,128)(2,1)S(1)}, bf16[2,256,256]{2,1,0:T(8,128)(2,1)S(1)}, u32[]{:S(2)}, u32[]{:S(2)}) collective-permute-start(bf16[2,256,256]{2,1,0:T(8,128)(2,1)S(1)} %get-tuple-element.45.refs_0_.refs_4_.refs_6_), channel_id=1, source_target_pairs={{0,8},{2,10},{4,12},{6,14},{8,16},{10,18},{12,20},{14,22},{16,24},... | collective-permute-start | bytes 786440 | tf_op jit(solution)/shard_map/ppermute | solution.py:554
  48.1 15.4 %collective-permute-start.10 = (bf16[2,128,256]{2,1,0:T(8,128)(2,1)S(1)}, bf16[2,128,256]{2,1,0:T(8,128)(2,1)S(1)}, u32[]{:S(2)}, u32[]{:S(2)}) collective-permute-start(bf16[2,128,256]{2,1,0:T(8,128)(2,1)S(1)} %pick_summary.1), channel_id=1, source_target_pairs={{0,16},{2,18},{4,20},{6,22},{1,17},{3,19},{5,21},{7,23}} | collective-permute-start | bytes 393224 | tf_op jit(solution)/shard_map/ppermute | solution.py:580
  52.7 20.1 %collective-permute-start.7 = (bf16[2,256,256]{2,1,0:T(8,128)(2,1)S(1)}, bf16[2,256,256]{2,1,0:T(8,128)(2,1)S(1)}, u32[]{:S(2)}, u32[]{:S(2)}) collective-permute-start(bf16[2,256,256]{2,1,0:T(8,128)(2,1)S(1)} %collective-permute-done.3.refs_1_.refs_5_.refs_7_), channel_id=1, source_target_pairs={{0,8},{2,10},{4,12},{6,14},{8,16},{10,18},{12,20},{14,22},{16,24},... | collective-permute-start | bytes 786440 | tf_op jit(solution)/shard_map/ppermute | solution.py:554
  54.1 18.6 %collective-permute-start.8 = (bf16[2,256,256]{2,1,0:T(8,128)(2,1)S(1)}, bf16[2,256,256]{2,1,0:T(8,128)(2,1)}, u32[]{:S(2)}, u32[]{:S(2)}) collective-permute-start(bf16[2,256,256]{2,1,0:T(8,128)(2,1)S(1)} %collective-permute-done.4.refs_2_.refs_6_.refs_8_), channel_id=1, source_target_pairs={{0,8},{2,10},{4,12},{6,14},{8,16},{10,18},{12,20},{14,22},{16,24},... | collective-permute-start | bytes 786440 | tf_op jit(solution)/shard_map/ppermute | solution.py:554
  57.5 15.4 %collective-permute-start.9 = (bf16[2,256,256]{2,1,0:T(8,128)(2,1)S(1)}, bf16[2,256,256]{2,1,0:T(8,128)(2,1)}, u32[]{:S(2)}, u32[]{:S(2)}) collective-permute-start(bf16[2,256,256]{2,1,0:T(8,128)(2,1)S(1)} %collective-permute-done.5.refs_3_.refs_7_.refs_9_), channel_id=1, source_target_pairs={{0,8},{2,10},{4,12},{6,14},{8,16},{10,18},{12,20},{14,22},{16,24},... | collective-permute-start | bytes 786440 | tf_op jit(solution)/shard_map/ppermute | solution.py:554
  63.6 41.8 %collective-permute-start.25 = (bf16[512,1024]{1,0:T(8,128)(2,1)S(1)}, bf16[512,1024]{1,0:T(8,128)(2,1)S(1)}, u32[]{:S(2)}, u32[]{:S(2)}) collective-permute-start(bf16[512,1024]{1,0:T(8,128)(2,1)S(1)} %join_columns.1.mine_ref), channel_id=1, source_target_pairs={{0,1},{1,0},{2,3},{3,2},{4,5},{5,4},{6,7},{7,6},{8,9},{9,8},{10,11... | collective-permute-start | bytes 3145736 | tf_op jit(solution)/shard_map/ppermute | solution.py:585
  71.5 49.5 %collective-permute-start.13 = (bf16[2,256,256]{2,1,0:T(8,128)(2,1)}, bf16[2,256,256]{2,1,0:T(8,128)(2,1)S(1)}, u32[]{:S(2)}, u32[]{:S(2)}) collective-permute-start(bf16[2,256,256]{2,1,0:T(8,128)(2,1)} %get-tuple-element.47.refs_0_), channel_id=1, source_target_pairs={{8,0},{10,2},{12,4},{14,6},{16,8},{18,10},{20,12},{22,14},{24,16},... | collective-permute-start | bytes 786440 | tf_op jit(solution)/shard_map/ppermute | solution.py:554
  77.9 16.3 %collective-permute-start.26 = (bf16[1024,128]{1,0:T(8,128)(2,1)S(1)}, bf16[1024,128]{1,0:T(8,128)(2,1)S(1)}, u32[]{:S(2)}, u32[]{:S(2)}) collective-permute-start(bf16[1024,128]{1,0:T(8,128)(2,1)S(1)} %get-tuple-element.76.refs_0_), channel_id=1, source_target_pairs={{0,2},{2,0},{4,6},{6,4},{8,10},{10,8},{12,14},{14,12},{16,18},{18,... | collective-permute-start | bytes 786440 | tf_op jit(solution)/shard_map/ppermute | solution.py:546
  80.9 15.4 %collective-permute-start.27 = (bf16[1024,128]{1,0:T(8,128)(2,1)S(1)}, bf16[1024,128]{1,0:T(8,128)(2,1)S(1)}, u32[]{:S(2)}, u32[]{:S(2)}) collective-permute-start(bf16[1024,128]{1,0:T(8,128)(2,1)S(1)} %get-tuple-element.76.refs_0_), channel_id=1, source_target_pairs={{0,4},{2,6},{4,0},{6,2},{8,12},{10,14},{12,8},{14,10},{16,20},{18,... | collective-permute-start | bytes 786440 | tf_op jit(solution)/shard_map/ppermute | solution.py:546
  81.4 15.4 %collective-permute-start.28 = (bf16[1024,128]{1,0:T(8,128)(2,1)S(1)}, bf16[1024,128]{1,0:T(8,128)(2,1)S(1)}, u32[]{:S(2)}, u32[]{:S(2)}) collective-permute-start(bf16[1024,128]{1,0:T(8,128)(2,1)S(1)} %get-tuple-element.76.refs_0_), channel_id=1, source_target_pairs={{0,6},{2,4},{4,2},{6,0},{8,14},{10,12},{12,10},{14,8},{16,22},{18,... | collective-permute-start | bytes 786440 | tf_op jit(solution)/shard_map/ppermute | solution.py:546
  94.3 15.5 %collective-permute-start.30 = (bf16[1024,128]{1,0:T(8,128)(2,1)S(1)}, bf16[1024,128]{1,0:T(8,128)(2,1)S(1)}, u32[]{:S(2)}, u32[]{:S(2)}) collective-permute-start(bf16[1024,128]{1,0:T(8,128)(2,1)S(1)} %get-tuple-element.80.refs_0_), channel_id=1, source_target_pairs={{0,2},{2,0},{4,6},{6,4},{8,10},{10,8},{12,14},{14,12},{16,18},{18,... | collective-permute-start | bytes 786440 | tf_op jit(solution)/shard_map/ppermute | solution.py:546
  96.3 14.8 %collective-permute-start.31 = (bf16[1024,128]{1,0:T(8,128)(2,1)S(1)}, bf16[1024,128]{1,0:T(8,128)(2,1)S(1)}, u32[]{:S(2)}, u32[]{:S(2)}) collective-permute-start(bf16[1024,128]{1,0:T(8,128)(2,1)S(1)} %get-tuple-element.80.refs_0_), channel_id=1, source_target_pairs={{0,4},{2,6},{4,0},{6,2},{8,12},{10,14},{12,8},{14,10},{16,20},{18,... | collective-permute-start | bytes 786440 | tf_op jit(solution)/shard_map/ppermute | solution.py:546
  96.8 15.6 %collective-permute-start.32 = (bf16[1024,128]{1,0:T(8,128)(2,1)S(1)}, bf16[1024,128]{1,0:T(8,128)(2,1)S(1)}, u32[]{:S(2)}, u32[]{:S(2)}) collective-permute-start(bf16[1024,128]{1,0:T(8,128)(2,1)S(1)} %get-tuple-element.80.refs_0_), channel_id=1, source_target_pairs={{0,6},{2,4},{4,2},{6,0},{8,14},{10,12},{12,10},{14,8},{16,22},{18,... | collective-permute-start | bytes 786440 | tf_op jit(solution)/shard_map/ppermute | solution.py:546
  105.3 17.7 %collective-permute-start.14 = (bf16[2,256,256]{2,1,0:T(8,128)(2,1)}, bf16[2,256,256]{2,1,0:T(8,128)(2,1)S(1)}, u32[]{:S(2)}, u32[]{:S(2)}) collective-permute-start(bf16[2,256,256]{2,1,0:T(8,128)(2,1)} %collective-permute-done.refs_1_), channel_id=1, source_target_pairs={{8,0},{10,2},{12,4},{14,6},{16,8},{18,10},{20,12},{22,14},{24,16},... | collective-permute-start | bytes 786440 | tf_op jit(solution)/shard_map/ppermute | solution.py:554
  109.8 15.3 %collective-permute-start.15 = (bf16[2,256,256]{2,1,0:T(8,128)(2,1)S(1)}, bf16[2,256,256]{2,1,0:T(8,128)(2,1)S(1)}, u32[]{:S(2)}, u32[]{:S(2)}) collective-permute-start(bf16[2,256,256]{2,1,0:T(8,128)(2,1)S(1)} %copy-done.28), channel_id=1, source_target_pairs={{8,0},{10,2},{12,4},{14,6},{16,8},{18,10},{20,12},{22,14},{24,16},... | collective-permute-start | bytes 786440 | tf_op jit(solution)/shard_map/ppermute | solution.py:554
  111.1 18.7 %collective-permute-start.16 = (bf16[2,256,256]{2,1,0:T(8,128)(2,1)S(1)}, bf16[2,256,256]{2,1,0:T(8,128)(2,1)S(1)}, u32[]{:S(2)}, u32[]{:S(2)}) collective-permute-start(bf16[2,256,256]{2,1,0:T(8,128)(2,1)S(1)} %copy-done.31), channel_id=1, source_target_pairs={{8,0},{10,2},{12,4},{14,6},{16,8},{18,10},{20,12},{22,14},{24,16},... | collective-permute-start | bytes 786440 | tf_op jit(solution)/shard_map/ppermute | solution.py:554
  112.4 60.0 %collective-permute-start.29 = (bf16[2,256,512]{2,1,0:T(8,128)(2,1)}, bf16[2,256,512]{2,1,0:T(8,128)(2,1)}, u32[]{:S(2)}, u32[]{:S(2)}) collective-permute-start(bf16[2,256,512]{2,1,0:T(8,128)(2,1)} %get-tuple-element.78), channel_id=1, source_target_pairs={{0,8},{2,10},{4,12},{6,14},{8,0},{10,2},{12,4},{14,6},{16,24},{18,... | collective-permute-start | bytes 1572872 | tf_op jit(solution)/shard_map/ppermute | solution.py:558
  121.7 51.9 %collective-permute-start.33 = (bf16[2,256,512]{2,1,0:T(8,128)(2,1)}, bf16[2,256,512]{2,1,0:T(8,128)(2,1)}, u32[]{:S(2)}, u32[]{:S(2)}) collective-permute-start(bf16[2,256,512]{2,1,0:T(8,128)(2,1)} %get-tuple-element.82), channel_id=1, source_target_pairs={{0,8},{2,10},{4,12},{6,14},{8,0},{10,2},{12,4},{14,6},{16,24},{18,... | collective-permute-start | bytes 1572872 | tf_op jit(solution)/shard_map/ppermute | solution.py:558
  123.8 30.0 %collective-permute-start.12 = (f32[4,4,256]{2,1,0:T(4,128)}, f32[4,4,256]{2,1,0:T(4,128)}, u32[]{:S(2)}, u32[]{:S(2)}) collective-permute-start(f32[4,4,256]{2,1,0:T(4,128)} %get-tuple-element.55.stats_ref), channel_id=1, source_target_pairs={{8,0},{10,2},{12,4},{14,6},{16,8},{18,10},{20,12},{22,14},{24,16},... | collective-permute-start | bytes 49160 | tf_op jit(solution)/shard_map/ppermute | solution.py:554
  125.8 40.1 %collective-permute-start.17 = (bf16[2,128,256]{2,1,0:T(8,128)(2,1)}, bf16[2,128,256]{2,1,0:T(8,128)(2,1)S(1)}, u32[]{:S(2)}, u32[]{:S(2)}) collective-permute-start(bf16[2,128,256]{2,1,0:T(8,128)(2,1)} %pad_maximum_fusion), channel_id=1, source_target_pairs={{16,0},{18,2},{20,4},{22,6},{17,1},{19,3},{21,5},{23,7}} | collective-permute-start | bytes 393224 | tf_op jit(solution)/shard_map/ppermute | solution.py:617
  130.6 35.3 %collective-permute-start.18 = (bf16[2,128,256]{2,1,0:T(8,128)(2,1)}, bf16[2,128,256]{2,1,0:T(8,128)(2,1)}, u32[]{:S(2)}, u32[]{:S(2)}) collective-permute-start(bf16[2,128,256]{2,1,0:T(8,128)(2,1)} %pad_maximum_fusion.1), channel_id=1, source_target_pairs={{24,0},{26,2},{28,4},{30,6},{25,1},{27,3},{29,5},{31,7}} | collective-permute-start | bytes 393224 | tf_op jit(solution)/shard_map/ppermute | solution.py:617
  170.4 15.0 %collective-permute-start.20 = (bf16[3,256,256]{2,1,0:T(8,128)(2,1)S(1)}, bf16[3,256,256]{2,1,0:T(8,128)(2,1)S(1)}, u32[]{:S(2)}, u32[]{:S(2)}) collective-permute-start(bf16[3,256,256]{2,1,0:T(8,128)(2,1)S(1)} %get-tuple-element.66), channel_id=1, source_target_pairs={{0,4},{2,6},{4,0},{6,2},{8,12},{10,14},{12,8},{14,10},{16,20},{18,... | collective-permute-start | bytes 1179656 | tf_op jit(solution)/shard_map/ppermute | solution.py:546
  171.8 13.7 %collective-permute-start.21 = (bf16[3,256,256]{2,1,0:T(8,128)(2,1)S(1)}, bf16[3,256,256]{2,1,0:T(8,128)(2,1)S(1)}, u32[]{:S(2)}, u32[]{:S(2)}) collective-permute-start(bf16[3,256,256]{2,1,0:T(8,128)(2,1)S(1)} %get-tuple-element.67), channel_id=1, source_target_pairs={{0,6},{2,4},{4,2},{6,0},{8,14},{10,12},{12,10},{14,8},{16,22},{18,... | collective-permute-start | bytes 1179656 | tf_op jit(solution)/shard_map/ppermute | solution.py:546
  173.6 14.7 %collective-permute-start.34 = (bf16[1,256,512]{2,1,0:T(8,128)(2,1)S(1)}, bf16[1,256,512]{2,1,0:T(8,128)(2,1)S(1)}, u32[]{:S(2)}, u32[]{:S(2)}) collective-permute-start(bf16[1,256,512]{2,1,0:T(8,128)(2,1)S(1)} %get-tuple-element.84), channel_id=1, source_target_pairs={{0,16},{2,18},{4,20},{6,22},{8,24},{10,26},{12,28},{14,30},{16,0},... | collective-permute-start | bytes 786440 | tf_op jit(solution)/shard_map/ppermute | solution.py:558
  174.8 18.6 %collective-permute-start.35 = (bf16[1,256,512]{2,1,0:T(8,128)(2,1)S(1)}, bf16[1,256,512]{2,1,0:T(8,128)(2,1)S(1)}, u32[]{:S(2)}, u32[]{:S(2)}) collective-permute-start(bf16[1,256,512]{2,1,0:T(8,128)(2,1)S(1)} %get-tuple-element.85), channel_id=1, source_target_pairs={{0,16},{2,18},{4,20},{6,22},{8,24},{10,26},{12,28},{14,30},{16,0},... | collective-permute-start | bytes 786440 | tf_op jit(solution)/shard_map/ppermute | solution.py:558
  (44 other events, 451.6 us)

commit v3 on v2

v3 whole, which is shorter than its diff:
```python
import functools
import math

import jax
import jax.numpy as jnp
from jax import lax
from jax.experimental import pallas as pl
from jax.experimental.pallas import tpu as pltpu
from jax.sharding import PartitionSpec as P

HD = 128
BLK = 128
LOCAL = 8
STRIDE = 16
PAIR = 2 * BLK
SPAN = LOCAL + 1
SCALE = HD ** (-0.5)
SCALE2 = SCALE * math.log2(math.e)
MIB = 1024 * 1024

NT = (((1,), (1,)), ((), ()))
NN = (((1,), (0,)), ((), ()))
TN = (((0,), (0,)), ((), ()))
SMEM = pl.BlockSpec(memory_space=pltpu.SMEM)
VMEM = pl.BlockSpec(memory_space=pltpu.VMEM)


def shape(dims, dtype=jnp.bfloat16):
    return jax.ShapeDtypeStruct(dims, dtype)


def dot(a, b, dims):
    return lax.dot_general(a, b, dims, preferred_element_type=jnp.float32)


def params(size):
    return pltpu.CompilerParams(vmem_limit_bytes=size * MIB)


def cost(flops, size, exps=0):
    return pl.CostEstimate(flops=1, bytes_accessed=1, transcendentals=0)


def call(body, scalars, arrays, outs, scratch, estimate, name, size=16):
    return pl.pallas_call(
        body,
        out_shape=outs,
        in_specs=[SMEM] * len(scalars) + [VMEM] * len(arrays),
        out_specs=[VMEM] * len(outs),
        scratch_shapes=scratch,
        compiler_params=params(size),
        cost_estimate=estimate,
        name=name,
    )(*scalars, *arrays)


def one_head(refs, head):
    return [ref.at[(slice(None),) * (ref.ndim - 1) + (pl.ds(head * HD, HD),)] for ref in refs]


def split_refs(refs, counts):
    refs, taken = list(refs), []
    for count in counts:
        taken.append(refs[:count])
        refs = refs[count:]
    return taken, refs


def pack_kv(keys, values, meta, group, width):
    rows = keys.shape[0]

    def body(meta_ref, k_ref, v_ref, *outs):
        me = meta_ref[0]
        for k in range(group):
            at = pl.multiple_of((me ^ k) * width, width)
            outs[k][0] = k_ref[:, pl.ds(at, width)]
            outs[k][1] = v_ref[:, pl.ds(at, width)]

    return call(
        body, (meta,), (keys, values), [shape((2, rows, width))] * group, [],
        cost(0, 4 * keys.size * 2), "pack_kv",
    )


def grads_packed(queries, out_grad, proj_weight, meta, group, width):
    rows, depth = out_grad.shape

    def body(meta_ref, q_ref, og_ref, w_ref, *outs):
        step = pl.program_id(0)
        got = dot(og_ref[...], w_ref[...], NN).astype(jnp.bfloat16)
        for k in range(group):

            @pl.when(step == k)
            def _():
                outs[k][0] = q_ref[...]
                outs[k][1] = got

    return pl.pallas_call(
        body,
        out_shape=[shape((2, rows, width))] * group,
        grid_spec=pltpu.PrefetchScalarGridSpec(
            num_scalar_prefetch=1,
            grid=(group,),
            in_specs=[
                pl.BlockSpec((rows, width), lambda i, m: (0, m[0] ^ i)),
                pl.BlockSpec((rows, depth), lambda i, m: (0, 0)),
                pl.BlockSpec((depth, width), lambda i, m: (0, m[0] ^ i)),
            ],
            out_specs=[pl.BlockSpec((2, rows, width), lambda i, m: (0, 0, 0))] * group,
        ),
        compiler_params=params(16),
        cost_estimate=cost(2 * rows * depth * width * group, 12 * 1024 * 1024),
        name="attn_grad",
    )(meta, queries, out_grad, proj_weight)


def pack_out_grad(out_grad, meta, group, parts):
    rows, depth = out_grad.shape
    each = depth // (group * parts)
    half = parts // 2

    def body(meta_ref, og_ref, *outs):
        me, core = meta_ref[0], meta_ref[3]
        for k in range(group):
            for part in range(half):
                at = ((core * half + part) * group + (me ^ k)) * each
                at = pl.multiple_of(at, each)
                outs[k][part * each : (part + 1) * each, :] = og_ref[:, pl.ds(at, each)].T

    return call(
        body, (meta,), (out_grad,), [shape((half * each, rows))] * group, [],
        cost(0, 3 * out_grad.size), "pack_out_grad",
    )


def join_columns(pieces, meta, group):
    height, rows = pieces[0].shape

    def body(meta_ref, *refs):
        me = meta_ref[0]
        for k in range(group):
            at = pl.multiple_of((me ^ k) * rows, rows)
            refs[group][:, pl.ds(at, rows)] = refs[k][...]

    return call(
        body, (meta,), tuple(pieces), [shape((height, group * rows))], [],
        cost(0, 2 * 1024 * 1024), "join_columns",
    )[0]


def assemble_kv(pieces, meta, group):
    rows, width = pieces[0].shape[1:]

    def body(meta_ref, *refs):
        me = meta_ref[0]
        pool, rest, strided = refs[group:]
        for k in range(group):
            pool[:, pl.ds(pl.multiple_of((me ^ k) * rows, rows), rows), :] = refs[k][...]
            if k > 0:
                rest[k - 1] = refs[k][...]
        strided[...] = pool[:, pl.ds(pl.multiple_of(meta_ref[2] * BLK, BLK), BLK), :]

    return call(
        body, (meta,), tuple(pieces),
        [
            shape((2, group * rows, width)),
            shape((group - 1, 2, rows, width)),
            shape((2, BLK, width)),
        ],
        [], cost(0, 3 * 1024 * 1024), "assemble_kv",
    )


def assemble(pieces, meta, group):
    lead, rows, width = pieces[0].shape

    def body(meta_ref, *refs):
        me = meta_ref[0]
        for k in range(group):
            at = pl.multiple_of((me ^ k) * rows, rows)
            refs[group][:, pl.ds(at, rows), :] = refs[k][...]

    return call(
        body, (meta,), tuple(pieces), [shape((lead, group * rows, width))], [],
        cost(0, 2 * 1024 * 1024), "assemble",
    )[0]


def masks_of(layout, meta, parts, slots):
    width = layout.shape[1]
    pairs = LOCAL // 2

    def body(meta_ref, table, own_ref, next_ref):
        at_group = meta_ref[1]
        low_half = lax.broadcasted_iota(jnp.int32, (1, PAIR), 1) < BLK

        def bits_of(group_at, row):
            block = group_at * LOCAL + row
            base = block - row % 2 - (LOCAL - 1)
            at = jnp.minimum(block, table.shape[0] - 1)
            bits = jnp.int32(0)
            for c in range(width):
                entry = table[at, c]
                near = entry >= jnp.maximum(block - (LOCAL - 1), 0)
                place = jnp.where(near, entry - base, SPAN + jnp.maximum(entry, 0) // STRIDE)
                bit = jnp.left_shift(jnp.int32(1), place)
                bits = bits | jnp.where(entry >= 0, bit, 0)
            return jnp.where(group_at < parts, bits, 0)

        def row_of(first, second, place):
            one = jnp.where((jnp.right_shift(first, place) & 1) == 1, 0.0, -jnp.inf)
            two = jnp.where((jnp.right_shift(second, place) & 1) == 1, 0.0, -jnp.inf)
            return jnp.where(low_half, one, two).astype(jnp.float32)

        for t in range(pairs):
            first, second = bits_of(at_group, 2 * t), bits_of(at_group, 2 * t + 1)
            for place in range(SPAN + slots):
                own_ref[t, place : place + 1, :] = row_of(first, second, place)
            first, second = bits_of(at_group + 1, 2 * t), bits_of(at_group + 1, 2 * t + 1)
            for place in range(SPAN):
                next_ref[t, place : place + 1, :] = row_of(first, second, place)
            even = at_group % 2 == 0
            place = SPAN + at_group // 2
            first, second = jnp.where(even, first, 0), jnp.where(even, second, 0)
            next_ref[t, SPAN : SPAN + 1, :] = row_of(first, second, place)

    return call(
        body, (meta, layout), (),
        [
            shape((pairs, SPAN + slots, PAIR), jnp.float32),
            shape((pairs, SPAN + 1, PAIR), jnp.float32),
        ],
        [], cost(0, 128 * 1024), "masks",
    )


def fill_pools(meta_ref, own, prev, rest, far, k_pool, v_pool, group, rows, slots):
    me, at_group, offset = meta_ref[0], meta_ref[1], meta_ref[2]
    whole = group * rows
    k_pool[whole : 2 * whole, :] = own[0]
    v_pool[whole : 2 * whole, :] = own[1]
    for k in range(group):
        at = pl.multiple_of((me ^ k) * rows, rows)
        k_pool[pl.ds(at, rows), :] = prev[0] if k == 0 else rest[k - 1, 0]
        v_pool[pl.ds(at, rows), :] = prev[1] if k == 0 else rest[k - 1, 1]
    tail = jnp.zeros((slots * BLK, k_pool.shape[1]), k_pool.dtype)
    k_pool[2 * whole :, :] = tail
    v_pool[2 * whole :, :] = tail

    @pl.when(at_group % 2 == 1)
    def _():
        to = pl.multiple_of(2 * whole + (at_group // 2) * BLK, BLK)
        start = pl.multiple_of(offset * BLK, BLK)
        k_pool[pl.ds(to, BLK), :] = k_pool[pl.ds(start, BLK), :]
        v_pool[pl.ds(to, BLK), :] = v_pool[pl.ds(start, BLK), :]

    for index, ref in enumerate(far):
        distance = index + 2

        @pl.when((at_group >= distance) & ((at_group - distance) % 2 == 0))
        def _():
            to = pl.multiple_of(2 * whole + ((at_group - distance) // 2) * BLK, BLK)
            k_pool[pl.ds(to, BLK), :] = ref[0]
            v_pool[pl.ds(to, BLK), :] = ref[1]


def causal_masks():
    key_at = lax.broadcasted_iota(jnp.int32, (BLK, PAIR), 0)
    query_at = lax.broadcasted_iota(jnp.int32, (BLK, PAIR), 1)
    first = (key_at <= query_at) | (query_at >= BLK)
    second = key_at <= query_at - BLK
    return first, second


def masked_scores(keys, query, bias, masks):
    raw = dot(keys, query, NT) * SCALE2
    tiles = []
    for j in range(keys.shape[0] // BLK):
        tile = raw[j * BLK : (j + 1) * BLK] + bias[j]
        if masks is not None and j in (LOCAL - 1, LOCAL):
            tile = jnp.where(masks[j - LOCAL + 1], tile, -jnp.inf)
        tiles.append(tile)
    return jnp.concatenate(tiles, axis=0)


def bias_rows(bias_ref, t, picked):
    return [bias_ref[t, j : j + 1, :] for j in picked]


def forward(head, qd, own, prev, rest, far, bias, stats, meta, group, slots):
    whole = qd.shape[1]
    rows = whole // group
    pairs = whole // PAIR
    counts = (4, len(far))

    def body(meta_ref, bias_ref, before_ref, *refs):
        (around, far_refs), refs = split_refs(refs, counts)
        qd_ref, *around = one_head(around, head)
        far_refs = one_head(far_refs, head)
        out_ref, stats_ref, k_pool, v_pool = refs
        fill_pools(meta_ref, *around, far_refs, k_pool, v_pool, group, rows, slots)
        stats_ref[...] = before_ref[...]
        masks = causal_masks()
        for t in range(pairs):
            here = slice(t * PAIR, (t + 1) * PAIR)
            window = slice(t * PAIR + BLK, t * PAIR + BLK + SPAN * BLK)
            keys = jnp.concatenate([k_pool[window, :], k_pool[2 * whole :, :]], axis=0)
            vals = jnp.concatenate([v_pool[window, :], v_pool[2 * whole :, :]], axis=0)
            s = masked_scores(keys, qd_ref[0, here, :], bias_rows(bias_ref, t, range(SPAN + slots)), masks)
            top = jnp.max(s, axis=0, keepdims=True)
            e = jnp.exp2(s - top)
            total = jnp.sum(e, axis=0, keepdims=True)
            low = (e * (1.0 / total)).astype(jnp.bfloat16)
            out = dot(low, vals, TN).astype(jnp.bfloat16)
            out_ref[here, :] = out
            product = out.astype(jnp.float32) * qd_ref[1, here, :].astype(jnp.float32)
            stats_ref[t, 2 * head : 2 * head + 1, :] = top + jnp.log2(total)
            stats_ref[t, 2 * head + 1 : 2 * head + 2, :] = jnp.sum(product.T, axis=0, keepdims=True)

    span = (SPAN + slots) * BLK
    return call(
        body, (meta,), (bias, stats, qd, own, prev, rest, *far),
        [shape((whole, HD)), shape(stats.shape, jnp.float32)],
        [pltpu.VMEM((2 * whole + slots * BLK, HD), jnp.bfloat16)] * 2,
        cost(4 * whole * span * HD * 2, 3 * 1024 * 1024, whole * span),
        f"attention_{head}", 24,
    )


def backward(head, qd, own, prev, rest, far, before, bias, stats, meta, group, slots):
    whole, width = qd.shape[1:]
    rows = whole // group
    pairs = whole // PAIR
    counts = (4, len(far), len(before))
    everything = 2 * whole + slots * BLK

    def body(meta_ref, bias_ref, stats_ref, *refs):
        (around, far_refs, before_refs), refs = split_refs(refs, counts)
        qd_ref, *around = one_head(around, head)
        far_refs = one_head(far_refs, head)
        ((dq_ref, grad_ref), far_outs), refs = split_refs(refs, (2, len(far)))
        k_pool, v_pool, far_sum = refs
        at_group = meta_ref[1]
        fill_pools(meta_ref, *around, far_refs, k_pool, v_pool, group, rows, slots)
        masks = causal_masks()
        grad_ref[...] = jnp.zeros_like(grad_ref)
        far_sum[...] = jnp.zeros_like(far_sum)
        for t in range(pairs):
            here = slice(t * PAIR, (t + 1) * PAIR)
            window = slice(t * PAIR + BLK, t * PAIR + BLK + SPAN * BLK)
            others = max(whole - (t * PAIR + BLK), 0)
            end = SPAN * BLK
            mine = slice(t * PAIR + BLK + others - whole, t * PAIR + BLK + end - whole)
            keys = jnp.concatenate([k_pool[window, :], k_pool[2 * whole :, :]], axis=0)
            vals = jnp.concatenate([v_pool[window, :], v_pool[2 * whole :, :]], axis=0)
            query, grad = qd_ref[0, here, :], qd_ref[1, here, :]
            s = masked_scores(keys, query, bias_rows(bias_ref, t, range(SPAN + slots)), masks)
            probs = jnp.exp2(s - stats_ref[t, 2 * head : 2 * head + 1, :])
            delta = stats_ref[t, 2 * head + 1 : 2 * head + 2, :]
            ds = (probs * (dot(vals, grad, NT) - delta)).astype(jnp.bfloat16)
            low = probs.astype(jnp.bfloat16)
            dq_ref[here, :] = (dot(ds, keys, TN) * SCALE).astype(jnp.bfloat16)
            grad_ref[0, mine, :] += dot(ds[others:end], query, NN)
            grad_ref[1, mine, :] += dot(low[others:end], grad, NN)
            far_sum[0] += dot(ds[end:], query, NN)
            far_sum[1] += dot(low[end:], grad, NN)
        for index, ref in enumerate(far_outs):
            slot = jnp.maximum(at_group - index - 2, 0) // 2
            start = pl.multiple_of(slot * BLK, BLK)
            ref[...] = before_refs[index][...]
            lanes = slice(head * HD, (head + 1) * HD)
            ref[0, :, lanes] = (far_sum[0, pl.ds(start, BLK), :] * SCALE).astype(jnp.bfloat16)
            ref[1, :, lanes] = far_sum[1, pl.ds(start, BLK), :].astype(jnp.bfloat16)

    span = (SPAN + slots) * BLK
    outs = call(
        body, (meta,), (bias, stats, qd, own, prev, rest, *far, *before),
        [shape((whole, HD)), shape((2, whole, HD), jnp.float32)]
        + [shape((2, BLK, width))] * len(far),
        [
            pltpu.VMEM((everything, HD), jnp.bfloat16),
            pltpu.VMEM((everything, HD), jnp.bfloat16),
            pltpu.VMEM((2, slots * BLK, HD), jnp.float32),
        ],
        cost(8 * whole * span * HD * 2, 4 * 1024 * 1024, whole * span),
        f"attention_back_{head}", 24,
    )
    return outs[0], outs[1], outs[2:]


def backward_next(grads, qd, own, bias, stats, meta):
    whole, width = qd.shape[1:]
    heads = width // HD
    pairs = whole // PAIR

    def body(meta_ref, bias_ref, stats_ref, *refs):
        (grad_refs, (qd_ref, own_ref, out)), refs = split_refs(refs, (heads, 3))
        strided = pl.ds(pl.multiple_of(meta_ref[2] * BLK, BLK), BLK)
        for h in range(heads):
            lanes = slice(h * HD, (h + 1) * HD)
            out[0, :, lanes] = grad_refs[h][0]
            out[1, :, lanes] = grad_refs[h][1]
            for t in range(pairs):
                here = slice(t * PAIR, (t + 1) * PAIR)
                window = slice(t * PAIR + BLK, whole)
                near = (whole - BLK) // BLK - t * (PAIR // BLK)
                keys = jnp.concatenate([own_ref[0, window, lanes], own_ref[0, strided, lanes]], axis=0)
                vals = jnp.concatenate([own_ref[1, window, lanes], own_ref[1, strided, lanes]], axis=0)
                query, grad = qd_ref[0, here, lanes], qd_ref[1, here, lanes]
                rows_here = bias_rows(bias_ref, t, list(range(near)) + [SPAN])
                s = masked_scores(keys, query, rows_here, None)
                probs = jnp.exp2(s - stats_ref[t, 2 * h : 2 * h + 1, :])
                delta = stats_ref[t, 2 * h + 1 : 2 * h + 2, :]
                ds = (probs * (dot(vals, grad, NT) - delta)).astype(jnp.bfloat16)
                dk = dot(ds, query, NN)
                dv = dot(probs.astype(jnp.bfloat16), grad, NN)
                out[0, window, lanes] += dk[: near * BLK]
                out[1, window, lanes] += dv[: near * BLK]
                out[0, strided, lanes] += dk[near * BLK :]
                out[1, strided, lanes] += dv[near * BLK :]
        out[0] = out[0] * SCALE

    return call(
        body, (meta,), (bias, stats, *grads, qd, own),
        [shape((2, whole, width), jnp.float32)], [],
        cost(8 * whole * 5 * BLK * width, 7 * 1024 * 1024, whole * 5 * BLK * heads),
        "attention_back_next", 24,
    )[0]


def combine(dq, own, far, meta, group, rows):
    whole, width = own.shape[1:]

    def body(meta_ref, own_ref, *refs):
        (dq_refs, far_refs, outs, (acc,)), refs = split_refs(refs, (len(dq), len(far), group, 1))
        me, offset = meta_ref[0], meta_ref[2]
        acc[...] = own_ref[...]
        at = pl.multiple_of(offset * BLK, BLK)
        for ref in far_refs:
            acc[:, pl.ds(at, BLK), :] += ref[...].astype(jnp.float32)
        for k in range(group):
            here = pl.ds(pl.multiple_of((me ^ k) * rows, rows), rows)
            for h in range(len(dq)):
                outs[k][0, :, h * HD : (h + 1) * HD] = dq_refs[h][here, :]
            outs[k][1] = acc[0, here, :].astype(jnp.bfloat16)
            outs[k][2] = acc[1, here, :].astype(jnp.bfloat16)

    return call(
        body, (meta,), (own, *dq, *far), [shape((3, rows, width))] * group,
        [pltpu.VMEM((2, whole, width), jnp.float32)],
        cost(0, 4 * 1024 * 1024), "combine",
    )


def project(head, mine, theirs, attn, before, meta, group, parts):
    height, whole = mine.shape
    each = 2 * height // parts
    full = group * HD
    more = parts // 2 - 1

    def body(meta_ref, mine_ref, theirs_ref, *refs):
        (attn_refs, before_refs, outs), refs = split_refs(refs, (group, len(before), 6))
        keep, first, odds, evens, pool, total = outs
        for ref in before_refs:
            first[:head] = ref[...]
        me, at_group, core = meta_ref[0], meta_ref[1], meta_ref[3]
        for k in range(group):
            at = pl.multiple_of((me ^ k) * HD, HD)
            pool[:, pl.ds(at, HD)] = attn_refs[k][...]
        upper = pl.ds(pl.multiple_of(core * height, height), height)
        lower = pl.ds(pl.multiple_of((1 - core) * height, height), height)
        total[upper, :] = dot(mine_ref[...], pool[...], NN)
        total[lower, :] = dot(theirs_ref[...], pool[...], NN)
        for m in range(parts):
            part = total[pl.ds(pl.multiple_of((at_group ^ m) * each, each), each), :]
            if m == 0:
                keep[...] = part
            elif m == 1:
                first[head] = part.astype(jnp.bfloat16)
            elif m % 2 == 1:
                odds[m // 2 - 1] = part.astype(jnp.bfloat16)
            else:
                evens[m // 2 - 1] = part

    return call(
        body, (meta,), (mine, theirs, *attn, *before),
        [
            shape((each, full), jnp.float32),
            shape((head + 1, each, full)),
            shape((more, each, full)),
            shape((more, each, full), jnp.float32),
        ],
        [pltpu.VMEM((whole, full), jnp.bfloat16), pltpu.VMEM((2 * height, full), jnp.float32)],
        cost(4 * height * whole * full, 6 * 1024 * 1024), f"project_{head}",
    )


def halve(head, evens, arrived):
    count, each, full = evens.shape
    more = (count - 1) // 2

    def body(evens_ref, arrived_ref, first, *rest):
        for m in range(1, count + 1):
            summed = evens_ref[m - 1] + arrived_ref[m - 1].astype(jnp.float32)
            if m == 1:
                first[...] = summed.astype(jnp.bfloat16)
            elif m % 2 == 1:
                rest[0][m // 2 - 1] = summed.astype(jnp.bfloat16)
            else:
                rest[1][m // 2 - 1] = summed

    others = [shape((more, each, full)), shape((more, each, full), jnp.float32)]
    return call(
        body, (), (evens, arrived), [shape((each, full))] + (others if more else []), [],
        cost(0, 3 * 1024 * 1024), f"halve_{head}",
    )


def finish(keep, neighbour, arrived, group):
    heads = len(keep)
    count = len(arrived[0])
    each = keep[0].shape[0]

    def body(*refs):
        (keep_refs, arrived_refs, (first, out)), refs = split_refs(refs, (heads, heads * count, 2))
        for h in range(heads):
            total = keep_refs[h][...] + first[h].astype(jnp.float32)
            for ref in arrived_refs[h * count : (h + 1) * count]:
                total = total + ref[...].astype(jnp.float32)
            for j in range(group):
                at = (j * heads + h) * HD
                out[:, at : at + HD] = total[:, j * HD : (j + 1) * HD]

    flat = [piece for pieces in arrived for piece in pieces]
    return call(
        body, (), (*keep, *flat, neighbour),
        [shape((each, group * heads * HD), jnp.float32)], [],
        cost(0, 3 * 1024 * 1024), "finish",
    )[0]


def unpack(pieces, meta, group):
    rows, width = pieces[0].shape[1:]

    def body(meta_ref, *refs):
        me = meta_ref[0]
        for k in range(group):
            at = pl.ds(pl.multiple_of((me ^ k) * width, width), width)
            for which in range(3):
                refs[group + which][:, at] = refs[k][which]

    return call(
        body, (meta,), tuple(pieces), [shape((rows, group * width))] * 3, [],
        cost(0, 3 * 1024 * 1024), "unpack",
    )


def after(value, *others):
    return lax.optimization_barrier((value, *others))[0]


def local(devices, queries, keys, values, out_grad, proj_weight, layout):
    rows, columns = queries.shape
    group = LOCAL * BLK // rows
    parts = devices // group
    width = columns // group
    heads = width // HD
    blocks = layout.shape[0]
    slots = blocks // STRIDE
    position = lax.axis_index("seq")
    me, at_group = position % group, position // group
    core = lax.axis_index("head")
    offset = layout[blocks - 1, 0] % STRIDE
    place = jnp.stack([me, at_group]).astype(jnp.int32)
    meta = jnp.stack([me, at_group, offset, core]).astype(jnp.int32)

    def swap(piece, k):
        route = [(i, (i // group) * group + ((i % group) ^ k)) for i in range(devices)]
        return lax.ppermute(piece, "seq", route)

    def shifted(piece, distance):
        route = [
            (i, i + distance * group)
            for i in range(devices)
            if 0 <= i + distance * group < devices
        ]
        return lax.ppermute(piece, "seq", route)

    def swap_groups(piece, bit):
        route = [(i, ((i // group) ^ bit) * group + i % group) for i in range(devices)]
        return lax.ppermute(piece, "seq", route)

    def summary_route(distance, back):
        route = [
            (i, i + distance * group)
            for i in range(devices - distance * group)
            if (i // group) % 2 == 0
        ]
        return [(b, a) for a, b in route] if back else route

    def exchange(pieces):
        return [pieces[0]] + [swap(pieces[k], k) for k in range(1, group)]

    def add_up(head, odds, evens, before, token):
        arrivals, bit = [], 2
        odds = after(odds, *jax.tree.leaves(before))
        while True:
            first, *more = halve(head, evens, odds)
            token = after(token, first)
            arrivals.append(swap_groups(first, bit))
            if not more:
                return arrivals, token
            odds, evens = swap_groups(more[0], bit), more[1]
            bit *= 2

    kv = pack_kv(keys, values, place, group, width)
    own_kv = exchange(kv)
    prev = shifted(kv[0], 1)
    early = after(place, own_kv[1])
    qd_cut = grads_packed(queries, out_grad, proj_weight, early, group, width)
    pool, others, strided = assemble_kv(own_kv, after(meta, prev, qd_cut[0]), group)
    rest = shifted(others, 1)
    qd_pieces = exchange(qd_cut)
    bias, bias_next = masks_of(layout, after(meta, strided), parts, slots)
    qd = assemble(qd_pieces, after(meta, bias), group)
    next_qd = shifted(qd, -1)
    strided = after(strided, qd)
    far = [
        lax.ppermute(strided, "seq", summary_route(distance, False))
        for distance in range(2, parts)
    ]
    og = exchange(pack_out_grad(out_grad, after(meta, rest, *far), group, parts))

    stats = jnp.zeros((LOCAL // 2, 2 * heads, PAIR), jnp.float32)
    order = after(meta, og[0])
    attn = []
    for h in range(heads):
        got, stats = forward(h, qd, pool, prev, rest, far, bias, stats, order, group, slots)
        attn.append([got] + [swap(got, k) for k in range(1, group)])
        if h == 0:
            mine = join_columns(og, after(meta, got), group)
            theirs = lax.ppermute(mine, "head", [(0, 1), (1, 0)])
        order = after(meta, got, mine)
    next_stats = shifted(stats, -1)

    dq, grads, keep, finals, firsts = [], [], [], [], []
    far_grads = [jnp.zeros((2, BLK, width), jnp.bfloat16) for _ in far]
    order = after(meta, stats, theirs)
    for h in range(heads):
        got = backward(
            h, qd, pool, prev, rest, far, far_grads, bias, stats, order, group, slots
        )
        dq.append(got[0])
        grads.append(got[1])
        far_grads = got[2]
        order = after(order, got[0], next_stats)
        if h > 0:
            sums, order = add_up(h - 1, odds, evens, got[0], order)
            finals.append(sums)
        kept, first, odds, evens = project(
            h, mine, theirs, attn[h], firsts, order, group, parts
        )
        keep.append(kept)
        firsts = [first]
        odds = swap_groups(odds, 1)
        order = after(meta, first, next_qd)
    neighbour = swap_groups(first, 1)
    far_back = [
        lax.ppermute(piece, "seq", summary_route(index + 2, True))
        for index, piece in enumerate(far_grads)
    ]
    own_grad = backward_next(grads, next_qd, pool, bias_next, next_stats, order)
    sums, order = add_up(heads - 1, odds, evens, (own_grad, finals[0]), meta)
    finals.append(sums)
    final = exchange(combine(dq, own_grad, far_back, order, group, rows))
    query_grad, key_grad, value_grad = unpack(final, meta, group)
    proj_grad = finish(keep, neighbour, finals, group)
    return (query_grad, key_grad, value_grad, proj_grad)


def solution(mesh):
    split = P(("dp", "seq"), "head")
    return jax.shard_map(
        functools.partial(local, mesh.shape["seq"]),
        mesh=mesh,
        in_specs=(split, split, split, P(("dp", "seq"), None), P(None, "head"), P()),
        out_specs=(split, split, split, split),
        check_vma=False,
    )
```

time: 196 us -> 157 us (0.80)
  local copies, waits for them, and re-layouts: 27.7 us -> 10.1 us
  starting transfers between devices: 59 us -> 43.9 us
  Pallas kernels: 49.7 us -> 42.3 us
  waiting for transfers between devices: 52.3 us -> 56.8 us
  other arithmetic: 2.9 us -> 0.15 us
    ppermute x4 -> x5, waiting for transfers between devices: 6.04 us -> 21.4 us  [swap_groups(): return lax.ppermute(piece, 'seq', route)]
    unnamed x80 -> x17, local copies, waits for them, and re-layouts: 21.7 us -> 8.84 us
    ppermute x9 -> x4, starting transfers between devices: 18.4 us -> 9.56 us  [shifted(): return lax.ppermute(piece, 'seq', route)]
    ppermute x9 -> x4, waiting for transfers between devices: 20.3 us -> 12.6 us  [shifted(): return lax.ppermute(piece, 'seq', route)]
    pallas_call x16 -> x18, Pallas kernels: 42.4 us -> 36.6 us  [call(): pl.pallas_call(body, out_shape=outs, in_specs=[SMEM] * len(scalars) + [VM...]
    ppermute x2, waiting for transfers between devices: 7.77 us -> 2.88 us  [local(): lax.ppermute(strided, 'seq', summary_route(distance, False))]
    ppermute x4 -> x5, starting transfers between devices: 7.7 us -> 4.45 us  [swap_groups(): return lax.ppermute(piece, 'seq', route)]
    reshape x4 -> x0, local copies, waits for them, and re-layouts: 2.28 us -> none  [as_bias(): return jnp.repeat(bias, BLK, axis=2)]
  transfers between devices with their start and end apart: 36 -> 32, of which waited for: 9 -> 13; matrix products, arithmetic and copies ran while one was open for 5% -> 1% of each run, Pallas kernels for 20% -> 22%
where the time goes in v3:
time: 157 us; the launch traced here: 156 us
  waiting for transfers between devices  56.8 us (36%)
  starting transfers between devices  43.9 us (28%)
  Pallas kernels  42.3 us (27%)
  local copies, waits for them, and re-layouts  10.1 us (6%)
  between operations  2.88 us (2%)
    pallas_call x18, Pallas kernels, call(): pl.pallas_call(body, out_shape=outs, in_specs=[SMEM] * len(scalars) + [VM...  36.6 us
    ppermute x18, starting transfers between devices, swap(): return lax.ppermute(piece, 'seq', route)  22.8 us
    ppermute x5, waiting for transfers between devices, swap_groups(): return lax.ppermute(piece, 'seq', route)  21.4 us
    ppermute x18, waiting for transfers between devices, swap(): return lax.ppermute(piece, 'seq', route)  20 us
    ppermute x4, waiting for transfers between devices, shifted(): return lax.ppermute(piece, 'seq', route)  12.6 us
    ppermute x4, starting transfers between devices, shifted(): return lax.ppermute(piece, 'seq', route)  9.56 us
    unnamed x17, local copies, waits for them, and re-layouts  8.84 us
    pallas_call x1, Pallas kernels, grads_packed(): pl.pallas_call(body, out_shape=[shape((2, rows, width))] * group, grid_sp...  5.67 us
  transfers between devices with their start and end apart: 32, of which 13 were waited for; matrix products, arithmetic and copies ran while one was open for 1% of the time, Pallas kernels for 22%

profile of v3, /device:TPU:0, one launch (start us, length us, event | category | flops | bytes accessed | tf_op | source)
XLA Modules:
  0.0 156.2 jit_solution(16128864856776561052)
XLA Ops:
  3.5 3.0 %collective-permute-start.1 = (bf16[2,256,256]{2,1,0:T(8,128)(2,1)S(1)}, bf16[2,256,256]{2,1,0:T(8,128)(2,1)S(1)}, u32[]{:S(2)}, u32[]{:S(2)}) collective-permute-start(bf16[2,256,256]{2,1,0:T(8,128)(2,1)S(1)} %get-tuple-element.67), channel_id=1, source_target_pairs={{0,2},{2,0},{4,6},{6,4},{8,10},{10,8},{12,14},{14,12},{16,18},{18,... | collective-permute-start | bytes 786440 | tf_op jit(solution)/shard_map/ppermute | solution.py:579
  6.5 3.5 %collective-permute-start = (bf16[2,256,256]{2,1,0:T(8,128)(2,1)S(1)}, bf16[2,256,256]{2,1,0:T(8,128)(2,1)S(1)}, u32[]{:S(2)}, u32[]{:S(2)}) collective-permute-start(bf16[2,256,256]{2,1,0:T(8,128)(2,1)S(1)} %get-tuple-element.66.refs_0_), channel_id=1, source_target_pairs={{0,8},{2,10},{4,12},{6,14},{8,16},{10,18},{12,20},{14,22},{16,24},... | collective-permute-start | bytes 786440 | tf_op jit(solution)/shard_map/ppermute | solution.py:587
  10.0 1.6 %collective-permute-start.2 = (bf16[2,256,256]{2,1,0:T(8,128)(2,1)S(1)}, bf16[2,256,256]{2,1,0:T(8,128)(2,1)S(1)}, u32[]{:S(2)}, u32[]{:S(2)}) collective-permute-start(bf16[2,256,256]{2,1,0:T(8,128)(2,1)S(1)} %get-tuple-element.71), channel_id=1, source_target_pairs={{0,4},{2,6},{4,0},{6,2},{8,12},{10,14},{12,8},{14,10},{16,20},{18,... | collective-permute-start | bytes 786440 | tf_op jit(solution)/shard_map/ppermute | solution.py:579
  15.4 3.4 %copy-done = bf16[4096,1024]{1,0:T(8,128)(2,1)S(1)} copy-done((bf16[4096,1024]{1,0:T(8,128)(2,1)S(1)}, bf16[4096,1024]{1,0:T(8,128)(2,1)}, u32[]{:S(2)}) %copy-start) | copy-done | bytes 8388632
  18.8 1.6 %copy-done.1 = bf16[256,4096]{1,0:T(8,128)(2,1)S(1)} copy-done((bf16[256,4096]{1,0:T(8,128)(2,1)S(1)}, bf16[256,4096]{1,0:T(8,128)(2,1)}, u32[]{:S(2)}) %copy-start.1) | copy-done | bytes 2097176
  21.4 5.7 %attn_grad.1 = (bf16[2,256,256]{2,1,0:T(8,128)(2,1)S(1)}, bf16[2,256,256]{2,1,0:T(8,128)(2,1)}, bf16[2,256,256]{2,1,0:T(8,128)(2,1)}, bf16[2,256,256]{2,1,0:T(8,128)(2,1)S(1)}) custom-call(s32[2]{0:T(128)S(1)} %pad_add_fusion.1.meta_ref, bf16[256,1024]{1,0:T(8,128)(2,1)S(1)} %copy-done.3, bf16[256,4096]{1,0:T(8,128)(2,1)S(1)} %copy-done.1, ...), custom_call_target="tpu_custom_call" | custom-call | flops 1 | bytes 1 | tf_op jit(solution)/shard_map/attn_grad/pallas_call | solution.py:98
  27.1 1.5 assemble_kv.1
  29.3 3.5 %collective-permute-start.4 = (bf16[3,2,256,256]{3,2,1,0:T(8,128)(2,1)}, bf16[3,2,256,256]{3,2,1,0:T(8,128)(2,1)S(1)}, u32[]{:S(2)}, u32[]{:S(2)}) collective-permute-start(bf16[3,2,256,256]{3,2,1,0:T(8,128)(2,1)} %get-tuple-element.73), channel_id=1, source_target_pairs={{0,8},{2,10},{4,12},{6,14},{8,16},{10,18},{12,20},{14,22},{16,24},... | collective-permute-start | bytes 2359304 | tf_op jit(solution)/shard_map/ppermute | solution.py:587
  32.8 1.6 collective-permute-start.5
  36.4 1.9 %masks.1 = (f32[4,11,256]{2,1,0:T(8,128)S(1)}, f32[4,10,256]{2,1,0:T(8,128)S(1)}) custom-call(s32[4]{0:T(128)S(1)} %pad_add_fusion.meta_ref, s32[32,10]{1,0:T(8,128)S(1)} %copy.10.table), custom_call_target="tpu_custom_call" | custom-call | flops 1 | bytes 1 | tf_op jit(solution)/shard_map/masks/pallas_call | solution.py:45
  38.3 4.0 %collective-permute-done.5.refs_1_ = bf16[2,256,256]{2,1,0:T(8,128)(2,1)S(1)} collective-permute-done((bf16[2,256,256]{2,1,0:T(8,128)(2,1)}, bf16[2,256,256]{2,1,0:T(8,128)(2,1)S(1)}, u32[]{:S(2)}, u32[]{:S(2)}) %collective-permute-start.5) | collective-permute-done | bytes 262176 | tf_op jit(solution)/shard_map/ppermute | solution.py:579
  42.3 4.2 %collective-permute-done.6.refs_2_ = bf16[2,256,256]{2,1,0:T(8,128)(2,1)S(1)} collective-permute-done((bf16[2,256,256]{2,1,0:T(8,128)(2,1)}, bf16[2,256,256]{2,1,0:T(8,128)(2,1)S(1)}, u32[]{:S(2)}, u32[]{:S(2)}) %collective-permute-start.6) | collective-permute-done | bytes 262176 | tf_op jit(solution)/shard_map/ppermute | solution.py:579
  47.1 3.2 %collective-permute-start.8 = (bf16[2,128,256]{2,1,0:T(8,128)(2,1)}, bf16[2,128,256]{2,1,0:T(8,128)(2,1)S(1)}, u32[]{:S(2)}, u32[]{:S(2)}) collective-permute-start(bf16[2,128,256]{2,1,0:T(8,128)(2,1)} %copy-done.6), channel_id=1, source_target_pairs={{0,16},{2,18},{4,20},{6,22},{1,17},{3,19},{5,21},{7,23}} | collective-permute-start | bytes 393224 | tf_op jit(solution)/shard_map/ppermute | solution.py:629
  56.8 1.5 collective-permute-start.11
  58.9 4.5 %attention_0.1 = (bf16[1024,128]{1,0:T(8,128)(2,1)S(1)}, f32[4,4,256]{2,1,0:T(4,128)S(1)}) custom-call(s32[4]{0:T(128)S(1)} %pad_add_fusion.meta_ref, f32[4,11,256]{2,1,0:T(8,128)S(1)} %get-tuple-element.76.bias_ref, f32[4,4,256]{2,1,0:T(4,128)S(1)} %broadcast_in_dim.3.before_ref, bf16[2,1024,256]{2,1,0:T(8,128)(2,1)S(1)} %assemble.1.refs_0_, ...), custom_call_target="tpu_custom_call" | custom-call | flops 1 | bytes 1 | tf_op jit(solution)/shard_map/attention_0/pallas_call | solution.py:45
  63.7 4.4 %collective-permute-done.11.refs_2_ = bf16[512,256]{1,0:T(8,128)(2,1)S(1)} collective-permute-done((bf16[512,256]{1,0:T(8,128)(2,1)S(1)}, bf16[512,256]{1,0:T(8,128)(2,1)S(1)}, u32[]{:S(2)}, u32[]{:S(2)}) %collective-permute-start.11) | collective-permute-done | bytes 262176 | tf_op jit(solution)/shard_map/ppermute | solution.py:579
  70.2 1.5 collective-permute-start.15
  73.7 4.7 %attention_1.1 = (bf16[1024,128]{1,0:T(8,128)(2,1)S(1)}, f32[4,4,256]{2,1,0:T(4,128)S(1)}) custom-call(s32[4]{0:T(128)S(1)} %pad_add_fusion.meta_ref, f32[4,11,256]{2,1,0:T(8,128)S(1)} %get-tuple-element.76.bias_ref, f32[4,4,256]{2,1,0:T(4,128)S(1)} %get-tuple-element.92.before_ref, bf16[2,1024,256]{2,1,0:T(8,128)(2,1)S(1)} %assemble.1.refs_0_, ...), custom_call_target="tpu_custom_call" | custom-call | flops 1 | bytes 1 | tf_op jit(solution)/shard_map/attention_1/pallas_call | solution.py:45
  79.8 4.3 %attention_back_0.1 = (bf16[1024,128]{1,0:T(8,128)(2,1)S(1)}, f32[2,1024,128]{2,1,0:T(8,128)S(1)}, bf16[2,128,256]{2,1,0:T(8,128)(2,1)S(1)}, bf16[2,128,256]{2,1,0:T(8,128)(2,1)S(1)}) custom-call(s32[4]{0:T(128)S(1)} %pad_add_fusion.meta_ref, f32[4,11,256]{2,1,0:T(8,128)S(1)} %get-tuple-element.76.bias_ref, f32[4,4,256]{2,1,0:T(4,128)S(1)} %get-tuple-element.93.stats_ref, ...), custom_call_target="tpu_custom_call" | custom-call | flops 1 | bytes 1 | tf_op jit(solution)/shard_map/attention_back_0/pallas_call | solution.py:45
  84.1 12.6 %collective-permute-done.14.stats_ref = f32[4,4,256]{2,1,0:T(4,128)S(1)} collective-permute-done((f32[4,4,256]{2,1,0:T(4,128)S(1)}, f32[4,4,256]{2,1,0:T(4,128)S(1)}, u32[]{:S(2)}, u32[]{:S(2)}) %collective-permute-start.14) | collective-permute-done | bytes 16416 | tf_op jit(solution)/shard_map/ppermute | solution.py:587
  96.7 2.2 %project_0.1 = (f32[256,512]{1,0:T(8,128)S(1)}, bf16[1,256,512]{2,1,0:T(8,128)(2,1)S(1)}, bf16[1,256,512]{2,1,0:T(8,128)(2,1)S(1)}, f32[1,256,512]{2,1,0:T(8,128)S(1)}) custom-call(s32[4]{0:T(128)S(1)} %pad_add_fusion.meta_ref, bf16[512,1024]{1,0:T(8,128)(2,1)S(1)} %join_columns.1.mine_ref, bf16[512,1024]{1,0:T(8,128)(2,1)S(1)} %collective-permute-done.13.theirs_ref, ...), custom_call_target="tpu_custom_call" | custom-call | flops 1 | bytes 1 | tf_op jit(solution)/shard_map/project_0/pallas_call | solution.py:45
  101.1 1.6 collective-permute-start.22
  102.6 4.5 %attention_back_1.1 = (bf16[1024,128]{1,0:T(8,128)(2,1)S(1)}, f32[2,1024,128]{2,1,0:T(8,128)S(1)}, bf16[2,128,256]{2,1,0:T(8,128)(2,1)S(1)}, bf16[2,128,256]{2,1,0:T(8,128)(2,1)S(1)}) custom-call(s32[4]{0:T(128)S(1)} %pad_add_fusion.meta_ref, f32[4,11,256]{2,1,0:T(8,128)S(1)} %get-tuple-element.76.bias_ref, f32[4,4,256]{2,1,0:T(4,128)S(1)} %get-tuple-element.93.stats_ref, ...), custom_call_target="tpu_custom_call" | custom-call | flops 1 | bytes 1 | tf_op jit(solution)/shard_map/attention_back_1/pallas_call | solution.py:45
  109.4 4.3 %collective-permute-done.22.refs_3_ = bf16[1024,128]{1,0:T(8,128)(2,1)S(1)} collective-permute-done((bf16[1024,128]{1,0:T(8,128)(2,1)S(1)}, bf16[1024,128]{1,0:T(8,128)(2,1)S(1)}, u32[]{:S(2)}, u32[]{:S(2)}) %collective-permute-start.22) | collective-permute-done | bytes 262176 | tf_op jit(solution)/shard_map/ppermute | solution.py:579
  113.7 2.1 %project_1.1 = (f32[256,512]{1,0:T(8,128)S(1)}, bf16[2,256,512]{2,1,0:T(8,128)(2,1)S(1)}, bf16[1,256,512]{2,1,0:T(8,128)(2,1)S(1)}, f32[1,256,512]{2,1,0:T(8,128)S(1)}) custom-call(s32[4]{0:T(128)S(1)} %pad_add_fusion.meta_ref, bf16[512,1024]{1,0:T(8,128)(2,1)S(1)} %join_columns.1.mine_ref, bf16[512,1024]{1,0:T(8,128)(2,1)S(1)} %collective-permute-done.13.theirs_ref, ...), custom_call_target="tpu_custom_call" | custom-call | flops 1 | bytes 1 | tf_op jit(solution)/shard_map/project_1/pallas_call | solution.py:45
  115.8 1.7 %collective-permute-start.23 = (bf16[1,256,512]{2,1,0:T(8,128)(2,1)S(1)}, bf16[1,256,512]{2,1,0:T(8,128)(2,1)S(1)}, u32[]{:S(2)}, u32[]{:S(2)}) collective-permute-start(bf16[1,256,512]{2,1,0:T(8,128)(2,1)S(1)} %get-tuple-element.109), channel_id=1, source_target_pairs={{0,8},{2,10},{4,12},{6,14},{8,0},{10,2},{12,4},{14,6},{16,24},{18,... | collective-permute-start | bytes 786440 | tf_op jit(solution)/shard_map/ppermute | solution.py:591
  117.6 2.3 %collective-permute-start.24 = (bf16[256,512]{1,0:T(8,128)(2,1)S(1)}, bf16[256,512]{1,0:T(8,128)(2,1)S(1)}, u32[]{:S(2)}, u32[]{:S(2)}) collective-permute-start(bf16[256,512]{1,0:T(8,128)(2,1)S(1)} %halve_0.1), channel_id=1, source_target_pairs={{0,16},{2,18},{4,20},{6,22},{8,24},{10,26},{12,28},{14,30},{16,0},... | collective-permute-start | bytes 786440 | tf_op jit(solution)/shard_map/ppermute | solution.py:591
  122.6 3.9 %attention_back_next.1.own_ref = f32[2,1024,256]{2,1,0:T(8,128)S(1)} custom-call(s32[4]{0:T(128)S(1)} %pad_add_fusion.meta_ref, f32[4,10,256]{2,1,0:T(8,128)S(1)} %get-tuple-element.112.bias_ref, f32[4,4,256]{2,1,0:T(4,128)S(1)} %collective-permute-done.14.stats_ref, f32[2,1024,128]{2,1,0:T(8,128)S(1)} %get-tuple-element.113.refs_0_, ...), custom_call_target="tpu_custom_call" | custom-call | flops 1 | bytes 1 | tf_op jit(solution)/shard_map/attention_back_next/pallas_call | solution.py:45
  126.5 9.8 %collective-permute-done.23.arrived_ref = bf16[1,256,512]{2,1,0:T(8,128)(2,1)S(1)} collective-permute-done((bf16[1,256,512]{2,1,0:T(8,128)(2,1)S(1)}, bf16[1,256,512]{2,1,0:T(8,128)(2,1)S(1)}, u32[]{:S(2)}, u32[]{:S(2)}) %collective-permute-start.23) | collective-permute-done | bytes 262176 | tf_op jit(solution)/shard_map/ppermute | solution.py:591
  137.7 1.7 %collective-permute-start.28 = (bf16[3,256,256]{2,1,0:T(8,128)(2,1)S(1)}, bf16[3,256,256]{2,1,0:T(8,128)(2,1)S(1)}, u32[]{:S(2)}, u32[]{:S(2)}) collective-permute-start(bf16[3,256,256]{2,1,0:T(8,128)(2,1)S(1)} %get-tuple-element.121), channel_id=1, source_target_pairs={{0,4},{2,6},{4,0},{6,2},{8,12},{10,14},{12,8},{14,10},{16,20},{18,... | collective-permute-start | bytes 1179656 | tf_op jit(solution)/shard_map/ppermute | solution.py:579
  140.8 11.6 %collective-permute-done.30.refs_3_ = bf16[256,512]{1,0:T(8,128)(2,1)S(1)} collective-permute-done((bf16[256,512]{1,0:T(8,128)(2,1)S(1)}, bf16[256,512]{1,0:T(8,128)(2,1)S(1)}, u32[]{:S(2)}, u32[]{:S(2)}) %collective-permute-start.30) | collective-permute-done | bytes 262176 | tf_op jit(solution)/shard_map/ppermute | solution.py:591
  154.3 1.9 %unpack.1 = (bf16[256,1024]{1,0:T(8,128)(2,1)}, bf16[256,1024]{1,0:T(8,128)(2,1)}, bf16[256,1024]{1,0:T(8,128)(2,1)}) custom-call(s32[4]{0:T(128)S(1)} %pad_add_fusion.meta_ref, bf16[3,256,256]{2,1,0:T(8,128)(2,1)S(1)} %get-tuple-element.119.refs_0_, bf16[3,256,256]{2,1,0:T(8,128)(2,1)S(1)} %collective-permute-done.27.refs_1_, ...), custom_call_target="tpu_custom_call" | custom-call | flops 1 | bytes 1 | tf_op jit(solution)/shard_map/unpack/pallas_call | solution.py:45
  (73 shorter events, 33.6 us)
Async XLA Ops:
  3.5 11.9 %collective-permute-start.1 = (bf16[2,256,256]{2,1,0:T(8,128)(2,1)S(1)}, bf16[2,256,256]{2,1,0:T(8,128)(2,1)S(1)}, u32[]{:S(2)}, u32[]{:S(2)}) collective-permute-start(bf16[2,256,256]{2,1,0:T(8,128)(2,1)S(1)} %get-tuple-element.67), channel_id=1, source_target_pairs={{0,2},{2,0},{4,6},{6,4},{8,10},{10,8},{12,14},{14,12},{16,18},{18,... | collective-permute-start | bytes 786440 | tf_op jit(solution)/shard_map/ppermute | solution.py:579
  6.5 20.6 %collective-permute-start = (bf16[2,256,256]{2,1,0:T(8,128)(2,1)S(1)}, bf16[2,256,256]{2,1,0:T(8,128)(2,1)S(1)}, u32[]{:S(2)}, u32[]{:S(2)}) collective-permute-start(bf16[2,256,256]{2,1,0:T(8,128)(2,1)S(1)} %get-tuple-element.66.refs_0_), channel_id=1, source_target_pairs={{0,8},{2,10},{4,12},{6,14},{8,16},{10,18},{12,20},{14,22},{16,24},... | collective-permute-start | bytes 786440 | tf_op jit(solution)/shard_map/ppermute | solution.py:587
  10.0 17.1 %collective-permute-start.2 = (bf16[2,256,256]{2,1,0:T(8,128)(2,1)S(1)}, bf16[2,256,256]{2,1,0:T(8,128)(2,1)S(1)}, u32[]{:S(2)}, u32[]{:S(2)}) collective-permute-start(bf16[2,256,256]{2,1,0:T(8,128)(2,1)S(1)} %get-tuple-element.71), channel_id=1, source_target_pairs={{0,4},{2,6},{4,0},{6,2},{8,12},{10,14},{12,8},{14,10},{16,20},{18,... | collective-permute-start | bytes 786440 | tf_op jit(solution)/shard_map/ppermute | solution.py:579
  11.6 15.5 %collective-permute-start.3 = (bf16[2,256,256]{2,1,0:T(8,128)(2,1)S(1)}, bf16[2,256,256]{2,1,0:T(8,128)(2,1)S(1)}, u32[]{:S(2)}, u32[]{:S(2)}) collective-permute-start(bf16[2,256,256]{2,1,0:T(8,128)(2,1)S(1)} %get-tuple-element.72), channel_id=1, source_target_pairs={{0,6},{2,4},{4,2},{6,0},{8,14},{10,12},{12,10},{14,8},{16,22},{18,... | collective-permute-start | bytes 786440 | tf_op jit(solution)/shard_map/ppermute | solution.py:579
  29.3 25.2 %collective-permute-start.4 = (bf16[3,2,256,256]{3,2,1,0:T(8,128)(2,1)}, bf16[3,2,256,256]{3,2,1,0:T(8,128)(2,1)S(1)}, u32[]{:S(2)}, u32[]{:S(2)}) collective-permute-start(bf16[3,2,256,256]{3,2,1,0:T(8,128)(2,1)} %get-tuple-element.73), channel_id=1, source_target_pairs={{0,8},{2,10},{4,12},{6,14},{8,16},{10,18},{12,20},{14,22},{16,24},... | collective-permute-start | bytes 2359304 | tf_op jit(solution)/shard_map/ppermute | solution.py:587
  32.8 9.5 %collective-permute-start.5 = (bf16[2,256,256]{2,1,0:T(8,128)(2,1)}, bf16[2,256,256]{2,1,0:T(8,128)(2,1)S(1)}, u32[]{:S(2)}, u32[]{:S(2)}) collective-permute-start(bf16[2,256,256]{2,1,0:T(8,128)(2,1)} %get-tuple-element.78), channel_id=1, source_target_pairs={{0,2},{2,0},{4,6},{6,4},{8,10},{10,8},{12,14},{14,12},{16,18},{18,... | collective-permute-start | bytes 786440 | tf_op jit(solution)/shard_map/ppermute | solution.py:579
  34.3 12.2 %collective-permute-start.6 = (bf16[2,256,256]{2,1,0:T(8,128)(2,1)}, bf16[2,256,256]{2,1,0:T(8,128)(2,1)S(1)}, u32[]{:S(2)}, u32[]{:S(2)}) collective-permute-start(bf16[2,256,256]{2,1,0:T(8,128)(2,1)} %get-tuple-element.79), channel_id=1, source_target_pairs={{0,4},{2,6},{4,0},{6,2},{8,12},{10,14},{12,8},{14,10},{16,20},{18,... | collective-permute-start | bytes 786440 | tf_op jit(solution)/shard_map/ppermute | solution.py:579
  35.8 10.7 %collective-permute-start.7 = (bf16[2,256,256]{2,1,0:T(8,128)(2,1)S(1)}, bf16[2,256,256]{2,1,0:T(8,128)(2,1)S(1)}, u32[]{:S(2)}, u32[]{:S(2)}) collective-permute-start(bf16[2,256,256]{2,1,0:T(8,128)(2,1)S(1)} %get-tuple-element.80), channel_id=1, source_target_pairs={{0,6},{2,4},{4,2},{6,0},{8,14},{10,12},{12,10},{14,8},{16,22},{18,... | collective-permute-start | bytes 786440 | tf_op jit(solution)/shard_map/ppermute | solution.py:579
  47.1 6.0 %collective-permute-start.8 = (bf16[2,128,256]{2,1,0:T(8,128)(2,1)}, bf16[2,128,256]{2,1,0:T(8,128)(2,1)S(1)}, u32[]{:S(2)}, u32[]{:S(2)}) collective-permute-start(bf16[2,128,256]{2,1,0:T(8,128)(2,1)} %copy-done.6), channel_id=1, source_target_pairs={{0,16},{2,18},{4,20},{6,22},{1,17},{3,19},{5,21},{7,23}} | collective-permute-start | bytes 393224 | tf_op jit(solution)/shard_map/ppermute | solution.py:629
  50.3 4.2 %collective-permute-start.9 = (bf16[2,128,256]{2,1,0:T(8,128)(2,1)}, bf16[2,128,256]{2,1,0:T(8,128)(2,1)S(1)}, u32[]{:S(2)}, u32[]{:S(2)}) collective-permute-start(bf16[2,128,256]{2,1,0:T(8,128)(2,1)} %copy-done.6), channel_id=1, source_target_pairs={{0,24},{2,26},{4,28},{6,30},{1,25},{3,27},{5,29},{7,31}} | collective-permute-start | bytes 393224 | tf_op jit(solution)/shard_map/ppermute | solution.py:629
  55.4 8.3 %collective-permute-start.10 = (bf16[512,256]{1,0:T(8,128)(2,1)S(1)}, bf16[512,256]{1,0:T(8,128)(2,1)S(1)}, u32[]{:S(2)}, u32[]{:S(2)}) collective-permute-start(bf16[512,256]{1,0:T(8,128)(2,1)S(1)} %get-tuple-element.88), channel_id=1, source_target_pairs={{0,2},{2,0},{4,6},{6,4},{8,10},{10,8},{12,14},{14,12},{16,18},{18,... | collective-permute-start | bytes 786440 | tf_op jit(solution)/shard_map/ppermute | solution.py:579
  56.8 11.3 %collective-permute-start.11 = (bf16[512,256]{1,0:T(8,128)(2,1)S(1)}, bf16[512,256]{1,0:T(8,128)(2,1)S(1)}, u32[]{:S(2)}, u32[]{:S(2)}) collective-permute-start(bf16[512,256]{1,0:T(8,128)(2,1)S(1)} %get-tuple-element.89), channel_id=1, source_target_pairs={{0,4},{2,6},{4,0},{6,2},{8,12},{10,14},{12,8},{14,10},{16,20},{18,... | collective-permute-start | bytes 786440 | tf_op jit(solution)/shard_map/ppermute | solution.py:579
  58.3 9.8 %collective-permute-start.12 = (bf16[512,256]{1,0:T(8,128)(2,1)S(1)}, bf16[512,256]{1,0:T(8,128)(2,1)S(1)}, u32[]{:S(2)}, u32[]{:S(2)}) collective-permute-start(bf16[512,256]{1,0:T(8,128)(2,1)S(1)} %get-tuple-element.90), channel_id=1, source_target_pairs={{0,6},{2,4},{4,2},{6,0},{8,14},{10,12},{12,10},{14,8},{16,22},{18,... | collective-permute-start | bytes 786440 | tf_op jit(solution)/shard_map/ppermute | solution.py:579
  68.8 9.6 %collective-permute-start.13 = (bf16[512,1024]{1,0:T(8,128)(2,1)S(1)}, bf16[512,1024]{1,0:T(8,128)(2,1)S(1)}, u32[]{:S(2)}, u32[]{:S(2)}) collective-permute-start(bf16[512,1024]{1,0:T(8,128)(2,1)S(1)} %join_columns.1.mine_ref), channel_id=1, source_target_pairs={{0,1},{1,0},{2,3},{3,2},{4,5},{5,4},{6,7},{7,6},{8,9},{9,8},{10,11... | collective-permute-start | bytes 3145736 | tf_op jit(solution)/shard_map/ppermute | solution.py:642
  68.9 33.8 %collective-permute-start.18 = (bf16[2,1024,256]{2,1,0:T(8,128)(2,1)S(1)}, bf16[2,1024,256]{2,1,0:T(8,128)(2,1)S(1)}, u32[]{:S(2)}, u32[]{:S(2)}) collective-permute-start(bf16[2,1024,256]{2,1,0:T(8,128)(2,1)S(1)} %assemble.1.refs_0_), channel_id=1, source_target_pairs={{8,0},{10,2},{12,4},{14,6},{16,8},{18,10},{20,12},{22,14},{24,16},... | collective-permute-start | bytes 3145736 | tf_op jit(solution)/shard_map/ppermute | solution.py:587
  70.2 26.5 %collective-permute-start.15 = (bf16[1024,128]{1,0:T(8,128)(2,1)S(1)}, bf16[1024,128]{1,0:T(8,128)(2,1)S(1)}, u32[]{:S(2)}, u32[]{:S(2)}) collective-permute-start(bf16[1024,128]{1,0:T(8,128)(2,1)S(1)} %get-tuple-element.86.refs_0_), channel_id=1, source_target_pairs={{0,2},{2,0},{4,6},{6,4},{8,10},{10,8},{12,14},{14,12},{16,18},{18,... | collective-permute-start | bytes 786440 | tf_op jit(solution)/shard_map/ppermute | solution.py:579
  71.7 25.0 %collective-permute-start.16 = (bf16[1024,128]{1,0:T(8,128)(2,1)S(1)}, bf16[1024,128]{1,0:T(8,128)(2,1)S(1)}, u32[]{:S(2)}, u32[]{:S(2)}) collective-permute-start(bf16[1024,128]{1,0:T(8,128)(2,1)S(1)} %get-tuple-element.86.refs_0_), channel_id=1, source_target_pairs={{0,4},{2,6},{4,0},{6,2},{8,12},{10,14},{12,8},{14,10},{16,20},{18,... | collective-permute-start | bytes 786440 | tf_op jit(solution)/shard_map/ppermute | solution.py:579
  72.3 24.3 %collective-permute-start.17 = (bf16[1024,128]{1,0:T(8,128)(2,1)S(1)}, bf16[1024,128]{1,0:T(8,128)(2,1)S(1)}, u32[]{:S(2)}, u32[]{:S(2)}) collective-permute-start(bf16[1024,128]{1,0:T(8,128)(2,1)S(1)} %get-tuple-element.86.refs_0_), channel_id=1, source_target_pairs={{0,6},{2,4},{4,2},{6,0},{8,14},{10,12},{12,10},{14,8},{16,22},{18,... | collective-permute-start | bytes 786440 | tf_op jit(solution)/shard_map/ppermute | solution.py:579
  78.4 18.2 %collective-permute-start.14 = (f32[4,4,256]{2,1,0:T(4,128)S(1)}, f32[4,4,256]{2,1,0:T(4,128)S(1)}, u32[]{:S(2)}, u32[]{:S(2)}) collective-permute-start(f32[4,4,256]{2,1,0:T(4,128)S(1)} %get-tuple-element.93.stats_ref), channel_id=1, source_target_pairs={{8,0},{10,2},{12,4},{14,6},{16,8},{18,10},{20,12},{22,14},{24,16},... | collective-permute-start | bytes 49160 | tf_op jit(solution)/shard_map/ppermute | solution.py:587
  98.9 8.3 %collective-permute-start.19 = (bf16[1,256,512]{2,1,0:T(8,128)(2,1)S(1)}, bf16[1,256,512]{2,1,0:T(8,128)(2,1)S(1)}, u32[]{:S(2)}, u32[]{:S(2)}) collective-permute-start(bf16[1,256,512]{2,1,0:T(8,128)(2,1)S(1)} %get-tuple-element.104), channel_id=1, source_target_pairs={{0,8},{2,10},{4,12},{6,14},{8,0},{10,2},{12,4},{14,6},{16,24},{18,... | collective-permute-start | bytes 786440 | tf_op jit(solution)/shard_map/ppermute | solution.py:591
  99.2 9.2 %collective-permute-start.20 = (bf16[1024,128]{1,0:T(8,128)(2,1)S(1)}, bf16[1024,128]{1,0:T(8,128)(2,1)S(1)}, u32[]{:S(2)}, u32[]{:S(2)}) collective-permute-start(bf16[1024,128]{1,0:T(8,128)(2,1)S(1)} %get-tuple-element.107.refs_0_), channel_id=1, source_target_pairs={{0,2},{2,0},{4,6},{6,4},{8,10},{10,8},{12,14},{14,12},{16,18},{18,... | collective-permute-start | bytes 786440 | tf_op jit(solution)/shard_map/ppermute | solution.py:579
  100.5 8.9 %collective-permute-start.21 = (bf16[1024,128]{1,0:T(8,128)(2,1)S(1)}, bf16[1024,128]{1,0:T(8,128)(2,1)S(1)}, u32[]{:S(2)}, u32[]{:S(2)}) collective-permute-start(bf16[1024,128]{1,0:T(8,128)(2,1)S(1)} %get-tuple-element.107.refs_0_), channel_id=1, source_target_pairs={{0,4},{2,6},{4,0},{6,2},{8,12},{10,14},{12,8},{14,10},{16,20},{18,... | collective-permute-start | bytes 786440 | tf_op jit(solution)/shard_map/ppermute | solution.py:579
  101.1 12.6 %collective-permute-start.22 = (bf16[1024,128]{1,0:T(8,128)(2,1)S(1)}, bf16[1024,128]{1,0:T(8,128)(2,1)S(1)}, u32[]{:S(2)}, u32[]{:S(2)}) collective-permute-start(bf16[1024,128]{1,0:T(8,128)(2,1)S(1)} %get-tuple-element.107.refs_0_), channel_id=1, source_target_pairs={{0,6},{2,4},{4,2},{6,0},{8,14},{10,12},{12,10},{14,8},{16,22},{18,... | collective-permute-start | bytes 786440 | tf_op jit(solution)/shard_map/ppermute | solution.py:579
  115.8 20.5 %collective-permute-start.23 = (bf16[1,256,512]{2,1,0:T(8,128)(2,1)S(1)}, bf16[1,256,512]{2,1,0:T(8,128)(2,1)S(1)}, u32[]{:S(2)}, u32[]{:S(2)}) collective-permute-start(bf16[1,256,512]{2,1,0:T(8,128)(2,1)S(1)} %get-tuple-element.109), channel_id=1, source_target_pairs={{0,8},{2,10},{4,12},{6,14},{8,0},{10,2},{12,4},{14,6},{16,24},{18,... | collective-permute-start | bytes 786440 | tf_op jit(solution)/shard_map/ppermute | solution.py:591
  117.6 18.7 %collective-permute-start.24 = (bf16[256,512]{1,0:T(8,128)(2,1)S(1)}, bf16[256,512]{1,0:T(8,128)(2,1)S(1)}, u32[]{:S(2)}, u32[]{:S(2)}) collective-permute-start(bf16[256,512]{1,0:T(8,128)(2,1)S(1)} %halve_0.1), channel_id=1, source_target_pairs={{0,16},{2,18},{4,20},{6,22},{8,24},{10,26},{12,28},{14,30},{16,0},... | collective-permute-start | bytes 786440 | tf_op jit(solution)/shard_map/ppermute | solution.py:591
  119.9 16.4 %collective-permute-start.25 = (bf16[2,128,256]{2,1,0:T(8,128)(2,1)S(1)}, bf16[2,128,256]{2,1,0:T(8,128)(2,1)S(1)}, u32[]{:S(2)}, u32[]{:S(2)}) collective-permute-start(bf16[2,128,256]{2,1,0:T(8,128)(2,1)S(1)} %get-tuple-element.117), channel_id=1, source_target_pairs={{16,0},{18,2},{20,4},{22,6},{17,1},{19,3},{21,5},{23,7}} | collective-permute-start | bytes 393224 | tf_op jit(solution)/shard_map/ppermute | solution.py:669
  121.2 15.2 %collective-permute-start.26 = (bf16[2,128,256]{2,1,0:T(8,128)(2,1)S(1)}, bf16[2,128,256]{2,1,0:T(8,128)(2,1)S(1)}, u32[]{:S(2)}, u32[]{:S(2)}) collective-permute-start(bf16[2,128,256]{2,1,0:T(8,128)(2,1)S(1)} %get-tuple-element.118), channel_id=1, source_target_pairs={{24,0},{26,2},{28,4},{30,6},{25,1},{27,3},{29,5},{31,7}} | collective-permute-start | bytes 393224 | tf_op jit(solution)/shard_map/ppermute | solution.py:669
  122.5 29.9 %collective-permute-start.31 = (bf16[2,256,512]{2,1,0:T(8,128)(2,1)S(1)}, bf16[2,256,512]{2,1,0:T(8,128)(2,1)S(1)}, u32[]{:S(2)}, u32[]{:S(2)}) collective-permute-start(bf16[2,256,512]{2,1,0:T(8,128)(2,1)S(1)} %get-tuple-element.110), channel_id=1, source_target_pairs={{0,8},{2,10},{4,12},{6,14},{8,0},{10,2},{12,4},{14,6},{16,24},{18,... | collective-permute-start | bytes 1572872 | tf_op jit(solution)/shard_map/ppermute | solution.py:591
  137.3 16.3 %collective-permute-start.27 = (bf16[3,256,256]{2,1,0:T(8,128)(2,1)S(1)}, bf16[3,256,256]{2,1,0:T(8,128)(2,1)S(1)}, u32[]{:S(2)}, u32[]{:S(2)}) collective-permute-start(bf16[3,256,256]{2,1,0:T(8,128)(2,1)S(1)} %get-tuple-element.120), channel_id=1, source_target_pairs={{0,2},{2,0},{4,6},{6,4},{8,10},{10,8},{12,14},{14,12},{16,18},{18,... | collective-permute-start | bytes 1179656 | tf_op jit(solution)/shard_map/ppermute | solution.py:579
  137.7 16.5 %collective-permute-start.28 = (bf16[3,256,256]{2,1,0:T(8,128)(2,1)S(1)}, bf16[3,256,256]{2,1,0:T(8,128)(2,1)S(1)}, u32[]{:S(2)}, u32[]{:S(2)}) collective-permute-start(bf16[3,256,256]{2,1,0:T(8,128)(2,1)S(1)} %get-tuple-element.121), channel_id=1, source_target_pairs={{0,4},{2,6},{4,0},{6,2},{8,12},{10,14},{12,8},{14,10},{16,20},{18,... | collective-permute-start | bytes 1179656 | tf_op jit(solution)/shard_map/ppermute | solution.py:579
  139.4 14.9 %collective-permute-start.29 = (bf16[3,256,256]{2,1,0:T(8,128)(2,1)S(1)}, bf16[3,256,256]{2,1,0:T(8,128)(2,1)S(1)}, u32[]{:S(2)}, u32[]{:S(2)}) collective-permute-start(bf16[3,256,256]{2,1,0:T(8,128)(2,1)S(1)} %get-tuple-element.122), channel_id=1, source_target_pairs={{0,6},{2,4},{4,2},{6,0},{8,14},{10,12},{12,10},{14,8},{16,22},{18,... | collective-permute-start | bytes 1179656 | tf_op jit(solution)/shard_map/ppermute | solution.py:579
  140.8 11.6 %collective-permute-start.30 = (bf16[256,512]{1,0:T(8,128)(2,1)S(1)}, bf16[256,512]{1,0:T(8,128)(2,1)S(1)}, u32[]{:S(2)}, u32[]{:S(2)}) collective-permute-start(bf16[256,512]{1,0:T(8,128)(2,1)S(1)} %halve_1.1), channel_id=1, source_target_pairs={{0,16},{2,18},{4,20},{6,22},{8,24},{10,26},{12,28},{14,30},{16,0},... | collective-permute-start | bytes 786440 | tf_op jit(solution)/shard_map/ppermute | solution.py:591
  (8 other events, 41.8 us)

commit v4 on v3

--- a/solution.py
+++ b/solution.py
@@ -23,6 +23,7 @@
 TN = (((0,), (0,)), ((), ()))
 SMEM = pl.BlockSpec(memory_space=pltpu.SMEM)
 VMEM = pl.BlockSpec(memory_space=pltpu.VMEM)
+HBM = pl.BlockSpec(memory_space=pltpu.HBM)
 
 
 def shape(dims, dtype=jnp.bfloat16):
@@ -66,49 +67,77 @@
     return taken, refs
 
 
+def copied(*copies):
+    for copy in copies:
+        copy.start()
+    for copy in copies:
+        copy.wait()
+
+
 def pack_kv(keys, values, meta, group, width):
     rows = keys.shape[0]
 
-    def body(meta_ref, k_ref, v_ref, *outs):
+    def body(meta_ref, k_ref, v_ref, *refs):
+        outs, sems = refs[:group], refs[group]
         me = meta_ref[0]
-        for k in range(group):
-            at = pl.multiple_of((me ^ k) * width, width)
-            outs[k][0] = k_ref[:, pl.ds(at, width)]
-            outs[k][1] = v_ref[:, pl.ds(at, width)]
-
-    return call(
-        body, (meta,), (keys, values), [shape((2, rows, width))] * group, [],
-        cost(0, 4 * keys.size * 2), "pack_kv",
-    )
-
-
-def grads_packed(queries, out_grad, proj_weight, meta, group, width):
-    rows, depth = out_grad.shape
-
-    def body(meta_ref, q_ref, og_ref, w_ref, *outs):
-        step = pl.program_id(0)
-        got = dot(og_ref[...], w_ref[...], NN).astype(jnp.bfloat16)
-        for k in range(group):
-
-            @pl.when(step == k)
-            def _():
-                outs[k][0] = q_ref[...]
-                outs[k][1] = got
+        copies = []
+        for k in range(group):
+            at = pl.ds(pl.multiple_of((me ^ k) * width, width), width)
+            for which, source in enumerate((k_ref, v_ref)):
+                copies.append(
+                    pltpu.make_async_copy(source.at[:, at], outs[k].at[which], sems.at[k, which])
+                )
+        copied(*copies)
 
     return pl.pallas_call(
         body,
         out_shape=[shape((2, rows, width))] * group,
-        grid_spec=pltpu.PrefetchScalarGridSpec(
-            num_scalar_prefetch=1,
-            grid=(group,),
-            in_specs=[
-                pl.BlockSpec((rows, width), lambda i, m: (0, m[0] ^ i)),
-                pl.BlockSpec((rows, depth), lambda i, m: (0, 0)),
-                pl.BlockSpec((depth, width), lambda i, m: (0, m[0] ^ i)),
-            ],
-            out_specs=[pl.BlockSpec((2, rows, width), lambda i, m: (0, 0, 0))] * group,
-        ),
+        in_specs=[SMEM, HBM, HBM],
+        out_specs=[VMEM] * group,
+        scratch_shapes=[pltpu.SemaphoreType.DMA((group, 2))],
         compiler_params=params(16),
+        cost_estimate=cost(0, 4 * keys.size * 2),
+        name="pack_kv",
+    )(meta, keys, values)
+
+
+def grads_packed(queries, out_grad, proj_weight, meta, group, width):
+    rows, depth = out_grad.shape
+
+    def body(meta_ref, q_ref, og_ref, w_ref, *refs):
+        outs, (og, w, q_sems, w_sems, og_sem) = refs[:group], refs[group:]
+        me = meta_ref[0]
+        og_copy = pltpu.make_async_copy(og_ref, og, og_sem)
+        og_copy.start()
+        q_copies, w_copies = [], []
+        for k in range(group):
+            at = pl.ds(pl.multiple_of((me ^ k) * width, width), width)
+            w_copies.append(pltpu.make_async_copy(w_ref.at[:, at], w.at[k], w_sems.at[k]))
+            w_copies[k].start()
+        for k in range(group):
+            at = pl.ds(pl.multiple_of((me ^ k) * width, width), width)
+            q_copies.append(pltpu.make_async_copy(q_ref.at[:, at], outs[k].at[0], q_sems.at[k]))
+            q_copies[k].start()
+        og_copy.wait()
+        for k in range(group):
+            w_copies[k].wait()
+            outs[k][1] = dot(og[...], w[k], NN).astype(jnp.bfloat16)
+        for k in range(group):
+            q_copies[k].wait()
+
+    return pl.pallas_call(
+        body,
+        out_shape=[shape((2, rows, width))] * group,
+        in_specs=[SMEM, HBM, HBM, HBM],
+        out_specs=[VMEM] * group,
+        scratch_shapes=[
+            pltpu.VMEM((rows, depth), jnp.bfloat16),
+            pltpu.VMEM((group, depth, width), jnp.bfloat16),
+            pltpu.SemaphoreType.DMA((group,)),
+            pltpu.SemaphoreType.DMA((group,)),
+            pltpu.SemaphoreType.DMA,
+        ],
+        compiler_params=params(24),
         cost_estimate=cost(2 * rows * depth * width * group, 12 * 1024 * 1024),
         name="attn_grad",
     )(meta, queries, out_grad, proj_weight)
@@ -119,18 +148,35 @@
     each = depth // (group * parts)
     half = parts // 2
 
-    def body(meta_ref, og_ref, *outs):
+    def body(meta_ref, og_ref, *refs):
+        outs, (held, sems) = refs[:group], refs[group:]
         me, core = meta_ref[0], meta_ref[3]
+        copies = []
         for k in range(group):
             for part in range(half):
                 at = ((core * half + part) * group + (me ^ k)) * each
-                at = pl.multiple_of(at, each)
-                outs[k][part * each : (part + 1) * each, :] = og_ref[:, pl.ds(at, each)].T
-
-    return call(
-        body, (meta,), (out_grad,), [shape((half * each, rows))] * group, [],
-        cost(0, 3 * out_grad.size), "pack_out_grad",
-    )
+                at = pl.ds(pl.multiple_of(at, each), each)
+                copies.append(
+                    pltpu.make_async_copy(og_ref.at[:, at], held.at[k, part], sems.at[k, part])
+                )
+        copied(*copies)
+        for k in range(group):
+            for part in range(half):
+                outs[k][part * each : (part + 1) * each, :] = held[k, part].T
+
+    return pl.pallas_call(
+        body,
+        out_shape=[shape((half * each, rows))] * group,
+        in_specs=[SMEM, HBM],
+        out_specs=[VMEM] * group,
+        scratch_shapes=[
+            pltpu.VMEM((group, half, rows, each), jnp.bfloat16),
+            pltpu.SemaphoreType.DMA((group, half)),
+        ],
+        compiler_params=params(16),
+        cost_estimate=cost(0, 3 * out_grad.size),
+        name="pack_out_grad",
+    )(meta, out_grad)
 
 
 def join_columns(pieces, meta, group):
@@ -620,16 +666,15 @@
     qd_cut = grads_packed(queries, out_grad, proj_weight, early, group, width)
     pool, others, strided = assemble_kv(own_kv, after(meta, prev, qd_cut[0]), group)
     rest = shifted(others, 1)
-    qd_pieces = exchange(qd_cut)
-    bias, bias_next = masks_of(layout, after(meta, strided), parts, slots)
-    qd = assemble(qd_pieces, after(meta, bias), group)
-    next_qd = shifted(qd, -1)
-    strided = after(strided, qd)
     far = [
         lax.ppermute(strided, "seq", summary_route(distance, False))
         for distance in range(2, parts)
     ]
-    og = exchange(pack_out_grad(out_grad, after(meta, rest, *far), group, parts))
+    qd_pieces = exchange(qd_cut)
+    bias, bias_next = masks_of(layout, after(meta, strided), parts, slots)
+    qd = assemble(qd_pieces, after(meta, bias, *far), group)
+    next_qd = shifted(qd, -1)
+    og = exchange(pack_out_grad(out_grad, after(meta, qd), group, parts))
 
     stats = jnp.zeros((LOCAL // 2, 2 * heads, PAIR), jnp.float32)
     order = after(meta, og[0])
@@ -641,7 +686,7 @@
             mine = join_columns(og, after(meta, got), group)
             theirs = lax.ppermute(mine, "head", [(0, 1), (1, 0)])
         order = after(meta, got, mine)
-    next_stats = shifted(stats, -1)
+    next_stats = shifted(after(stats, next_qd), -1)
 
     dq, grads, keep, finals, firsts = [], [], [], [], []
     far_grads = [jnp.zeros((2, BLK, width), jnp.bfloat16) for _ in far]
@@ -663,7 +708,7 @@
         keep.append(kept)
         firsts = [first]
         odds = swap_groups(odds, 1)
-        order = after(meta, first, next_qd)
+        order = after(meta, first)
     neighbour = swap_groups(first, 1)
     far_back = [
         lax.ppermute(piece, "seq", summary_route(index + 2, True))

time: 157 us -> 145 us (0.924)
  waiting for transfers between devices: 56.8 us -> 42.1 us
  Pallas kernels: 42.3 us -> 44.7 us
    ppermute x18, waiting for transfers between devices: 20 us -> 5.83 us  [swap(): return lax.ppermute(piece, 'seq', route)]
    ppermute x2, waiting for transfers between devices: 2.88 us -> 12.9 us  [local(): lax.ppermute(strided, 'seq', summary_route(distance, False))]
    ppermute x4, waiting for transfers between devices: 12.6 us -> 5.56 us  [shifted(): return lax.ppermute(piece, 'seq', route)]
    ppermute x5, waiting for transfers between devices: 21.4 us -> 15.6 us  [swap_groups(): return lax.ppermute(piece, 'seq', route)]
    pallas_call x1 -> x3, Pallas kernels: 5.67 us -> 9.63 us  [the longest x1 7.73 us: grads_packed(): pl.pallas_call(body, out_shape=[shape((2, rows, width))] * group, in_spec...]
    ppermute x2, waiting for transfers between devices: 0.01 us -> 2.15 us  [local(): lax.ppermute(piece, 'seq', summary_route(index + 2, True))]
    pallas_call x18 -> x16, Pallas kernels: 36.6 us -> 35.1 us  [call(): pl.pallas_call(body, out_shape=outs, in_specs=[SMEM] * len(scalars) + [VM...]
    unnamed x17 -> x15, local copies, waits for them, and re-layouts: 8.84 us -> 8.19 us
  transfers between devices with their start and end apart: 32 -> 32, of which waited for: 13 -> 9; matrix products, arithmetic and copies ran while one was open for 1% -> 1% of each run, Pallas kernels for 22% -> 25%
where the time goes in v4:
time: 145 us
  starting transfers between devices  45.3 us (31%)
  Pallas kernels  44.7 us (31%)
  waiting for transfers between devices  42.1 us (29%)
  local copies, waits for them, and re-layouts  9.48 us (7%)
  between operations  2.96 us (2%)
    pallas_call x16, Pallas kernels, call(): pl.pallas_call(body, out_shape=outs, in_specs=[SMEM] * len(scalars) + [VM...  35.1 us
    ppermute x18, starting transfers between devices, swap(): return lax.ppermute(piece, 'seq', route)  22.8 us
    ppermute x5, waiting for transfers between devices, swap_groups(): return lax.ppermute(piece, 'seq', route)  15.6 us
    ppermute x2, waiting for transfers between devices, local(): lax.ppermute(strided, 'seq', summary_route(distance, False))  12.9 us
    ppermute x4, starting transfers between devices, shifted(): return lax.ppermute(piece, 'seq', route)  9.55 us
    unnamed x15, local copies, waits for them, and re-layouts  8.19 us
    pallas_call x1, Pallas kernels, grads_packed(): pl.pallas_call(body, out_shape=[shape((2, rows, width))] * group, in_spec...  7.73 us
    ppermute x18, waiting for transfers between devices, swap(): return lax.ppermute(piece, 'seq', route)  5.83 us
  transfers between devices with their start and end apart: 32, of which 9 were waited for; matrix products, arithmetic and copies ran while one was open for 1% of the time, Pallas kernels for 25%

profile of v4, /device:TPU:0, one launch (start us, length us, event | category | flops | bytes accessed | tf_op | source)
XLA Modules:
  0.0 144.7 jit_solution(17499220946968900423)
XLA Ops:
  3.6 3.0 %collective-permute-start.1 = (bf16[2,256,256]{2,1,0:T(8,128)(2,1)S(1)}, bf16[2,256,256]{2,1,0:T(8,128)(2,1)S(1)}, u32[]{:S(2)}, u32[]{:S(2)}) collective-permute-start(bf16[2,256,256]{2,1,0:T(8,128)(2,1)S(1)} %get-tuple-element.67), channel_id=1, source_target_pairs={{0,2},{2,0},{4,6},{6,4},{8,10},{10,8},{12,14},{14,12},{16,18},{18,... | collective-permute-start | bytes 786440 | tf_op jit(solution)/shard_map/ppermute | solution.py:625
  6.6 3.5 %collective-permute-start = (bf16[2,256,256]{2,1,0:T(8,128)(2,1)S(1)}, bf16[2,256,256]{2,1,0:T(8,128)(2,1)S(1)}, u32[]{:S(2)}, u32[]{:S(2)}) collective-permute-start(bf16[2,256,256]{2,1,0:T(8,128)(2,1)S(1)} %get-tuple-element.66.refs_0_), channel_id=1, source_target_pairs={{0,8},{2,10},{4,12},{6,14},{8,16},{10,18},{12,20},{14,22},{16,24},... | collective-permute-start | bytes 786440 | tf_op jit(solution)/shard_map/ppermute | solution.py:633
  10.1 1.6 %collective-permute-start.2 = (bf16[2,256,256]{2,1,0:T(8,128)(2,1)S(1)}, bf16[2,256,256]{2,1,0:T(8,128)(2,1)S(1)}, u32[]{:S(2)}, u32[]{:S(2)}) collective-permute-start(bf16[2,256,256]{2,1,0:T(8,128)(2,1)S(1)} %get-tuple-element.71), channel_id=1, source_target_pairs={{0,4},{2,6},{4,0},{6,2},{8,12},{10,14},{12,8},{14,10},{16,20},{18,... | collective-permute-start | bytes 786440 | tf_op jit(solution)/shard_map/ppermute | solution.py:625
  15.5 3.4 %copy-done = bf16[4096,1024]{1,0:T(8,128)(2,1)S(1)} copy-done((bf16[4096,1024]{1,0:T(8,128)(2,1)S(1)}, bf16[4096,1024]{1,0:T(8,128)(2,1)}, u32[]{:S(2)}) %copy-start) | copy-done | bytes 8388632
  18.9 1.6 %copy-done.1 = bf16[256,4096]{1,0:T(8,128)(2,1)S(1)} copy-done((bf16[256,4096]{1,0:T(8,128)(2,1)S(1)}, bf16[256,4096]{1,0:T(8,128)(2,1)}, u32[]{:S(2)}) %copy-start.1) | copy-done | bytes 2097176
  21.5 7.7 %attn_grad.1 = (bf16[2,256,256]{2,1,0:T(8,128)(2,1)S(1)}, bf16[2,256,256]{2,1,0:T(8,128)(2,1)}, bf16[2,256,256]{2,1,0:T(8,128)(2,1)}, bf16[2,256,256]{2,1,0:T(8,128)(2,1)}) custom-call(s32[2]{0:T(128)S(1)} %pad_add_fusion.1.meta_ref, bf16[256,1024]{1,0:T(8,128)(2,1)S(1)} %copy-done.3, bf16[256,4096]{1,0:T(8,128)(2,1)S(1)} %copy-done.1, ...), custom_call_target="tpu_custom_call" | custom-call | flops 1 | bytes 1 | tf_op jit(solution)/shard_map/attn_grad/pallas_call | solution.py:128
  29.3 1.6 %assemble_kv.1 = (bf16[2,1024,256]{2,1,0:T(8,128)(2,1)S(1)}, bf16[3,2,256,256]{3,2,1,0:T(8,128)(2,1)}, bf16[2,128,256]{2,1,0:T(8,128)(2,1)}) custom-call(s32[4]{0:T(128)S(1)} %pad_add_fusion.meta_ref, bf16[2,256,256]{2,1,0:T(8,128)(2,1)S(1)} %get-tuple-element.66.refs_0_, bf16[2,256,256]{2,1,0:T(8,128)(2,1)S(1)} %collective-permute-done.1.refs_1_, ...), custom_call_target="tpu_custom_call" | custom-call | flops 1 | bytes 1 | tf_op jit(solution)/shard_map/assemble_kv/pallas_call | solution.py:46
  30.8 3.5 %collective-permute-start.9 = (bf16[3,2,256,256]{3,2,1,0:T(8,128)(2,1)}, bf16[3,2,256,256]{3,2,1,0:T(8,128)(2,1)S(1)}, u32[]{:S(2)}, u32[]{:S(2)}) collective-permute-start(bf16[3,2,256,256]{3,2,1,0:T(8,128)(2,1)} %get-tuple-element.84), channel_id=1, source_target_pairs={{0,8},{2,10},{4,12},{6,14},{8,16},{10,18},{12,20},{14,22},{16,24},... | collective-permute-start | bytes 2359304 | tf_op jit(solution)/shard_map/ppermute | solution.py:633
  34.3 3.3 %collective-permute-start.4 = (bf16[2,128,256]{2,1,0:T(8,128)(2,1)}, bf16[2,128,256]{2,1,0:T(8,128)(2,1)S(1)}, u32[]{:S(2)}, u32[]{:S(2)}) collective-permute-start(bf16[2,128,256]{2,1,0:T(8,128)(2,1)} %get-tuple-element.73), channel_id=1, source_target_pairs={{0,16},{2,18},{4,20},{6,22},{1,17},{3,19},{5,21},{7,23}} | collective-permute-start | bytes 393224 | tf_op jit(solution)/shard_map/ppermute | solution.py:670
  37.6 1.6 %collective-permute-start.6 = (bf16[2,256,256]{2,1,0:T(8,128)(2,1)}, bf16[2,256,256]{2,1,0:T(8,128)(2,1)S(1)}, u32[]{:S(2)}, u32[]{:S(2)}) collective-permute-start(bf16[2,256,256]{2,1,0:T(8,128)(2,1)} %get-tuple-element.77), channel_id=1, source_target_pairs={{0,2},{2,0},{4,6},{6,4},{8,10},{10,8},{12,14},{14,12},{16,18},{18,... | collective-permute-start | bytes 786440 | tf_op jit(solution)/shard_map/ppermute | solution.py:625
  39.2 1.5 %collective-permute-start.7 = (bf16[2,256,256]{2,1,0:T(8,128)(2,1)}, bf16[2,256,256]{2,1,0:T(8,128)(2,1)S(1)}, u32[]{:S(2)}, u32[]{:S(2)}) collective-permute-start(bf16[2,256,256]{2,1,0:T(8,128)(2,1)} %get-tuple-element.78), channel_id=1, source_target_pairs={{0,4},{2,6},{4,0},{6,2},{8,12},{10,14},{12,8},{14,10},{16,20},{18,... | collective-permute-start | bytes 786440 | tf_op jit(solution)/shard_map/ppermute | solution.py:625
  41.2 12.1 %collective-permute-done.4.refs_4_ = bf16[2,128,256]{2,1,0:T(8,128)(2,1)S(1)} collective-permute-done((bf16[2,128,256]{2,1,0:T(8,128)(2,1)}, bf16[2,128,256]{2,1,0:T(8,128)(2,1)S(1)}, u32[]{:S(2)}, u32[]{:S(2)}) %collective-permute-start.4) | collective-permute-done | bytes 131104 | tf_op jit(solution)/shard_map/ppermute | solution.py:670
  54.7 1.9 %masks.1 = (f32[4,11,256]{2,1,0:T(8,128)S(1)}, f32[4,10,256]{2,1,0:T(8,128)S(1)}) custom-call(s32[4]{0:T(128)S(1)} %pad_add_fusion.meta_ref, s32[32,10]{1,0:T(8,128)S(1)} %copy.10.table), custom_call_target="tpu_custom_call" | custom-call | flops 1 | bytes 1 | tf_op jit(solution)/shard_map/masks/pallas_call | solution.py:46
  59.2 1.6 %collective-permute-start.10 = (bf16[512,256]{1,0:T(8,128)(2,1)S(1)}, bf16[512,256]{1,0:T(8,128)(2,1)S(1)}, u32[]{:S(2)}, u32[]{:S(2)}) collective-permute-start(bf16[512,256]{1,0:T(8,128)(2,1)S(1)} %get-tuple-element.87), channel_id=1, source_target_pairs={{0,2},{2,0},{4,6},{6,4},{8,10},{10,8},{12,14},{14,12},{16,18},{18,... | collective-permute-start | bytes 786440 | tf_op jit(solution)/shard_map/ppermute | solution.py:625
  60.8 1.5 %collective-permute-start.11 = (bf16[512,256]{1,0:T(8,128)(2,1)S(1)}, bf16[512,256]{1,0:T(8,128)(2,1)S(1)}, u32[]{:S(2)}, u32[]{:S(2)}) collective-permute-start(bf16[512,256]{1,0:T(8,128)(2,1)S(1)} %get-tuple-element.88), channel_id=1, source_target_pairs={{0,4},{2,6},{4,0},{6,2},{8,12},{10,14},{12,8},{14,10},{16,20},{18,... | collective-permute-start | bytes 786440 | tf_op jit(solution)/shard_map/ppermute | solution.py:625
  64.1 4.5 %attention_0.1 = (bf16[1024,128]{1,0:T(8,128)(2,1)S(1)}, f32[4,4,256]{2,1,0:T(4,128)S(1)}) custom-call(s32[4]{0:T(128)S(1)} %pad_add_fusion.meta_ref, f32[4,11,256]{2,1,0:T(8,128)S(1)} %get-tuple-element.75.bias_ref, f32[4,4,256]{2,1,0:T(4,128)S(1)} %broadcast_in_dim.3.before_ref, bf16[2,1024,256]{2,1,0:T(8,128)(2,1)S(1)} %assemble.1.refs_0_, ...), custom_call_target="tpu_custom_call" | custom-call | flops 1 | bytes 1 | tf_op jit(solution)/shard_map/attention_0/pallas_call | solution.py:46
  68.6 2.9 %collective-permute-done.11.refs_2_ = bf16[512,256]{1,0:T(8,128)(2,1)S(1)} collective-permute-done((bf16[512,256]{1,0:T(8,128)(2,1)S(1)}, bf16[512,256]{1,0:T(8,128)(2,1)S(1)}, u32[]{:S(2)}, u32[]{:S(2)}) %collective-permute-start.11) | collective-permute-done | bytes 262176 | tf_op jit(solution)/shard_map/ppermute | solution.py:625
  75.8 4.7 %attention_1.1 = (bf16[1024,128]{1,0:T(8,128)(2,1)S(1)}, f32[4,4,256]{2,1,0:T(4,128)S(1)}) custom-call(s32[4]{0:T(128)S(1)} %pad_add_fusion.meta_ref, f32[4,11,256]{2,1,0:T(8,128)S(1)} %get-tuple-element.75.bias_ref, f32[4,4,256]{2,1,0:T(4,128)S(1)} %get-tuple-element.91.before_ref, bf16[2,1024,256]{2,1,0:T(8,128)(2,1)S(1)} %assemble.1.refs_0_, ...), custom_call_target="tpu_custom_call" | custom-call | flops 1 | bytes 1 | tf_op jit(solution)/shard_map/attention_1/pallas_call | solution.py:46
  80.5 5.5 %collective-permute-done.14.refs_2_ = bf16[2,1024,256]{2,1,0:T(8,128)(2,1)S(1)} collective-permute-done((bf16[2,1024,256]{2,1,0:T(8,128)(2,1)S(1)}, bf16[2,1024,256]{2,1,0:T(8,128)(2,1)S(1)}, u32[]{:S(2)}, u32[]{:S(2)}) %collective-permute-start.14) | collective-permute-done | bytes 1048608 | tf_op jit(solution)/shard_map/ppermute | solution.py:633
  87.4 4.3 %attention_back_0.1 = (bf16[1024,128]{1,0:T(8,128)(2,1)S(1)}, f32[2,1024,128]{2,1,0:T(8,128)S(1)}, bf16[2,128,256]{2,1,0:T(8,128)(2,1)S(1)}, bf16[2,128,256]{2,1,0:T(8,128)(2,1)S(1)}) custom-call(s32[4]{0:T(128)S(1)} %pad_add_fusion.meta_ref, f32[4,11,256]{2,1,0:T(8,128)S(1)} %get-tuple-element.75.bias_ref, f32[4,4,256]{2,1,0:T(4,128)S(1)} %get-tuple-element.95.stats_ref, ...), custom_call_target="tpu_custom_call" | custom-call | flops 1 | bytes 1 | tf_op jit(solution)/shard_map/attention_back_0/pallas_call | solution.py:46
  91.8 2.2 %project_0.1 = (f32[256,512]{1,0:T(8,128)S(1)}, bf16[1,256,512]{2,1,0:T(8,128)(2,1)S(1)}, bf16[1,256,512]{2,1,0:T(8,128)(2,1)S(1)}, f32[1,256,512]{2,1,0:T(8,128)S(1)}) custom-call(s32[4]{0:T(128)S(1)} %pad_add_fusion.meta_ref, bf16[512,1024]{1,0:T(8,128)(2,1)S(1)} %join_columns.1.mine_ref, bf16[512,1024]{1,0:T(8,128)(2,1)S(1)} %collective-permute-done.13.theirs_ref, ...), custom_call_target="tpu_custom_call" | custom-call | flops 1 | bytes 1 | tf_op jit(solution)/shard_map/project_0/pallas_call | solution.py:46
  93.9 2.7 %collective-permute-start.19 = (bf16[1,256,512]{2,1,0:T(8,128)(2,1)S(1)}, bf16[1,256,512]{2,1,0:T(8,128)(2,1)S(1)}, u32[]{:S(2)}, u32[]{:S(2)}) collective-permute-start(bf16[1,256,512]{2,1,0:T(8,128)(2,1)S(1)} %get-tuple-element.104), channel_id=1, source_target_pairs={{0,8},{2,10},{4,12},{6,14},{8,0},{10,2},{12,4},{14,6},{16,24},{18,... | collective-permute-start | bytes 786440 | tf_op jit(solution)/shard_map/ppermute | solution.py:637
  98.2 1.5 %collective-permute-start.21 = (bf16[1024,128]{1,0:T(8,128)(2,1)S(1)}, bf16[1024,128]{1,0:T(8,128)(2,1)S(1)}, u32[]{:S(2)}, u32[]{:S(2)}) collective-permute-start(bf16[1024,128]{1,0:T(8,128)(2,1)S(1)} %get-tuple-element.107.refs_0_), channel_id=1, source_target_pairs={{0,4},{2,6},{4,0},{6,2},{8,12},{10,14},{12,8},{14,10},{16,20},{18,... | collective-permute-start | bytes 786440 | tf_op jit(solution)/shard_map/ppermute | solution.py:625
  100.2 4.5 %attention_back_1.1 = (bf16[1024,128]{1,0:T(8,128)(2,1)S(1)}, f32[2,1024,128]{2,1,0:T(8,128)S(1)}, bf16[2,128,256]{2,1,0:T(8,128)(2,1)S(1)}, bf16[2,128,256]{2,1,0:T(8,128)(2,1)S(1)}) custom-call(s32[4]{0:T(128)S(1)} %pad_add_fusion.meta_ref, f32[4,11,256]{2,1,0:T(8,128)S(1)} %get-tuple-element.75.bias_ref, f32[4,4,256]{2,1,0:T(4,128)S(1)} %get-tuple-element.95.stats_ref, ...), custom_call_target="tpu_custom_call" | custom-call | flops 1 | bytes 1 | tf_op jit(solution)/shard_map/attention_back_1/pallas_call | solution.py:46
  104.8 2.6 %collective-permute-done.21.refs_2_ = bf16[1024,128]{1,0:T(8,128)(2,1)S(1)} collective-permute-done((bf16[1024,128]{1,0:T(8,128)(2,1)S(1)}, bf16[1024,128]{1,0:T(8,128)(2,1)S(1)}, u32[]{:S(2)}, u32[]{:S(2)}) %collective-permute-start.21) | collective-permute-done | bytes 262176 | tf_op jit(solution)/shard_map/ppermute | solution.py:625
  107.3 2.1 %project_1.1 = (f32[256,512]{1,0:T(8,128)S(1)}, bf16[2,256,512]{2,1,0:T(8,128)(2,1)S(1)}, bf16[1,256,512]{2,1,0:T(8,128)(2,1)S(1)}, f32[1,256,512]{2,1,0:T(8,128)S(1)}) custom-call(s32[4]{0:T(128)S(1)} %pad_add_fusion.meta_ref, bf16[512,1024]{1,0:T(8,128)(2,1)S(1)} %join_columns.1.mine_ref, bf16[512,1024]{1,0:T(8,128)(2,1)S(1)} %collective-permute-done.13.theirs_ref, ...), custom_call_target="tpu_custom_call" | custom-call | flops 1 | bytes 1 | tf_op jit(solution)/shard_map/project_1/pallas_call | solution.py:46
  109.6 2.1 %collective-permute-start.24 = (bf16[256,512]{1,0:T(8,128)(2,1)S(1)}, bf16[256,512]{1,0:T(8,128)(2,1)S(1)}, u32[]{:S(2)}, u32[]{:S(2)}) collective-permute-start(bf16[256,512]{1,0:T(8,128)(2,1)S(1)} %halve_0.1), channel_id=1, source_target_pairs={{0,16},{2,18},{4,20},{6,22},{8,24},{10,26},{12,28},{14,30},{16,0},... | collective-permute-start | bytes 786440 | tf_op jit(solution)/shard_map/ppermute | solution.py:637
  115.1 3.9 %attention_back_next.1.own_ref = f32[2,1024,256]{2,1,0:T(8,128)S(1)} custom-call(s32[4]{0:T(128)S(1)} %pad_add_fusion.meta_ref, f32[4,10,256]{2,1,0:T(8,128)S(1)} %get-tuple-element.112.bias_ref, f32[4,4,256]{2,1,0:T(4,128)S(1)} %collective-permute-done.15.stats_ref, f32[2,1024,128]{2,1,0:T(8,128)S(1)} %get-tuple-element.113.refs_0_, ...), custom_call_target="tpu_custom_call" | custom-call | flops 1 | bytes 1 | tf_op jit(solution)/shard_map/attention_back_next/pallas_call | solution.py:46
  119.0 7.6 %collective-permute-done.23.arrived_ref = bf16[1,256,512]{2,1,0:T(8,128)(2,1)S(1)} collective-permute-done((bf16[1,256,512]{2,1,0:T(8,128)(2,1)S(1)}, bf16[1,256,512]{2,1,0:T(8,128)(2,1)S(1)}, u32[]{:S(2)}, u32[]{:S(2)}) %collective-permute-start.23) | collective-permute-done | bytes 262176 | tf_op jit(solution)/shard_map/ppermute | solution.py:637
  126.7 2.1 %collective-permute-done.26.refs_3_ = bf16[2,128,256]{2,1,0:T(8,128)(2,1)S(1)} collective-permute-done((bf16[2,128,256]{2,1,0:T(8,128)(2,1)S(1)}, bf16[2,128,256]{2,1,0:T(8,128)(2,1)S(1)}, u32[]{:S(2)}, u32[]{:S(2)}) %collective-permute-start.26) | collective-permute-done | bytes 131104 | tf_op jit(solution)/shard_map/ppermute | solution.py:714
  133.4 8.0 %collective-permute-done.30.refs_3_ = bf16[256,512]{1,0:T(8,128)(2,1)S(1)} collective-permute-done((bf16[256,512]{1,0:T(8,128)(2,1)S(1)}, bf16[256,512]{1,0:T(8,128)(2,1)S(1)}, u32[]{:S(2)}, u32[]{:S(2)}) %collective-permute-start.30) | collective-permute-done | bytes 262176 | tf_op jit(solution)/shard_map/ppermute | solution.py:637
  142.8 1.9 %unpack.1 = (bf16[256,1024]{1,0:T(8,128)(2,1)}, bf16[256,1024]{1,0:T(8,128)(2,1)}, bf16[256,1024]{1,0:T(8,128)(2,1)}) custom-call(s32[4]{0:T(128)S(1)} %pad_add_fusion.meta_ref, bf16[3,256,256]{2,1,0:T(8,128)(2,1)S(1)} %get-tuple-element.119.refs_0_, bf16[3,256,256]{2,1,0:T(8,128)(2,1)S(1)} %collective-permute-done.27.refs_1_, ...), custom_call_target="tpu_custom_call" | custom-call | flops 1 | bytes 1 | tf_op jit(solution)/shard_map/unpack/pallas_call | solution.py:46
  (71 shorter events, 29.1 us)
Async XLA Ops:
  3.6 11.9 %collective-permute-start.1 = (bf16[2,256,256]{2,1,0:T(8,128)(2,1)S(1)}, bf16[2,256,256]{2,1,0:T(8,128)(2,1)S(1)}, u32[]{:S(2)}, u32[]{:S(2)}) collective-permute-start(bf16[2,256,256]{2,1,0:T(8,128)(2,1)S(1)} %get-tuple-element.67), channel_id=1, source_target_pairs={{0,2},{2,0},{4,6},{6,4},{8,10},{10,8},{12,14},{14,12},{16,18},{18,... | collective-permute-start | bytes 786440 | tf_op jit(solution)/shard_map/ppermute | solution.py:625
  6.6 22.6 %collective-permute-start = (bf16[2,256,256]{2,1,0:T(8,128)(2,1)S(1)}, bf16[2,256,256]{2,1,0:T(8,128)(2,1)S(1)}, u32[]{:S(2)}, u32[]{:S(2)}) collective-permute-start(bf16[2,256,256]{2,1,0:T(8,128)(2,1)S(1)} %get-tuple-element.66.refs_0_), channel_id=1, source_target_pairs={{0,8},{2,10},{4,12},{6,14},{8,16},{10,18},{12,20},{14,22},{16,24},... | collective-permute-start | bytes 786440 | tf_op jit(solution)/shard_map/ppermute | solution.py:633
  10.1 19.1 %collective-permute-start.2 = (bf16[2,256,256]{2,1,0:T(8,128)(2,1)S(1)}, bf16[2,256,256]{2,1,0:T(8,128)(2,1)S(1)}, u32[]{:S(2)}, u32[]{:S(2)}) collective-permute-start(bf16[2,256,256]{2,1,0:T(8,128)(2,1)S(1)} %get-tuple-element.71), channel_id=1, source_target_pairs={{0,4},{2,6},{4,0},{6,2},{8,12},{10,14},{12,8},{14,10},{16,20},{18,... | collective-permute-start | bytes 786440 | tf_op jit(solution)/shard_map/ppermute | solution.py:625
  11.7 17.6 %collective-permute-start.3 = (bf16[2,256,256]{2,1,0:T(8,128)(2,1)S(1)}, bf16[2,256,256]{2,1,0:T(8,128)(2,1)S(1)}, u32[]{:S(2)}, u32[]{:S(2)}) collective-permute-start(bf16[2,256,256]{2,1,0:T(8,128)(2,1)S(1)} %get-tuple-element.72), channel_id=1, source_target_pairs={{0,6},{2,4},{4,2},{6,0},{8,14},{10,12},{12,10},{14,8},{16,22},{18,... | collective-permute-start | bytes 786440 | tf_op jit(solution)/shard_map/ppermute | solution.py:625
  30.8 33.2 %collective-permute-start.9 = (bf16[3,2,256,256]{3,2,1,0:T(8,128)(2,1)}, bf16[3,2,256,256]{3,2,1,0:T(8,128)(2,1)S(1)}, u32[]{:S(2)}, u32[]{:S(2)}) collective-permute-start(bf16[3,2,256,256]{3,2,1,0:T(8,128)(2,1)} %get-tuple-element.84), channel_id=1, source_target_pairs={{0,8},{2,10},{4,12},{6,14},{8,16},{10,18},{12,20},{14,22},{16,24},... | collective-permute-start | bytes 2359304 | tf_op jit(solution)/shard_map/ppermute | solution.py:633
  34.3 19.0 %collective-permute-start.4 = (bf16[2,128,256]{2,1,0:T(8,128)(2,1)}, bf16[2,128,256]{2,1,0:T(8,128)(2,1)S(1)}, u32[]{:S(2)}, u32[]{:S(2)}) collective-permute-start(bf16[2,128,256]{2,1,0:T(8,128)(2,1)} %get-tuple-element.73), channel_id=1, source_target_pairs={{0,16},{2,18},{4,20},{6,22},{1,17},{3,19},{5,21},{7,23}} | collective-permute-start | bytes 393224 | tf_op jit(solution)/shard_map/ppermute | solution.py:670
  37.6 19.8 %collective-permute-start.6 = (bf16[2,256,256]{2,1,0:T(8,128)(2,1)}, bf16[2,256,256]{2,1,0:T(8,128)(2,1)S(1)}, u32[]{:S(2)}, u32[]{:S(2)}) collective-permute-start(bf16[2,256,256]{2,1,0:T(8,128)(2,1)} %get-tuple-element.77), channel_id=1, source_target_pairs={{0,2},{2,0},{4,6},{6,4},{8,10},{10,8},{12,14},{14,12},{16,18},{18,... | collective-permute-start | bytes 786440 | tf_op jit(solution)/shard_map/ppermute | solution.py:625
  39.2 18.2 %collective-permute-start.7 = (bf16[2,256,256]{2,1,0:T(8,128)(2,1)}, bf16[2,256,256]{2,1,0:T(8,128)(2,1)S(1)}, u32[]{:S(2)}, u32[]{:S(2)}) collective-permute-start(bf16[2,256,256]{2,1,0:T(8,128)(2,1)} %get-tuple-element.78), channel_id=1, source_target_pairs={{0,4},{2,6},{4,0},{6,2},{8,12},{10,14},{12,8},{14,10},{16,20},{18,... | collective-permute-start | bytes 786440 | tf_op jit(solution)/shard_map/ppermute | solution.py:625
  40.7 16.7 %collective-permute-start.8 = (bf16[2,256,256]{2,1,0:T(8,128)(2,1)}, bf16[2,256,256]{2,1,0:T(8,128)(2,1)S(1)}, u32[]{:S(2)}, u32[]{:S(2)}) collective-permute-start(bf16[2,256,256]{2,1,0:T(8,128)(2,1)} %get-tuple-element.79), channel_id=1, source_target_pairs={{0,6},{2,4},{4,2},{6,0},{8,14},{10,12},{12,10},{14,8},{16,22},{18,... | collective-permute-start | bytes 786440 | tf_op jit(solution)/shard_map/ppermute | solution.py:625
  53.3 4.1 %collective-permute-start.5 = (bf16[2,128,256]{2,1,0:T(8,128)(2,1)}, bf16[2,128,256]{2,1,0:T(8,128)(2,1)S(1)}, u32[]{:S(2)}, u32[]{:S(2)}) collective-permute-start(bf16[2,128,256]{2,1,0:T(8,128)(2,1)} %get-tuple-element.73), channel_id=1, source_target_pairs={{0,24},{2,26},{4,28},{6,30},{1,25},{3,27},{5,29},{7,31}} | collective-permute-start | bytes 393224 | tf_op jit(solution)/shard_map/ppermute | solution.py:670
  59.2 9.4 %collective-permute-start.10 = (bf16[512,256]{1,0:T(8,128)(2,1)S(1)}, bf16[512,256]{1,0:T(8,128)(2,1)S(1)}, u32[]{:S(2)}, u32[]{:S(2)}) collective-permute-start(bf16[512,256]{1,0:T(8,128)(2,1)S(1)} %get-tuple-element.87), channel_id=1, source_target_pairs={{0,2},{2,0},{4,6},{6,4},{8,10},{10,8},{12,14},{14,12},{16,18},{18,... | collective-permute-start | bytes 786440 | tf_op jit(solution)/shard_map/ppermute | solution.py:625
  60.8 10.8 %collective-permute-start.11 = (bf16[512,256]{1,0:T(8,128)(2,1)S(1)}, bf16[512,256]{1,0:T(8,128)(2,1)S(1)}, u32[]{:S(2)}, u32[]{:S(2)}) collective-permute-start(bf16[512,256]{1,0:T(8,128)(2,1)S(1)} %get-tuple-element.88), channel_id=1, source_target_pairs={{0,4},{2,6},{4,0},{6,2},{8,12},{10,14},{12,8},{14,10},{16,20},{18,... | collective-permute-start | bytes 786440 | tf_op jit(solution)/shard_map/ppermute | solution.py:625
  62.3 9.2 %collective-permute-start.12 = (bf16[512,256]{1,0:T(8,128)(2,1)S(1)}, bf16[512,256]{1,0:T(8,128)(2,1)S(1)}, u32[]{:S(2)}, u32[]{:S(2)}) collective-permute-start(bf16[512,256]{1,0:T(8,128)(2,1)S(1)} %get-tuple-element.89), channel_id=1, source_target_pairs={{0,6},{2,4},{4,2},{6,0},{8,14},{10,12},{12,10},{14,8},{16,22},{18,... | collective-permute-start | bytes 786440 | tf_op jit(solution)/shard_map/ppermute | solution.py:625
  62.8 23.3 %collective-permute-start.14 = (bf16[2,1024,256]{2,1,0:T(8,128)(2,1)S(1)}, bf16[2,1024,256]{2,1,0:T(8,128)(2,1)S(1)}, u32[]{:S(2)}, u32[]{:S(2)}) collective-permute-start(bf16[2,1024,256]{2,1,0:T(8,128)(2,1)S(1)} %assemble.1.refs_0_), channel_id=1, source_target_pairs={{8,0},{10,2},{12,4},{14,6},{16,8},{18,10},{20,12},{22,14},{24,16},... | collective-permute-start | bytes 3145736 | tf_op jit(solution)/shard_map/ppermute | solution.py:633
  72.2 15.2 %collective-permute-start.13 = (bf16[512,1024]{1,0:T(8,128)(2,1)S(1)}, bf16[512,1024]{1,0:T(8,128)(2,1)S(1)}, u32[]{:S(2)}, u32[]{:S(2)}) collective-permute-start(bf16[512,1024]{1,0:T(8,128)(2,1)S(1)} %join_columns.1.mine_ref), channel_id=1, source_target_pairs={{0,1},{1,0},{2,3},{3,2},{4,5},{5,4},{6,7},{7,6},{8,9},{9,8},{10,11... | collective-permute-start | bytes 3145736 | tf_op jit(solution)/shard_map/ppermute | solution.py:687
  72.3 19.5 %collective-permute-start.16 = (bf16[1024,128]{1,0:T(8,128)(2,1)S(1)}, bf16[1024,128]{1,0:T(8,128)(2,1)S(1)}, u32[]{:S(2)}, u32[]{:S(2)}) collective-permute-start(bf16[1024,128]{1,0:T(8,128)(2,1)S(1)} %get-tuple-element.85.refs_0_), channel_id=1, source_target_pairs={{0,2},{2,0},{4,6},{6,4},{8,10},{10,8},{12,14},{14,12},{16,18},{18,... | collective-permute-start | bytes 786440 | tf_op jit(solution)/shard_map/ppermute | solution.py:625
  73.6 18.2 %collective-permute-start.17 = (bf16[1024,128]{1,0:T(8,128)(2,1)S(1)}, bf16[1024,128]{1,0:T(8,128)(2,1)S(1)}, u32[]{:S(2)}, u32[]{:S(2)}) collective-permute-start(bf16[1024,128]{1,0:T(8,128)(2,1)S(1)} %get-tuple-element.85.refs_0_), channel_id=1, source_target_pairs={{0,4},{2,6},{4,0},{6,2},{8,12},{10,14},{12,8},{14,10},{16,20},{18,... | collective-permute-start | bytes 786440 | tf_op jit(solution)/shard_map/ppermute | solution.py:625
  74.4 17.4 %collective-permute-start.18 = (bf16[1024,128]{1,0:T(8,128)(2,1)S(1)}, bf16[1024,128]{1,0:T(8,128)(2,1)S(1)}, u32[]{:S(2)}, u32[]{:S(2)}) collective-permute-start(bf16[1024,128]{1,0:T(8,128)(2,1)S(1)} %get-tuple-element.85.refs_0_), channel_id=1, source_target_pairs={{0,6},{2,4},{4,2},{6,0},{8,14},{10,12},{12,10},{14,8},{16,22},{18,... | collective-permute-start | bytes 786440 | tf_op jit(solution)/shard_map/ppermute | solution.py:625
  86.1 5.6 %collective-permute-start.15 = (f32[4,4,256]{2,1,0:T(4,128)S(1)}, f32[4,4,256]{2,1,0:T(4,128)S(1)}, u32[]{:S(2)}, u32[]{:S(2)}) collective-permute-start(f32[4,4,256]{2,1,0:T(4,128)S(1)} %get-tuple-element.95.stats_ref), channel_id=1, source_target_pairs={{8,0},{10,2},{12,4},{14,6},{16,8},{18,10},{20,12},{22,14},{24,16},... | collective-permute-start | bytes 49160 | tf_op jit(solution)/shard_map/ppermute | solution.py:633
  93.9 10.8 %collective-permute-start.19 = (bf16[1,256,512]{2,1,0:T(8,128)(2,1)S(1)}, bf16[1,256,512]{2,1,0:T(8,128)(2,1)S(1)}, u32[]{:S(2)}, u32[]{:S(2)}) collective-permute-start(bf16[1,256,512]{2,1,0:T(8,128)(2,1)S(1)} %get-tuple-element.104), channel_id=1, source_target_pairs={{0,8},{2,10},{4,12},{6,14},{8,0},{10,2},{12,4},{14,6},{16,24},{18,... | collective-permute-start | bytes 786440 | tf_op jit(solution)/shard_map/ppermute | solution.py:637
  96.7 8.1 %collective-permute-start.20 = (bf16[1024,128]{1,0:T(8,128)(2,1)S(1)}, bf16[1024,128]{1,0:T(8,128)(2,1)S(1)}, u32[]{:S(2)}, u32[]{:S(2)}) collective-permute-start(bf16[1024,128]{1,0:T(8,128)(2,1)S(1)} %get-tuple-element.107.refs_0_), channel_id=1, source_target_pairs={{0,2},{2,0},{4,6},{6,4},{8,10},{10,8},{12,14},{14,12},{16,18},{18,... | collective-permute-start | bytes 786440 | tf_op jit(solution)/shard_map/ppermute | solution.py:625
  98.2 9.2 %collective-permute-start.21 = (bf16[1024,128]{1,0:T(8,128)(2,1)S(1)}, bf16[1024,128]{1,0:T(8,128)(2,1)S(1)}, u32[]{:S(2)}, u32[]{:S(2)}) collective-permute-start(bf16[1024,128]{1,0:T(8,128)(2,1)S(1)} %get-tuple-element.107.refs_0_), channel_id=1, source_target_pairs={{0,4},{2,6},{4,0},{6,2},{8,12},{10,14},{12,8},{14,10},{16,20},{18,... | collective-permute-start | bytes 786440 | tf_op jit(solution)/shard_map/ppermute | solution.py:625
  99.7 7.7 %collective-permute-start.22 = (bf16[1024,128]{1,0:T(8,128)(2,1)S(1)}, bf16[1024,128]{1,0:T(8,128)(2,1)S(1)}, u32[]{:S(2)}, u32[]{:S(2)}) collective-permute-start(bf16[1024,128]{1,0:T(8,128)(2,1)S(1)} %get-tuple-element.107.refs_0_), channel_id=1, source_target_pairs={{0,6},{2,4},{4,2},{6,0},{8,14},{10,12},{12,10},{14,8},{16,22},{18,... | collective-permute-start | bytes 786440 | tf_op jit(solution)/shard_map/ppermute | solution.py:625
  109.5 17.2 %collective-permute-start.23 = (bf16[1,256,512]{2,1,0:T(8,128)(2,1)S(1)}, bf16[1,256,512]{2,1,0:T(8,128)(2,1)S(1)}, u32[]{:S(2)}, u32[]{:S(2)}) collective-permute-start(bf16[1,256,512]{2,1,0:T(8,128)(2,1)S(1)} %get-tuple-element.109), channel_id=1, source_target_pairs={{0,8},{2,10},{4,12},{6,14},{8,0},{10,2},{12,4},{14,6},{16,24},{18,... | collective-permute-start | bytes 786440 | tf_op jit(solution)/shard_map/ppermute | solution.py:637
  109.6 17.1 %collective-permute-start.24 = (bf16[256,512]{1,0:T(8,128)(2,1)S(1)}, bf16[256,512]{1,0:T(8,128)(2,1)S(1)}, u32[]{:S(2)}, u32[]{:S(2)}) collective-permute-start(bf16[256,512]{1,0:T(8,128)(2,1)S(1)} %halve_0.1), channel_id=1, source_target_pairs={{0,16},{2,18},{4,20},{6,22},{8,24},{10,26},{12,28},{14,30},{16,0},... | collective-permute-start | bytes 786440 | tf_op jit(solution)/shard_map/ppermute | solution.py:637
  111.8 15.0 %collective-permute-start.25 = (bf16[2,128,256]{2,1,0:T(8,128)(2,1)S(1)}, bf16[2,128,256]{2,1,0:T(8,128)(2,1)S(1)}, u32[]{:S(2)}, u32[]{:S(2)}) collective-permute-start(bf16[2,128,256]{2,1,0:T(8,128)(2,1)S(1)} %get-tuple-element.117), channel_id=1, source_target_pairs={{16,0},{18,2},{20,4},{22,6},{17,1},{19,3},{21,5},{23,7}} | collective-permute-start | bytes 393224 | tf_op jit(solution)/shard_map/ppermute | solution.py:714
  113.0 15.8 %collective-permute-start.26 = (bf16[2,128,256]{2,1,0:T(8,128)(2,1)S(1)}, bf16[2,128,256]{2,1,0:T(8,128)(2,1)S(1)}, u32[]{:S(2)}, u32[]{:S(2)}) collective-permute-start(bf16[2,128,256]{2,1,0:T(8,128)(2,1)S(1)} %get-tuple-element.118), channel_id=1, source_target_pairs={{24,0},{26,2},{28,4},{30,6},{25,1},{27,3},{29,5},{31,7}} | collective-permute-start | bytes 393224 | tf_op jit(solution)/shard_map/ppermute | solution.py:714
  114.3 27.0 %collective-permute-start.31 = (bf16[2,256,512]{2,1,0:T(8,128)(2,1)S(1)}, bf16[2,256,512]{2,1,0:T(8,128)(2,1)S(1)}, u32[]{:S(2)}, u32[]{:S(2)}) collective-permute-start(bf16[2,256,512]{2,1,0:T(8,128)(2,1)S(1)} %get-tuple-element.110), channel_id=1, source_target_pairs={{0,8},{2,10},{4,12},{6,14},{8,0},{10,2},{12,4},{14,6},{16,24},{18,... | collective-permute-start | bytes 1572872 | tf_op jit(solution)/shard_map/ppermute | solution.py:637
  129.8 12.7 %collective-permute-start.27 = (bf16[3,256,256]{2,1,0:T(8,128)(2,1)S(1)}, bf16[3,256,256]{2,1,0:T(8,128)(2,1)S(1)}, u32[]{:S(2)}, u32[]{:S(2)}) collective-permute-start(bf16[3,256,256]{2,1,0:T(8,128)(2,1)S(1)} %get-tuple-element.120), channel_id=1, source_target_pairs={{0,2},{2,0},{4,6},{6,4},{8,10},{10,8},{12,14},{14,12},{16,18},{18,... | collective-permute-start | bytes 1179656 | tf_op jit(solution)/shard_map/ppermute | solution.py:625
  130.8 11.7 %collective-permute-start.28 = (bf16[3,256,256]{2,1,0:T(8,128)(2,1)S(1)}, bf16[3,256,256]{2,1,0:T(8,128)(2,1)S(1)}, u32[]{:S(2)}, u32[]{:S(2)}) collective-permute-start(bf16[3,256,256]{2,1,0:T(8,128)(2,1)S(1)} %get-tuple-element.121), channel_id=1, source_target_pairs={{0,4},{2,6},{4,0},{6,2},{8,12},{10,14},{12,8},{14,10},{16,20},{18,... | collective-permute-start | bytes 1179656 | tf_op jit(solution)/shard_map/ppermute | solution.py:625
  131.9 10.9 %collective-permute-start.29 = (bf16[3,256,256]{2,1,0:T(8,128)(2,1)S(1)}, bf16[3,256,256]{2,1,0:T(8,128)(2,1)S(1)}, u32[]{:S(2)}, u32[]{:S(2)}) collective-permute-start(bf16[3,256,256]{2,1,0:T(8,128)(2,1)S(1)} %get-tuple-element.122), channel_id=1, source_target_pairs={{0,6},{2,4},{4,2},{6,0},{8,14},{10,12},{12,10},{14,8},{16,22},{18,... | collective-permute-start | bytes 1179656 | tf_op jit(solution)/shard_map/ppermute | solution.py:625
  133.4 8.0 %collective-permute-start.30 = (bf16[256,512]{1,0:T(8,128)(2,1)S(1)}, bf16[256,512]{1,0:T(8,128)(2,1)S(1)}, u32[]{:S(2)}, u32[]{:S(2)}) collective-permute-start(bf16[256,512]{1,0:T(8,128)(2,1)S(1)} %halve_1.1), channel_id=1, source_target_pairs={{0,16},{2,18},{4,20},{6,22},{8,24},{10,26},{12,28},{14,30},{16,0},... | collective-permute-start | bytes 786440 | tf_op jit(solution)/shard_map/ppermute | solution.py:637
  (7 other events, 44.6 us)

commit v5 on v4

--- a/solution.py
+++ b/solution.py
@@ -24,6 +24,7 @@
 SMEM = pl.BlockSpec(memory_space=pltpu.SMEM)
 VMEM = pl.BlockSpec(memory_space=pltpu.VMEM)
 HBM = pl.BlockSpec(memory_space=pltpu.HBM)
+ANY = pl.BlockSpec(memory_space=pl.ANY)
 
 
 def shape(dims, dtype=jnp.bfloat16):
@@ -95,7 +96,7 @@
         in_specs=[SMEM, HBM, HBM],
         out_specs=[VMEM] * group,
         scratch_shapes=[pltpu.SemaphoreType.DMA((group, 2))],
-        compiler_params=params(16),
+        compiler_params=params(60),
         cost_estimate=cost(0, 4 * keys.size * 2),
         name="pack_kv",
     )(meta, keys, values)
@@ -137,7 +138,7 @@
             pltpu.SemaphoreType.DMA((group,)),
             pltpu.SemaphoreType.DMA,
         ],
-        compiler_params=params(24),
+        compiler_params=params(60),
         cost_estimate=cost(2 * rows * depth * width * group, 12 * 1024 * 1024),
         name="attn_grad",
     )(meta, queries, out_grad, proj_weight)
@@ -199,22 +200,30 @@
 
     def body(meta_ref, *refs):
         me = meta_ref[0]
-        pool, rest, strided = refs[group:]
-        for k in range(group):
-            pool[:, pl.ds(pl.multiple_of((me ^ k) * rows, rows), rows), :] = refs[k][...]
+        pool, rest, strided, sems = refs[group:]
+        copies = []
+        for k in range(group):
+            at = pl.ds(pl.multiple_of((me ^ k) * rows, rows), rows)
+            copies.append(pltpu.make_async_copy(refs[k], pool.at[:, at, :], sems.at[0, k]))
             if k > 0:
-                rest[k - 1] = refs[k][...]
+                copies.append(pltpu.make_async_copy(refs[k], rest.at[k - 1], sems.at[1, k]))
+        copied(*copies)
         strided[...] = pool[:, pl.ds(pl.multiple_of(meta_ref[2] * BLK, BLK), BLK), :]
 
-    return call(
-        body, (meta,), tuple(pieces),
-        [
+    return pl.pallas_call(
+        body,
+        out_shape=[
             shape((2, group * rows, width)),
             shape((group - 1, 2, rows, width)),
             shape((2, BLK, width)),
         ],
-        [], cost(0, 3 * 1024 * 1024), "assemble_kv",
-    )
+        in_specs=[SMEM] + [ANY] * group,
+        out_specs=[VMEM] * 3,
+        scratch_shapes=[pltpu.SemaphoreType.DMA((2, group))],
+        compiler_params=params(16),
+        cost_estimate=cost(0, 3 * MIB),
+        name="assemble_kv",
+    )(meta, *pieces)
 
 
 def assemble(pieces, meta, group):
@@ -222,14 +231,23 @@
 
     def body(meta_ref, *refs):
         me = meta_ref[0]
-        for k in range(group):
-            at = pl.multiple_of((me ^ k) * rows, rows)
-            refs[group][:, pl.ds(at, rows), :] = refs[k][...]
-
-    return call(
-        body, (meta,), tuple(pieces), [shape((lead, group * rows, width))], [],
-        cost(0, 2 * 1024 * 1024), "assemble",
-    )[0]
+        copies = []
+        for k in range(group):
+            at = pl.ds(pl.multiple_of((me ^ k) * rows, rows), rows)
+            target = refs[group].at[:, at, :]
+            copies.append(pltpu.make_async_copy(refs[k], target, refs[group + 1].at[k]))
+        copied(*copies)
+
+    return pl.pallas_call(
+        body,
+        out_shape=shape((lead, group * rows, width)),
+        in_specs=[SMEM] + [ANY] * group,
+        out_specs=VMEM,
+        scratch_shapes=[pltpu.SemaphoreType.DMA((group,))],
+        compiler_params=params(16),
+        cost_estimate=cost(0, 2 * MIB),
+        name="assemble",
+    )(meta, *pieces)
 
 
 def masks_of(layout, meta, parts, slots):
@@ -590,15 +608,27 @@
 
     def body(meta_ref, *refs):
         me = meta_ref[0]
+        outs, sems = refs[group:-1], refs[-1]
+        copies = []
         for k in range(group):
             at = pl.ds(pl.multiple_of((me ^ k) * width, width), width)
             for which in range(3):
-                refs[group + which][:, at] = refs[k][which]
-
-    return call(
-        body, (meta,), tuple(pieces), [shape((rows, group * width))] * 3, [],
-        cost(0, 3 * 1024 * 1024), "unpack",
-    )
+                target = outs[which].at[:, at]
+                copies.append(
+                    pltpu.make_async_copy(refs[k].at[which], target, sems.at[k, which])
+                )
+        copied(*copies)
+
+    return pl.pallas_call(
+        body,
+        out_shape=[shape((rows, group * width))] * 3,
+        in_specs=[SMEM] + [ANY] * group,
+        out_specs=[ANY] * 3,
+        scratch_shapes=[pltpu.SemaphoreType.DMA((group, 3))],
+        compiler_params=params(16),
+        cost_estimate=cost(0, 3 * MIB),
+        name="unpack",
+    )(meta, *pieces)
 
 
 def after(value, *others):
@@ -672,9 +702,9 @@
     ]
     qd_pieces = exchange(qd_cut)
     bias, bias_next = masks_of(layout, after(meta, strided), parts, slots)
-    qd = assemble(qd_pieces, after(meta, bias, *far), group)
+    qd = assemble(qd_pieces, after(meta, bias), group)
     next_qd = shifted(qd, -1)
-    og = exchange(pack_out_grad(out_grad, after(meta, qd), group, parts))
+    og = exchange(pack_out_grad(out_grad, after(meta, qd, *far), group, parts))
 
     stats = jnp.zeros((LOCAL // 2, 2 * heads, PAIR), jnp.float32)
     order = after(meta, og[0])
@@ -714,6 +744,7 @@
         lax.ppermute(piece, "seq", summary_route(index + 2, True))
         for index, piece in enumerate(far_grads)
     ]
+    order = after(order, finals[0])
     own_grad = backward_next(grads, next_qd, pool, bias_next, next_stats, order)
     sums, order = add_up(heads - 1, odds, evens, (own_grad, finals[0]), meta)
     finals.append(sums)

time: 145 us -> 141 us (0.972)
  local copies, waits for them, and re-layouts: 9.48 us -> 2.33 us
  Pallas kernels: 44.7 us -> 49.6 us
  waiting for transfers between devices: 42.1 us -> 38.5 us
    unnamed x15 -> x9, local copies, waits for them, and re-layouts: 8.19 us -> 1.05 us
    ppermute x2, waiting for transfers between devices: 12.9 us -> 6.11 us  [local(): lax.ppermute(strided, 'seq', summary_route(distance, False))]
    ppermute x5, waiting for transfers between devices: 15.6 us -> 20.3 us  [swap_groups(): return lax.ppermute(piece, 'seq', route)]
    pallas_call x16 -> x13, Pallas kernels: 35.1 us -> 31 us  [call(): pl.pallas_call(body, out_shape=outs, in_specs=[SMEM] * len(scalars) + [VM...]
    pallas_call x0 -> x3, Pallas kernels: none -> 4.08 us  [the longest x1 1.78 us: unpack(): pl.pallas_call(body, out_shape=[shape((rows, group * width))] * 3, in_spe...]
    pallas_call x1, Pallas kernels: 7.73 us -> 10.4 us  [grads_packed(): pl.pallas_call(body, out_shape=[shape((2, rows, width))] * group, in_spec...]
    pallas_call x1, Pallas kernels: 0.78 us -> 3 us  [pack_kv(): pl.pallas_call(body, out_shape=[shape((2, rows, width))] * group, in_spec...]
    ppermute x2, waiting for transfers between devices: 2.15 us -> 0.01 us  [local(): lax.ppermute(piece, 'seq', summary_route(index + 2, True))]
  transfers between devices with their start and end apart: 32 -> 32, of which waited for: 9 -> 10; matrix products, arithmetic and copies ran while one was open for 1% -> 1% of each run, Pallas kernels for 25% -> 29%
where the time goes in v5:
time: 141 us
  Pallas kernels  49.6 us (35%)
  starting transfers between devices  46.3 us (33%)
  waiting for transfers between devices  38.5 us (27%)
  between operations  3.15 us (2%)
  local copies, waits for them, and re-layouts  2.33 us (2%)
    pallas_call x13, Pallas kernels, call(): pl.pallas_call(body, out_shape=outs, in_specs=[SMEM] * len(scalars) + [VM...  31 us
    ppermute x18, starting transfers between devices, swap(): return lax.ppermute(piece, 'seq', route)  22.8 us
    ppermute x5, waiting for transfers between devices, swap_groups(): return lax.ppermute(piece, 'seq', route)  20.3 us
    pallas_call x1, Pallas kernels, grads_packed(): pl.pallas_call(body, out_shape=[shape((2, rows, width))] * group, in_spec...  10.4 us
    ppermute x4, starting transfers between devices, shifted(): return lax.ppermute(piece, 'seq', route)  9.56 us
    ppermute x18, waiting for transfers between devices, swap(): return lax.ppermute(piece, 'seq', route)  6.59 us
    ppermute x2, waiting for transfers between devices, local(): lax.ppermute(strided, 'seq', summary_route(distance, False))  6.11 us
    ppermute x5, starting transfers between devices, swap_groups(): return lax.ppermute(piece, 'seq', route)  6.01 us
  transfers between devices with their start and end apart: 32, of which 10 were waited for; matrix products, arithmetic and copies ran while one was open for 1% of the time, Pallas kernels for 29%

profile of v5, /device:TPU:0, one launch (start us, length us, event | category | flops | bytes accessed | tf_op | source)
XLA Modules:
  0.0 140.6 jit_solution(14965143711868605316)
XLA Ops:
  1.3 3.0 %pack_kv.1 = (bf16[2,256,256]{2,1,0:T(8,128)(2,1)}, bf16[2,256,256]{2,1,0:T(8,128)(2,1)}, bf16[2,256,256]{2,1,0:T(8,128)(2,1)}, bf16[2,256,256]{2,1,0:T(8,128)(2,1)}) custom-call(s32[2]{0:T(128)} %pad_add_fusion.1.meta_ref, bf16[256,1024]{1,0:T(8,128)(2,1)} %k_ref.1, bf16[256,1024]{1,0:T(8,128)(2,1)} %v_ref.1), custom_call_target="tpu_custom_call" | custom-call | flops 1 | bytes 1 | tf_op jit(solution)/shard_map/pack_kv/pallas_call | solution.py:93
  4.3 3.0 %collective-permute-start.1 = (bf16[2,256,256]{2,1,0:T(8,128)(2,1)}, bf16[2,256,256]{2,1,0:T(8,128)(2,1)S(1)}, u32[]{:S(2)}, u32[]{:S(2)}) collective-permute-start(bf16[2,256,256]{2,1,0:T(8,128)(2,1)} %get-tuple-element.68), channel_id=1, source_target_pairs={{0,2},{2,0},{4,6},{6,4},{8,10},{10,8},{12,14},{14,12},{16,18},{18,... | collective-permute-start | bytes 786440 | tf_op jit(solution)/shard_map/ppermute | solution.py:655
  7.3 3.5 %collective-permute-start = (bf16[2,256,256]{2,1,0:T(8,128)(2,1)}, bf16[2,256,256]{2,1,0:T(8,128)(2,1)S(1)}, u32[]{:S(2)}, u32[]{:S(2)}) collective-permute-start(bf16[2,256,256]{2,1,0:T(8,128)(2,1)} %get-tuple-element.67.refs_0_), channel_id=1, source_target_pairs={{0,8},{2,10},{4,12},{6,14},{8,16},{10,18},{12,20},{14,22},{16,24},... | collective-permute-start | bytes 786440 | tf_op jit(solution)/shard_map/ppermute | solution.py:663
  10.8 1.6 %collective-permute-start.2 = (bf16[2,256,256]{2,1,0:T(8,128)(2,1)}, bf16[2,256,256]{2,1,0:T(8,128)(2,1)S(1)}, u32[]{:S(2)}, u32[]{:S(2)}) collective-permute-start(bf16[2,256,256]{2,1,0:T(8,128)(2,1)} %get-tuple-element.72), channel_id=1, source_target_pairs={{0,4},{2,6},{4,0},{6,2},{8,12},{10,14},{12,8},{14,10},{16,20},{18,... | collective-permute-start | bytes 786440 | tf_op jit(solution)/shard_map/ppermute | solution.py:655
  16.2 10.4 %attn_grad.1 = (bf16[2,256,256]{2,1,0:T(8,128)(2,1)}, bf16[2,256,256]{2,1,0:T(8,128)(2,1)}, bf16[2,256,256]{2,1,0:T(8,128)(2,1)}, bf16[2,256,256]{2,1,0:T(8,128)(2,1)}) custom-call(s32[2]{0:T(128)} %pad_add_fusion.1.meta_ref, bf16[256,1024]{1,0:T(8,128)(2,1)} %q_ref.1, bf16[256,4096]{1,0:T(8,128)(2,1)} %og_ref.3, bf16[4096,1024]{1,0:T(8,128)(2,1)} %w_ref.1), custom_call_target="tpu_custom_call" | custom-call | flops 1 | bytes 1 | tf_op jit(solution)/shard_map/attn_grad/pallas_call | solution.py:129
  26.7 1.6 %assemble_kv.1 = (bf16[2,1024,256]{2,1,0:T(8,128)(2,1)S(1)}, bf16[3,2,256,256]{3,2,1,0:T(8,128)(2,1)}, bf16[2,128,256]{2,1,0:T(8,128)(2,1)S(1)}) custom-call(s32[4]{0:T(128)S(1)} %pad_add_fusion.meta_ref, bf16[2,256,256]{2,1,0:T(8,128)(2,1)S(1)} %copy-done.2, bf16[2,256,256]{2,1,0:T(8,128)(2,1)S(1)} %collective-permute-done.1.refs_1_, ...), custom_call_target="tpu_custom_call" | custom-call | flops 1 | bytes 1 | tf_op jit(solution)/shard_map/assemble_kv/pallas_call | solution.py:213
  28.3 3.5 %collective-permute-start.9 = (bf16[3,2,256,256]{3,2,1,0:T(8,128)(2,1)}, bf16[3,2,256,256]{3,2,1,0:T(8,128)(2,1)S(1)}, u32[]{:S(2)}, u32[]{:S(2)}) collective-permute-start(bf16[3,2,256,256]{3,2,1,0:T(8,128)(2,1)} %get-tuple-element.85), channel_id=1, source_target_pairs={{0,8},{2,10},{4,12},{6,14},{8,16},{10,18},{12,20},{14,22},{16,24},... | collective-permute-start | bytes 2359304 | tf_op jit(solution)/shard_map/ppermute | solution.py:663
  31.8 1.6 %collective-permute-start.4 = (bf16[2,256,256]{2,1,0:T(8,128)(2,1)}, bf16[2,256,256]{2,1,0:T(8,128)(2,1)S(1)}, u32[]{:S(2)}, u32[]{:S(2)}) collective-permute-start(bf16[2,256,256]{2,1,0:T(8,128)(2,1)} %get-tuple-element.78), channel_id=1, source_target_pairs={{0,2},{2,0},{4,6},{6,4},{8,10},{10,8},{12,14},{14,12},{16,18},{18,... | collective-permute-start | bytes 786440 | tf_op jit(solution)/shard_map/ppermute | solution.py:655
  33.4 1.5 %collective-permute-start.5 = (bf16[2,256,256]{2,1,0:T(8,128)(2,1)}, bf16[2,256,256]{2,1,0:T(8,128)(2,1)S(1)}, u32[]{:S(2)}, u32[]{:S(2)}) collective-permute-start(bf16[2,256,256]{2,1,0:T(8,128)(2,1)} %get-tuple-element.79), channel_id=1, source_target_pairs={{0,4},{2,6},{4,0},{6,2},{8,12},{10,14},{12,8},{14,10},{16,20},{18,... | collective-permute-start | bytes 786440 | tf_op jit(solution)/shard_map/ppermute | solution.py:655
  35.4 3.4 %collective-permute-start.7 = (bf16[2,128,256]{2,1,0:T(8,128)(2,1)S(1)}, bf16[2,128,256]{2,1,0:T(8,128)(2,1)S(1)}, u32[]{:S(2)}, u32[]{:S(2)}) collective-permute-start(bf16[2,128,256]{2,1,0:T(8,128)(2,1)S(1)} %get-tuple-element.74), channel_id=1, source_target_pairs={{0,16},{2,18},{4,20},{6,22},{1,17},{3,19},{5,21},{7,23}} | collective-permute-start | bytes 393224 | tf_op jit(solution)/shard_map/ppermute | solution.py:700
  38.8 2.6 %collective-permute-done.4.refs_1_ = bf16[2,256,256]{2,1,0:T(8,128)(2,1)S(1)} collective-permute-done((bf16[2,256,256]{2,1,0:T(8,128)(2,1)}, bf16[2,256,256]{2,1,0:T(8,128)(2,1)S(1)}, u32[]{:S(2)}, u32[]{:S(2)}) %collective-permute-start.4) | collective-permute-done | bytes 262176 | tf_op jit(solution)/shard_map/ppermute | solution.py:655
  41.3 1.9 %collective-permute-start.8 = (bf16[2,128,256]{2,1,0:T(8,128)(2,1)S(1)}, bf16[2,128,256]{2,1,0:T(8,128)(2,1)S(1)}, u32[]{:S(2)}, u32[]{:S(2)}) collective-permute-start(bf16[2,128,256]{2,1,0:T(8,128)(2,1)S(1)} %get-tuple-element.74), channel_id=1, source_target_pairs={{0,24},{2,26},{4,28},{6,30},{1,25},{3,27},{5,29},{7,31}} | collective-permute-start | bytes 393224 | tf_op jit(solution)/shard_map/ppermute | solution.py:700
  43.4 1.9 %masks.1 = (f32[4,11,256]{2,1,0:T(8,128)S(1)}, f32[4,10,256]{2,1,0:T(8,128)S(1)}) custom-call(s32[4]{0:T(128)S(1)} %pad_add_fusion.meta_ref, s32[32,10]{1,0:T(8,128)S(1)} %copy.10.table), custom_call_target="tpu_custom_call" | custom-call | flops 1 | bytes 1 | tf_op jit(solution)/shard_map/masks/pallas_call | solution.py:47
  47.2 4.7 %collective-permute-done.7.refs_4_ = bf16[2,128,256]{2,1,0:T(8,128)(2,1)S(1)} collective-permute-done((bf16[2,128,256]{2,1,0:T(8,128)(2,1)S(1)}, bf16[2,128,256]{2,1,0:T(8,128)(2,1)S(1)}, u32[]{:S(2)}, u32[]{:S(2)}) %collective-permute-start.7) | collective-permute-done | bytes 131104 | tf_op jit(solution)/shard_map/ppermute | solution.py:700
  54.4 1.6 %collective-permute-start.10 = (bf16[512,256]{1,0:T(8,128)(2,1)S(1)}, bf16[512,256]{1,0:T(8,128)(2,1)S(1)}, u32[]{:S(2)}, u32[]{:S(2)}) collective-permute-start(bf16[512,256]{1,0:T(8,128)(2,1)S(1)} %get-tuple-element.88), channel_id=1, source_target_pairs={{0,2},{2,0},{4,6},{6,4},{8,10},{10,8},{12,14},{14,12},{16,18},{18,... | collective-permute-start | bytes 786440 | tf_op jit(solution)/shard_map/ppermute | solution.py:655
  56.0 1.5 %collective-permute-start.11 = (bf16[512,256]{1,0:T(8,128)(2,1)S(1)}, bf16[512,256]{1,0:T(8,128)(2,1)S(1)}, u32[]{:S(2)}, u32[]{:S(2)}) collective-permute-start(bf16[512,256]{1,0:T(8,128)(2,1)S(1)} %get-tuple-element.89), channel_id=1, source_target_pairs={{0,4},{2,6},{4,0},{6,2},{8,12},{10,14},{12,8},{14,10},{16,20},{18,... | collective-permute-start | bytes 786440 | tf_op jit(solution)/shard_map/ppermute | solution.py:655
  59.3 4.5 %attention_0.1 = (bf16[1024,128]{1,0:T(8,128)(2,1)S(1)}, f32[4,4,256]{2,1,0:T(4,128)S(1)}) custom-call(s32[4]{0:T(128)S(1)} %pad_add_fusion.meta_ref, f32[4,11,256]{2,1,0:T(8,128)S(1)} %get-tuple-element.76.bias_ref, f32[4,4,256]{2,1,0:T(4,128)S(1)} %broadcast_in_dim.3.before_ref, bf16[2,1024,256]{2,1,0:T(8,128)(2,1)S(1)} %assemble.1.refs_0_, ...), custom_call_target="tpu_custom_call" | custom-call | flops 1 | bytes 1 | tf_op jit(solution)/shard_map/attention_0/pallas_call | solution.py:47
  63.8 3.5 %collective-permute-done.11.refs_2_ = bf16[512,256]{1,0:T(8,128)(2,1)S(1)} collective-permute-done((bf16[512,256]{1,0:T(8,128)(2,1)S(1)}, bf16[512,256]{1,0:T(8,128)(2,1)S(1)}, u32[]{:S(2)}, u32[]{:S(2)}) %collective-permute-start.11) | collective-permute-done | bytes 262176 | tf_op jit(solution)/shard_map/ppermute | solution.py:655
  71.6 4.7 %attention_1.1 = (bf16[1024,128]{1,0:T(8,128)(2,1)S(1)}, f32[4,4,256]{2,1,0:T(4,128)S(1)}) custom-call(s32[4]{0:T(128)S(1)} %pad_add_fusion.meta_ref, f32[4,11,256]{2,1,0:T(8,128)S(1)} %get-tuple-element.76.bias_ref, f32[4,4,256]{2,1,0:T(4,128)S(1)} %get-tuple-element.92.before_ref, bf16[2,1024,256]{2,1,0:T(8,128)(2,1)S(1)} %assemble.1.refs_0_, ...), custom_call_target="tpu_custom_call" | custom-call | flops 1 | bytes 1 | tf_op jit(solution)/shard_map/attention_1/pallas_call | solution.py:47
  76.3 5.5 %collective-permute-done.14.refs_2_ = bf16[2,1024,256]{2,1,0:T(8,128)(2,1)S(1)} collective-permute-done((bf16[2,1024,256]{2,1,0:T(8,128)(2,1)S(1)}, bf16[2,1024,256]{2,1,0:T(8,128)(2,1)S(1)}, u32[]{:S(2)}, u32[]{:S(2)}) %collective-permute-start.14) | collective-permute-done | bytes 1048608 | tf_op jit(solution)/shard_map/ppermute | solution.py:663
  83.2 4.3 %attention_back_0.1 = (bf16[1024,128]{1,0:T(8,128)(2,1)S(1)}, f32[2,1024,128]{2,1,0:T(8,128)S(1)}, bf16[2,128,256]{2,1,0:T(8,128)(2,1)S(1)}, bf16[2,128,256]{2,1,0:T(8,128)(2,1)S(1)}) custom-call(s32[4]{0:T(128)S(1)} %pad_add_fusion.meta_ref, f32[4,11,256]{2,1,0:T(8,128)S(1)} %get-tuple-element.76.bias_ref, f32[4,4,256]{2,1,0:T(4,128)S(1)} %get-tuple-element.96.stats_ref, ...), custom_call_target="tpu_custom_call" | custom-call | flops 1 | bytes 1 | tf_op jit(solution)/shard_map/attention_back_0/pallas_call | solution.py:47
  87.5 2.2 %project_0.1 = (f32[256,512]{1,0:T(8,128)S(1)}, bf16[1,256,512]{2,1,0:T(8,128)(2,1)S(1)}, bf16[1,256,512]{2,1,0:T(8,128)(2,1)S(1)}, f32[1,256,512]{2,1,0:T(8,128)S(1)}) custom-call(s32[4]{0:T(128)S(1)} %pad_add_fusion.meta_ref, bf16[512,1024]{1,0:T(8,128)(2,1)S(1)} %join_columns.1.mine_ref, bf16[512,1024]{1,0:T(8,128)(2,1)S(1)} %collective-permute-done.13.theirs_ref, ...), custom_call_target="tpu_custom_call" | custom-call | flops 1 | bytes 1 | tf_op jit(solution)/shard_map/project_0/pallas_call | solution.py:47
  89.7 2.7 %collective-permute-start.19 = (bf16[1,256,512]{2,1,0:T(8,128)(2,1)S(1)}, bf16[1,256,512]{2,1,0:T(8,128)(2,1)S(1)}, u32[]{:S(2)}, u32[]{:S(2)}) collective-permute-start(bf16[1,256,512]{2,1,0:T(8,128)(2,1)S(1)} %get-tuple-element.105), channel_id=1, source_target_pairs={{0,8},{2,10},{4,12},{6,14},{8,0},{10,2},{12,4},{14,6},{16,24},{18,... | collective-permute-start | bytes 786440 | tf_op jit(solution)/shard_map/ppermute | solution.py:667
  95.9 4.5 %attention_back_1.1 = (bf16[1024,128]{1,0:T(8,128)(2,1)S(1)}, f32[2,1024,128]{2,1,0:T(8,128)S(1)}, bf16[2,128,256]{2,1,0:T(8,128)(2,1)S(1)}, bf16[2,128,256]{2,1,0:T(8,128)(2,1)S(1)}) custom-call(s32[4]{0:T(128)S(1)} %pad_add_fusion.meta_ref, f32[4,11,256]{2,1,0:T(8,128)S(1)} %get-tuple-element.76.bias_ref, f32[4,4,256]{2,1,0:T(4,128)S(1)} %get-tuple-element.96.stats_ref, ...), custom_call_target="tpu_custom_call" | custom-call | flops 1 | bytes 1 | tf_op jit(solution)/shard_map/attention_back_1/pallas_call | solution.py:47
  100.5 2.4 %collective-permute-start.24 = (bf16[256,512]{1,0:T(8,128)(2,1)S(1)}, bf16[256,512]{1,0:T(8,128)(2,1)S(1)}, u32[]{:S(2)}, u32[]{:S(2)}) collective-permute-start(bf16[256,512]{1,0:T(8,128)(2,1)S(1)} %halve_0.1), channel_id=1, source_target_pairs={{0,16},{2,18},{4,20},{6,22},{8,24},{10,26},{12,28},{14,30},{16,0},... | collective-permute-start | bytes 786440 | tf_op jit(solution)/shard_map/ppermute | solution.py:667
  103.1 2.1 %project_1.1 = (f32[256,512]{1,0:T(8,128)S(1)}, bf16[2,256,512]{2,1,0:T(8,128)(2,1)S(1)}, bf16[1,256,512]{2,1,0:T(8,128)(2,1)S(1)}, f32[1,256,512]{2,1,0:T(8,128)S(1)}) custom-call(s32[4]{0:T(128)S(1)} %pad_add_fusion.meta_ref, bf16[512,1024]{1,0:T(8,128)(2,1)S(1)} %join_columns.1.mine_ref, bf16[512,1024]{1,0:T(8,128)(2,1)S(1)} %collective-permute-done.13.theirs_ref, ...), custom_call_target="tpu_custom_call" | custom-call | flops 1 | bytes 1 | tf_op jit(solution)/shard_map/project_1/pallas_call | solution.py:47
  108.7 4.5 %collective-permute-done.24.refs_2_ = bf16[256,512]{1,0:T(8,128)(2,1)S(1)} collective-permute-done((bf16[256,512]{1,0:T(8,128)(2,1)S(1)}, bf16[256,512]{1,0:T(8,128)(2,1)S(1)}, u32[]{:S(2)}, u32[]{:S(2)}) %collective-permute-start.24) | collective-permute-done | bytes 262176 | tf_op jit(solution)/shard_map/ppermute | solution.py:667
  113.2 3.9 %attention_back_next.1.own_ref = f32[2,1024,256]{2,1,0:T(8,128)S(1)} custom-call(s32[4]{0:T(128)S(1)} %pad_add_fusion.meta_ref, f32[4,10,256]{2,1,0:T(8,128)S(1)} %get-tuple-element.114.bias_ref, f32[4,4,256]{2,1,0:T(4,128)S(1)} %collective-permute-done.15.stats_ref, f32[2,1024,128]{2,1,0:T(8,128)S(1)} %get-tuple-element.115.refs_0_, ...), custom_call_target="tpu_custom_call" | custom-call | flops 1 | bytes 1 | tf_op jit(solution)/shard_map/attention_back_next/pallas_call | solution.py:47
  117.2 6.7 %collective-permute-done.23.arrived_ref = bf16[1,256,512]{2,1,0:T(8,128)(2,1)S(1)} collective-permute-done((bf16[1,256,512]{2,1,0:T(8,128)(2,1)S(1)}, bf16[1,256,512]{2,1,0:T(8,128)(2,1)S(1)}, u32[]{:S(2)}, u32[]{:S(2)}) %collective-permute-start.23) | collective-permute-done | bytes 262176 | tf_op jit(solution)/shard_map/ppermute | solution.py:667
  126.2 1.6 %collective-permute-start.28 = (bf16[3,256,256]{2,1,0:T(8,128)(2,1)S(1)}, bf16[3,256,256]{2,1,0:T(8,128)(2,1)S(1)}, u32[]{:S(2)}, u32[]{:S(2)}) collective-permute-start(bf16[3,256,256]{2,1,0:T(8,128)(2,1)S(1)} %get-tuple-element.123), channel_id=1, source_target_pairs={{0,4},{2,6},{4,0},{6,2},{8,12},{10,14},{12,8},{14,10},{16,20},{18,... | collective-permute-start | bytes 1179656 | tf_op jit(solution)/shard_map/ppermute | solution.py:655
  128.4 9.1 %collective-permute-done.30.refs_3_ = bf16[256,512]{1,0:T(8,128)(2,1)S(1)} collective-permute-done((bf16[256,512]{1,0:T(8,128)(2,1)S(1)}, bf16[256,512]{1,0:T(8,128)(2,1)S(1)}, u32[]{:S(2)}, u32[]{:S(2)}) %collective-permute-start.30) | collective-permute-done | bytes 262176 | tf_op jit(solution)/shard_map/ppermute | solution.py:667
  138.6 1.8 %unpack.1 = (bf16[256,1024]{1,0:T(8,128)(2,1)}, bf16[256,1024]{1,0:T(8,128)(2,1)}, bf16[256,1024]{1,0:T(8,128)(2,1)}) custom-call(s32[4]{0:T(128)S(1)} %pad_add_fusion.meta_ref, bf16[3,256,256]{2,1,0:T(8,128)(2,1)S(1)} %get-tuple-element.121.refs_0_, bf16[3,256,256]{2,1,0:T(8,128)(2,1)S(1)} %collective-permute-done.27.refs_1_, ...), custom_call_target="tpu_custom_call" | custom-call | flops 1 | bytes 1 | tf_op jit(solution)/shard_map/unpack/pallas_call | solution.py:622
  (65 shorter events, 26.2 us)
Async XLA Ops:
  4.3 11.9 %collective-permute-start.1 = (bf16[2,256,256]{2,1,0:T(8,128)(2,1)}, bf16[2,256,256]{2,1,0:T(8,128)(2,1)S(1)}, u32[]{:S(2)}, u32[]{:S(2)}) collective-permute-start(bf16[2,256,256]{2,1,0:T(8,128)(2,1)} %get-tuple-element.68), channel_id=1, source_target_pairs={{0,2},{2,0},{4,6},{6,4},{8,10},{10,8},{12,14},{14,12},{16,18},{18,... | collective-permute-start | bytes 786440 | tf_op jit(solution)/shard_map/ppermute | solution.py:655
  7.3 19.3 %collective-permute-start = (bf16[2,256,256]{2,1,0:T(8,128)(2,1)}, bf16[2,256,256]{2,1,0:T(8,128)(2,1)S(1)}, u32[]{:S(2)}, u32[]{:S(2)}) collective-permute-start(bf16[2,256,256]{2,1,0:T(8,128)(2,1)} %get-tuple-element.67.refs_0_), channel_id=1, source_target_pairs={{0,8},{2,10},{4,12},{6,14},{8,16},{10,18},{12,20},{14,22},{16,24},... | collective-permute-start | bytes 786440 | tf_op jit(solution)/shard_map/ppermute | solution.py:663
  10.8 15.8 %collective-permute-start.2 = (bf16[2,256,256]{2,1,0:T(8,128)(2,1)}, bf16[2,256,256]{2,1,0:T(8,128)(2,1)S(1)}, u32[]{:S(2)}, u32[]{:S(2)}) collective-permute-start(bf16[2,256,256]{2,1,0:T(8,128)(2,1)} %get-tuple-element.72), channel_id=1, source_target_pairs={{0,4},{2,6},{4,0},{6,2},{8,12},{10,14},{12,8},{14,10},{16,20},{18,... | collective-permute-start | bytes 786440 | tf_op jit(solution)/shard_map/ppermute | solution.py:655
  12.4 14.2 %collective-permute-start.3 = (bf16[2,256,256]{2,1,0:T(8,128)(2,1)}, bf16[2,256,256]{2,1,0:T(8,128)(2,1)S(1)}, u32[]{:S(2)}, u32[]{:S(2)}) collective-permute-start(bf16[2,256,256]{2,1,0:T(8,128)(2,1)} %get-tuple-element.73), channel_id=1, source_target_pairs={{0,6},{2,4},{4,2},{6,0},{8,14},{10,12},{12,10},{14,8},{16,22},{18,... | collective-permute-start | bytes 786440 | tf_op jit(solution)/shard_map/ppermute | solution.py:655
  28.3 31.0 %collective-permute-start.9 = (bf16[3,2,256,256]{3,2,1,0:T(8,128)(2,1)}, bf16[3,2,256,256]{3,2,1,0:T(8,128)(2,1)S(1)}, u32[]{:S(2)}, u32[]{:S(2)}) collective-permute-start(bf16[3,2,256,256]{3,2,1,0:T(8,128)(2,1)} %get-tuple-element.85), channel_id=1, source_target_pairs={{0,8},{2,10},{4,12},{6,14},{8,16},{10,18},{12,20},{14,22},{16,24},... | collective-permute-start | bytes 2359304 | tf_op jit(solution)/shard_map/ppermute | solution.py:663
  31.8 9.5 %collective-permute-start.4 = (bf16[2,256,256]{2,1,0:T(8,128)(2,1)}, bf16[2,256,256]{2,1,0:T(8,128)(2,1)S(1)}, u32[]{:S(2)}, u32[]{:S(2)}) collective-permute-start(bf16[2,256,256]{2,1,0:T(8,128)(2,1)} %get-tuple-element.78), channel_id=1, source_target_pairs={{0,2},{2,0},{4,6},{6,4},{8,10},{10,8},{12,14},{14,12},{16,18},{18,... | collective-permute-start | bytes 786440 | tf_op jit(solution)/shard_map/ppermute | solution.py:655
  33.4 12.2 %collective-permute-start.5 = (bf16[2,256,256]{2,1,0:T(8,128)(2,1)}, bf16[2,256,256]{2,1,0:T(8,128)(2,1)S(1)}, u32[]{:S(2)}, u32[]{:S(2)}) collective-permute-start(bf16[2,256,256]{2,1,0:T(8,128)(2,1)} %get-tuple-element.79), channel_id=1, source_target_pairs={{0,4},{2,6},{4,0},{6,2},{8,12},{10,14},{12,8},{14,10},{16,20},{18,... | collective-permute-start | bytes 786440 | tf_op jit(solution)/shard_map/ppermute | solution.py:655
  34.9 10.7 %collective-permute-start.6 = (bf16[2,256,256]{2,1,0:T(8,128)(2,1)}, bf16[2,256,256]{2,1,0:T(8,128)(2,1)S(1)}, u32[]{:S(2)}, u32[]{:S(2)}) collective-permute-start(bf16[2,256,256]{2,1,0:T(8,128)(2,1)} %get-tuple-element.80), channel_id=1, source_target_pairs={{0,6},{2,4},{4,2},{6,0},{8,14},{10,12},{12,10},{14,8},{16,22},{18,... | collective-permute-start | bytes 786440 | tf_op jit(solution)/shard_map/ppermute | solution.py:655
  35.4 16.5 %collective-permute-start.7 = (bf16[2,128,256]{2,1,0:T(8,128)(2,1)S(1)}, bf16[2,128,256]{2,1,0:T(8,128)(2,1)S(1)}, u32[]{:S(2)}, u32[]{:S(2)}) collective-permute-start(bf16[2,128,256]{2,1,0:T(8,128)(2,1)S(1)} %get-tuple-element.74), channel_id=1, source_target_pairs={{0,16},{2,18},{4,20},{6,22},{1,17},{3,19},{5,21},{7,23}} | collective-permute-start | bytes 393224 | tf_op jit(solution)/shard_map/ppermute | solution.py:700
  41.3 12.0 %collective-permute-start.8 = (bf16[2,128,256]{2,1,0:T(8,128)(2,1)S(1)}, bf16[2,128,256]{2,1,0:T(8,128)(2,1)S(1)}, u32[]{:S(2)}, u32[]{:S(2)}) collective-permute-start(bf16[2,128,256]{2,1,0:T(8,128)(2,1)S(1)} %get-tuple-element.74), channel_id=1, source_target_pairs={{0,24},{2,26},{4,28},{6,30},{1,25},{3,27},{5,29},{7,31}} | collective-permute-start | bytes 393224 | tf_op jit(solution)/shard_map/ppermute | solution.py:700
  54.4 9.4 %collective-permute-start.10 = (bf16[512,256]{1,0:T(8,128)(2,1)S(1)}, bf16[512,256]{1,0:T(8,128)(2,1)S(1)}, u32[]{:S(2)}, u32[]{:S(2)}) collective-permute-start(bf16[512,256]{1,0:T(8,128)(2,1)S(1)} %get-tuple-element.88), channel_id=1, source_target_pairs={{0,2},{2,0},{4,6},{6,4},{8,10},{10,8},{12,14},{14,12},{16,18},{18,... | collective-permute-start | bytes 786440 | tf_op jit(solution)/shard_map/ppermute | solution.py:655
  56.0 11.3 %collective-permute-start.11 = (bf16[512,256]{1,0:T(8,128)(2,1)S(1)}, bf16[512,256]{1,0:T(8,128)(2,1)S(1)}, u32[]{:S(2)}, u32[]{:S(2)}) collective-permute-start(bf16[512,256]{1,0:T(8,128)(2,1)S(1)} %get-tuple-element.89), channel_id=1, source_target_pairs={{0,4},{2,6},{4,0},{6,2},{8,12},{10,14},{12,8},{14,10},{16,20},{18,... | collective-permute-start | bytes 786440 | tf_op jit(solution)/shard_map/ppermute | solution.py:655
  57.5 9.8 %collective-permute-start.12 = (bf16[512,256]{1,0:T(8,128)(2,1)S(1)}, bf16[512,256]{1,0:T(8,128)(2,1)S(1)}, u32[]{:S(2)}, u32[]{:S(2)}) collective-permute-start(bf16[512,256]{1,0:T(8,128)(2,1)S(1)} %get-tuple-element.90), channel_id=1, source_target_pairs={{0,6},{2,4},{4,2},{6,0},{8,14},{10,12},{12,10},{14,8},{16,22},{18,... | collective-permute-start | bytes 786440 | tf_op jit(solution)/shard_map/ppermute | solution.py:655
  58.0 23.9 %collective-permute-start.14 = (bf16[2,1024,256]{2,1,0:T(8,128)(2,1)S(1)}, bf16[2,1024,256]{2,1,0:T(8,128)(2,1)S(1)}, u32[]{:S(2)}, u32[]{:S(2)}) collective-permute-start(bf16[2,1024,256]{2,1,0:T(8,128)(2,1)S(1)} %assemble.1.refs_0_), channel_id=1, source_target_pairs={{8,0},{10,2},{12,4},{14,6},{16,8},{18,10},{20,12},{22,14},{24,16},... | collective-permute-start | bytes 3145736 | tf_op jit(solution)/shard_map/ppermute | solution.py:663
  68.0 15.2 %collective-permute-start.13 = (bf16[512,1024]{1,0:T(8,128)(2,1)S(1)}, bf16[512,1024]{1,0:T(8,128)(2,1)S(1)}, u32[]{:S(2)}, u32[]{:S(2)}) collective-permute-start(bf16[512,1024]{1,0:T(8,128)(2,1)S(1)} %join_columns.1.mine_ref), channel_id=1, source_target_pairs={{0,1},{1,0},{2,3},{3,2},{4,5},{5,4},{6,7},{7,6},{8,9},{9,8},{10,11... | collective-permute-start | bytes 3145736 | tf_op jit(solution)/shard_map/ppermute | solution.py:717
  68.1 19.4 %collective-permute-start.16 = (bf16[1024,128]{1,0:T(8,128)(2,1)S(1)}, bf16[1024,128]{1,0:T(8,128)(2,1)S(1)}, u32[]{:S(2)}, u32[]{:S(2)}) collective-permute-start(bf16[1024,128]{1,0:T(8,128)(2,1)S(1)} %get-tuple-element.86.refs_0_), channel_id=1, source_target_pairs={{0,2},{2,0},{4,6},{6,4},{8,10},{10,8},{12,14},{14,12},{16,18},{18,... | collective-permute-start | bytes 786440 | tf_op jit(solution)/shard_map/ppermute | solution.py:655
  69.3 18.2 %collective-permute-start.17 = (bf16[1024,128]{1,0:T(8,128)(2,1)S(1)}, bf16[1024,128]{1,0:T(8,128)(2,1)S(1)}, u32[]{:S(2)}, u32[]{:S(2)}) collective-permute-start(bf16[1024,128]{1,0:T(8,128)(2,1)S(1)} %get-tuple-element.86.refs_0_), channel_id=1, source_target_pairs={{0,4},{2,6},{4,0},{6,2},{8,12},{10,14},{12,8},{14,10},{16,20},{18,... | collective-permute-start | bytes 786440 | tf_op jit(solution)/shard_map/ppermute | solution.py:655
  70.2 17.3 %collective-permute-start.18 = (bf16[1024,128]{1,0:T(8,128)(2,1)S(1)}, bf16[1024,128]{1,0:T(8,128)(2,1)S(1)}, u32[]{:S(2)}, u32[]{:S(2)}) collective-permute-start(bf16[1024,128]{1,0:T(8,128)(2,1)S(1)} %get-tuple-element.86.refs_0_), channel_id=1, source_target_pairs={{0,6},{2,4},{4,2},{6,0},{8,14},{10,12},{12,10},{14,8},{16,22},{18,... | collective-permute-start | bytes 786440 | tf_op jit(solution)/shard_map/ppermute | solution.py:655
  81.8 5.6 %collective-permute-start.15 = (f32[4,4,256]{2,1,0:T(4,128)S(1)}, f32[4,4,256]{2,1,0:T(4,128)S(1)}, u32[]{:S(2)}, u32[]{:S(2)}) collective-permute-start(f32[4,4,256]{2,1,0:T(4,128)S(1)} %get-tuple-element.96.stats_ref), channel_id=1, source_target_pairs={{8,0},{10,2},{12,4},{14,6},{16,8},{18,10},{20,12},{22,14},{24,16},... | collective-permute-start | bytes 49160 | tf_op jit(solution)/shard_map/ppermute | solution.py:663
  89.7 10.8 %collective-permute-start.19 = (bf16[1,256,512]{2,1,0:T(8,128)(2,1)S(1)}, bf16[1,256,512]{2,1,0:T(8,128)(2,1)S(1)}, u32[]{:S(2)}, u32[]{:S(2)}) collective-permute-start(bf16[1,256,512]{2,1,0:T(8,128)(2,1)S(1)} %get-tuple-element.105), channel_id=1, source_target_pairs={{0,8},{2,10},{4,12},{6,14},{8,0},{10,2},{12,4},{14,6},{16,24},{18,... | collective-permute-start | bytes 786440 | tf_op jit(solution)/shard_map/ppermute | solution.py:667
  92.4 10.5 %collective-permute-start.20 = (bf16[1024,128]{1,0:T(8,128)(2,1)S(1)}, bf16[1024,128]{1,0:T(8,128)(2,1)S(1)}, u32[]{:S(2)}, u32[]{:S(2)}) collective-permute-start(bf16[1024,128]{1,0:T(8,128)(2,1)S(1)} %get-tuple-element.108.refs_0_), channel_id=1, source_target_pairs={{0,2},{2,0},{4,6},{6,4},{8,10},{10,8},{12,14},{14,12},{16,18},{18,... | collective-permute-start | bytes 786440 | tf_op jit(solution)/shard_map/ppermute | solution.py:655
  93.9 9.2 %collective-permute-start.21 = (bf16[1024,128]{1,0:T(8,128)(2,1)S(1)}, bf16[1024,128]{1,0:T(8,128)(2,1)S(1)}, u32[]{:S(2)}, u32[]{:S(2)}) collective-permute-start(bf16[1024,128]{1,0:T(8,128)(2,1)S(1)} %get-tuple-element.108.refs_0_), channel_id=1, source_target_pairs={{0,4},{2,6},{4,0},{6,2},{8,12},{10,14},{12,8},{14,10},{16,20},{18,... | collective-permute-start | bytes 786440 | tf_op jit(solution)/shard_map/ppermute | solution.py:655
  95.4 7.7 %collective-permute-start.22 = (bf16[1024,128]{1,0:T(8,128)(2,1)S(1)}, bf16[1024,128]{1,0:T(8,128)(2,1)S(1)}, u32[]{:S(2)}, u32[]{:S(2)}) collective-permute-start(bf16[1024,128]{1,0:T(8,128)(2,1)S(1)} %get-tuple-element.108.refs_0_), channel_id=1, source_target_pairs={{0,6},{2,4},{4,2},{6,0},{8,14},{10,12},{12,10},{14,8},{16,22},{18,... | collective-permute-start | bytes 786440 | tf_op jit(solution)/shard_map/ppermute | solution.py:655
  100.5 12.7 %collective-permute-start.24 = (bf16[256,512]{1,0:T(8,128)(2,1)S(1)}, bf16[256,512]{1,0:T(8,128)(2,1)S(1)}, u32[]{:S(2)}, u32[]{:S(2)}) collective-permute-start(bf16[256,512]{1,0:T(8,128)(2,1)S(1)} %halve_0.1), channel_id=1, source_target_pairs={{0,16},{2,18},{4,20},{6,22},{8,24},{10,26},{12,28},{14,30},{16,0},... | collective-permute-start | bytes 786440 | tf_op jit(solution)/shard_map/ppermute | solution.py:667
  105.2 18.6 %collective-permute-start.23 = (bf16[1,256,512]{2,1,0:T(8,128)(2,1)S(1)}, bf16[1,256,512]{2,1,0:T(8,128)(2,1)S(1)}, u32[]{:S(2)}, u32[]{:S(2)}) collective-permute-start(bf16[1,256,512]{2,1,0:T(8,128)(2,1)S(1)} %get-tuple-element.110), channel_id=1, source_target_pairs={{0,8},{2,10},{4,12},{6,14},{8,0},{10,2},{12,4},{14,6},{16,24},{18,... | collective-permute-start | bytes 786440 | tf_op jit(solution)/shard_map/ppermute | solution.py:667
  105.5 18.4 %collective-permute-start.25 = (bf16[2,128,256]{2,1,0:T(8,128)(2,1)S(1)}, bf16[2,128,256]{2,1,0:T(8,128)(2,1)S(1)}, u32[]{:S(2)}, u32[]{:S(2)}) collective-permute-start(bf16[2,128,256]{2,1,0:T(8,128)(2,1)S(1)} %get-tuple-element.119), channel_id=1, source_target_pairs={{16,0},{18,2},{20,4},{22,6},{17,1},{19,3},{21,5},{23,7}} | collective-permute-start | bytes 393224 | tf_op jit(solution)/shard_map/ppermute | solution.py:744
  106.8 17.1 %collective-permute-start.26 = (bf16[2,128,256]{2,1,0:T(8,128)(2,1)S(1)}, bf16[2,128,256]{2,1,0:T(8,128)(2,1)S(1)}, u32[]{:S(2)}, u32[]{:S(2)}) collective-permute-start(bf16[2,128,256]{2,1,0:T(8,128)(2,1)S(1)} %get-tuple-element.120), channel_id=1, source_target_pairs={{24,0},{26,2},{28,4},{30,6},{25,1},{27,3},{29,5},{31,7}} | collective-permute-start | bytes 393224 | tf_op jit(solution)/shard_map/ppermute | solution.py:744
  108.1 29.4 %collective-permute-start.31 = (bf16[2,256,512]{2,1,0:T(8,128)(2,1)S(1)}, bf16[2,256,512]{2,1,0:T(8,128)(2,1)S(1)}, u32[]{:S(2)}, u32[]{:S(2)}) collective-permute-start(bf16[2,256,512]{2,1,0:T(8,128)(2,1)S(1)} %get-tuple-element.111), channel_id=1, source_target_pairs={{0,8},{2,10},{4,12},{6,14},{8,0},{10,2},{12,4},{14,6},{16,24},{18,... | collective-permute-start | bytes 1572872 | tf_op jit(solution)/shard_map/ppermute | solution.py:667
  124.8 13.8 %collective-permute-start.27 = (bf16[3,256,256]{2,1,0:T(8,128)(2,1)S(1)}, bf16[3,256,256]{2,1,0:T(8,128)(2,1)S(1)}, u32[]{:S(2)}, u32[]{:S(2)}) collective-permute-start(bf16[3,256,256]{2,1,0:T(8,128)(2,1)S(1)} %get-tuple-element.122), channel_id=1, source_target_pairs={{0,2},{2,0},{4,6},{6,4},{8,10},{10,8},{12,14},{14,12},{16,18},{18,... | collective-permute-start | bytes 1179656 | tf_op jit(solution)/shard_map/ppermute | solution.py:655
  126.2 12.4 %collective-permute-start.28 = (bf16[3,256,256]{2,1,0:T(8,128)(2,1)S(1)}, bf16[3,256,256]{2,1,0:T(8,128)(2,1)S(1)}, u32[]{:S(2)}, u32[]{:S(2)}) collective-permute-start(bf16[3,256,256]{2,1,0:T(8,128)(2,1)S(1)} %get-tuple-element.123), channel_id=1, source_target_pairs={{0,4},{2,6},{4,0},{6,2},{8,12},{10,14},{12,8},{14,10},{16,20},{18,... | collective-permute-start | bytes 1179656 | tf_op jit(solution)/shard_map/ppermute | solution.py:655
  127.8 10.8 %collective-permute-start.29 = (bf16[3,256,256]{2,1,0:T(8,128)(2,1)S(1)}, bf16[3,256,256]{2,1,0:T(8,128)(2,1)S(1)}, u32[]{:S(2)}, u32[]{:S(2)}) collective-permute-start(bf16[3,256,256]{2,1,0:T(8,128)(2,1)S(1)} %get-tuple-element.124), channel_id=1, source_target_pairs={{0,6},{2,4},{4,2},{6,0},{8,14},{10,12},{12,10},{14,8},{16,22},{18,... | collective-permute-start | bytes 1179656 | tf_op jit(solution)/shard_map/ppermute | solution.py:655
  128.4 9.1 %collective-permute-start.30 = (bf16[256,512]{1,0:T(8,128)(2,1)S(1)}, bf16[256,512]{1,0:T(8,128)(2,1)S(1)}, u32[]{:S(2)}, u32[]{:S(2)}) collective-permute-start(bf16[256,512]{1,0:T(8,128)(2,1)S(1)} %halve_1.1), channel_id=1, source_target_pairs={{0,16},{2,18},{4,20},{6,22},{8,24},{10,26},{12,28},{14,30},{16,0},... | collective-permute-start | bytes 786440 | tf_op jit(solution)/shard_map/ppermute | solution.py:667
  (4 other events, 48.5 us)

commit v6 on v5

--- a/solution.py
+++ b/solution.py
@@ -79,134 +79,105 @@
     rows = keys.shape[0]
 
     def body(meta_ref, k_ref, v_ref, *refs):
-        outs, sems = refs[:group], refs[group]
+        outs, (k_in, v_in, sems) = refs[:group], refs[group:]
         me = meta_ref[0]
-        copies = []
+        copied(
+            pltpu.make_async_copy(k_ref, k_in, sems.at[0]),
+            pltpu.make_async_copy(v_ref, v_in, sems.at[1]),
+        )
         for k in range(group):
             at = pl.ds(pl.multiple_of((me ^ k) * width, width), width)
-            for which, source in enumerate((k_ref, v_ref)):
-                copies.append(
-                    pltpu.make_async_copy(source.at[:, at], outs[k].at[which], sems.at[k, which])
-                )
-        copied(*copies)
+            outs[k][0] = k_in[:, at]
+            outs[k][1] = v_in[:, at]
 
     return pl.pallas_call(
         body,
         out_shape=[shape((2, rows, width))] * group,
         in_specs=[SMEM, HBM, HBM],
         out_specs=[VMEM] * group,
-        scratch_shapes=[pltpu.SemaphoreType.DMA((group, 2))],
+        scratch_shapes=[
+            pltpu.VMEM(keys.shape, jnp.bfloat16),
+            pltpu.VMEM(keys.shape, jnp.bfloat16),
+            pltpu.SemaphoreType.DMA((2,)),
+        ],
         compiler_params=params(60),
         cost_estimate=cost(0, 4 * keys.size * 2),
         name="pack_kv",
     )(meta, keys, values)
 
 
-def grads_packed(queries, out_grad, proj_weight, meta, group, width):
+def grads_packed(queries, out_grad, proj_weight, meta, group, parts):
     rows, depth = out_grad.shape
+    columns = queries.shape[1]
+    width = columns // group
+    each = depth // (group * parts)
+    half = parts // 2
+    chunks = 8
+    step = depth // chunks
+    assert rows == width
 
     def body(meta_ref, q_ref, og_ref, w_ref, *refs):
-        outs, (og, w, q_sems, w_sems, og_sem) = refs[:group], refs[group:]
-        me = meta_ref[0]
-        og_copy = pltpu.make_async_copy(og_ref, og, og_sem)
+        outs, (q, og, w, total, sems, w_sems) = refs[:group], refs[group:]
+        me, core = meta_ref[0], meta_ref[2]
+        og_copy = pltpu.make_async_copy(og_ref, og, sems.at[0])
+        q_copy = pltpu.make_async_copy(q_ref, q, sems.at[1])
         og_copy.start()
-        q_copies, w_copies = [], []
+        w_copies = []
+        for c in range(chunks):
+            at = slice(c * step, (c + 1) * step)
+            w_copies.append(pltpu.make_async_copy(w_ref.at[at, :], w.at[at, :], w_sems.at[c]))
+            w_copies[c].start()
+        q_copy.start()
+        og_copy.wait()
+        for k in range(group):
+            for part in range(half):
+                at = ((core * half + part) * group + (me ^ k)) * each
+                at = pl.multiple_of(at, each)
+                to = 2 * rows + part * each
+                outs[k][to : to + each, :] = og[:, pl.ds(at, each)].T
+        for c in range(chunks):
+            at = slice(c * step, (c + 1) * step)
+            w_copies[c].wait()
+            got = dot(og[:, at], w[at, :], NN)
+            if c == 0:
+                total[...] = got
+            else:
+                total[...] += got
+        q_copy.wait()
         for k in range(group):
             at = pl.ds(pl.multiple_of((me ^ k) * width, width), width)
-            w_copies.append(pltpu.make_async_copy(w_ref.at[:, at], w.at[k], w_sems.at[k]))
-            w_copies[k].start()
-        for k in range(group):
-            at = pl.ds(pl.multiple_of((me ^ k) * width, width), width)
-            q_copies.append(pltpu.make_async_copy(q_ref.at[:, at], outs[k].at[0], q_sems.at[k]))
-            q_copies[k].start()
-        og_copy.wait()
-        for k in range(group):
-            w_copies[k].wait()
-            outs[k][1] = dot(og[...], w[k], NN).astype(jnp.bfloat16)
-        for k in range(group):
-            q_copies[k].wait()
+            outs[k][:rows, :] = q[:, at]
+            outs[k][rows : 2 * rows, :] = total[:, at].astype(jnp.bfloat16)
 
     return pl.pallas_call(
         body,
-        out_shape=[shape((2, rows, width))] * group,
+        out_shape=[shape((2 * rows + half * each, rows))] * group,
         in_specs=[SMEM, HBM, HBM, HBM],
         out_specs=[VMEM] * group,
         scratch_shapes=[
+            pltpu.VMEM((rows, columns), jnp.bfloat16),
             pltpu.VMEM((rows, depth), jnp.bfloat16),
-            pltpu.VMEM((group, depth, width), jnp.bfloat16),
-            pltpu.SemaphoreType.DMA((group,)),
-            pltpu.SemaphoreType.DMA((group,)),
-            pltpu.SemaphoreType.DMA,
+            pltpu.VMEM((depth, columns), jnp.bfloat16),
+            pltpu.VMEM((rows, columns), jnp.float32),
+            pltpu.SemaphoreType.DMA((2,)),
+            pltpu.SemaphoreType.DMA((chunks,)),
         ],
         compiler_params=params(60),
-        cost_estimate=cost(2 * rows * depth * width * group, 12 * 1024 * 1024),
+        cost_estimate=cost(2 * rows * depth * columns, 12 * 1024 * 1024),
         name="attn_grad",
     )(meta, queries, out_grad, proj_weight)
 
 
-def pack_out_grad(out_grad, meta, group, parts):
-    rows, depth = out_grad.shape
-    each = depth // (group * parts)
-    half = parts // 2
-
-    def body(meta_ref, og_ref, *refs):
-        outs, (held, sems) = refs[:group], refs[group:]
-        me, core = meta_ref[0], meta_ref[3]
-        copies = []
-        for k in range(group):
-            for part in range(half):
-                at = ((core * half + part) * group + (me ^ k)) * each
-                at = pl.ds(pl.multiple_of(at, each), each)
-                copies.append(
-                    pltpu.make_async_copy(og_ref.at[:, at], held.at[k, part], sems.at[k, part])
-                )
-        copied(*copies)
-        for k in range(group):
-            for part in range(half):
-                outs[k][part * each : (part + 1) * each, :] = held[k, part].T
-
-    return pl.pallas_call(
-        body,
-        out_shape=[shape((half * each, rows))] * group,
-        in_specs=[SMEM, HBM],
-        out_specs=[VMEM] * group,
-        scratch_shapes=[
-            pltpu.VMEM((group, half, rows, each), jnp.bfloat16),
-            pltpu.SemaphoreType.DMA((group, half)),
-        ],
-        compiler_params=params(16),
-        cost_estimate=cost(0, 3 * out_grad.size),
-        name="pack_out_grad",
-    )(meta, out_grad)
-
-
-def join_columns(pieces, meta, group):
-    height, rows = pieces[0].shape
+def assemble_kv(pieces, meta, group):
+    rows, width = pieces[0].shape[1:]
 
     def body(meta_ref, *refs):
         me = meta_ref[0]
-        for k in range(group):
-            at = pl.multiple_of((me ^ k) * rows, rows)
-            refs[group][:, pl.ds(at, rows)] = refs[k][...]
-
-    return call(
-        body, (meta,), tuple(pieces), [shape((height, group * rows))], [],
-        cost(0, 2 * 1024 * 1024), "join_columns",
-    )[0]
-
-
-def assemble_kv(pieces, meta, group):
-    rows, width = pieces[0].shape[1:]
-
-    def body(meta_ref, *refs):
-        me = meta_ref[0]
-        pool, rest, strided, sems = refs[group:]
+        pool, strided, sems = refs[group:]
         copies = []
         for k in range(group):
             at = pl.ds(pl.multiple_of((me ^ k) * rows, rows), rows)
-            copies.append(pltpu.make_async_copy(refs[k], pool.at[:, at, :], sems.at[0, k]))
-            if k > 0:
-                copies.append(pltpu.make_async_copy(refs[k], rest.at[k - 1], sems.at[1, k]))
+            copies.append(pltpu.make_async_copy(refs[k], pool.at[:, at, :], sems.at[k]))
         copied(*copies)
         strided[...] = pool[:, pl.ds(pl.multiple_of(meta_ref[2] * BLK, BLK), BLK), :]
 
@@ -214,12 +185,11 @@
         body,
         out_shape=[
             shape((2, group * rows, width)),
-            shape((group - 1, 2, rows, width)),
             shape((2, BLK, width)),
         ],
         in_specs=[SMEM] + [ANY] * group,
-        out_specs=[VMEM] * 3,
-        scratch_shapes=[pltpu.SemaphoreType.DMA((2, group))],
+        out_specs=[VMEM] * 2,
+        scratch_shapes=[pltpu.SemaphoreType.DMA((group,))],
         compiler_params=params(16),
         cost_estimate=cost(0, 3 * MIB),
         name="assemble_kv",
@@ -227,27 +197,23 @@
 
 
 def assemble(pieces, meta, group):
-    lead, rows, width = pieces[0].shape
+    rows = pieces[0].shape[1]
+    height = pieces[0].shape[0] - 2 * rows
 
     def body(meta_ref, *refs):
         me = meta_ref[0]
-        copies = []
+        qd, og = refs[group:]
         for k in range(group):
             at = pl.ds(pl.multiple_of((me ^ k) * rows, rows), rows)
-            target = refs[group].at[:, at, :]
-            copies.append(pltpu.make_async_copy(refs[k], target, refs[group + 1].at[k]))
-        copied(*copies)
-
-    return pl.pallas_call(
-        body,
-        out_shape=shape((lead, group * rows, width)),
-        in_specs=[SMEM] + [ANY] * group,
-        out_specs=VMEM,
-        scratch_shapes=[pltpu.SemaphoreType.DMA((group,))],
-        compiler_params=params(16),
-        cost_estimate=cost(0, 2 * MIB),
-        name="assemble",
-    )(meta, *pieces)
+            qd[0, at, :] = refs[k][:rows, :]
+            qd[1, at, :] = refs[k][rows : 2 * rows, :]
+            og[:, at] = refs[k][2 * rows :, :]
+
+    return call(
+        body, (meta,), tuple(pieces),
+        [shape((2, group * rows, rows)), shape((height, group * rows))], [],
+        cost(0, 4 * MIB), "assemble",
+    )
 
 
 def masks_of(layout, meta, parts, slots):
@@ -298,15 +264,13 @@
     )
 
 
-def fill_pools(meta_ref, own, prev, rest, far, k_pool, v_pool, group, rows, slots):
-    me, at_group, offset = meta_ref[0], meta_ref[1], meta_ref[2]
-    whole = group * rows
+def fill_pools(meta_ref, own, prev, far, k_pool, v_pool, slots):
+    at_group, offset = meta_ref[1], meta_ref[2]
+    whole = own.shape[1]
+    k_pool[:whole, :] = prev[0]
+    v_pool[:whole, :] = prev[1]
     k_pool[whole : 2 * whole, :] = own[0]
     v_pool[whole : 2 * whole, :] = own[1]
-    for k in range(group):
-        at = pl.multiple_of((me ^ k) * rows, rows)
-        k_pool[pl.ds(at, rows), :] = prev[0] if k == 0 else rest[k - 1, 0]
-        v_pool[pl.ds(at, rows), :] = prev[1] if k == 0 else rest[k - 1, 1]
     tail = jnp.zeros((slots * BLK, k_pool.shape[1]), k_pool.dtype)
     k_pool[2 * whole :, :] = tail
     v_pool[2 * whole :, :] = tail
@@ -351,18 +315,17 @@
     return [bias_ref[t, j : j + 1, :] for j in picked]
 
 
-def forward(head, qd, own, prev, rest, far, bias, stats, meta, group, slots):
+def forward(head, qd, own, prev, far, bias, stats, meta, group, slots):
     whole = qd.shape[1]
-    rows = whole // group
     pairs = whole // PAIR
-    counts = (4, len(far))
+    counts = (3, len(far))
 
     def body(meta_ref, bias_ref, before_ref, *refs):
         (around, far_refs), refs = split_refs(refs, counts)
         qd_ref, *around = one_head(around, head)
         far_refs = one_head(far_refs, head)
         out_ref, stats_ref, k_pool, v_pool = refs
-        fill_pools(meta_ref, *around, far_refs, k_pool, v_pool, group, rows, slots)
+        fill_pools(meta_ref, *around, far_refs, k_pool, v_pool, slots)
         stats_ref[...] = before_ref[...]
         masks = causal_masks()
         for t in range(pairs):
@@ -383,7 +346,7 @@
 
     span = (SPAN + slots) * BLK
     return call(
-        body, (meta,), (bias, stats, qd, own, prev, rest, *far),
+        body, (meta,), (bias, stats, qd, own, prev, *far),
         [shape((whole, HD)), shape(stats.shape, jnp.float32)],
         [pltpu.VMEM((2 * whole + slots * BLK, HD), jnp.bfloat16)] * 2,
         cost(4 * whole * span * HD * 2, 3 * 1024 * 1024, whole * span),
@@ -391,11 +354,10 @@
     )
 
 
-def backward(head, qd, own, prev, rest, far, before, bias, stats, meta, group, slots):
+def backward(head, qd, own, prev, far, before, bias, stats, meta, group, slots):
     whole, width = qd.shape[1:]
-    rows = whole // group
     pairs = whole // PAIR
-    counts = (4, len(far), len(before))
+    counts = (3, len(far), len(before))
     everything = 2 * whole + slots * BLK
 
     def body(meta_ref, bias_ref, stats_ref, *refs):
@@ -405,7 +367,7 @@
         ((dq_ref, grad_ref), far_outs), refs = split_refs(refs, (2, len(far)))
         k_pool, v_pool, far_sum = refs
         at_group = meta_ref[1]
-        fill_pools(meta_ref, *around, far_refs, k_pool, v_pool, group, rows, slots)
+        fill_pools(meta_ref, *around, far_refs, k_pool, v_pool, slots)
         masks = causal_masks()
         grad_ref[...] = jnp.zeros_like(grad_ref)
         far_sum[...] = jnp.zeros_like(far_sum)
@@ -438,7 +400,7 @@
 
     span = (SPAN + slots) * BLK
     outs = call(
-        body, (meta,), (bias, stats, qd, own, prev, rest, *far, *before),
+        body, (meta,), (bias, stats, qd, own, prev, *far, *before),
         [shape((whole, HD)), shape((2, whole, HD), jnp.float32)]
         + [shape((2, BLK, width))] * len(far),
         [
@@ -647,7 +609,7 @@
     me, at_group = position % group, position // group
     core = lax.axis_index("head")
     offset = layout[blocks - 1, 0] % STRIDE
-    place = jnp.stack([me, at_group]).astype(jnp.int32)
+    place = jnp.stack([me, at_group, core]).astype(jnp.int32)
     meta = jnp.stack([me, at_group, offset, core]).astype(jnp.int32)
 
     def swap(piece, k):
@@ -691,45 +653,41 @@
 
     kv = pack_kv(keys, values, place, group, width)
     own_kv = exchange(kv)
-    prev = shifted(kv[0], 1)
-    early = after(place, own_kv[1])
-    qd_cut = grads_packed(queries, out_grad, proj_weight, early, group, width)
-    pool, others, strided = assemble_kv(own_kv, after(meta, prev, qd_cut[0]), group)
-    rest = shifted(others, 1)
+    early = after(place, own_kv[1], own_kv[2])
+    qd_cut = grads_packed(queries, out_grad, proj_weight, early, group, parts)
+    pool, strided = assemble_kv(own_kv, after(meta, qd_cut[0]), group)
+    prev = shifted(pool, 1)
+    qd_pieces = exchange(qd_cut)
     far = [
         lax.ppermute(strided, "seq", summary_route(distance, False))
         for distance in range(2, parts)
     ]
-    qd_pieces = exchange(qd_cut)
     bias, bias_next = masks_of(layout, after(meta, strided), parts, slots)
-    qd = assemble(qd_pieces, after(meta, bias), group)
+    qd, mine = assemble(qd_pieces, after(meta, bias, prev, *far), group)
+    theirs = lax.ppermute(mine, "head", [(0, 1), (1, 0)])
     next_qd = shifted(qd, -1)
-    og = exchange(pack_out_grad(out_grad, after(meta, qd, *far), group, parts))
 
     stats = jnp.zeros((LOCAL // 2, 2 * heads, PAIR), jnp.float32)
-    order = after(meta, og[0])
+    order = meta
     attn = []
     for h in range(heads):
-        got, stats = forward(h, qd, pool, prev, rest, far, bias, stats, order, group, slots)
+        got, stats = forward(h, qd, pool, prev, far, bias, stats, order, group, slots)
         attn.append([got] + [swap(got, k) for k in range(1, group)])
-        if h == 0:
-            mine = join_columns(og, after(meta, got), group)
-            theirs = lax.ppermute(mine, "head", [(0, 1), (1, 0)])
-        order = after(meta, got, mine)
-    next_stats = shifted(after(stats, next_qd), -1)
+        order = after(meta, got, theirs)
 
     dq, grads, keep, finals, firsts = [], [], [], [], []
     far_grads = [jnp.zeros((2, BLK, width), jnp.bfloat16) for _ in far]
     order = after(meta, stats, theirs)
     for h in range(heads):
         got = backward(
-            h, qd, pool, prev, rest, far, far_grads, bias, stats, order, group, slots
+            h, qd, pool, prev, far, far_grads, bias, stats, order, group, slots
         )
         dq.append(got[0])
         grads.append(got[1])
         far_grads = got[2]
-        order = after(order, got[0], next_stats)
+        order = after(order, got[0])
         if h > 0:
+            order = after(order, next_stats)
             sums, order = add_up(h - 1, odds, evens, got[0], order)
             finals.append(sums)
         kept, first, odds, evens = project(
@@ -739,6 +697,8 @@
         firsts = [first]
         odds = swap_groups(odds, 1)
         order = after(meta, first)
+        if h == 0:
+            next_stats = shifted(after(stats, next_qd, first), -1)
     neighbour = swap_groups(first, 1)
     far_back = [
         lax.ppermute(piece, "seq", summary_route(index + 2, True))

time: 141 us -> 140 us (level)
  waiting for transfers between devices: 38.5 us -> 46.2 us
  starting transfers between devices: 46.3 us -> 40.6 us
  Pallas kernels: 49.6 us -> 46.4 us
    ppermute x2, waiting for transfers between devices: 6.11 us -> 12.7 us  [local(): lax.ppermute(strided, 'seq', summary_route(distance, False))]
    ppermute x18 -> x15, waiting for transfers between devices: 6.59 us -> 12.9 us  [swap(): return lax.ppermute(piece, 'seq', route)]
    ppermute x4 -> x3, waiting for transfers between devices: 5.55 us -> 0.01 us  [shifted(): return lax.ppermute(piece, 'seq', route)]
    pallas_call x4 -> x2, Pallas kernels: 13.8 us -> 10 us  [the longest x1 8.73 us: grads_packed(): pl.pallas_call(body, out_shape=[shape((2 * rows + half * each, rows))] *...]
    ppermute x18 -> x15, starting transfers between devices: 22.8 us -> 19.1 us  [swap(): return lax.ppermute(piece, 'seq', route)]
    ppermute x4 -> x3, starting transfers between devices: 9.56 us -> 6.12 us  [shifted(): return lax.ppermute(piece, 'seq', route)]
  transfers between devices with their start and end apart: 32 -> 28, of which waited for: 10 -> 12; matrix products, arithmetic and copies ran while one was open for 1% -> 1% of each run, Pallas kernels for 29% -> 28%
where the time goes in v6:
time: 140 us; the launch traced here: 139 us
  Pallas kernels  46.4 us (33%)
  waiting for transfers between devices  46.2 us (33%)
  starting transfers between devices  40.6 us (29%)
  between operations  3.09 us (2%)
  local copies, waits for them, and re-layouts  2.41 us (2%)
    pallas_call x13, Pallas kernels, call(): pl.pallas_call(body, out_shape=outs, in_specs=[SMEM] * len(scalars) + [VM...  31.6 us
    ppermute x5, waiting for transfers between devices, swap_groups(): return lax.ppermute(piece, 'seq', route)  20.6 us
    ppermute x15, starting transfers between devices, swap(): return lax.ppermute(piece, 'seq', route)  19.1 us
    ppermute x15, waiting for transfers between devices, swap(): return lax.ppermute(piece, 'seq', route)  12.9 us
    ppermute x2, waiting for transfers between devices, local(): lax.ppermute(strided, 'seq', summary_route(distance, False))  12.7 us
    pallas_call x1, Pallas kernels, grads_packed(): pl.pallas_call(body, out_shape=[shape((2 * rows + half * each, rows))] *...  8.73 us
    ppermute x5, starting transfers between devices, swap_groups(): return lax.ppermute(piece, 'seq', route)  6.95 us
    ppermute x3, starting transfers between devices, shifted(): return lax.ppermute(piece, 'seq', route)  6.12 us
  transfers between devices with their start and end apart: 28, of which 12 were waited for; matrix products, arithmetic and copies ran while one was open for 1% of the time, Pallas kernels for 28%

profile of v6, /device:TPU:0, one launch (start us, length us, event | category | flops | bytes accessed | tf_op | source)
XLA Modules:
  0.0 139.3 jit_solution(16192188981176088645)
XLA Ops:
  1.2 3.0 %pack_kv.1 = (bf16[2,256,256]{2,1,0:T(8,128)(2,1)}, bf16[2,256,256]{2,1,0:T(8,128)(2,1)}, bf16[2,256,256]{2,1,0:T(8,128)(2,1)}, bf16[2,256,256]{2,1,0:T(8,128)(2,1)}) custom-call(s32[3]{0:T(128)} %pad_add_fusion.1.meta_ref, bf16[256,1024]{1,0:T(8,128)(2,1)} %k_ref.1, bf16[256,1024]{1,0:T(8,128)(2,1)} %v_ref.1), custom_call_target="tpu_custom_call" | custom-call | flops 1 | bytes 1 | tf_op jit(solution)/shard_map/pack_kv/pallas_call | solution.py:93
  4.2 3.0 %collective-permute-start = (bf16[2,256,256]{2,1,0:T(8,128)(2,1)}, bf16[2,256,256]{2,1,0:T(8,128)(2,1)S(1)}, u32[]{:S(2)}, u32[]{:S(2)}) collective-permute-start(bf16[2,256,256]{2,1,0:T(8,128)(2,1)} %get-tuple-element.62), channel_id=1, source_target_pairs={{0,2},{2,0},{4,6},{6,4},{8,10},{10,8},{12,14},{14,12},{16,18},{18,... | collective-permute-start | bytes 786440 | tf_op jit(solution)/shard_map/ppermute | solution.py:617
  7.2 1.5 %collective-permute-start.1 = (bf16[2,256,256]{2,1,0:T(8,128)(2,1)}, bf16[2,256,256]{2,1,0:T(8,128)(2,1)S(1)}, u32[]{:S(2)}, u32[]{:S(2)}) collective-permute-start(bf16[2,256,256]{2,1,0:T(8,128)(2,1)} %get-tuple-element.63), channel_id=1, source_target_pairs={{0,4},{2,6},{4,0},{6,2},{8,12},{10,14},{12,8},{14,10},{16,20},{18,... | collective-permute-start | bytes 786440 | tf_op jit(solution)/shard_map/ppermute | solution.py:617
  12.1 2.5 %collective-permute-done.refs_1_ = bf16[2,256,256]{2,1,0:T(8,128)(2,1)S(1)} collective-permute-done((bf16[2,256,256]{2,1,0:T(8,128)(2,1)}, bf16[2,256,256]{2,1,0:T(8,128)(2,1)S(1)}, u32[]{:S(2)}, u32[]{:S(2)}) %collective-permute-start) | collective-permute-done | bytes 262176 | tf_op jit(solution)/shard_map/ppermute | solution.py:617
  14.6 6.2 %collective-permute-done.1.refs_2_ = bf16[2,256,256]{2,1,0:T(8,128)(2,1)S(1)} collective-permute-done((bf16[2,256,256]{2,1,0:T(8,128)(2,1)}, bf16[2,256,256]{2,1,0:T(8,128)(2,1)S(1)}, u32[]{:S(2)}, u32[]{:S(2)}) %collective-permute-start.1) | collective-permute-done | bytes 262176 | tf_op jit(solution)/shard_map/ppermute | solution.py:617
  20.8 8.7 %attn_grad.1 = (bf16[1024,256]{1,0:T(8,128)(2,1)}, bf16[1024,256]{1,0:T(8,128)(2,1)}, bf16[1024,256]{1,0:T(8,128)(2,1)}, bf16[1024,256]{1,0:T(8,128)(2,1)}) custom-call(s32[3]{0:T(128)} %pad_add_fusion.1.meta_ref, bf16[256,1024]{1,0:T(8,128)(2,1)} %q_ref.1, bf16[256,4096]{1,0:T(8,128)(2,1)} %og_ref.1, bf16[4096,1024]{1,0:T(8,128)(2,1)} %w_ref.1), custom_call_target="tpu_custom_call" | custom-call | flops 1 | bytes 1 | tf_op jit(solution)/shard_map/attn_grad/pallas_call | solution.py:152
  30.9 3.5 %collective-permute-start.3 = (bf16[2,1024,256]{2,1,0:T(8,128)(2,1)S(1)}, bf16[2,1024,256]{2,1,0:T(8,128)(2,1)S(1)}, u32[]{:S(2)}, u32[]{:S(2)}) collective-permute-start(bf16[2,1024,256]{2,1,0:T(8,128)(2,1)S(1)} %get-tuple-element.72.refs_1_.refs_3_), channel_id=1, source_target_pairs={{0,8},{2,10},{4,12},{6,14},{8,16},{10,18},{12,20},{14,22},{16,24},... | collective-permute-start | bytes 3145736 | tf_op jit(solution)/shard_map/ppermute | solution.py:625
  34.5 2.0 %collective-permute-start.7 = (bf16[1024,256]{1,0:T(8,128)(2,1)}, bf16[1024,256]{1,0:T(8,128)(2,1)S(1)}, u32[]{:S(2)}, u32[]{:S(2)}) collective-permute-start(bf16[1024,256]{1,0:T(8,128)(2,1)} %get-tuple-element.75), channel_id=1, source_target_pairs={{0,4},{2,6},{4,0},{6,2},{8,12},{10,14},{12,8},{14,10},{16,20},{18,... | collective-permute-start | bytes 1572872 | tf_op jit(solution)/shard_map/ppermute | solution.py:617
  36.6 1.4 %collective-permute-start.8 = (bf16[1024,256]{1,0:T(8,128)(2,1)}, bf16[1024,256]{1,0:T(8,128)(2,1)}, u32[]{:S(2)}, u32[]{:S(2)}) collective-permute-start(bf16[1024,256]{1,0:T(8,128)(2,1)} %get-tuple-element.76), channel_id=1, source_target_pairs={{0,6},{2,4},{4,2},{6,0},{8,14},{10,12},{12,10},{14,8},{16,22},{18,... | collective-permute-start | bytes 1572872 | tf_op jit(solution)/shard_map/ppermute | solution.py:617
  38.0 4.4 %collective-permute-start.4 = (bf16[2,128,256]{2,1,0:T(8,128)(2,1)}, bf16[2,128,256]{2,1,0:T(8,128)(2,1)S(1)}, u32[]{:S(2)}, u32[]{:S(2)}) collective-permute-start(bf16[2,128,256]{2,1,0:T(8,128)(2,1)} %get-tuple-element.69), channel_id=1, source_target_pairs={{0,16},{2,18},{4,20},{6,22},{1,17},{3,19},{5,21},{7,23}} | collective-permute-start | bytes 393224 | tf_op jit(solution)/shard_map/ppermute | solution.py:662
  42.4 11.9 %collective-permute-done.4.refs_3_ = bf16[2,128,256]{2,1,0:T(8,128)(2,1)S(1)} collective-permute-done((bf16[2,128,256]{2,1,0:T(8,128)(2,1)}, bf16[2,128,256]{2,1,0:T(8,128)(2,1)S(1)}, u32[]{:S(2)}, u32[]{:S(2)}) %collective-permute-start.4) | collective-permute-done | bytes 131104 | tf_op jit(solution)/shard_map/ppermute | solution.py:662
  55.7 1.9 %masks.1 = (f32[4,11,256]{2,1,0:T(8,128)S(1)}, f32[4,10,256]{2,1,0:T(8,128)S(1)}) custom-call(s32[4]{0:T(128)S(1)} %pad_add_fusion.meta_ref, s32[32,10]{1,0:T(8,128)S(1)} %copy.10.table), custom_call_target="tpu_custom_call" | custom-call | flops 1 | bytes 1 | tf_op jit(solution)/shard_map/masks/pallas_call | solution.py:47
  62.2 4.5 %attention_0.1 = (bf16[1024,128]{1,0:T(8,128)(2,1)S(1)}, f32[4,4,256]{2,1,0:T(4,128)S(1)}) custom-call(s32[4]{0:T(128)S(1)} %pad_add_fusion.meta_ref, f32[4,11,256]{2,1,0:T(8,128)S(1)} %get-tuple-element.71.bias_ref, f32[4,4,256]{2,1,0:T(4,128)S(1)} %broadcast_in_dim.3.before_ref, bf16[2,1024,256]{2,1,0:T(8,128)(2,1)S(1)} %get-tuple-element.77.refs_0_, ...), custom_call_target="tpu_custom_call" | custom-call | flops 1 | bytes 1 | tf_op jit(solution)/shard_map/attention_0/pallas_call | solution.py:47
  67.3 1.9 %collective-permute-start.11 = (bf16[1024,128]{1,0:T(8,128)(2,1)S(1)}, bf16[1024,128]{1,0:T(8,128)(2,1)S(1)}, u32[]{:S(2)}, u32[]{:S(2)}) collective-permute-start(bf16[1024,128]{1,0:T(8,128)(2,1)S(1)} %get-tuple-element.78.refs_0_), channel_id=1, source_target_pairs={{0,4},{2,6},{4,0},{6,2},{8,12},{10,14},{12,8},{14,10},{16,20},{18,... | collective-permute-start | bytes 786440 | tf_op jit(solution)/shard_map/ppermute | solution.py:617
  69.3 1.4 collective-permute-start.12
  70.7 4.7 %attention_1.1 = (bf16[1024,128]{1,0:T(8,128)(2,1)S(1)}, f32[4,4,256]{2,1,0:T(4,128)S(1)}) custom-call(s32[4]{0:T(128)S(1)} %pad_add_fusion.meta_ref, f32[4,11,256]{2,1,0:T(8,128)S(1)} %get-tuple-element.71.bias_ref, f32[4,4,256]{2,1,0:T(4,128)S(1)} %get-tuple-element.81.before_ref, bf16[2,1024,256]{2,1,0:T(8,128)(2,1)S(1)} %get-tuple-element.77.refs_0_, ...), custom_call_target="tpu_custom_call" | custom-call | flops 1 | bytes 1 | tf_op jit(solution)/shard_map/attention_1/pallas_call | solution.py:47
  75.4 4.3 %attention_back_0.1 = (bf16[1024,128]{1,0:T(8,128)(2,1)S(1)}, f32[2,1024,128]{2,1,0:T(8,128)S(1)}, bf16[2,128,256]{2,1,0:T(8,128)(2,1)S(1)}, bf16[2,128,256]{2,1,0:T(8,128)(2,1)S(1)}) custom-call(s32[4]{0:T(128)S(1)} %pad_add_fusion.meta_ref, f32[4,11,256]{2,1,0:T(8,128)S(1)} %get-tuple-element.71.bias_ref, f32[4,4,256]{2,1,0:T(4,128)S(1)} %get-tuple-element.92.stats_ref, ...), custom_call_target="tpu_custom_call" | custom-call | flops 1 | bytes 1 | tf_op jit(solution)/shard_map/attention_back_0/pallas_call | solution.py:47
  79.7 1.4 collective-permute-done.11.refs_2_
  81.1 1.8 %collective-permute-done.12.refs_3_ = bf16[1024,128]{1,0:T(8,128)(2,1)S(1)} collective-permute-done((bf16[1024,128]{1,0:T(8,128)(2,1)S(1)}, bf16[1024,128]{1,0:T(8,128)(2,1)S(1)}, u32[]{:S(2)}, u32[]{:S(2)}) %collective-permute-start.12) | collective-permute-done | bytes 262176 | tf_op jit(solution)/shard_map/ppermute | solution.py:617
  83.0 2.2 %project_0.1 = (f32[256,512]{1,0:T(8,128)S(1)}, bf16[1,256,512]{2,1,0:T(8,128)(2,1)S(1)}, bf16[1,256,512]{2,1,0:T(8,128)(2,1)S(1)}, f32[1,256,512]{2,1,0:T(8,128)S(1)}) custom-call(s32[4]{0:T(128)S(1)} %pad_add_fusion.meta_ref, bf16[512,1024]{1,0:T(8,128)(2,1)S(1)} %get-tuple-element.79.mine_ref, bf16[512,1024]{1,0:T(8,128)(2,1)S(1)} %collective-permute-done.9.theirs_ref, ...), custom_call_target="tpu_custom_call" | custom-call | flops 1 | bytes 1 | tf_op jit(solution)/shard_map/project_0/pallas_call | solution.py:47
  85.1 2.4 %collective-permute-start.15 = (bf16[1,256,512]{2,1,0:T(8,128)(2,1)S(1)}, bf16[1,256,512]{2,1,0:T(8,128)(2,1)S(1)}, u32[]{:S(2)}, u32[]{:S(2)}) collective-permute-start(bf16[1,256,512]{2,1,0:T(8,128)(2,1)S(1)} %get-tuple-element.95), channel_id=1, source_target_pairs={{0,8},{2,10},{4,12},{6,14},{8,0},{10,2},{12,4},{14,6},{16,24},{18,... | collective-permute-start | bytes 786440 | tf_op jit(solution)/shard_map/ppermute | solution.py:629
  88.1 1.7 %collective-permute-start.17 = (bf16[1024,128]{1,0:T(8,128)(2,1)S(1)}, bf16[1024,128]{1,0:T(8,128)(2,1)S(1)}, u32[]{:S(2)}, u32[]{:S(2)}) collective-permute-start(bf16[1024,128]{1,0:T(8,128)(2,1)S(1)} %get-tuple-element.98.refs_0_), channel_id=1, source_target_pairs={{0,4},{2,6},{4,0},{6,2},{8,12},{10,14},{12,8},{14,10},{16,20},{18,... | collective-permute-start | bytes 786440 | tf_op jit(solution)/shard_map/ppermute | solution.py:617
  92.4 4.5 %attention_back_1.1 = (bf16[1024,128]{1,0:T(8,128)(2,1)S(1)}, f32[2,1024,128]{2,1,0:T(8,128)S(1)}, bf16[2,128,256]{2,1,0:T(8,128)(2,1)S(1)}, bf16[2,128,256]{2,1,0:T(8,128)(2,1)S(1)}) custom-call(s32[4]{0:T(128)S(1)} %pad_add_fusion.meta_ref, f32[4,11,256]{2,1,0:T(8,128)S(1)} %get-tuple-element.71.bias_ref, f32[4,4,256]{2,1,0:T(4,128)S(1)} %get-tuple-element.92.stats_ref, ...), custom_call_target="tpu_custom_call" | custom-call | flops 1 | bytes 1 | tf_op jit(solution)/shard_map/attention_back_1/pallas_call | solution.py:47
  97.0 3.1 %collective-permute-start.20 = (bf16[256,512]{1,0:T(8,128)(2,1)S(1)}, bf16[256,512]{1,0:T(8,128)(2,1)S(1)}, u32[]{:S(2)}, u32[]{:S(2)}) collective-permute-start(bf16[256,512]{1,0:T(8,128)(2,1)S(1)} %halve_0.1), channel_id=1, source_target_pairs={{0,16},{2,18},{4,20},{6,22},{8,24},{10,26},{12,28},{14,30},{16,0},... | collective-permute-start | bytes 786440 | tf_op jit(solution)/shard_map/ppermute | solution.py:629
  100.9 2.1 %project_1.1 = (f32[256,512]{1,0:T(8,128)S(1)}, bf16[2,256,512]{2,1,0:T(8,128)(2,1)S(1)}, bf16[1,256,512]{2,1,0:T(8,128)(2,1)S(1)}, f32[1,256,512]{2,1,0:T(8,128)S(1)}) custom-call(s32[4]{0:T(128)S(1)} %pad_add_fusion.meta_ref, bf16[512,1024]{1,0:T(8,128)(2,1)S(1)} %get-tuple-element.79.mine_ref, bf16[512,1024]{1,0:T(8,128)(2,1)S(1)} %collective-permute-done.9.theirs_ref, ...), custom_call_target="tpu_custom_call" | custom-call | flops 1 | bytes 1 | tf_op jit(solution)/shard_map/project_1/pallas_call | solution.py:47
  103.0 1.3 collective-permute-start.19
  107.0 6.6 %collective-permute-done.20.refs_2_ = bf16[256,512]{1,0:T(8,128)(2,1)S(1)} collective-permute-done((bf16[256,512]{1,0:T(8,128)(2,1)S(1)}, bf16[256,512]{1,0:T(8,128)(2,1)S(1)}, u32[]{:S(2)}, u32[]{:S(2)}) %collective-permute-start.20) | collective-permute-done | bytes 262176 | tf_op jit(solution)/shard_map/ppermute | solution.py:629
  113.6 3.9 %attention_back_next.1.own_ref = f32[2,1024,256]{2,1,0:T(8,128)S(1)} custom-call(s32[4]{0:T(128)S(1)} %pad_add_fusion.meta_ref, f32[4,10,256]{2,1,0:T(8,128)S(1)} %get-tuple-element.104.bias_ref, f32[4,4,256]{2,1,0:T(4,128)S(1)} %collective-permute-done.14.stats_ref, f32[2,1024,128]{2,1,0:T(8,128)S(1)} %get-tuple-element.105.refs_0_, ...), custom_call_target="tpu_custom_call" | custom-call | flops 1 | bytes 1 | tf_op jit(solution)/shard_map/attention_back_next/pallas_call | solution.py:47
  117.5 4.4 %collective-permute-done.19.arrived_ref = bf16[1,256,512]{2,1,0:T(8,128)(2,1)S(1)} collective-permute-done((bf16[1,256,512]{2,1,0:T(8,128)(2,1)S(1)}, bf16[1,256,512]{2,1,0:T(8,128)(2,1)S(1)}, u32[]{:S(2)}, u32[]{:S(2)}) %collective-permute-start.19) | collective-permute-done | bytes 262176 | tf_op jit(solution)/shard_map/ppermute | solution.py:629
  124.7 1.7 %collective-permute-start.25 = (bf16[3,256,256]{2,1,0:T(8,128)(2,1)S(1)}, bf16[3,256,256]{2,1,0:T(8,128)(2,1)S(1)}, u32[]{:S(2)}, u32[]{:S(2)}) collective-permute-start(bf16[3,256,256]{2,1,0:T(8,128)(2,1)S(1)} %get-tuple-element.114), channel_id=1, source_target_pairs={{0,6},{2,4},{4,2},{6,0},{8,14},{10,12},{12,10},{14,8},{16,22},{18,... | collective-permute-start | bytes 1179656 | tf_op jit(solution)/shard_map/ppermute | solution.py:617
  126.5 9.2 %collective-permute-done.26.refs_3_ = bf16[256,512]{1,0:T(8,128)(2,1)S(1)} collective-permute-done((bf16[256,512]{1,0:T(8,128)(2,1)S(1)}, bf16[256,512]{1,0:T(8,128)(2,1)S(1)}, u32[]{:S(2)}, u32[]{:S(2)}) %collective-permute-start.26) | collective-permute-done | bytes 262176 | tf_op jit(solution)/shard_map/ppermute | solution.py:629
  137.4 1.8 %unpack.1 = (bf16[256,1024]{1,0:T(8,128)(2,1)}, bf16[256,1024]{1,0:T(8,128)(2,1)}, bf16[256,1024]{1,0:T(8,128)(2,1)}) custom-call(s32[4]{0:T(128)S(1)} %pad_add_fusion.meta_ref, bf16[3,256,256]{2,1,0:T(8,128)(2,1)S(1)} %get-tuple-element.111.refs_0_, bf16[3,256,256]{2,1,0:T(8,128)(2,1)S(1)} %collective-permute-done.23.refs_1_, ...), custom_call_target="tpu_custom_call" | custom-call | flops 1 | bytes 1 | tf_op jit(solution)/shard_map/unpack/pallas_call | solution.py:584
  (53 shorter events, 20.8 us)
Async XLA Ops:
  4.2 10.3 %collective-permute-start = (bf16[2,256,256]{2,1,0:T(8,128)(2,1)}, bf16[2,256,256]{2,1,0:T(8,128)(2,1)S(1)}, u32[]{:S(2)}, u32[]{:S(2)}) collective-permute-start(bf16[2,256,256]{2,1,0:T(8,128)(2,1)} %get-tuple-element.62), channel_id=1, source_target_pairs={{0,2},{2,0},{4,6},{6,4},{8,10},{10,8},{12,14},{14,12},{16,18},{18,... | collective-permute-start | bytes 786440 | tf_op jit(solution)/shard_map/ppermute | solution.py:617
  7.2 13.6 %collective-permute-start.1 = (bf16[2,256,256]{2,1,0:T(8,128)(2,1)}, bf16[2,256,256]{2,1,0:T(8,128)(2,1)S(1)}, u32[]{:S(2)}, u32[]{:S(2)}) collective-permute-start(bf16[2,256,256]{2,1,0:T(8,128)(2,1)} %get-tuple-element.63), channel_id=1, source_target_pairs={{0,4},{2,6},{4,0},{6,2},{8,12},{10,14},{12,8},{14,10},{16,20},{18,... | collective-permute-start | bytes 786440 | tf_op jit(solution)/shard_map/ppermute | solution.py:617
  8.7 20.8 %collective-permute-start.2 = (bf16[2,256,256]{2,1,0:T(8,128)(2,1)}, bf16[2,256,256]{2,1,0:T(8,128)(2,1)S(1)}, u32[]{:S(2)}, u32[]{:S(2)}) collective-permute-start(bf16[2,256,256]{2,1,0:T(8,128)(2,1)} %get-tuple-element.68), channel_id=1, source_target_pairs={{0,6},{2,4},{4,2},{6,0},{8,14},{10,12},{12,10},{14,8},{16,22},{18,... | collective-permute-start | bytes 786440 | tf_op jit(solution)/shard_map/ppermute | solution.py:617
  12.1 17.5 %copy-start.1 = (bf16[2,256,256]{2,1,0:T(8,128)(2,1)S(1)}, bf16[2,256,256]{2,1,0:T(8,128)(2,1)}, u32[]{:S(2)}) copy-start(bf16[2,256,256]{2,1,0:T(8,128)(2,1)} %get-tuple-element.67.refs_0_) | copy-start | bytes 786436
  12.1 43.6 %copy-start.2 = (s32[32,10]{0,1:T(8,128)S(1)}, s32[32,10]{0,1:T(8,128)}, u32[]{:S(2)}) copy-start(s32[32,10]{0,1:T(8,128)} %param.11) | copy-start | bytes 3844
  30.9 27.6 %collective-permute-start.3 = (bf16[2,1024,256]{2,1,0:T(8,128)(2,1)S(1)}, bf16[2,1024,256]{2,1,0:T(8,128)(2,1)S(1)}, u32[]{:S(2)}, u32[]{:S(2)}) collective-permute-start(bf16[2,1024,256]{2,1,0:T(8,128)(2,1)S(1)} %get-tuple-element.72.refs_1_.refs_3_), channel_id=1, source_target_pairs={{0,8},{2,10},{4,12},{6,14},{8,16},{10,18},{12,20},{14,22},{16,24},... | collective-permute-start | bytes 3145736 | tf_op jit(solution)/shard_map/ppermute | solution.py:625
  34.4 24.0 %collective-permute-start.6 = (bf16[1024,256]{1,0:T(8,128)(2,1)}, bf16[1024,256]{1,0:T(8,128)(2,1)S(1)}, u32[]{:S(2)}, u32[]{:S(2)}) collective-permute-start(bf16[1024,256]{1,0:T(8,128)(2,1)} %get-tuple-element.74), channel_id=1, source_target_pairs={{0,2},{2,0},{4,6},{6,4},{8,10},{10,8},{12,14},{14,12},{16,18},{18,... | collective-permute-start | bytes 1572872 | tf_op jit(solution)/shard_map/ppermute | solution.py:617
  34.5 23.9 %collective-permute-start.7 = (bf16[1024,256]{1,0:T(8,128)(2,1)}, bf16[1024,256]{1,0:T(8,128)(2,1)S(1)}, u32[]{:S(2)}, u32[]{:S(2)}) collective-permute-start(bf16[1024,256]{1,0:T(8,128)(2,1)} %get-tuple-element.75), channel_id=1, source_target_pairs={{0,4},{2,6},{4,0},{6,2},{8,12},{10,14},{12,8},{14,10},{16,20},{18,... | collective-permute-start | bytes 1572872 | tf_op jit(solution)/shard_map/ppermute | solution.py:617
  36.6 21.9 %collective-permute-start.8 = (bf16[1024,256]{1,0:T(8,128)(2,1)}, bf16[1024,256]{1,0:T(8,128)(2,1)}, u32[]{:S(2)}, u32[]{:S(2)}) collective-permute-start(bf16[1024,256]{1,0:T(8,128)(2,1)} %get-tuple-element.76), channel_id=1, source_target_pairs={{0,6},{2,4},{4,2},{6,0},{8,14},{10,12},{12,10},{14,8},{16,22},{18,... | collective-permute-start | bytes 1572872 | tf_op jit(solution)/shard_map/ppermute | solution.py:617
  38.0 16.3 %collective-permute-start.4 = (bf16[2,128,256]{2,1,0:T(8,128)(2,1)}, bf16[2,128,256]{2,1,0:T(8,128)(2,1)S(1)}, u32[]{:S(2)}, u32[]{:S(2)}) collective-permute-start(bf16[2,128,256]{2,1,0:T(8,128)(2,1)} %get-tuple-element.69), channel_id=1, source_target_pairs={{0,16},{2,18},{4,20},{6,22},{1,17},{3,19},{5,21},{7,23}} | collective-permute-start | bytes 393224 | tf_op jit(solution)/shard_map/ppermute | solution.py:662
  54.3 4.1 %collective-permute-start.5 = (bf16[2,128,256]{2,1,0:T(8,128)(2,1)}, bf16[2,128,256]{2,1,0:T(8,128)(2,1)S(1)}, u32[]{:S(2)}, u32[]{:S(2)}) collective-permute-start(bf16[2,128,256]{2,1,0:T(8,128)(2,1)} %get-tuple-element.69), channel_id=1, source_target_pairs={{0,24},{2,26},{4,28},{6,30},{1,25},{3,27},{5,29},{7,31}} | collective-permute-start | bytes 393224 | tf_op jit(solution)/shard_map/ppermute | solution.py:662
  58.5 1.0 copy-start
  60.8 9.9 %collective-permute-start.9 = (bf16[512,1024]{1,0:T(8,128)(2,1)S(1)}, bf16[512,1024]{1,0:T(8,128)(2,1)S(1)}, u32[]{:S(2)}, u32[]{:S(2)}) collective-permute-start(bf16[512,1024]{1,0:T(8,128)(2,1)S(1)} %get-tuple-element.79.mine_ref), channel_id=1, source_target_pairs={{0,1},{1,0},{2,3},{3,2},{4,5},{5,4},{6,7},{7,6},{8,9},{9,8},{10,11... | collective-permute-start | bytes 3145736 | tf_op jit(solution)/shard_map/ppermute | solution.py:667
  60.8 30.2 %collective-permute-start.13 = (bf16[2,1024,256]{2,1,0:T(8,128)(2,1)S(1)}, bf16[2,1024,256]{2,1,0:T(8,128)(2,1)S(1)}, u32[]{:S(2)}, u32[]{:S(2)}) collective-permute-start(bf16[2,1024,256]{2,1,0:T(8,128)(2,1)S(1)} %get-tuple-element.77.refs_0_), channel_id=1, source_target_pairs={{8,0},{10,2},{12,4},{14,6},{16,8},{18,10},{20,12},{22,14},{24,16},... | collective-permute-start | bytes 3145736 | tf_op jit(solution)/shard_map/ppermute | solution.py:625
  66.7 13.1 %collective-permute-start.10 = (bf16[1024,128]{1,0:T(8,128)(2,1)S(1)}, bf16[1024,128]{1,0:T(8,128)(2,1)S(1)}, u32[]{:S(2)}, u32[]{:S(2)}) collective-permute-start(bf16[1024,128]{1,0:T(8,128)(2,1)S(1)} %get-tuple-element.78.refs_0_), channel_id=1, source_target_pairs={{0,2},{2,0},{4,6},{6,4},{8,10},{10,8},{12,14},{14,12},{16,18},{18,... | collective-permute-start | bytes 786440 | tf_op jit(solution)/shard_map/ppermute | solution.py:617
  67.3 13.8 %collective-permute-start.11 = (bf16[1024,128]{1,0:T(8,128)(2,1)S(1)}, bf16[1024,128]{1,0:T(8,128)(2,1)S(1)}, u32[]{:S(2)}, u32[]{:S(2)}) collective-permute-start(bf16[1024,128]{1,0:T(8,128)(2,1)S(1)} %get-tuple-element.78.refs_0_), channel_id=1, source_target_pairs={{0,4},{2,6},{4,0},{6,2},{8,12},{10,14},{12,8},{14,10},{16,20},{18,... | collective-permute-start | bytes 786440 | tf_op jit(solution)/shard_map/ppermute | solution.py:617
  69.3 13.7 %collective-permute-start.12 = (bf16[1024,128]{1,0:T(8,128)(2,1)S(1)}, bf16[1024,128]{1,0:T(8,128)(2,1)S(1)}, u32[]{:S(2)}, u32[]{:S(2)}) collective-permute-start(bf16[1024,128]{1,0:T(8,128)(2,1)S(1)} %get-tuple-element.78.refs_0_), channel_id=1, source_target_pairs={{0,6},{2,4},{4,2},{6,0},{8,14},{10,12},{12,10},{14,8},{16,22},{18,... | collective-permute-start | bytes 786440 | tf_op jit(solution)/shard_map/ppermute | solution.py:617
  85.1 11.8 %collective-permute-start.15 = (bf16[1,256,512]{2,1,0:T(8,128)(2,1)S(1)}, bf16[1,256,512]{2,1,0:T(8,128)(2,1)S(1)}, u32[]{:S(2)}, u32[]{:S(2)}) collective-permute-start(bf16[1,256,512]{2,1,0:T(8,128)(2,1)S(1)} %get-tuple-element.95), channel_id=1, source_target_pairs={{0,8},{2,10},{4,12},{6,14},{8,0},{10,2},{12,4},{14,6},{16,24},{18,... | collective-permute-start | bytes 786440 | tf_op jit(solution)/shard_map/ppermute | solution.py:629
  87.6 12.5 %collective-permute-start.16 = (bf16[1024,128]{1,0:T(8,128)(2,1)S(1)}, bf16[1024,128]{1,0:T(8,128)(2,1)S(1)}, u32[]{:S(2)}, u32[]{:S(2)}) collective-permute-start(bf16[1024,128]{1,0:T(8,128)(2,1)S(1)} %get-tuple-element.98.refs_0_), channel_id=1, source_target_pairs={{0,2},{2,0},{4,6},{6,4},{8,10},{10,8},{12,14},{14,12},{16,18},{18,... | collective-permute-start | bytes 786440 | tf_op jit(solution)/shard_map/ppermute | solution.py:617
  88.1 12.7 %collective-permute-start.17 = (bf16[1024,128]{1,0:T(8,128)(2,1)S(1)}, bf16[1024,128]{1,0:T(8,128)(2,1)S(1)}, u32[]{:S(2)}, u32[]{:S(2)}) collective-permute-start(bf16[1024,128]{1,0:T(8,128)(2,1)S(1)} %get-tuple-element.98.refs_0_), channel_id=1, source_target_pairs={{0,4},{2,6},{4,0},{6,2},{8,12},{10,14},{12,8},{14,10},{16,20},{18,... | collective-permute-start | bytes 786440 | tf_op jit(solution)/shard_map/ppermute | solution.py:617
  89.9 11.0 %collective-permute-start.18 = (bf16[1024,128]{1,0:T(8,128)(2,1)S(1)}, bf16[1024,128]{1,0:T(8,128)(2,1)S(1)}, u32[]{:S(2)}, u32[]{:S(2)}) collective-permute-start(bf16[1024,128]{1,0:T(8,128)(2,1)S(1)} %get-tuple-element.98.refs_0_), channel_id=1, source_target_pairs={{0,6},{2,4},{4,2},{6,0},{8,14},{10,12},{12,10},{14,8},{16,22},{18,... | collective-permute-start | bytes 786440 | tf_op jit(solution)/shard_map/ppermute | solution.py:617
  91.1 5.8 %collective-permute-start.14 = (f32[4,4,256]{2,1,0:T(4,128)S(1)}, f32[4,4,256]{2,1,0:T(4,128)S(1)}, u32[]{:S(2)}, u32[]{:S(2)}) collective-permute-start(f32[4,4,256]{2,1,0:T(4,128)S(1)} %get-tuple-element.92.stats_ref), channel_id=1, source_target_pairs={{8,0},{10,2},{12,4},{14,6},{16,8},{18,10},{20,12},{22,14},{24,16},... | collective-permute-start | bytes 49160 | tf_op jit(solution)/shard_map/ppermute | solution.py:625
  97.0 16.6 %collective-permute-start.20 = (bf16[256,512]{1,0:T(8,128)(2,1)S(1)}, bf16[256,512]{1,0:T(8,128)(2,1)S(1)}, u32[]{:S(2)}, u32[]{:S(2)}) collective-permute-start(bf16[256,512]{1,0:T(8,128)(2,1)S(1)} %halve_0.1), channel_id=1, source_target_pairs={{0,16},{2,18},{4,20},{6,22},{8,24},{10,26},{12,28},{14,30},{16,0},... | collective-permute-start | bytes 786440 | tf_op jit(solution)/shard_map/ppermute | solution.py:629
  103.0 18.9 %collective-permute-start.19 = (bf16[1,256,512]{2,1,0:T(8,128)(2,1)S(1)}, bf16[1,256,512]{2,1,0:T(8,128)(2,1)S(1)}, u32[]{:S(2)}, u32[]{:S(2)}) collective-permute-start(bf16[1,256,512]{2,1,0:T(8,128)(2,1)S(1)} %get-tuple-element.100), channel_id=1, source_target_pairs={{0,8},{2,10},{4,12},{6,14},{8,0},{10,2},{12,4},{14,6},{16,24},{18,... | collective-permute-start | bytes 786440 | tf_op jit(solution)/shard_map/ppermute | solution.py:629
  104.3 17.6 %collective-permute-start.21 = (bf16[2,128,256]{2,1,0:T(8,128)(2,1)S(1)}, bf16[2,128,256]{2,1,0:T(8,128)(2,1)S(1)}, u32[]{:S(2)}, u32[]{:S(2)}) collective-permute-start(bf16[2,128,256]{2,1,0:T(8,128)(2,1)S(1)} %get-tuple-element.109), channel_id=1, source_target_pairs={{16,0},{18,2},{20,4},{22,6},{17,1},{19,3},{21,5},{23,7}} | collective-permute-start | bytes 393224 | tf_op jit(solution)/shard_map/ppermute | solution.py:704
  105.6 16.4 %collective-permute-start.22 = (bf16[2,128,256]{2,1,0:T(8,128)(2,1)S(1)}, bf16[2,128,256]{2,1,0:T(8,128)(2,1)S(1)}, u32[]{:S(2)}, u32[]{:S(2)}) collective-permute-start(bf16[2,128,256]{2,1,0:T(8,128)(2,1)S(1)} %get-tuple-element.110), channel_id=1, source_target_pairs={{24,0},{26,2},{28,4},{30,6},{25,1},{27,3},{29,5},{31,7}} | collective-permute-start | bytes 393224 | tf_op jit(solution)/shard_map/ppermute | solution.py:704
  106.9 29.1 %collective-permute-start.27 = (bf16[2,256,512]{2,1,0:T(8,128)(2,1)S(1)}, bf16[2,256,512]{2,1,0:T(8,128)(2,1)S(1)}, u32[]{:S(2)}, u32[]{:S(2)}) collective-permute-start(bf16[2,256,512]{2,1,0:T(8,128)(2,1)S(1)} %get-tuple-element.101), channel_id=1, source_target_pairs={{0,8},{2,10},{4,12},{6,14},{8,0},{10,2},{12,4},{14,6},{16,24},{18,... | collective-permute-start | bytes 1572872 | tf_op jit(solution)/shard_map/ppermute | solution.py:629
  122.9 14.3 %collective-permute-start.23 = (bf16[3,256,256]{2,1,0:T(8,128)(2,1)S(1)}, bf16[3,256,256]{2,1,0:T(8,128)(2,1)S(1)}, u32[]{:S(2)}, u32[]{:S(2)}) collective-permute-start(bf16[3,256,256]{2,1,0:T(8,128)(2,1)S(1)} %get-tuple-element.112), channel_id=1, source_target_pairs={{0,2},{2,0},{4,6},{6,4},{8,10},{10,8},{12,14},{14,12},{16,18},{18,... | collective-permute-start | bytes 1179656 | tf_op jit(solution)/shard_map/ppermute | solution.py:617
  123.8 13.5 %collective-permute-start.24 = (bf16[3,256,256]{2,1,0:T(8,128)(2,1)S(1)}, bf16[3,256,256]{2,1,0:T(8,128)(2,1)S(1)}, u32[]{:S(2)}, u32[]{:S(2)}) collective-permute-start(bf16[3,256,256]{2,1,0:T(8,128)(2,1)S(1)} %get-tuple-element.113), channel_id=1, source_target_pairs={{0,4},{2,6},{4,0},{6,2},{8,12},{10,14},{12,8},{14,10},{16,20},{18,... | collective-permute-start | bytes 1179656 | tf_op jit(solution)/shard_map/ppermute | solution.py:617
  124.7 12.6 %collective-permute-start.25 = (bf16[3,256,256]{2,1,0:T(8,128)(2,1)S(1)}, bf16[3,256,256]{2,1,0:T(8,128)(2,1)S(1)}, u32[]{:S(2)}, u32[]{:S(2)}) collective-permute-start(bf16[3,256,256]{2,1,0:T(8,128)(2,1)S(1)} %get-tuple-element.114), channel_id=1, source_target_pairs={{0,6},{2,4},{4,2},{6,0},{8,14},{10,12},{12,10},{14,8},{16,22},{18,... | collective-permute-start | bytes 1179656 | tf_op jit(solution)/shard_map/ppermute | solution.py:617
  126.5 9.2 %collective-permute-start.26 = (bf16[256,512]{1,0:T(8,128)(2,1)S(1)}, bf16[256,512]{1,0:T(8,128)(2,1)S(1)}, u32[]{:S(2)}, u32[]{:S(2)}) collective-permute-start(bf16[256,512]{1,0:T(8,128)(2,1)S(1)} %halve_1.1), channel_id=1, source_target_pairs={{0,16},{2,18},{4,20},{6,22},{8,24},{10,26},{12,28},{14,30},{16,0},... | collective-permute-start | bytes 786440 | tf_op jit(solution)/shard_map/ppermute | solution.py:629

commit v7 on v6

--- a/solution.py
+++ b/solution.py
@@ -645,21 +645,25 @@
         while True:
             first, *more = halve(head, evens, odds)
             token = after(token, first)
+            done = first
             arrivals.append(swap_groups(first, bit))
             if not more:
-                return arrivals, token
+                return arrivals, token, done
             odds, evens = swap_groups(more[0], bit), more[1]
             bit *= 2
 
     kv = pack_kv(keys, values, place, group, width)
     own_kv = exchange(kv)
-    early = after(place, own_kv[1], own_kv[2])
+    early = after(place, own_kv[1])
     qd_cut = grads_packed(queries, out_grad, proj_weight, early, group, parts)
     pool, strided = assemble_kv(own_kv, after(meta, qd_cut[0]), group)
     prev = shifted(pool, 1)
     qd_pieces = exchange(qd_cut)
+    later = after(strided, qd_pieces[1])
     far = [
-        lax.ppermute(strided, "seq", summary_route(distance, False))
+        lax.ppermute(
+            strided if distance == 2 else later, "seq", summary_route(distance, False)
+        )
         for distance in range(2, parts)
     ]
     bias, bias_next = masks_of(layout, after(meta, strided), parts, slots)
@@ -675,42 +679,39 @@
         attn.append([got] + [swap(got, k) for k in range(1, group)])
         order = after(meta, got, theirs)
 
-    dq, grads, keep, finals, firsts = [], [], [], [], []
+    dq, grads, keep, finals = [], [], [], []
     far_grads = [jnp.zeros((2, BLK, width), jnp.bfloat16) for _ in far]
-    order = after(meta, stats, theirs)
+    order, first = after(meta, stats, theirs), []
     for h in range(heads):
-        got = backward(
-            h, qd, pool, prev, far, far_grads, bias, stats, order, group, slots
-        )
+        got = backward(h, qd, pool, prev, far, far_grads, bias, stats, order, group, slots)
         dq.append(got[0])
         grads.append(got[1])
         far_grads = got[2]
-        order = after(order, got[0])
+        order = after(meta, got[0])
         if h > 0:
             order = after(order, next_stats)
-            sums, order = add_up(h - 1, odds, evens, got[0], order)
+        kept, first, odds, evens = project(h, mine, theirs, attn[h], first, order, group, parts)
+        keep.append(kept)
+        first, odds = [first], swap_groups(odds, 1)
+        order = after(meta, *first)
+        if h == 0:
+            next_stats = shifted(after(stats, next_qd, *first), -1)
+        if h < heads - 1:
+            sums, order, _ = add_up(h, odds, evens, first, order)
             finals.append(sums)
-        kept, first, odds, evens = project(
-            h, mine, theirs, attn[h], firsts, order, group, parts
-        )
-        keep.append(kept)
-        firsts = [first]
-        odds = swap_groups(odds, 1)
-        order = after(meta, first)
-        if h == 0:
-            next_stats = shifted(after(stats, next_qd, first), -1)
-    neighbour = swap_groups(first, 1)
     far_back = [
         lax.ppermute(piece, "seq", summary_route(index + 2, True))
         for index, piece in enumerate(far_grads)
     ]
     order = after(order, finals[0])
     own_grad = backward_next(grads, next_qd, pool, bias_next, next_stats, order)
-    sums, order = add_up(heads - 1, odds, evens, (own_grad, finals[0]), meta)
+    final_cut = combine(dq, own_grad, far_back, meta, group, rows)
+    final = exchange(final_cut)
+    sums, _, _ = add_up(heads - 1, odds, evens, final_cut, meta)
     finals.append(sums)
-    final = exchange(combine(dq, own_grad, far_back, order, group, rows))
+    neighbour = swap_groups(after(first[0], final_cut[0]), 1)
+    proj_grad = finish(keep, neighbour, finals, group)
     query_grad, key_grad, value_grad = unpack(final, meta, group)
-    proj_grad = finish(keep, neighbour, finals, group)
     return (query_grad, key_grad, value_grad, proj_grad)
 
 

time: 140 us -> 138 us (0.986)
  waiting for transfers between devices: 46.2 us -> 39.1 us
  starting transfers between devices: 40.6 us -> 45.9 us
    ppermute x5, waiting for transfers between devices: 20.6 us -> 3.8 us  [swap_groups(): return lax.ppermute(piece, 'seq', route)]
    ppermute x15, waiting for transfers between devices: 12.9 us -> 23 us  [swap(): return lax.ppermute(piece, 'seq', route)]
    ppermute x2, waiting for transfers between devices: 12.7 us -> 5.68 us  [local(): lax.ppermute(strided if distance == 2 else later, 'seq', summary_route(di...]
    ppermute x3, waiting for transfers between devices: 0.01 us -> 5.03 us  [shifted(): return lax.ppermute(piece, 'seq', route)]
    ppermute x5, starting transfers between devices: 6.95 us -> 10.3 us  [swap_groups(): return lax.ppermute(piece, 'seq', route)]
    ppermute x2, starting transfers between devices: 5.71 us -> 7.67 us  [local(): lax.ppermute(strided if distance == 2 else later, 'seq', summary_route(di...]
    ppermute x2, waiting for transfers between devices: 0.01 us -> 1.6 us  [local(): lax.ppermute(piece, 'seq', summary_route(index + 2, True))]
  transfers between devices with their start and end apart: 28 -> 28, of which waited for: 12 -> 11; matrix products, arithmetic and copies ran while one was open for 1% -> 1% of each run, Pallas kernels for 28% -> 29%
where the time goes in v7:
time: 138 us; the launch traced here: 137 us
  Pallas kernels  46.4 us (34%)
  starting transfers between devices  45.9 us (33%)
  waiting for transfers between devices  39.1 us (28%)
  between operations  2.93 us (2%)
  local copies, waits for them, and re-layouts  2.41 us (2%)
    pallas_call x13, Pallas kernels, call(): pl.pallas_call(body, out_shape=outs, in_specs=[SMEM] * len(scalars) + [VM...  31.6 us
    ppermute x15, waiting for transfers between devices, swap(): return lax.ppermute(piece, 'seq', route)  23 us
    ppermute x15, starting transfers between devices, swap(): return lax.ppermute(piece, 'seq', route)  18.6 us
    ppermute x5, starting transfers between devices, swap_groups(): return lax.ppermute(piece, 'seq', route)  10.3 us
    pallas_call x1, Pallas kernels, grads_packed(): pl.pallas_call(body, out_shape=[shape((2 * rows + half * each, rows))] *...  8.73 us
    ppermute x2, starting transfers between devices, local(): lax.ppermute(strided if distance == 2 else later, 'seq', summary_route(di...  7.67 us
    ppermute x3, starting transfers between devices, shifted(): return lax.ppermute(piece, 'seq', route)  6.69 us
    ppermute x2, waiting for transfers between devices, local(): lax.ppermute(strided if distance == 2 else later, 'seq', summary_route(di...  5.68 us
  transfers between devices with their start and end apart: 28, of which 11 were waited for; matrix products, arithmetic and copies ran while one was open for 1% of the time, Pallas kernels for 29%

profile of v7, /device:TPU:0, one launch (start us, length us, event | category | flops | bytes accessed | tf_op | source)
XLA Modules:
  0.0 137.5 jit_solution(10279623189235705355)
XLA Ops:
  1.3 3.0 %pack_kv.1 = (bf16[2,256,256]{2,1,0:T(8,128)(2,1)}, bf16[2,256,256]{2,1,0:T(8,128)(2,1)}, bf16[2,256,256]{2,1,0:T(8,128)(2,1)}, bf16[2,256,256]{2,1,0:T(8,128)(2,1)}) custom-call(s32[3]{0:T(128)} %pad_add_fusion.1.meta_ref, bf16[256,1024]{1,0:T(8,128)(2,1)} %k_ref.1, bf16[256,1024]{1,0:T(8,128)(2,1)} %v_ref.1), custom_call_target="tpu_custom_call" | custom-call | flops 1 | bytes 1 | tf_op jit(solution)/shard_map/pack_kv/pallas_call | solution.py:93
  4.3 3.0 %collective-permute-start = (bf16[2,256,256]{2,1,0:T(8,128)(2,1)}, bf16[2,256,256]{2,1,0:T(8,128)(2,1)S(1)}, u32[]{:S(2)}, u32[]{:S(2)}) collective-permute-start(bf16[2,256,256]{2,1,0:T(8,128)(2,1)} %get-tuple-element.63), channel_id=1, source_target_pairs={{0,2},{2,0},{4,6},{6,4},{8,10},{10,8},{12,14},{14,12},{16,18},{18,... | collective-permute-start | bytes 786440 | tf_op jit(solution)/shard_map/ppermute | solution.py:617
  12.1 2.5 %collective-permute-done.refs_1_ = bf16[2,256,256]{2,1,0:T(8,128)(2,1)S(1)} collective-permute-done((bf16[2,256,256]{2,1,0:T(8,128)(2,1)}, bf16[2,256,256]{2,1,0:T(8,128)(2,1)S(1)}, u32[]{:S(2)}, u32[]{:S(2)}) %collective-permute-start) | collective-permute-done | bytes 262176 | tf_op jit(solution)/shard_map/ppermute | solution.py:617
  14.6 8.7 %attn_grad.1 = (bf16[1024,256]{1,0:T(8,128)(2,1)}, bf16[1024,256]{1,0:T(8,128)(2,1)}, bf16[1024,256]{1,0:T(8,128)(2,1)}, bf16[1024,256]{1,0:T(8,128)(2,1)}) custom-call(s32[3]{0:T(128)} %pad_add_fusion.1.meta_ref, bf16[256,1024]{1,0:T(8,128)(2,1)} %q_ref.1, bf16[256,4096]{1,0:T(8,128)(2,1)} %og_ref.1, bf16[4096,1024]{1,0:T(8,128)(2,1)} %w_ref.1), custom_call_target="tpu_custom_call" | custom-call | flops 1 | bytes 1 | tf_op jit(solution)/shard_map/attn_grad/pallas_call | solution.py:152
  24.7 4.1 %collective-permute-start.3 = (bf16[2,1024,256]{2,1,0:T(8,128)(2,1)S(1)}, bf16[2,1024,256]{2,1,0:T(8,128)(2,1)S(1)}, u32[]{:S(2)}, u32[]{:S(2)}) collective-permute-start(bf16[2,1024,256]{2,1,0:T(8,128)(2,1)S(1)} %get-tuple-element.73.refs_1_.refs_3_), channel_id=1, source_target_pairs={{0,8},{2,10},{4,12},{6,14},{8,16},{10,18},{12,20},{14,22},{16,24},... | collective-permute-start | bytes 3145736 | tf_op jit(solution)/shard_map/ppermute | solution.py:625
  28.8 1.6 %collective-permute-start.5 = (bf16[1024,256]{1,0:T(8,128)(2,1)}, bf16[1024,256]{1,0:T(8,128)(2,1)S(1)}, u32[]{:S(2)}, u32[]{:S(2)}) collective-permute-start(bf16[1024,256]{1,0:T(8,128)(2,1)} %get-tuple-element.74), channel_id=1, source_target_pairs={{0,2},{2,0},{4,6},{6,4},{8,10},{10,8},{12,14},{14,12},{16,18},{18,... | collective-permute-start | bytes 1572872 | tf_op jit(solution)/shard_map/ppermute | solution.py:617
  32.4 4.4 %collective-permute-start.4 = (bf16[2,128,256]{2,1,0:T(8,128)(2,1)}, bf16[2,128,256]{2,1,0:T(8,128)(2,1)S(1)}, u32[]{:S(2)}, u32[]{:S(2)}) collective-permute-start(bf16[2,128,256]{2,1,0:T(8,128)(2,1)} %get-tuple-element.75), channel_id=1, source_target_pairs={{0,16},{2,18},{4,20},{6,22},{1,17},{3,19},{5,21},{7,23}} | collective-permute-start | bytes 393224 | tf_op jit(solution)/shard_map/ppermute | solution.py:664
  36.8 7.2 %collective-permute-done.5.refs_1_ = bf16[1024,256]{1,0:T(8,128)(2,1)S(1)} collective-permute-done((bf16[1024,256]{1,0:T(8,128)(2,1)}, bf16[1024,256]{1,0:T(8,128)(2,1)S(1)}, u32[]{:S(2)}, u32[]{:S(2)}) %collective-permute-start.5) | collective-permute-done | bytes 524320 | tf_op jit(solution)/shard_map/ppermute | solution.py:617
  44.0 3.2 %collective-permute-start.6 = (bf16[2,128,256]{2,1,0:T(8,128)(2,1)}, bf16[2,128,256]{2,1,0:T(8,128)(2,1)S(1)}, u32[]{:S(2)}, u32[]{:S(2)}) collective-permute-start(bf16[2,128,256]{2,1,0:T(8,128)(2,1)} %get-tuple-element.75), channel_id=1, source_target_pairs={{0,24},{2,26},{4,28},{6,30},{1,25},{3,27},{5,29},{7,31}} | collective-permute-start | bytes 393224 | tf_op jit(solution)/shard_map/ppermute | solution.py:664
  47.3 1.9 %masks.1 = (f32[4,11,256]{2,1,0:T(8,128)S(1)}, f32[4,10,256]{2,1,0:T(8,128)S(1)}) custom-call(s32[4]{0:T(128)S(1)} %pad_add_fusion.meta_ref, s32[32,10]{1,0:T(8,128)S(1)} %copy.10.table), custom_call_target="tpu_custom_call" | custom-call | flops 1 | bytes 1 | tf_op jit(solution)/shard_map/masks/pallas_call | solution.py:47
  49.2 4.3 %collective-permute-done.4.refs_3_ = bf16[2,128,256]{2,1,0:T(8,128)(2,1)S(1)} collective-permute-done((bf16[2,128,256]{2,1,0:T(8,128)(2,1)}, bf16[2,128,256]{2,1,0:T(8,128)(2,1)S(1)}, u32[]{:S(2)}, u32[]{:S(2)}) %collective-permute-start.4) | collective-permute-done | bytes 131104 | tf_op jit(solution)/shard_map/ppermute | solution.py:664
  58.6 4.5 %attention_0.1 = (bf16[1024,128]{1,0:T(8,128)(2,1)S(1)}, f32[4,4,256]{2,1,0:T(4,128)S(1)}) custom-call(s32[4]{0:T(128)S(1)} %pad_add_fusion.meta_ref, f32[4,11,256]{2,1,0:T(8,128)S(1)} %get-tuple-element.72.bias_ref, f32[4,4,256]{2,1,0:T(4,128)S(1)} %broadcast_in_dim.3.before_ref, bf16[2,1024,256]{2,1,0:T(8,128)(2,1)S(1)} %get-tuple-element.79.refs_0_, ...), custom_call_target="tpu_custom_call" | custom-call | flops 1 | bytes 1 | tf_op jit(solution)/shard_map/attention_0/pallas_call | solution.py:47
  63.1 1.6 %collective-permute-start.10 = (bf16[1024,128]{1,0:T(8,128)(2,1)S(1)}, bf16[1024,128]{1,0:T(8,128)(2,1)S(1)}, u32[]{:S(2)}, u32[]{:S(2)}) collective-permute-start(bf16[1024,128]{1,0:T(8,128)(2,1)S(1)} %get-tuple-element.80.refs_0_), channel_id=1, source_target_pairs={{0,2},{2,0},{4,6},{6,4},{8,10},{10,8},{12,14},{14,12},{16,18},{18,... | collective-permute-start | bytes 786440 | tf_op jit(solution)/shard_map/ppermute | solution.py:617
  64.7 1.5 %collective-permute-start.11 = (bf16[1024,128]{1,0:T(8,128)(2,1)S(1)}, bf16[1024,128]{1,0:T(8,128)(2,1)S(1)}, u32[]{:S(2)}, u32[]{:S(2)}) collective-permute-start(bf16[1024,128]{1,0:T(8,128)(2,1)S(1)} %get-tuple-element.80.refs_0_), channel_id=1, source_target_pairs={{0,4},{2,6},{4,0},{6,2},{8,12},{10,14},{12,8},{14,10},{16,20},{18,... | collective-permute-start | bytes 786440 | tf_op jit(solution)/shard_map/ppermute | solution.py:617
  66.7 4.7 %attention_1.1 = (bf16[1024,128]{1,0:T(8,128)(2,1)S(1)}, f32[4,4,256]{2,1,0:T(4,128)S(1)}) custom-call(s32[4]{0:T(128)S(1)} %pad_add_fusion.meta_ref, f32[4,11,256]{2,1,0:T(8,128)S(1)} %get-tuple-element.72.bias_ref, f32[4,4,256]{2,1,0:T(4,128)S(1)} %get-tuple-element.83.before_ref, bf16[2,1024,256]{2,1,0:T(8,128)(2,1)S(1)} %get-tuple-element.79.refs_0_, ...), custom_call_target="tpu_custom_call" | custom-call | flops 1 | bytes 1 | tf_op jit(solution)/shard_map/attention_1/pallas_call | solution.py:47
  71.4 4.3 %attention_back_0.1 = (bf16[1024,128]{1,0:T(8,128)(2,1)S(1)}, f32[2,1024,128]{2,1,0:T(8,128)S(1)}, bf16[2,128,256]{2,1,0:T(8,128)(2,1)S(1)}, bf16[2,128,256]{2,1,0:T(8,128)(2,1)S(1)}) custom-call(s32[4]{0:T(128)S(1)} %pad_add_fusion.meta_ref, f32[4,11,256]{2,1,0:T(8,128)S(1)} %get-tuple-element.72.bias_ref, f32[4,4,256]{2,1,0:T(4,128)S(1)} %get-tuple-element.98.stats_ref, ...), custom_call_target="tpu_custom_call" | custom-call | flops 1 | bytes 1 | tf_op jit(solution)/shard_map/attention_back_0/pallas_call | solution.py:47
  75.7 3.0 %collective-permute-done.11.refs_2_ = bf16[1024,128]{1,0:T(8,128)(2,1)S(1)} collective-permute-done((bf16[1024,128]{1,0:T(8,128)(2,1)S(1)}, bf16[1024,128]{1,0:T(8,128)(2,1)S(1)}, u32[]{:S(2)}, u32[]{:S(2)}) %collective-permute-start.11) | collective-permute-done | bytes 262176 | tf_op jit(solution)/shard_map/ppermute | solution.py:617
  78.7 2.2 %project_0.1 = (f32[256,512]{1,0:T(8,128)S(1)}, bf16[1,256,512]{2,1,0:T(8,128)(2,1)S(1)}, bf16[1,256,512]{2,1,0:T(8,128)(2,1)S(1)}, f32[1,256,512]{2,1,0:T(8,128)S(1)}) custom-call(s32[4]{0:T(128)S(1)} %pad_add_fusion.meta_ref, bf16[512,1024]{1,0:T(8,128)(2,1)S(1)} %get-tuple-element.81.mine_ref, bf16[512,1024]{1,0:T(8,128)(2,1)S(1)} %collective-permute-done.9.theirs_ref, ...), custom_call_target="tpu_custom_call" | custom-call | flops 1 | bytes 1 | tf_op jit(solution)/shard_map/project_0/pallas_call | solution.py:47
  80.9 2.4 %collective-permute-start.13 = (bf16[1,256,512]{2,1,0:T(8,128)(2,1)S(1)}, bf16[1,256,512]{2,1,0:T(8,128)(2,1)S(1)}, u32[]{:S(2)}, u32[]{:S(2)}) collective-permute-start(bf16[1,256,512]{2,1,0:T(8,128)(2,1)S(1)} %get-tuple-element.91), channel_id=1, source_target_pairs={{0,8},{2,10},{4,12},{6,14},{8,0},{10,2},{12,4},{14,6},{16,24},{18,... | collective-permute-start | bytes 786440 | tf_op jit(solution)/shard_map/ppermute | solution.py:629
  86.8 3.5 %collective-permute-done.13.arrived_ref = bf16[1,256,512]{2,1,0:T(8,128)(2,1)S(1)} collective-permute-done((bf16[1,256,512]{2,1,0:T(8,128)(2,1)S(1)}, bf16[1,256,512]{2,1,0:T(8,128)(2,1)S(1)}, u32[]{:S(2)}, u32[]{:S(2)}) %collective-permute-start.13) | collective-permute-done | bytes 262176 | tf_op jit(solution)/shard_map/ppermute | solution.py:629
  90.4 3.4 %collective-permute-start.19 = (bf16[256,512]{1,0:T(8,128)(2,1)S(1)}, bf16[256,512]{1,0:T(8,128)(2,1)S(1)}, u32[]{:S(2)}, u32[]{:S(2)}) collective-permute-start(bf16[256,512]{1,0:T(8,128)(2,1)S(1)} %halve_0.1), channel_id=1, source_target_pairs={{0,16},{2,18},{4,20},{6,22},{8,24},{10,26},{12,28},{14,30},{16,0},... | collective-permute-start | bytes 786440 | tf_op jit(solution)/shard_map/ppermute | solution.py:629
  95.1 4.5 %attention_back_1.1 = (bf16[1024,128]{1,0:T(8,128)(2,1)S(1)}, f32[2,1024,128]{2,1,0:T(8,128)S(1)}, bf16[2,128,256]{2,1,0:T(8,128)(2,1)S(1)}, bf16[2,128,256]{2,1,0:T(8,128)(2,1)S(1)}) custom-call(s32[4]{0:T(128)S(1)} %pad_add_fusion.meta_ref, f32[4,11,256]{2,1,0:T(8,128)S(1)} %get-tuple-element.72.bias_ref, f32[4,4,256]{2,1,0:T(4,128)S(1)} %get-tuple-element.98.stats_ref, ...), custom_call_target="tpu_custom_call" | custom-call | flops 1 | bytes 1 | tf_op jit(solution)/shard_map/attention_back_1/pallas_call | solution.py:47
  99.6 5.0 %collective-permute-done.15.stats_ref = f32[4,4,256]{2,1,0:T(4,128)S(1)} collective-permute-done((f32[4,4,256]{2,1,0:T(4,128)S(1)}, f32[4,4,256]{2,1,0:T(4,128)S(1)}, u32[]{:S(2)}, u32[]{:S(2)}) %collective-permute-start.15) | collective-permute-done | bytes 16416 | tf_op jit(solution)/shard_map/ppermute | solution.py:625
  107.3 2.1 %project_1.1 = (f32[256,512]{1,0:T(8,128)S(1)}, bf16[2,256,512]{2,1,0:T(8,128)(2,1)S(1)}, bf16[1,256,512]{2,1,0:T(8,128)(2,1)S(1)}, f32[1,256,512]{2,1,0:T(8,128)S(1)}) custom-call(s32[4]{0:T(128)S(1)} %pad_add_fusion.meta_ref, bf16[512,1024]{1,0:T(8,128)(2,1)S(1)} %get-tuple-element.81.mine_ref, bf16[512,1024]{1,0:T(8,128)(2,1)S(1)} %collective-permute-done.9.theirs_ref, ...), custom_call_target="tpu_custom_call" | custom-call | flops 1 | bytes 1 | tf_op jit(solution)/shard_map/project_1/pallas_call | solution.py:47
  109.5 3.9 %attention_back_next.1.own_ref = f32[2,1024,256]{2,1,0:T(8,128)S(1)} custom-call(s32[4]{0:T(128)S(1)} %pad_add_fusion.meta_ref, f32[4,10,256]{2,1,0:T(8,128)S(1)} %get-tuple-element.104.bias_ref, f32[4,4,256]{2,1,0:T(4,128)S(1)} %collective-permute-done.15.stats_ref, f32[2,1024,128]{2,1,0:T(8,128)S(1)} %get-tuple-element.105.refs_0_, ...), custom_call_target="tpu_custom_call" | custom-call | flops 1 | bytes 1 | tf_op jit(solution)/shard_map/attention_back_next/pallas_call | solution.py:47
  113.4 1.6 %collective-permute-done.21.refs_3_ = bf16[2,128,256]{2,1,0:T(8,128)(2,1)S(1)} collective-permute-done((bf16[2,128,256]{2,1,0:T(8,128)(2,1)S(1)}, bf16[2,128,256]{2,1,0:T(8,128)(2,1)S(1)}, u32[]{:S(2)}, u32[]{:S(2)}) %collective-permute-start.21) | collective-permute-done | bytes 131104 | tf_op jit(solution)/shard_map/ppermute | solution.py:703
  116.4 1.6 %collective-permute-start.22 = (bf16[3,256,256]{2,1,0:T(8,128)(2,1)S(1)}, bf16[3,256,256]{2,1,0:T(8,128)(2,1)S(1)}, u32[]{:S(2)}, u32[]{:S(2)}) collective-permute-start(bf16[3,256,256]{2,1,0:T(8,128)(2,1)S(1)} %get-tuple-element.110), channel_id=1, source_target_pairs={{0,2},{2,0},{4,6},{6,4},{8,10},{10,8},{12,14},{14,12},{16,18},{18,... | collective-permute-start | bytes 1179656 | tf_op jit(solution)/shard_map/ppermute | solution.py:617
  118.0 1.5 %collective-permute-start.23 = (bf16[3,256,256]{2,1,0:T(8,128)(2,1)S(1)}, bf16[3,256,256]{2,1,0:T(8,128)(2,1)S(1)}, u32[]{:S(2)}, u32[]{:S(2)}) collective-permute-start(bf16[3,256,256]{2,1,0:T(8,128)(2,1)S(1)} %get-tuple-element.111), channel_id=1, source_target_pairs={{0,4},{2,6},{4,0},{6,2},{8,12},{10,14},{12,8},{14,10},{16,20},{18,... | collective-permute-start | bytes 1179656 | tf_op jit(solution)/shard_map/ppermute | solution.py:617
  120.2 3.9 %collective-permute-start.26 = (bf16[256,512]{1,0:T(8,128)(2,1)S(1)}, bf16[256,512]{1,0:T(8,128)(2,1)S(1)}, u32[]{:S(2)}, u32[]{:S(2)}) collective-permute-start(bf16[256,512]{1,0:T(8,128)(2,1)S(1)} %halve_1.1), channel_id=1, source_target_pairs={{0,16},{2,18},{4,20},{6,22},{8,24},{10,26},{12,28},{14,30},{16,0},... | collective-permute-start | bytes 786440 | tf_op jit(solution)/shard_map/ppermute | solution.py:629
  124.1 4.3 %collective-permute-done.22.refs_1_ = bf16[3,256,256]{2,1,0:T(8,128)(2,1)S(1)} collective-permute-done((bf16[3,256,256]{2,1,0:T(8,128)(2,1)S(1)}, bf16[3,256,256]{2,1,0:T(8,128)(2,1)S(1)}, u32[]{:S(2)}, u32[]{:S(2)}) %collective-permute-start.22) | collective-permute-done | bytes 393248 | tf_op jit(solution)/shard_map/ppermute | solution.py:617
  128.5 6.0 %collective-permute-done.23.refs_2_ = bf16[3,256,256]{2,1,0:T(8,128)(2,1)S(1)} collective-permute-done((bf16[3,256,256]{2,1,0:T(8,128)(2,1)S(1)}, bf16[3,256,256]{2,1,0:T(8,128)(2,1)S(1)}, u32[]{:S(2)}, u32[]{:S(2)}) %collective-permute-start.23) | collective-permute-done | bytes 393248 | tf_op jit(solution)/shard_map/ppermute | solution.py:617
  134.5 1.8 %unpack.1 = (bf16[256,1024]{1,0:T(8,128)(2,1)}, bf16[256,1024]{1,0:T(8,128)(2,1)}, bf16[256,1024]{1,0:T(8,128)(2,1)}) custom-call(s32[4]{0:T(128)S(1)} %pad_add_fusion.meta_ref, bf16[3,256,256]{2,1,0:T(8,128)(2,1)S(1)} %get-tuple-element.109.refs_0_, bf16[3,256,256]{2,1,0:T(8,128)(2,1)S(1)} %collective-permute-done.22.refs_1_, ...), custom_call_target="tpu_custom_call" | custom-call | flops 1 | bytes 1 | tf_op jit(solution)/shard_map/unpack/pallas_call | solution.py:584
  (53 shorter events, 23.2 us)
Async XLA Ops:
  4.3 10.3 %collective-permute-start = (bf16[2,256,256]{2,1,0:T(8,128)(2,1)}, bf16[2,256,256]{2,1,0:T(8,128)(2,1)S(1)}, u32[]{:S(2)}, u32[]{:S(2)}) collective-permute-start(bf16[2,256,256]{2,1,0:T(8,128)(2,1)} %get-tuple-element.63), channel_id=1, source_target_pairs={{0,2},{2,0},{4,6},{6,4},{8,10},{10,8},{12,14},{14,12},{16,18},{18,... | collective-permute-start | bytes 786440 | tf_op jit(solution)/shard_map/ppermute | solution.py:617
  7.3 16.1 %collective-permute-start.1 = (bf16[2,256,256]{2,1,0:T(8,128)(2,1)}, bf16[2,256,256]{2,1,0:T(8,128)(2,1)S(1)}, u32[]{:S(2)}, u32[]{:S(2)}) collective-permute-start(bf16[2,256,256]{2,1,0:T(8,128)(2,1)} %get-tuple-element.68), channel_id=1, source_target_pairs={{0,4},{2,6},{4,0},{6,2},{8,12},{10,14},{12,8},{14,10},{16,20},{18,... | collective-permute-start | bytes 786440 | tf_op jit(solution)/shard_map/ppermute | solution.py:617
  8.8 14.6 %collective-permute-start.2 = (bf16[2,256,256]{2,1,0:T(8,128)(2,1)}, bf16[2,256,256]{2,1,0:T(8,128)(2,1)S(1)}, u32[]{:S(2)}, u32[]{:S(2)}) collective-permute-start(bf16[2,256,256]{2,1,0:T(8,128)(2,1)} %get-tuple-element.69), channel_id=1, source_target_pairs={{0,6},{2,4},{4,2},{6,0},{8,14},{10,12},{12,10},{14,8},{16,22},{18,... | collective-permute-start | bytes 786440 | tf_op jit(solution)/shard_map/ppermute | solution.py:617
  12.1 11.3 %copy-start.1 = (bf16[2,256,256]{2,1,0:T(8,128)(2,1)S(1)}, bf16[2,256,256]{2,1,0:T(8,128)(2,1)}, u32[]{:S(2)}) copy-start(bf16[2,256,256]{2,1,0:T(8,128)(2,1)} %get-tuple-element.67.refs_0_) | copy-start | bytes 786436
  12.1 35.1 %copy-start.2 = (s32[32,10]{0,1:T(8,128)S(1)}, s32[32,10]{0,1:T(8,128)}, u32[]{:S(2)}) copy-start(s32[32,10]{0,1:T(8,128)} %param.11) | copy-start | bytes 3844
  24.7 30.2 %collective-permute-start.3 = (bf16[2,1024,256]{2,1,0:T(8,128)(2,1)S(1)}, bf16[2,1024,256]{2,1,0:T(8,128)(2,1)S(1)}, u32[]{:S(2)}, u32[]{:S(2)}) collective-permute-start(bf16[2,1024,256]{2,1,0:T(8,128)(2,1)S(1)} %get-tuple-element.73.refs_1_.refs_3_), channel_id=1, source_target_pairs={{0,8},{2,10},{4,12},{6,14},{8,16},{10,18},{12,20},{14,22},{16,24},... | collective-permute-start | bytes 3145736 | tf_op jit(solution)/shard_map/ppermute | solution.py:625
  28.8 15.1 %collective-permute-start.5 = (bf16[1024,256]{1,0:T(8,128)(2,1)}, bf16[1024,256]{1,0:T(8,128)(2,1)S(1)}, u32[]{:S(2)}, u32[]{:S(2)}) collective-permute-start(bf16[1024,256]{1,0:T(8,128)(2,1)} %get-tuple-element.74), channel_id=1, source_target_pairs={{0,2},{2,0},{4,6},{6,4},{8,10},{10,8},{12,14},{14,12},{16,18},{18,... | collective-permute-start | bytes 1572872 | tf_op jit(solution)/shard_map/ppermute | solution.py:617
  30.4 24.5 %collective-permute-start.7 = (bf16[1024,256]{1,0:T(8,128)(2,1)}, bf16[1024,256]{1,0:T(8,128)(2,1)S(1)}, u32[]{:S(2)}, u32[]{:S(2)}) collective-permute-start(bf16[1024,256]{1,0:T(8,128)(2,1)} %get-tuple-element.77), channel_id=1, source_target_pairs={{0,4},{2,6},{4,0},{6,2},{8,12},{10,14},{12,8},{14,10},{16,20},{18,... | collective-permute-start | bytes 1572872 | tf_op jit(solution)/shard_map/ppermute | solution.py:617
  31.9 23.0 %collective-permute-start.8 = (bf16[1024,256]{1,0:T(8,128)(2,1)}, bf16[1024,256]{1,0:T(8,128)(2,1)}, u32[]{:S(2)}, u32[]{:S(2)}) collective-permute-start(bf16[1024,256]{1,0:T(8,128)(2,1)} %get-tuple-element.78), channel_id=1, source_target_pairs={{0,6},{2,4},{4,2},{6,0},{8,14},{10,12},{12,10},{14,8},{16,22},{18,... | collective-permute-start | bytes 1572872 | tf_op jit(solution)/shard_map/ppermute | solution.py:617
  32.4 21.1 %collective-permute-start.4 = (bf16[2,128,256]{2,1,0:T(8,128)(2,1)}, bf16[2,128,256]{2,1,0:T(8,128)(2,1)S(1)}, u32[]{:S(2)}, u32[]{:S(2)}) collective-permute-start(bf16[2,128,256]{2,1,0:T(8,128)(2,1)} %get-tuple-element.75), channel_id=1, source_target_pairs={{0,16},{2,18},{4,20},{6,22},{1,17},{3,19},{5,21},{7,23}} | collective-permute-start | bytes 393224 | tf_op jit(solution)/shard_map/ppermute | solution.py:664
  44.0 10.9 %collective-permute-start.6 = (bf16[2,128,256]{2,1,0:T(8,128)(2,1)}, bf16[2,128,256]{2,1,0:T(8,128)(2,1)S(1)}, u32[]{:S(2)}, u32[]{:S(2)}) collective-permute-start(bf16[2,128,256]{2,1,0:T(8,128)(2,1)} %get-tuple-element.75), channel_id=1, source_target_pairs={{0,24},{2,26},{4,28},{6,30},{1,25},{3,27},{5,29},{7,31}} | collective-permute-start | bytes 393224 | tf_op jit(solution)/shard_map/ppermute | solution.py:664
  54.9 1.0 copy-start
  57.2 9.5 %collective-permute-start.9 = (bf16[512,1024]{1,0:T(8,128)(2,1)S(1)}, bf16[512,1024]{1,0:T(8,128)(2,1)S(1)}, u32[]{:S(2)}, u32[]{:S(2)}) collective-permute-start(bf16[512,1024]{1,0:T(8,128)(2,1)S(1)} %get-tuple-element.81.mine_ref), channel_id=1, source_target_pairs={{0,1},{1,0},{2,3},{3,2},{4,5},{5,4},{6,7},{7,6},{8,9},{9,8},{10,11... | collective-permute-start | bytes 3145736 | tf_op jit(solution)/shard_map/ppermute | solution.py:671
  57.3 36.5 %collective-permute-start.14 = (bf16[2,1024,256]{2,1,0:T(8,128)(2,1)S(1)}, bf16[2,1024,256]{2,1,0:T(8,128)(2,1)S(1)}, u32[]{:S(2)}, u32[]{:S(2)}) collective-permute-start(bf16[2,1024,256]{2,1,0:T(8,128)(2,1)S(1)} %get-tuple-element.79.refs_0_), channel_id=1, source_target_pairs={{8,0},{10,2},{12,4},{14,6},{16,8},{18,10},{20,12},{22,14},{24,16},... | collective-permute-start | bytes 3145736 | tf_op jit(solution)/shard_map/ppermute | solution.py:625
  63.1 12.6 %collective-permute-start.10 = (bf16[1024,128]{1,0:T(8,128)(2,1)S(1)}, bf16[1024,128]{1,0:T(8,128)(2,1)S(1)}, u32[]{:S(2)}, u32[]{:S(2)}) collective-permute-start(bf16[1024,128]{1,0:T(8,128)(2,1)S(1)} %get-tuple-element.80.refs_0_), channel_id=1, source_target_pairs={{0,2},{2,0},{4,6},{6,4},{8,10},{10,8},{12,14},{14,12},{16,18},{18,... | collective-permute-start | bytes 786440 | tf_op jit(solution)/shard_map/ppermute | solution.py:617
  64.7 14.0 %collective-permute-start.11 = (bf16[1024,128]{1,0:T(8,128)(2,1)S(1)}, bf16[1024,128]{1,0:T(8,128)(2,1)S(1)}, u32[]{:S(2)}, u32[]{:S(2)}) collective-permute-start(bf16[1024,128]{1,0:T(8,128)(2,1)S(1)} %get-tuple-element.80.refs_0_), channel_id=1, source_target_pairs={{0,4},{2,6},{4,0},{6,2},{8,12},{10,14},{12,8},{14,10},{16,20},{18,... | collective-permute-start | bytes 786440 | tf_op jit(solution)/shard_map/ppermute | solution.py:617
  66.2 12.5 %collective-permute-start.12 = (bf16[1024,128]{1,0:T(8,128)(2,1)S(1)}, bf16[1024,128]{1,0:T(8,128)(2,1)S(1)}, u32[]{:S(2)}, u32[]{:S(2)}) collective-permute-start(bf16[1024,128]{1,0:T(8,128)(2,1)S(1)} %get-tuple-element.80.refs_0_), channel_id=1, source_target_pairs={{0,6},{2,4},{4,2},{6,0},{8,14},{10,12},{12,10},{14,8},{16,22},{18,... | collective-permute-start | bytes 786440 | tf_op jit(solution)/shard_map/ppermute | solution.py:617
  80.9 9.5 %collective-permute-start.13 = (bf16[1,256,512]{2,1,0:T(8,128)(2,1)S(1)}, bf16[1,256,512]{2,1,0:T(8,128)(2,1)S(1)}, u32[]{:S(2)}, u32[]{:S(2)}) collective-permute-start(bf16[1,256,512]{2,1,0:T(8,128)(2,1)S(1)} %get-tuple-element.91), channel_id=1, source_target_pairs={{0,8},{2,10},{4,12},{6,14},{8,0},{10,2},{12,4},{14,6},{16,24},{18,... | collective-permute-start | bytes 786440 | tf_op jit(solution)/shard_map/ppermute | solution.py:629
  83.3 22.6 %collective-permute-start.16 = (bf16[1024,128]{1,0:T(8,128)(2,1)S(1)}, bf16[1024,128]{1,0:T(8,128)(2,1)S(1)}, u32[]{:S(2)}, u32[]{:S(2)}) collective-permute-start(bf16[1024,128]{1,0:T(8,128)(2,1)S(1)} %get-tuple-element.100.refs_0_), channel_id=1, source_target_pairs={{0,2},{2,0},{4,6},{6,4},{8,10},{10,8},{12,14},{14,12},{16,18},{18,... | collective-permute-start | bytes 786440 | tf_op jit(solution)/shard_map/ppermute | solution.py:617
  84.6 22.7 %collective-permute-start.17 = (bf16[1024,128]{1,0:T(8,128)(2,1)S(1)}, bf16[1024,128]{1,0:T(8,128)(2,1)S(1)}, u32[]{:S(2)}, u32[]{:S(2)}) collective-permute-start(bf16[1024,128]{1,0:T(8,128)(2,1)S(1)} %get-tuple-element.100.refs_0_), channel_id=1, source_target_pairs={{0,4},{2,6},{4,0},{6,2},{8,12},{10,14},{12,8},{14,10},{16,20},{18,... | collective-permute-start | bytes 786440 | tf_op jit(solution)/shard_map/ppermute | solution.py:617
  85.4 21.9 %collective-permute-start.18 = (bf16[1024,128]{1,0:T(8,128)(2,1)S(1)}, bf16[1024,128]{1,0:T(8,128)(2,1)S(1)}, u32[]{:S(2)}, u32[]{:S(2)}) collective-permute-start(bf16[1024,128]{1,0:T(8,128)(2,1)S(1)} %get-tuple-element.100.refs_0_), channel_id=1, source_target_pairs={{0,6},{2,4},{4,2},{6,0},{8,14},{10,12},{12,10},{14,8},{16,22},{18,... | collective-permute-start | bytes 786440 | tf_op jit(solution)/shard_map/ppermute | solution.py:617
  90.4 19.1 %collective-permute-start.19 = (bf16[256,512]{1,0:T(8,128)(2,1)S(1)}, bf16[256,512]{1,0:T(8,128)(2,1)S(1)}, u32[]{:S(2)}, u32[]{:S(2)}) collective-permute-start(bf16[256,512]{1,0:T(8,128)(2,1)S(1)} %halve_0.1), channel_id=1, source_target_pairs={{0,16},{2,18},{4,20},{6,22},{8,24},{10,26},{12,28},{14,30},{16,0},... | collective-permute-start | bytes 786440 | tf_op jit(solution)/shard_map/ppermute | solution.py:629
  93.8 10.9 %collective-permute-start.15 = (f32[4,4,256]{2,1,0:T(4,128)S(1)}, f32[4,4,256]{2,1,0:T(4,128)S(1)}, u32[]{:S(2)}, u32[]{:S(2)}) collective-permute-start(f32[4,4,256]{2,1,0:T(4,128)S(1)} %get-tuple-element.98.stats_ref), channel_id=1, source_target_pairs={{8,0},{10,2},{12,4},{14,6},{16,8},{18,10},{20,12},{22,14},{24,16},... | collective-permute-start | bytes 49160 | tf_op jit(solution)/shard_map/ppermute | solution.py:625
  104.7 8.7 %collective-permute-start.20 = (bf16[2,128,256]{2,1,0:T(8,128)(2,1)S(1)}, bf16[2,128,256]{2,1,0:T(8,128)(2,1)S(1)}, u32[]{:S(2)}, u32[]{:S(2)}) collective-permute-start(bf16[2,128,256]{2,1,0:T(8,128)(2,1)S(1)} %get-tuple-element.107), channel_id=1, source_target_pairs={{16,0},{18,2},{20,4},{22,6},{17,1},{19,3},{21,5},{23,7}} | collective-permute-start | bytes 393224 | tf_op jit(solution)/shard_map/ppermute | solution.py:703
  106.0 9.0 %collective-permute-start.21 = (bf16[2,128,256]{2,1,0:T(8,128)(2,1)S(1)}, bf16[2,128,256]{2,1,0:T(8,128)(2,1)S(1)}, u32[]{:S(2)}, u32[]{:S(2)}) collective-permute-start(bf16[2,128,256]{2,1,0:T(8,128)(2,1)S(1)} %get-tuple-element.108), channel_id=1, source_target_pairs={{24,0},{26,2},{28,4},{30,6},{25,1},{27,3},{29,5},{31,7}} | collective-permute-start | bytes 393224 | tf_op jit(solution)/shard_map/ppermute | solution.py:703
  109.4 10.7 %collective-permute-start.25 = (bf16[1,256,512]{2,1,0:T(8,128)(2,1)S(1)}, bf16[1,256,512]{2,1,0:T(8,128)(2,1)S(1)}, u32[]{:S(2)}, u32[]{:S(2)}) collective-permute-start(bf16[1,256,512]{2,1,0:T(8,128)(2,1)S(1)} %get-tuple-element.119), channel_id=1, source_target_pairs={{0,8},{2,10},{4,12},{6,14},{8,0},{10,2},{12,4},{14,6},{16,24},{18,... | collective-permute-start | bytes 786440 | tf_op jit(solution)/shard_map/ppermute | solution.py:629
  115.9 20.4 %collective-permute-start.27 = (bf16[2,256,512]{2,1,0:T(8,128)(2,1)S(1)}, bf16[2,256,512]{2,1,0:T(8,128)(2,1)S(1)}, u32[]{:S(2)}, u32[]{:S(2)}) collective-permute-start(bf16[2,256,512]{2,1,0:T(8,128)(2,1)S(1)} %get-tuple-element.121), channel_id=1, source_target_pairs={{0,8},{2,10},{4,12},{6,14},{8,0},{10,2},{12,4},{14,6},{16,24},{18,... | collective-permute-start | bytes 1572872 | tf_op jit(solution)/shard_map/ppermute | solution.py:629
  116.4 12.1 %collective-permute-start.22 = (bf16[3,256,256]{2,1,0:T(8,128)(2,1)S(1)}, bf16[3,256,256]{2,1,0:T(8,128)(2,1)S(1)}, u32[]{:S(2)}, u32[]{:S(2)}) collective-permute-start(bf16[3,256,256]{2,1,0:T(8,128)(2,1)S(1)} %get-tuple-element.110), channel_id=1, source_target_pairs={{0,2},{2,0},{4,6},{6,4},{8,10},{10,8},{12,14},{14,12},{16,18},{18,... | collective-permute-start | bytes 1179656 | tf_op jit(solution)/shard_map/ppermute | solution.py:617
  118.0 16.5 %collective-permute-start.23 = (bf16[3,256,256]{2,1,0:T(8,128)(2,1)S(1)}, bf16[3,256,256]{2,1,0:T(8,128)(2,1)S(1)}, u32[]{:S(2)}, u32[]{:S(2)}) collective-permute-start(bf16[3,256,256]{2,1,0:T(8,128)(2,1)S(1)} %get-tuple-element.111), channel_id=1, source_target_pairs={{0,4},{2,6},{4,0},{6,2},{8,12},{10,14},{12,8},{14,10},{16,20},{18,... | collective-permute-start | bytes 1179656 | tf_op jit(solution)/shard_map/ppermute | solution.py:617
  119.5 15.0 %collective-permute-start.24 = (bf16[3,256,256]{2,1,0:T(8,128)(2,1)S(1)}, bf16[3,256,256]{2,1,0:T(8,128)(2,1)S(1)}, u32[]{:S(2)}, u32[]{:S(2)}) collective-permute-start(bf16[3,256,256]{2,1,0:T(8,128)(2,1)S(1)} %get-tuple-element.112), channel_id=1, source_target_pairs={{0,6},{2,4},{4,2},{6,0},{8,14},{10,12},{12,10},{14,8},{16,22},{18,... | collective-permute-start | bytes 1179656 | tf_op jit(solution)/shard_map/ppermute | solution.py:617
  120.2 16.1 %collective-permute-start.26 = (bf16[256,512]{1,0:T(8,128)(2,1)S(1)}, bf16[256,512]{1,0:T(8,128)(2,1)S(1)}, u32[]{:S(2)}, u32[]{:S(2)}) collective-permute-start(bf16[256,512]{1,0:T(8,128)(2,1)S(1)} %halve_1.1), channel_id=1, source_target_pairs={{0,16},{2,18},{4,20},{6,22},{8,24},{10,26},{12,28},{14,30},{16,0},... | collective-permute-start | bytes 786440 | tf_op jit(solution)/shard_map/ppermute | solution.py:629

commit v8 on v7

--- a/solution.py
+++ b/solution.py
@@ -202,18 +202,31 @@
 
     def body(meta_ref, *refs):
         me = meta_ref[0]
-        qd, og = refs[group:]
+        qd, og, sems = refs[group:]
+        copies = []
         for k in range(group):
             at = pl.ds(pl.multiple_of((me ^ k) * rows, rows), rows)
-            qd[0, at, :] = refs[k][:rows, :]
-            qd[1, at, :] = refs[k][rows : 2 * rows, :]
-            og[:, at] = refs[k][2 * rows :, :]
-
-    return call(
-        body, (meta,), tuple(pieces),
-        [shape((2, group * rows, rows)), shape((height, group * rows))], [],
-        cost(0, 4 * MIB), "assemble",
-    )
+            parts = (
+                (pl.ds(0, rows), qd.at[0, at, :]),
+                (pl.ds(rows, rows), qd.at[1, at, :]),
+                (pl.ds(2 * rows, height), og.at[:, at]),
+            )
+            for which, (source, target) in enumerate(parts):
+                copies.append(
+                    pltpu.make_async_copy(refs[k].at[source, :], target, sems.at[k, which])
+                )
+        copied(*copies)
+
+    return pl.pallas_call(
+        body,
+        out_shape=[shape((2, group * rows, rows)), shape((height, group * rows))],
+        in_specs=[SMEM] + [ANY] * group,
+        out_specs=[VMEM] * 2,
+        scratch_shapes=[pltpu.SemaphoreType.DMA((group, 3))],
+        compiler_params=params(16),
+        cost_estimate=cost(0, 4 * MIB),
+        name="assemble",
+    )(meta, *pieces)
 
 
 def masks_of(layout, meta, parts, slots):
@@ -688,8 +701,6 @@
         grads.append(got[1])
         far_grads = got[2]
         order = after(meta, got[0])
-        if h > 0:
-            order = after(order, next_stats)
         kept, first, odds, evens = project(h, mine, theirs, attn[h], first, order, group, parts)
         keep.append(kept)
         first, odds = [first], swap_groups(odds, 1)

time: 138 us -> 141 us (1.022)
  waiting for transfers between devices: 39.1 us -> 42 us
  Pallas kernels: 46.4 us -> 47.9 us
    ppermute x15, waiting for transfers between devices: 23 us -> 29.4 us  [swap(): return lax.ppermute(piece, 'seq', route)]
    pallas_call x0 -> x1, Pallas kernels: none -> 2.83 us  [assemble(): pl.pallas_call(body, out_shape=[shape((2, group * rows, rows)), shape((he...]
    ppermute x3, waiting for transfers between devices: 5.03 us -> 3.42 us  [shifted(): return lax.ppermute(piece, 'seq', route)]
    ppermute x2, waiting for transfers between devices: 1.6 us -> 0.01 us  [local(): lax.ppermute(piece, 'seq', summary_route(index + 2, True))]
    pallas_call x13 -> x12, Pallas kernels: 31.6 us -> 30.3 us  [call(): pl.pallas_call(body, out_shape=outs, in_specs=[SMEM] * len(scalars) + [VM...]
  transfers between devices with their start and end apart: 28 -> 28, of which waited for: 11 -> 9; matrix products, arithmetic and copies ran while one was open for 1% -> 1% of each run, Pallas kernels for 29% -> 28%
where the time goes in v8:
time: 141 us
  Pallas kernels  47.9 us (34%)
  starting transfers between devices  44.9 us (32%)
  waiting for transfers between devices  42 us (30%)
  between operations  2.94 us (2%)
  local copies, waits for them, and re-layouts  2.41 us (2%)
    pallas_call x12, Pallas kernels, call(): pl.pallas_call(body, out_shape=outs, in_specs=[SMEM] * len(scalars) + [VM...  30.3 us
    ppermute x15, waiting for transfers between devices, swap(): return lax.ppermute(piece, 'seq', route)  29.4 us
    ppermute x15, starting transfers between devices, swap(): return lax.ppermute(piece, 'seq', route)  18.6 us
    ppermute x5, starting transfers between devices, swap_groups(): return lax.ppermute(piece, 'seq', route)  9.21 us
    pallas_call x1, Pallas kernels, grads_packed(): pl.pallas_call(body, out_shape=[shape((2 * rows + half * each, rows))] *...  8.73 us
    ppermute x2, starting transfers between devices, local(): lax.ppermute(strided if distance == 2 else later, 'seq', summary_route(di...  7.67 us
    ppermute x3, starting transfers between devices, shifted(): return lax.ppermute(piece, 'seq', route)  6.7 us
    ppermute x2, waiting for transfers between devices, local(): lax.ppermute(strided if distance == 2 else later, 'seq', summary_route(di...  5.68 us
  transfers between devices with their start and end apart: 28, of which 9 were waited for; matrix products, arithmetic and copies ran while one was open for 1% of the time, Pallas kernels for 28%

profile of v8, /device:TPU:0, one launch (start us, length us, event | category | flops | bytes accessed | tf_op | source)
XLA Modules:
  0.0 140.9 jit_solution(4613982004703304712)
XLA Ops:
  1.3 3.0 %pack_kv.1 = (bf16[2,256,256]{2,1,0:T(8,128)(2,1)}, bf16[2,256,256]{2,1,0:T(8,128)(2,1)}, bf16[2,256,256]{2,1,0:T(8,128)(2,1)}, bf16[2,256,256]{2,1,0:T(8,128)(2,1)}) custom-call(s32[3]{0:T(128)} %pad_add_fusion.1.meta_ref, bf16[256,1024]{1,0:T(8,128)(2,1)} %k_ref.1, bf16[256,1024]{1,0:T(8,128)(2,1)} %v_ref.1), custom_call_target="tpu_custom_call" | custom-call | flops 1 | bytes 1 | tf_op jit(solution)/shard_map/pack_kv/pallas_call | solution.py:93
  4.3 3.0 %collective-permute-start = (bf16[2,256,256]{2,1,0:T(8,128)(2,1)}, bf16[2,256,256]{2,1,0:T(8,128)(2,1)S(1)}, u32[]{:S(2)}, u32[]{:S(2)}) collective-permute-start(bf16[2,256,256]{2,1,0:T(8,128)(2,1)} %get-tuple-element.62), channel_id=1, source_target_pairs={{0,2},{2,0},{4,6},{6,4},{8,10},{10,8},{12,14},{14,12},{16,18},{18,... | collective-permute-start | bytes 786440 | tf_op jit(solution)/shard_map/ppermute | solution.py:630
  12.1 2.5 %collective-permute-done.refs_1_ = bf16[2,256,256]{2,1,0:T(8,128)(2,1)S(1)} collective-permute-done((bf16[2,256,256]{2,1,0:T(8,128)(2,1)}, bf16[2,256,256]{2,1,0:T(8,128)(2,1)S(1)}, u32[]{:S(2)}, u32[]{:S(2)}) %collective-permute-start) | collective-permute-done | bytes 262176 | tf_op jit(solution)/shard_map/ppermute | solution.py:630
  14.6 8.7 %attn_grad.1 = (bf16[1024,256]{1,0:T(8,128)(2,1)}, bf16[1024,256]{1,0:T(8,128)(2,1)}, bf16[1024,256]{1,0:T(8,128)(2,1)}, bf16[1024,256]{1,0:T(8,128)(2,1)}) custom-call(s32[3]{0:T(128)} %pad_add_fusion.1.meta_ref, bf16[256,1024]{1,0:T(8,128)(2,1)} %q_ref.1, bf16[256,4096]{1,0:T(8,128)(2,1)} %og_ref.1, bf16[4096,1024]{1,0:T(8,128)(2,1)} %w_ref.1), custom_call_target="tpu_custom_call" | custom-call | flops 1 | bytes 1 | tf_op jit(solution)/shard_map/attn_grad/pallas_call | solution.py:152
  24.7 4.1 %collective-permute-start.3 = (bf16[2,1024,256]{2,1,0:T(8,128)(2,1)S(1)}, bf16[2,1024,256]{2,1,0:T(8,128)(2,1)S(1)}, u32[]{:S(2)}, u32[]{:S(2)}) collective-permute-start(bf16[2,1024,256]{2,1,0:T(8,128)(2,1)S(1)} %get-tuple-element.72.refs_1_.refs_3_), channel_id=1, source_target_pairs={{0,8},{2,10},{4,12},{6,14},{8,16},{10,18},{12,20},{14,22},{16,24},... | collective-permute-start | bytes 3145736 | tf_op jit(solution)/shard_map/ppermute | solution.py:638
  28.8 1.6 %collective-permute-start.5 = (bf16[1024,256]{1,0:T(8,128)(2,1)}, bf16[1024,256]{1,0:T(8,128)(2,1)S(1)}, u32[]{:S(2)}, u32[]{:S(2)}) collective-permute-start(bf16[1024,256]{1,0:T(8,128)(2,1)} %get-tuple-element.73), channel_id=1, source_target_pairs={{0,2},{2,0},{4,6},{6,4},{8,10},{10,8},{12,14},{14,12},{16,18},{18,... | collective-permute-start | bytes 1572872 | tf_op jit(solution)/shard_map/ppermute | solution.py:630
  30.4 1.5 %collective-permute-start.7 = (bf16[1024,256]{1,0:T(8,128)(2,1)}, bf16[1024,256]{1,0:T(8,128)(2,1)S(1)}, u32[]{:S(2)}, u32[]{:S(2)}) collective-permute-start(bf16[1024,256]{1,0:T(8,128)(2,1)} %get-tuple-element.76), channel_id=1, source_target_pairs={{0,4},{2,6},{4,0},{6,2},{8,12},{10,14},{12,8},{14,10},{16,20},{18,... | collective-permute-start | bytes 1572872 | tf_op jit(solution)/shard_map/ppermute | solution.py:630
  32.4 4.4 %collective-permute-start.4 = (bf16[2,128,256]{2,1,0:T(8,128)(2,1)}, bf16[2,128,256]{2,1,0:T(8,128)(2,1)S(1)}, u32[]{:S(2)}, u32[]{:S(2)}) collective-permute-start(bf16[2,128,256]{2,1,0:T(8,128)(2,1)} %get-tuple-element.74), channel_id=1, source_target_pairs={{0,16},{2,18},{4,20},{6,22},{1,17},{3,19},{5,21},{7,23}} | collective-permute-start | bytes 393224 | tf_op jit(solution)/shard_map/ppermute | solution.py:677
  36.8 7.2 %collective-permute-done.5.refs_1_ = bf16[1024,256]{1,0:T(8,128)(2,1)S(1)} collective-permute-done((bf16[1024,256]{1,0:T(8,128)(2,1)}, bf16[1024,256]{1,0:T(8,128)(2,1)S(1)}, u32[]{:S(2)}, u32[]{:S(2)}) %collective-permute-start.5) | collective-permute-done | bytes 524320 | tf_op jit(solution)/shard_map/ppermute | solution.py:630
  44.0 3.2 %collective-permute-start.6 = (bf16[2,128,256]{2,1,0:T(8,128)(2,1)}, bf16[2,128,256]{2,1,0:T(8,128)(2,1)S(1)}, u32[]{:S(2)}, u32[]{:S(2)}) collective-permute-start(bf16[2,128,256]{2,1,0:T(8,128)(2,1)} %get-tuple-element.74), channel_id=1, source_target_pairs={{0,24},{2,26},{4,28},{6,30},{1,25},{3,27},{5,29},{7,31}} | collective-permute-start | bytes 393224 | tf_op jit(solution)/shard_map/ppermute | solution.py:677
  47.3 1.9 %masks.1 = (f32[4,11,256]{2,1,0:T(8,128)S(1)}, f32[4,10,256]{2,1,0:T(8,128)S(1)}) custom-call(s32[4]{0:T(128)S(1)} %pad_add_fusion.meta_ref, s32[32,10]{1,0:T(8,128)S(1)} %copy.10.table), custom_call_target="tpu_custom_call" | custom-call | flops 1 | bytes 1 | tf_op jit(solution)/shard_map/masks/pallas_call | solution.py:47
  49.2 4.3 %collective-permute-done.4.refs_3_ = bf16[2,128,256]{2,1,0:T(8,128)(2,1)S(1)} collective-permute-done((bf16[2,128,256]{2,1,0:T(8,128)(2,1)}, bf16[2,128,256]{2,1,0:T(8,128)(2,1)S(1)}, u32[]{:S(2)}, u32[]{:S(2)}) %collective-permute-start.4) | collective-permute-done | bytes 131104 | tf_op jit(solution)/shard_map/ppermute | solution.py:677
  56.0 2.8 %assemble.1 = (bf16[2,1024,256]{2,1,0:T(8,128)(2,1)S(1)}, bf16[512,1024]{1,0:T(8,128)(2,1)S(1)}) custom-call(s32[4]{0:T(128)S(1)} %pad_add_fusion.meta_ref, bf16[1024,256]{1,0:T(8,128)(2,1)S(1)} %copy-done, bf16[1024,256]{1,0:T(8,128)(2,1)S(1)} %collective-permute-done.5.refs_1_, bf16[1024,256]{1,0:T(8,128)(2,1)S(1)} %collective-permute-done.7.refs_2_, ...), custom_call_target="tpu_custom_call" | custom-call | flops 1 | bytes 1 | tf_op jit(solution)/shard_map/assemble/pallas_call | solution.py:220
  60.2 4.5 %attention_0.1 = (bf16[1024,128]{1,0:T(8,128)(2,1)S(1)}, f32[4,4,256]{2,1,0:T(4,128)S(1)}) custom-call(s32[4]{0:T(128)S(1)} %pad_add_fusion.meta_ref, f32[4,11,256]{2,1,0:T(8,128)S(1)} %get-tuple-element.71.bias_ref, f32[4,4,256]{2,1,0:T(4,128)S(1)} %broadcast_in_dim.3.before_ref, bf16[2,1024,256]{2,1,0:T(8,128)(2,1)S(1)} %get-tuple-element.78.refs_0_, ...), custom_call_target="tpu_custom_call" | custom-call | flops 1 | bytes 1 | tf_op jit(solution)/shard_map/attention_0/pallas_call | solution.py:47
  64.7 1.6 %collective-permute-start.10 = (bf16[1024,128]{1,0:T(8,128)(2,1)S(1)}, bf16[1024,128]{1,0:T(8,128)(2,1)S(1)}, u32[]{:S(2)}, u32[]{:S(2)}) collective-permute-start(bf16[1024,128]{1,0:T(8,128)(2,1)S(1)} %get-tuple-element.79.refs_0_), channel_id=1, source_target_pairs={{0,2},{2,0},{4,6},{6,4},{8,10},{10,8},{12,14},{14,12},{16,18},{18,... | collective-permute-start | bytes 786440 | tf_op jit(solution)/shard_map/ppermute | solution.py:630
  68.3 4.7 %attention_1.1 = (bf16[1024,128]{1,0:T(8,128)(2,1)S(1)}, f32[4,4,256]{2,1,0:T(4,128)S(1)}) custom-call(s32[4]{0:T(128)S(1)} %pad_add_fusion.meta_ref, f32[4,11,256]{2,1,0:T(8,128)S(1)} %get-tuple-element.71.bias_ref, f32[4,4,256]{2,1,0:T(4,128)S(1)} %get-tuple-element.82.before_ref, bf16[2,1024,256]{2,1,0:T(8,128)(2,1)S(1)} %get-tuple-element.78.refs_0_, ...), custom_call_target="tpu_custom_call" | custom-call | flops 1 | bytes 1 | tf_op jit(solution)/shard_map/attention_1/pallas_call | solution.py:47
  73.0 4.3 %attention_back_0.1 = (bf16[1024,128]{1,0:T(8,128)(2,1)S(1)}, f32[2,1024,128]{2,1,0:T(8,128)S(1)}, bf16[2,128,256]{2,1,0:T(8,128)(2,1)S(1)}, bf16[2,128,256]{2,1,0:T(8,128)(2,1)S(1)}) custom-call(s32[4]{0:T(128)S(1)} %pad_add_fusion.meta_ref, f32[4,11,256]{2,1,0:T(8,128)S(1)} %get-tuple-element.71.bias_ref, f32[4,4,256]{2,1,0:T(4,128)S(1)} %get-tuple-element.102.stats_ref, ...), custom_call_target="tpu_custom_call" | custom-call | flops 1 | bytes 1 | tf_op jit(solution)/shard_map/attention_back_0/pallas_call | solution.py:47
  77.3 3.0 %collective-permute-done.11.refs_2_ = bf16[1024,128]{1,0:T(8,128)(2,1)S(1)} collective-permute-done((bf16[1024,128]{1,0:T(8,128)(2,1)S(1)}, bf16[1024,128]{1,0:T(8,128)(2,1)S(1)}, u32[]{:S(2)}, u32[]{:S(2)}) %collective-permute-start.11) | collective-permute-done | bytes 262176 | tf_op jit(solution)/shard_map/ppermute | solution.py:630
  80.3 2.2 %project_0.1 = (f32[256,512]{1,0:T(8,128)S(1)}, bf16[1,256,512]{2,1,0:T(8,128)(2,1)S(1)}, bf16[1,256,512]{2,1,0:T(8,128)(2,1)S(1)}, f32[1,256,512]{2,1,0:T(8,128)S(1)}) custom-call(s32[4]{0:T(128)S(1)} %pad_add_fusion.meta_ref, bf16[512,1024]{1,0:T(8,128)(2,1)S(1)} %get-tuple-element.80.mine_ref, bf16[512,1024]{1,0:T(8,128)(2,1)S(1)} %collective-permute-done.9.theirs_ref, ...), custom_call_target="tpu_custom_call" | custom-call | flops 1 | bytes 1 | tf_op jit(solution)/shard_map/project_0/pallas_call | solution.py:47
  82.5 2.4 %collective-permute-start.13 = (bf16[1,256,512]{2,1,0:T(8,128)(2,1)S(1)}, bf16[1,256,512]{2,1,0:T(8,128)(2,1)S(1)}, u32[]{:S(2)}, u32[]{:S(2)}) collective-permute-start(bf16[1,256,512]{2,1,0:T(8,128)(2,1)S(1)} %get-tuple-element.90), channel_id=1, source_target_pairs={{0,8},{2,10},{4,12},{6,14},{8,0},{10,2},{12,4},{14,6},{16,24},{18,... | collective-permute-start | bytes 786440 | tf_op jit(solution)/shard_map/ppermute | solution.py:642
  88.4 3.5 %collective-permute-done.13.arrived_ref = bf16[1,256,512]{2,1,0:T(8,128)(2,1)S(1)} collective-permute-done((bf16[1,256,512]{2,1,0:T(8,128)(2,1)S(1)}, bf16[1,256,512]{2,1,0:T(8,128)(2,1)S(1)}, u32[]{:S(2)}, u32[]{:S(2)}) %collective-permute-start.13) | collective-permute-done | bytes 262176 | tf_op jit(solution)/shard_map/ppermute | solution.py:642
  92.0 3.4 %collective-permute-start.17 = (bf16[256,512]{1,0:T(8,128)(2,1)S(1)}, bf16[256,512]{1,0:T(8,128)(2,1)S(1)}, u32[]{:S(2)}, u32[]{:S(2)}) collective-permute-start(bf16[256,512]{1,0:T(8,128)(2,1)S(1)} %halve_0.1), channel_id=1, source_target_pairs={{0,16},{2,18},{4,20},{6,22},{8,24},{10,26},{12,28},{14,30},{16,0},... | collective-permute-start | bytes 786440 | tf_op jit(solution)/shard_map/ppermute | solution.py:642
  95.4 4.5 %attention_back_1.1 = (bf16[1024,128]{1,0:T(8,128)(2,1)S(1)}, f32[2,1024,128]{2,1,0:T(8,128)S(1)}, bf16[2,128,256]{2,1,0:T(8,128)(2,1)S(1)}, bf16[2,128,256]{2,1,0:T(8,128)(2,1)S(1)}) custom-call(s32[4]{0:T(128)S(1)} %pad_add_fusion.meta_ref, f32[4,11,256]{2,1,0:T(8,128)S(1)} %get-tuple-element.71.bias_ref, f32[4,4,256]{2,1,0:T(4,128)S(1)} %get-tuple-element.102.stats_ref, ...), custom_call_target="tpu_custom_call" | custom-call | flops 1 | bytes 1 | tf_op jit(solution)/shard_map/attention_back_1/pallas_call | solution.py:47
  103.9 2.1 %project_1.1 = (f32[256,512]{1,0:T(8,128)S(1)}, bf16[2,256,512]{2,1,0:T(8,128)(2,1)S(1)}, bf16[1,256,512]{2,1,0:T(8,128)(2,1)S(1)}, f32[1,256,512]{2,1,0:T(8,128)S(1)}) custom-call(s32[4]{0:T(128)S(1)} %pad_add_fusion.meta_ref, bf16[512,1024]{1,0:T(8,128)(2,1)S(1)} %get-tuple-element.80.mine_ref, bf16[512,1024]{1,0:T(8,128)(2,1)S(1)} %collective-permute-done.9.theirs_ref, ...), custom_call_target="tpu_custom_call" | custom-call | flops 1 | bytes 1 | tf_op jit(solution)/shard_map/project_1/pallas_call | solution.py:47
  106.0 2.7 %collective-permute-start.25 = (bf16[1,256,512]{2,1,0:T(8,128)(2,1)S(1)}, bf16[1,256,512]{2,1,0:T(8,128)(2,1)S(1)}, u32[]{:S(2)}, u32[]{:S(2)}) collective-permute-start(bf16[1,256,512]{2,1,0:T(8,128)(2,1)S(1)} %get-tuple-element.117), channel_id=1, source_target_pairs={{0,8},{2,10},{4,12},{6,14},{8,0},{10,2},{12,4},{14,6},{16,24},{18,... | collective-permute-start | bytes 786440 | tf_op jit(solution)/shard_map/ppermute | solution.py:642
  108.7 3.4 %collective-permute-done.19.stats_ref = f32[4,4,256]{2,1,0:T(4,128)S(1)} collective-permute-done((f32[4,4,256]{2,1,0:T(4,128)S(1)}, f32[4,4,256]{2,1,0:T(4,128)S(1)}, u32[]{:S(2)}, u32[]{:S(2)}) %collective-permute-start.19) | collective-permute-done | bytes 16416 | tf_op jit(solution)/shard_map/ppermute | solution.py:638
  112.1 3.9 %attention_back_next.1.own_ref = f32[2,1024,256]{2,1,0:T(8,128)S(1)} custom-call(s32[4]{0:T(128)S(1)} %pad_add_fusion.meta_ref, f32[4,10,256]{2,1,0:T(8,128)S(1)} %get-tuple-element.101.bias_ref, f32[4,4,256]{2,1,0:T(4,128)S(1)} %collective-permute-done.19.stats_ref, f32[2,1024,128]{2,1,0:T(8,128)S(1)} %get-tuple-element.103.refs_0_, ...), custom_call_target="tpu_custom_call" | custom-call | flops 1 | bytes 1 | tf_op jit(solution)/shard_map/attention_back_next/pallas_call | solution.py:47
  117.5 1.6 %collective-permute-start.22 = (bf16[3,256,256]{2,1,0:T(8,128)(2,1)S(1)}, bf16[3,256,256]{2,1,0:T(8,128)(2,1)S(1)}, u32[]{:S(2)}, u32[]{:S(2)}) collective-permute-start(bf16[3,256,256]{2,1,0:T(8,128)(2,1)S(1)} %get-tuple-element.108), channel_id=1, source_target_pairs={{0,2},{2,0},{4,6},{6,4},{8,10},{10,8},{12,14},{14,12},{16,18},{18,... | collective-permute-start | bytes 1179656 | tf_op jit(solution)/shard_map/ppermute | solution.py:630
  119.1 1.5 %collective-permute-start.23 = (bf16[3,256,256]{2,1,0:T(8,128)(2,1)S(1)}, bf16[3,256,256]{2,1,0:T(8,128)(2,1)S(1)}, u32[]{:S(2)}, u32[]{:S(2)}) collective-permute-start(bf16[3,256,256]{2,1,0:T(8,128)(2,1)S(1)} %get-tuple-element.109), channel_id=1, source_target_pairs={{0,4},{2,6},{4,0},{6,2},{8,12},{10,14},{12,8},{14,10},{16,20},{18,... | collective-permute-start | bytes 1179656 | tf_op jit(solution)/shard_map/ppermute | solution.py:630
  121.1 8.4 %collective-permute-done.22.refs_1_ = bf16[3,256,256]{2,1,0:T(8,128)(2,1)S(1)} collective-permute-done((bf16[3,256,256]{2,1,0:T(8,128)(2,1)S(1)}, bf16[3,256,256]{2,1,0:T(8,128)(2,1)S(1)}, u32[]{:S(2)}, u32[]{:S(2)}) %collective-permute-start.22) | collective-permute-done | bytes 393248 | tf_op jit(solution)/shard_map/ppermute | solution.py:630
  129.6 8.3 %collective-permute-done.23.refs_2_ = bf16[3,256,256]{2,1,0:T(8,128)(2,1)S(1)} collective-permute-done((bf16[3,256,256]{2,1,0:T(8,128)(2,1)S(1)}, bf16[3,256,256]{2,1,0:T(8,128)(2,1)S(1)}, u32[]{:S(2)}, u32[]{:S(2)}) %collective-permute-start.23) | collective-permute-done | bytes 393248 | tf_op jit(solution)/shard_map/ppermute | solution.py:630
  137.9 1.8 %unpack.1 = (bf16[256,1024]{1,0:T(8,128)(2,1)}, bf16[256,1024]{1,0:T(8,128)(2,1)}, bf16[256,1024]{1,0:T(8,128)(2,1)}) custom-call(s32[4]{0:T(128)S(1)} %pad_add_fusion.meta_ref, bf16[3,256,256]{2,1,0:T(8,128)(2,1)S(1)} %get-tuple-element.107.refs_0_, bf16[3,256,256]{2,1,0:T(8,128)(2,1)S(1)} %collective-permute-done.22.refs_1_, ...), custom_call_target="tpu_custom_call" | custom-call | flops 1 | bytes 1 | tf_op jit(solution)/shard_map/unpack/pallas_call | solution.py:597
  (53 shorter events, 21.8 us)
Async XLA Ops:
  4.3 10.3 %collective-permute-start = (bf16[2,256,256]{2,1,0:T(8,128)(2,1)}, bf16[2,256,256]{2,1,0:T(8,128)(2,1)S(1)}, u32[]{:S(2)}, u32[]{:S(2)}) collective-permute-start(bf16[2,256,256]{2,1,0:T(8,128)(2,1)} %get-tuple-element.62), channel_id=1, source_target_pairs={{0,2},{2,0},{4,6},{6,4},{8,10},{10,8},{12,14},{14,12},{16,18},{18,... | collective-permute-start | bytes 786440 | tf_op jit(solution)/shard_map/ppermute | solution.py:630
  7.3 16.1 %collective-permute-start.1 = (bf16[2,256,256]{2,1,0:T(8,128)(2,1)}, bf16[2,256,256]{2,1,0:T(8,128)(2,1)S(1)}, u32[]{:S(2)}, u32[]{:S(2)}) collective-permute-start(bf16[2,256,256]{2,1,0:T(8,128)(2,1)} %get-tuple-element.67), channel_id=1, source_target_pairs={{0,4},{2,6},{4,0},{6,2},{8,12},{10,14},{12,8},{14,10},{16,20},{18,... | collective-permute-start | bytes 786440 | tf_op jit(solution)/shard_map/ppermute | solution.py:630
  8.8 14.6 %collective-permute-start.2 = (bf16[2,256,256]{2,1,0:T(8,128)(2,1)}, bf16[2,256,256]{2,1,0:T(8,128)(2,1)S(1)}, u32[]{:S(2)}, u32[]{:S(2)}) collective-permute-start(bf16[2,256,256]{2,1,0:T(8,128)(2,1)} %get-tuple-element.68), channel_id=1, source_target_pairs={{0,6},{2,4},{4,2},{6,0},{8,14},{10,12},{12,10},{14,8},{16,22},{18,... | collective-permute-start | bytes 786440 | tf_op jit(solution)/shard_map/ppermute | solution.py:630
  12.1 11.3 %copy-start.1 = (bf16[2,256,256]{2,1,0:T(8,128)(2,1)S(1)}, bf16[2,256,256]{2,1,0:T(8,128)(2,1)}, u32[]{:S(2)}) copy-start(bf16[2,256,256]{2,1,0:T(8,128)(2,1)} %get-tuple-element.66.refs_0_) | copy-start | bytes 786436
  12.1 35.1 %copy-start.2 = (s32[32,10]{0,1:T(8,128)S(1)}, s32[32,10]{0,1:T(8,128)}, u32[]{:S(2)}) copy-start(s32[32,10]{0,1:T(8,128)} %param.11) | copy-start | bytes 3844
  24.7 30.2 %collective-permute-start.3 = (bf16[2,1024,256]{2,1,0:T(8,128)(2,1)S(1)}, bf16[2,1024,256]{2,1,0:T(8,128)(2,1)S(1)}, u32[]{:S(2)}, u32[]{:S(2)}) collective-permute-start(bf16[2,1024,256]{2,1,0:T(8,128)(2,1)S(1)} %get-tuple-element.72.refs_1_.refs_3_), channel_id=1, source_target_pairs={{0,8},{2,10},{4,12},{6,14},{8,16},{10,18},{12,20},{14,22},{16,24},... | collective-permute-start | bytes 3145736 | tf_op jit(solution)/shard_map/ppermute | solution.py:638
  28.8 15.1 %collective-permute-start.5 = (bf16[1024,256]{1,0:T(8,128)(2,1)}, bf16[1024,256]{1,0:T(8,128)(2,1)S(1)}, u32[]{:S(2)}, u32[]{:S(2)}) collective-permute-start(bf16[1024,256]{1,0:T(8,128)(2,1)} %get-tuple-element.73), channel_id=1, source_target_pairs={{0,2},{2,0},{4,6},{6,4},{8,10},{10,8},{12,14},{14,12},{16,18},{18,... | collective-permute-start | bytes 1572872 | tf_op jit(solution)/shard_map/ppermute | solution.py:630
  30.4 24.5 %collective-permute-start.7 = (bf16[1024,256]{1,0:T(8,128)(2,1)}, bf16[1024,256]{1,0:T(8,128)(2,1)S(1)}, u32[]{:S(2)}, u32[]{:S(2)}) collective-permute-start(bf16[1024,256]{1,0:T(8,128)(2,1)} %get-tuple-element.76), channel_id=1, source_target_pairs={{0,4},{2,6},{4,0},{6,2},{8,12},{10,14},{12,8},{14,10},{16,20},{18,... | collective-permute-start | bytes 1572872 | tf_op jit(solution)/shard_map/ppermute | solution.py:630
  31.9 23.0 %collective-permute-start.8 = (bf16[1024,256]{1,0:T(8,128)(2,1)}, bf16[1024,256]{1,0:T(8,128)(2,1)}, u32[]{:S(2)}, u32[]{:S(2)}) collective-permute-start(bf16[1024,256]{1,0:T(8,128)(2,1)} %get-tuple-element.77), channel_id=1, source_target_pairs={{0,6},{2,4},{4,2},{6,0},{8,14},{10,12},{12,10},{14,8},{16,22},{18,... | collective-permute-start | bytes 1572872 | tf_op jit(solution)/shard_map/ppermute | solution.py:630
  32.4 21.1 %collective-permute-start.4 = (bf16[2,128,256]{2,1,0:T(8,128)(2,1)}, bf16[2,128,256]{2,1,0:T(8,128)(2,1)S(1)}, u32[]{:S(2)}, u32[]{:S(2)}) collective-permute-start(bf16[2,128,256]{2,1,0:T(8,128)(2,1)} %get-tuple-element.74), channel_id=1, source_target_pairs={{0,16},{2,18},{4,20},{6,22},{1,17},{3,19},{5,21},{7,23}} | collective-permute-start | bytes 393224 | tf_op jit(solution)/shard_map/ppermute | solution.py:677
  44.0 10.9 %collective-permute-start.6 = (bf16[2,128,256]{2,1,0:T(8,128)(2,1)}, bf16[2,128,256]{2,1,0:T(8,128)(2,1)S(1)}, u32[]{:S(2)}, u32[]{:S(2)}) collective-permute-start(bf16[2,128,256]{2,1,0:T(8,128)(2,1)} %get-tuple-element.74), channel_id=1, source_target_pairs={{0,24},{2,26},{4,28},{6,30},{1,25},{3,27},{5,29},{7,31}} | collective-permute-start | bytes 393224 | tf_op jit(solution)/shard_map/ppermute | solution.py:677
  54.9 1.0 copy-start
  58.8 9.5 %collective-permute-start.9 = (bf16[512,1024]{1,0:T(8,128)(2,1)S(1)}, bf16[512,1024]{1,0:T(8,128)(2,1)S(1)}, u32[]{:S(2)}, u32[]{:S(2)}) collective-permute-start(bf16[512,1024]{1,0:T(8,128)(2,1)S(1)} %get-tuple-element.80.mine_ref), channel_id=1, source_target_pairs={{0,1},{1,0},{2,3},{3,2},{4,5},{5,4},{6,7},{7,6},{8,9},{9,8},{10,11... | collective-permute-start | bytes 3145736 | tf_op jit(solution)/shard_map/ppermute | solution.py:684
  58.9 41.1 %collective-permute-start.18 = (bf16[2,1024,256]{2,1,0:T(8,128)(2,1)S(1)}, bf16[2,1024,256]{2,1,0:T(8,128)(2,1)S(1)}, u32[]{:S(2)}, u32[]{:S(2)}) collective-permute-start(bf16[2,1024,256]{2,1,0:T(8,128)(2,1)S(1)} %get-tuple-element.78.refs_0_), channel_id=1, source_target_pairs={{8,0},{10,2},{12,4},{14,6},{16,8},{18,10},{20,12},{22,14},{24,16},... | collective-permute-start | bytes 3145736 | tf_op jit(solution)/shard_map/ppermute | solution.py:638
  64.7 12.6 %collective-permute-start.10 = (bf16[1024,128]{1,0:T(8,128)(2,1)S(1)}, bf16[1024,128]{1,0:T(8,128)(2,1)S(1)}, u32[]{:S(2)}, u32[]{:S(2)}) collective-permute-start(bf16[1024,128]{1,0:T(8,128)(2,1)S(1)} %get-tuple-element.79.refs_0_), channel_id=1, source_target_pairs={{0,2},{2,0},{4,6},{6,4},{8,10},{10,8},{12,14},{14,12},{16,18},{18,... | collective-permute-start | bytes 786440 | tf_op jit(solution)/shard_map/ppermute | solution.py:630
  66.3 14.0 %collective-permute-start.11 = (bf16[1024,128]{1,0:T(8,128)(2,1)S(1)}, bf16[1024,128]{1,0:T(8,128)(2,1)S(1)}, u32[]{:S(2)}, u32[]{:S(2)}) collective-permute-start(bf16[1024,128]{1,0:T(8,128)(2,1)S(1)} %get-tuple-element.79.refs_0_), channel_id=1, source_target_pairs={{0,4},{2,6},{4,0},{6,2},{8,12},{10,14},{12,8},{14,10},{16,20},{18,... | collective-permute-start | bytes 786440 | tf_op jit(solution)/shard_map/ppermute | solution.py:630
  67.8 12.5 %collective-permute-start.12 = (bf16[1024,128]{1,0:T(8,128)(2,1)S(1)}, bf16[1024,128]{1,0:T(8,128)(2,1)S(1)}, u32[]{:S(2)}, u32[]{:S(2)}) collective-permute-start(bf16[1024,128]{1,0:T(8,128)(2,1)S(1)} %get-tuple-element.79.refs_0_), channel_id=1, source_target_pairs={{0,6},{2,4},{4,2},{6,0},{8,14},{10,12},{12,10},{14,8},{16,22},{18,... | collective-permute-start | bytes 786440 | tf_op jit(solution)/shard_map/ppermute | solution.py:630
  82.5 9.5 %collective-permute-start.13 = (bf16[1,256,512]{2,1,0:T(8,128)(2,1)S(1)}, bf16[1,256,512]{2,1,0:T(8,128)(2,1)S(1)}, u32[]{:S(2)}, u32[]{:S(2)}) collective-permute-start(bf16[1,256,512]{2,1,0:T(8,128)(2,1)S(1)} %get-tuple-element.90), channel_id=1, source_target_pairs={{0,8},{2,10},{4,12},{6,14},{8,0},{10,2},{12,4},{14,6},{16,24},{18,... | collective-permute-start | bytes 786440 | tf_op jit(solution)/shard_map/ppermute | solution.py:642
  84.9 16.3 %collective-permute-start.14 = (bf16[1024,128]{1,0:T(8,128)(2,1)S(1)}, bf16[1024,128]{1,0:T(8,128)(2,1)S(1)}, u32[]{:S(2)}, u32[]{:S(2)}) collective-permute-start(bf16[1024,128]{1,0:T(8,128)(2,1)S(1)} %get-tuple-element.97.refs_0_), channel_id=1, source_target_pairs={{0,2},{2,0},{4,6},{6,4},{8,10},{10,8},{12,14},{14,12},{16,18},{18,... | collective-permute-start | bytes 786440 | tf_op jit(solution)/shard_map/ppermute | solution.py:630
  86.1 16.4 %collective-permute-start.15 = (bf16[1024,128]{1,0:T(8,128)(2,1)S(1)}, bf16[1024,128]{1,0:T(8,128)(2,1)S(1)}, u32[]{:S(2)}, u32[]{:S(2)}) collective-permute-start(bf16[1024,128]{1,0:T(8,128)(2,1)S(1)} %get-tuple-element.97.refs_0_), channel_id=1, source_target_pairs={{0,4},{2,6},{4,0},{6,2},{8,12},{10,14},{12,8},{14,10},{16,20},{18,... | collective-permute-start | bytes 786440 | tf_op jit(solution)/shard_map/ppermute | solution.py:630
  87.0 16.9 %collective-permute-start.16 = (bf16[1024,128]{1,0:T(8,128)(2,1)S(1)}, bf16[1024,128]{1,0:T(8,128)(2,1)S(1)}, u32[]{:S(2)}, u32[]{:S(2)}) collective-permute-start(bf16[1024,128]{1,0:T(8,128)(2,1)S(1)} %get-tuple-element.97.refs_0_), channel_id=1, source_target_pairs={{0,6},{2,4},{4,2},{6,0},{8,14},{10,12},{12,10},{14,8},{16,22},{18,... | collective-permute-start | bytes 786440 | tf_op jit(solution)/shard_map/ppermute | solution.py:630
  92.0 16.7 %collective-permute-start.17 = (bf16[256,512]{1,0:T(8,128)(2,1)S(1)}, bf16[256,512]{1,0:T(8,128)(2,1)S(1)}, u32[]{:S(2)}, u32[]{:S(2)}) collective-permute-start(bf16[256,512]{1,0:T(8,128)(2,1)S(1)} %halve_0.1), channel_id=1, source_target_pairs={{0,16},{2,18},{4,20},{6,22},{8,24},{10,26},{12,28},{14,30},{16,0},... | collective-permute-start | bytes 786440 | tf_op jit(solution)/shard_map/ppermute | solution.py:642
  99.9 16.1 %collective-permute-start.20 = (bf16[2,128,256]{2,1,0:T(8,128)(2,1)S(1)}, bf16[2,128,256]{2,1,0:T(8,128)(2,1)S(1)}, u32[]{:S(2)}, u32[]{:S(2)}) collective-permute-start(bf16[2,128,256]{2,1,0:T(8,128)(2,1)S(1)} %get-tuple-element.105), channel_id=1, source_target_pairs={{16,0},{18,2},{20,4},{22,6},{17,1},{19,3},{21,5},{23,7}} | collective-permute-start | bytes 393224 | tf_op jit(solution)/shard_map/ppermute | solution.py:714
  101.2 14.8 %collective-permute-start.21 = (bf16[2,128,256]{2,1,0:T(8,128)(2,1)S(1)}, bf16[2,128,256]{2,1,0:T(8,128)(2,1)S(1)}, u32[]{:S(2)}, u32[]{:S(2)}) collective-permute-start(bf16[2,128,256]{2,1,0:T(8,128)(2,1)S(1)} %get-tuple-element.106), channel_id=1, source_target_pairs={{24,0},{26,2},{28,4},{30,6},{25,1},{27,3},{29,5},{31,7}} | collective-permute-start | bytes 393224 | tf_op jit(solution)/shard_map/ppermute | solution.py:714
  102.6 9.6 %collective-permute-start.19 = (f32[4,4,256]{2,1,0:T(4,128)S(1)}, f32[4,4,256]{2,1,0:T(4,128)S(1)}, u32[]{:S(2)}, u32[]{:S(2)}) collective-permute-start(f32[4,4,256]{2,1,0:T(4,128)S(1)} %get-tuple-element.102.stats_ref), channel_id=1, source_target_pairs={{8,0},{10,2},{12,4},{14,6},{16,8},{18,10},{20,12},{22,14},{24,16},... | collective-permute-start | bytes 49160 | tf_op jit(solution)/shard_map/ppermute | solution.py:638
  106.0 15.0 %collective-permute-start.25 = (bf16[1,256,512]{2,1,0:T(8,128)(2,1)S(1)}, bf16[1,256,512]{2,1,0:T(8,128)(2,1)S(1)}, u32[]{:S(2)}, u32[]{:S(2)}) collective-permute-start(bf16[1,256,512]{2,1,0:T(8,128)(2,1)S(1)} %get-tuple-element.117), channel_id=1, source_target_pairs={{0,8},{2,10},{4,12},{6,14},{8,0},{10,2},{12,4},{14,6},{16,24},{18,... | collective-permute-start | bytes 786440 | tf_op jit(solution)/shard_map/ppermute | solution.py:642
  116.9 22.8 %collective-permute-start.27 = (bf16[2,256,512]{2,1,0:T(8,128)(2,1)S(1)}, bf16[2,256,512]{2,1,0:T(8,128)(2,1)S(1)}, u32[]{:S(2)}, u32[]{:S(2)}) collective-permute-start(bf16[2,256,512]{2,1,0:T(8,128)(2,1)S(1)} %get-tuple-element.119), channel_id=1, source_target_pairs={{0,8},{2,10},{4,12},{6,14},{8,0},{10,2},{12,4},{14,6},{16,24},{18,... | collective-permute-start | bytes 1572872 | tf_op jit(solution)/shard_map/ppermute | solution.py:642
  117.5 12.0 %collective-permute-start.22 = (bf16[3,256,256]{2,1,0:T(8,128)(2,1)S(1)}, bf16[3,256,256]{2,1,0:T(8,128)(2,1)S(1)}, u32[]{:S(2)}, u32[]{:S(2)}) collective-permute-start(bf16[3,256,256]{2,1,0:T(8,128)(2,1)S(1)} %get-tuple-element.108), channel_id=1, source_target_pairs={{0,2},{2,0},{4,6},{6,4},{8,10},{10,8},{12,14},{14,12},{16,18},{18,... | collective-permute-start | bytes 1179656 | tf_op jit(solution)/shard_map/ppermute | solution.py:630
  119.1 18.8 %collective-permute-start.23 = (bf16[3,256,256]{2,1,0:T(8,128)(2,1)S(1)}, bf16[3,256,256]{2,1,0:T(8,128)(2,1)S(1)}, u32[]{:S(2)}, u32[]{:S(2)}) collective-permute-start(bf16[3,256,256]{2,1,0:T(8,128)(2,1)S(1)} %get-tuple-element.109), channel_id=1, source_target_pairs={{0,4},{2,6},{4,0},{6,2},{8,12},{10,14},{12,8},{14,10},{16,20},{18,... | collective-permute-start | bytes 1179656 | tf_op jit(solution)/shard_map/ppermute | solution.py:630
  120.6 17.3 %collective-permute-start.24 = (bf16[3,256,256]{2,1,0:T(8,128)(2,1)S(1)}, bf16[3,256,256]{2,1,0:T(8,128)(2,1)S(1)}, u32[]{:S(2)}, u32[]{:S(2)}) collective-permute-start(bf16[3,256,256]{2,1,0:T(8,128)(2,1)S(1)} %get-tuple-element.110), channel_id=1, source_target_pairs={{0,6},{2,4},{4,2},{6,0},{8,14},{10,12},{12,10},{14,8},{16,22},{18,... | collective-permute-start | bytes 1179656 | tf_op jit(solution)/shard_map/ppermute | solution.py:630
  121.1 18.6 %collective-permute-start.26 = (bf16[256,512]{1,0:T(8,128)(2,1)S(1)}, bf16[256,512]{1,0:T(8,128)(2,1)S(1)}, u32[]{:S(2)}, u32[]{:S(2)}) collective-permute-start(bf16[256,512]{1,0:T(8,128)(2,1)S(1)} %halve_1.1), channel_id=1, source_target_pairs={{0,16},{2,18},{4,20},{6,22},{8,24},{10,26},{12,28},{14,30},{16,0},... | collective-permute-start | bytes 786440 | tf_op jit(solution)/shard_map/ppermute | solution.py:642

commit v9 on v7

--- a/solution.py
+++ b/solution.py
@@ -688,8 +688,6 @@
         grads.append(got[1])
         far_grads = got[2]
         order = after(meta, got[0])
-        if h > 0:
-            order = after(order, next_stats)
         kept, first, odds, evens = project(h, mine, theirs, attn[h], first, order, group, parts)
         keep.append(kept)
         first, odds = [first], swap_groups(odds, 1)
@@ -697,7 +695,7 @@
         if h == 0:
             next_stats = shifted(after(stats, next_qd, *first), -1)
         if h < heads - 1:
-            sums, order, _ = add_up(h, odds, evens, first, order)
+            sums, order, _ = add_up(h, odds, evens, (first, next_stats), order)
             finals.append(sums)
     far_back = [
         lax.ppermute(piece, "seq", summary_route(index + 2, True))

time: 138 us -> 136 us (0.986)
  starting transfers between devices: 45.9 us -> 44 us
    ppermute x15, waiting for transfers between devices: 23 us -> 28.4 us  [swap(): return lax.ppermute(piece, 'seq', route)]
    ppermute x3, waiting for transfers between devices: 5.03 us -> 1.89 us  [shifted(): return lax.ppermute(piece, 'seq', route)]
    ppermute x5, starting transfers between devices: 10.3 us -> 7.48 us  [swap_groups(): return lax.ppermute(piece, 'seq', route)]
    ppermute x5, waiting for transfers between devices: 3.8 us -> 1.92 us  [swap_groups(): return lax.ppermute(piece, 'seq', route)]
  transfers between devices with their start and end apart: 28 -> 28, of which waited for: 11 -> 12; matrix products, arithmetic and copies ran while one was open for 1% -> 1% of each run, Pallas kernels for 29% -> 29%
where the time goes in v9:
time: 136 us
  Pallas kernels  46.3 us (34%)
  starting transfers between devices  44 us (32%)
  waiting for transfers between devices  39.6 us (29%)
  between operations  2.92 us (2%)
  local copies, waits for them, and re-layouts  2.41 us (2%)
    pallas_call x13, Pallas kernels, call(): pl.pallas_call(body, out_shape=outs, in_specs=[SMEM] * len(scalars) + [VM...  31.5 us
    ppermute x15, waiting for transfers between devices, swap(): return lax.ppermute(piece, 'seq', route)  28.4 us
    ppermute x15, starting transfers between devices, swap(): return lax.ppermute(piece, 'seq', route)  19.5 us
    pallas_call x1, Pallas kernels, grads_packed(): pl.pallas_call(body, out_shape=[shape((2 * rows + half * each, rows))] *...  8.73 us
    ppermute x2, starting transfers between devices, local(): lax.ppermute(strided if distance == 2 else later, 'seq', summary_route(di...  7.67 us
    ppermute x5, starting transfers between devices, swap_groups(): return lax.ppermute(piece, 'seq', route)  7.48 us
    ppermute x3, starting transfers between devices, shifted(): return lax.ppermute(piece, 'seq', route)  6.69 us
    ppermute x2, waiting for transfers between devices, local(): lax.ppermute(strided if distance == 2 else later, 'seq', summary_route(di...  5.68 us
  transfers between devices with their start and end apart: 28, of which 12 were waited for; matrix products, arithmetic and copies ran while one was open for 1% of the time, Pallas kernels for 29%

profile of v9, /device:TPU:0, one launch (start us, length us, event | category | flops | bytes accessed | tf_op | source)
XLA Modules:
  0.0 135.9 jit_solution(15926314724630700640)
XLA Ops:
  1.3 3.0 %pack_kv.1 = (bf16[2,256,256]{2,1,0:T(8,128)(2,1)}, bf16[2,256,256]{2,1,0:T(8,128)(2,1)}, bf16[2,256,256]{2,1,0:T(8,128)(2,1)}, bf16[2,256,256]{2,1,0:T(8,128)(2,1)}) custom-call(s32[3]{0:T(128)} %pad_add_fusion.1.meta_ref, bf16[256,1024]{1,0:T(8,128)(2,1)} %k_ref.1, bf16[256,1024]{1,0:T(8,128)(2,1)} %v_ref.1), custom_call_target="tpu_custom_call" | custom-call | flops 1 | bytes 1 | tf_op jit(solution)/shard_map/pack_kv/pallas_call | solution.py:93
  4.3 3.0 %collective-permute-start = (bf16[2,256,256]{2,1,0:T(8,128)(2,1)}, bf16[2,256,256]{2,1,0:T(8,128)(2,1)S(1)}, u32[]{:S(2)}, u32[]{:S(2)}) collective-permute-start(bf16[2,256,256]{2,1,0:T(8,128)(2,1)} %get-tuple-element.62), channel_id=1, source_target_pairs={{0,2},{2,0},{4,6},{6,4},{8,10},{10,8},{12,14},{14,12},{16,18},{18,... | collective-permute-start | bytes 786440 | tf_op jit(solution)/shard_map/ppermute | solution.py:617
  7.3 1.5 %collective-permute-start.1 = (bf16[2,256,256]{2,1,0:T(8,128)(2,1)}, bf16[2,256,256]{2,1,0:T(8,128)(2,1)S(1)}, u32[]{:S(2)}, u32[]{:S(2)}) collective-permute-start(bf16[2,256,256]{2,1,0:T(8,128)(2,1)} %get-tuple-element.67), channel_id=1, source_target_pairs={{0,4},{2,6},{4,0},{6,2},{8,12},{10,14},{12,8},{14,10},{16,20},{18,... | collective-permute-start | bytes 786440 | tf_op jit(solution)/shard_map/ppermute | solution.py:617
  12.1 2.5 %collective-permute-done.refs_1_ = bf16[2,256,256]{2,1,0:T(8,128)(2,1)S(1)} collective-permute-done((bf16[2,256,256]{2,1,0:T(8,128)(2,1)}, bf16[2,256,256]{2,1,0:T(8,128)(2,1)S(1)}, u32[]{:S(2)}, u32[]{:S(2)}) %collective-permute-start) | collective-permute-done | bytes 262176 | tf_op jit(solution)/shard_map/ppermute | solution.py:617
  14.6 8.7 %attn_grad.1 = (bf16[1024,256]{1,0:T(8,128)(2,1)}, bf16[1024,256]{1,0:T(8,128)(2,1)}, bf16[1024,256]{1,0:T(8,128)(2,1)}, bf16[1024,256]{1,0:T(8,128)(2,1)}) custom-call(s32[3]{0:T(128)} %pad_add_fusion.1.meta_ref, bf16[256,1024]{1,0:T(8,128)(2,1)} %q_ref.1, bf16[256,4096]{1,0:T(8,128)(2,1)} %og_ref.1, bf16[4096,1024]{1,0:T(8,128)(2,1)} %w_ref.1), custom_call_target="tpu_custom_call" | custom-call | flops 1 | bytes 1 | tf_op jit(solution)/shard_map/attn_grad/pallas_call | solution.py:152
  24.7 4.1 %collective-permute-start.3 = (bf16[2,1024,256]{2,1,0:T(8,128)(2,1)S(1)}, bf16[2,1024,256]{2,1,0:T(8,128)(2,1)S(1)}, u32[]{:S(2)}, u32[]{:S(2)}) collective-permute-start(bf16[2,1024,256]{2,1,0:T(8,128)(2,1)S(1)} %get-tuple-element.72.refs_1_.refs_3_), channel_id=1, source_target_pairs={{0,8},{2,10},{4,12},{6,14},{8,16},{10,18},{12,20},{14,22},{16,24},... | collective-permute-start | bytes 3145736 | tf_op jit(solution)/shard_map/ppermute | solution.py:625
  28.8 1.6 %collective-permute-start.5 = (bf16[1024,256]{1,0:T(8,128)(2,1)}, bf16[1024,256]{1,0:T(8,128)(2,1)S(1)}, u32[]{:S(2)}, u32[]{:S(2)}) collective-permute-start(bf16[1024,256]{1,0:T(8,128)(2,1)} %get-tuple-element.73), channel_id=1, source_target_pairs={{0,2},{2,0},{4,6},{6,4},{8,10},{10,8},{12,14},{14,12},{16,18},{18,... | collective-permute-start | bytes 1572872 | tf_op jit(solution)/shard_map/ppermute | solution.py:617
  30.4 1.5 %collective-permute-start.7 = (bf16[1024,256]{1,0:T(8,128)(2,1)}, bf16[1024,256]{1,0:T(8,128)(2,1)S(1)}, u32[]{:S(2)}, u32[]{:S(2)}) collective-permute-start(bf16[1024,256]{1,0:T(8,128)(2,1)} %get-tuple-element.76), channel_id=1, source_target_pairs={{0,4},{2,6},{4,0},{6,2},{8,12},{10,14},{12,8},{14,10},{16,20},{18,... | collective-permute-start | bytes 1572872 | tf_op jit(solution)/shard_map/ppermute | solution.py:617
  32.4 4.4 %collective-permute-start.4 = (bf16[2,128,256]{2,1,0:T(8,128)(2,1)}, bf16[2,128,256]{2,1,0:T(8,128)(2,1)S(1)}, u32[]{:S(2)}, u32[]{:S(2)}) collective-permute-start(bf16[2,128,256]{2,1,0:T(8,128)(2,1)} %get-tuple-element.74), channel_id=1, source_target_pairs={{0,16},{2,18},{4,20},{6,22},{1,17},{3,19},{5,21},{7,23}} | collective-permute-start | bytes 393224 | tf_op jit(solution)/shard_map/ppermute | solution.py:664
  36.8 7.2 %collective-permute-done.5.refs_1_ = bf16[1024,256]{1,0:T(8,128)(2,1)S(1)} collective-permute-done((bf16[1024,256]{1,0:T(8,128)(2,1)}, bf16[1024,256]{1,0:T(8,128)(2,1)S(1)}, u32[]{:S(2)}, u32[]{:S(2)}) %collective-permute-start.5) | collective-permute-done | bytes 524320 | tf_op jit(solution)/shard_map/ppermute | solution.py:617
  44.0 3.2 %collective-permute-start.6 = (bf16[2,128,256]{2,1,0:T(8,128)(2,1)}, bf16[2,128,256]{2,1,0:T(8,128)(2,1)S(1)}, u32[]{:S(2)}, u32[]{:S(2)}) collective-permute-start(bf16[2,128,256]{2,1,0:T(8,128)(2,1)} %get-tuple-element.74), channel_id=1, source_target_pairs={{0,24},{2,26},{4,28},{6,30},{1,25},{3,27},{5,29},{7,31}} | collective-permute-start | bytes 393224 | tf_op jit(solution)/shard_map/ppermute | solution.py:664
  47.3 1.9 %masks.1 = (f32[4,11,256]{2,1,0:T(8,128)S(1)}, f32[4,10,256]{2,1,0:T(8,128)S(1)}) custom-call(s32[4]{0:T(128)S(1)} %pad_add_fusion.meta_ref, s32[32,10]{1,0:T(8,128)S(1)} %copy.10.table), custom_call_target="tpu_custom_call" | custom-call | flops 1 | bytes 1 | tf_op jit(solution)/shard_map/masks/pallas_call | solution.py:47
  49.2 4.3 %collective-permute-done.4.refs_3_ = bf16[2,128,256]{2,1,0:T(8,128)(2,1)S(1)} collective-permute-done((bf16[2,128,256]{2,1,0:T(8,128)(2,1)}, bf16[2,128,256]{2,1,0:T(8,128)(2,1)S(1)}, u32[]{:S(2)}, u32[]{:S(2)}) %collective-permute-start.4) | collective-permute-done | bytes 131104 | tf_op jit(solution)/shard_map/ppermute | solution.py:664
  58.6 4.5 %attention_0.1 = (bf16[1024,128]{1,0:T(8,128)(2,1)S(1)}, f32[4,4,256]{2,1,0:T(4,128)S(1)}) custom-call(s32[4]{0:T(128)S(1)} %pad_add_fusion.meta_ref, f32[4,11,256]{2,1,0:T(8,128)S(1)} %get-tuple-element.71.bias_ref, f32[4,4,256]{2,1,0:T(4,128)S(1)} %broadcast_in_dim.3.before_ref, bf16[2,1024,256]{2,1,0:T(8,128)(2,1)S(1)} %get-tuple-element.78.refs_0_, ...), custom_call_target="tpu_custom_call" | custom-call | flops 1 | bytes 1 | tf_op jit(solution)/shard_map/attention_0/pallas_call | solution.py:47
  63.1 1.6 %collective-permute-start.10 = (bf16[1024,128]{1,0:T(8,128)(2,1)S(1)}, bf16[1024,128]{1,0:T(8,128)(2,1)S(1)}, u32[]{:S(2)}, u32[]{:S(2)}) collective-permute-start(bf16[1024,128]{1,0:T(8,128)(2,1)S(1)} %get-tuple-element.79.refs_0_), channel_id=1, source_target_pairs={{0,2},{2,0},{4,6},{6,4},{8,10},{10,8},{12,14},{14,12},{16,18},{18,... | collective-permute-start | bytes 786440 | tf_op jit(solution)/shard_map/ppermute | solution.py:617
  64.7 1.5 %collective-permute-start.11 = (bf16[1024,128]{1,0:T(8,128)(2,1)S(1)}, bf16[1024,128]{1,0:T(8,128)(2,1)S(1)}, u32[]{:S(2)}, u32[]{:S(2)}) collective-permute-start(bf16[1024,128]{1,0:T(8,128)(2,1)S(1)} %get-tuple-element.79.refs_0_), channel_id=1, source_target_pairs={{0,4},{2,6},{4,0},{6,2},{8,12},{10,14},{12,8},{14,10},{16,20},{18,... | collective-permute-start | bytes 786440 | tf_op jit(solution)/shard_map/ppermute | solution.py:617
  66.7 4.7 %attention_1.1 = (bf16[1024,128]{1,0:T(8,128)(2,1)S(1)}, f32[4,4,256]{2,1,0:T(4,128)S(1)}) custom-call(s32[4]{0:T(128)S(1)} %pad_add_fusion.meta_ref, f32[4,11,256]{2,1,0:T(8,128)S(1)} %get-tuple-element.71.bias_ref, f32[4,4,256]{2,1,0:T(4,128)S(1)} %get-tuple-element.82.before_ref, bf16[2,1024,256]{2,1,0:T(8,128)(2,1)S(1)} %get-tuple-element.78.refs_0_, ...), custom_call_target="tpu_custom_call" | custom-call | flops 1 | bytes 1 | tf_op jit(solution)/shard_map/attention_1/pallas_call | solution.py:47
  71.4 4.3 %attention_back_0.1 = (bf16[1024,128]{1,0:T(8,128)(2,1)S(1)}, f32[2,1024,128]{2,1,0:T(8,128)S(1)}, bf16[2,128,256]{2,1,0:T(8,128)(2,1)S(1)}, bf16[2,128,256]{2,1,0:T(8,128)(2,1)S(1)}) custom-call(s32[4]{0:T(128)S(1)} %pad_add_fusion.meta_ref, f32[4,11,256]{2,1,0:T(8,128)S(1)} %get-tuple-element.71.bias_ref, f32[4,4,256]{2,1,0:T(4,128)S(1)} %get-tuple-element.91.stats_ref, ...), custom_call_target="tpu_custom_call" | custom-call | flops 1 | bytes 1 | tf_op jit(solution)/shard_map/attention_back_0/pallas_call | solution.py:47
  75.7 3.0 %collective-permute-done.11.refs_2_ = bf16[1024,128]{1,0:T(8,128)(2,1)S(1)} collective-permute-done((bf16[1024,128]{1,0:T(8,128)(2,1)S(1)}, bf16[1024,128]{1,0:T(8,128)(2,1)S(1)}, u32[]{:S(2)}, u32[]{:S(2)}) %collective-permute-start.11) | collective-permute-done | bytes 262176 | tf_op jit(solution)/shard_map/ppermute | solution.py:617
  78.7 2.2 %project_0.1 = (f32[256,512]{1,0:T(8,128)S(1)}, bf16[1,256,512]{2,1,0:T(8,128)(2,1)S(1)}, bf16[1,256,512]{2,1,0:T(8,128)(2,1)S(1)}, f32[1,256,512]{2,1,0:T(8,128)S(1)}) custom-call(s32[4]{0:T(128)S(1)} %pad_add_fusion.meta_ref, bf16[512,1024]{1,0:T(8,128)(2,1)S(1)} %get-tuple-element.80.mine_ref, bf16[512,1024]{1,0:T(8,128)(2,1)S(1)} %collective-permute-done.9.theirs_ref, ...), custom_call_target="tpu_custom_call" | custom-call | flops 1 | bytes 1 | tf_op jit(solution)/shard_map/project_0/pallas_call | solution.py:47
  80.9 2.4 %collective-permute-start.13 = (bf16[1,256,512]{2,1,0:T(8,128)(2,1)S(1)}, bf16[1,256,512]{2,1,0:T(8,128)(2,1)S(1)}, u32[]{:S(2)}, u32[]{:S(2)}) collective-permute-start(bf16[1,256,512]{2,1,0:T(8,128)(2,1)S(1)} %get-tuple-element.90), channel_id=1, source_target_pairs={{0,8},{2,10},{4,12},{6,14},{8,0},{10,2},{12,4},{14,6},{16,24},{18,... | collective-permute-start | bytes 786440 | tf_op jit(solution)/shard_map/ppermute | solution.py:629
  86.4 1.6 %collective-permute-start.17 = (bf16[1024,128]{1,0:T(8,128)(2,1)S(1)}, bf16[1024,128]{1,0:T(8,128)(2,1)S(1)}, u32[]{:S(2)}, u32[]{:S(2)}) collective-permute-start(bf16[1024,128]{1,0:T(8,128)(2,1)S(1)} %get-tuple-element.98.refs_0_), channel_id=1, source_target_pairs={{0,4},{2,6},{4,0},{6,2},{8,12},{10,14},{12,8},{14,10},{16,20},{18,... | collective-permute-start | bytes 786440 | tf_op jit(solution)/shard_map/ppermute | solution.py:617
  90.8 3.4 %collective-permute-start.19 = (bf16[256,512]{1,0:T(8,128)(2,1)S(1)}, bf16[256,512]{1,0:T(8,128)(2,1)S(1)}, u32[]{:S(2)}, u32[]{:S(2)}) collective-permute-start(bf16[256,512]{1,0:T(8,128)(2,1)S(1)} %halve_0.1), channel_id=1, source_target_pairs={{0,16},{2,18},{4,20},{6,22},{8,24},{10,26},{12,28},{14,30},{16,0},... | collective-permute-start | bytes 786440 | tf_op jit(solution)/shard_map/ppermute | solution.py:629
  94.2 4.5 %attention_back_1.1 = (bf16[1024,128]{1,0:T(8,128)(2,1)S(1)}, f32[2,1024,128]{2,1,0:T(8,128)S(1)}, bf16[2,128,256]{2,1,0:T(8,128)(2,1)S(1)}, bf16[2,128,256]{2,1,0:T(8,128)(2,1)S(1)}) custom-call(s32[4]{0:T(128)S(1)} %pad_add_fusion.meta_ref, f32[4,11,256]{2,1,0:T(8,128)S(1)} %get-tuple-element.71.bias_ref, f32[4,4,256]{2,1,0:T(4,128)S(1)} %get-tuple-element.91.stats_ref, ...), custom_call_target="tpu_custom_call" | custom-call | flops 1 | bytes 1 | tf_op jit(solution)/shard_map/attention_back_1/pallas_call | solution.py:47
  101.4 2.1 %project_1.1 = (f32[256,512]{1,0:T(8,128)S(1)}, bf16[2,256,512]{2,1,0:T(8,128)(2,1)S(1)}, bf16[1,256,512]{2,1,0:T(8,128)(2,1)S(1)}, f32[1,256,512]{2,1,0:T(8,128)S(1)}) custom-call(s32[4]{0:T(128)S(1)} %pad_add_fusion.meta_ref, bf16[512,1024]{1,0:T(8,128)(2,1)S(1)} %get-tuple-element.80.mine_ref, bf16[512,1024]{1,0:T(8,128)(2,1)S(1)} %collective-permute-done.9.theirs_ref, ...), custom_call_target="tpu_custom_call" | custom-call | flops 1 | bytes 1 | tf_op jit(solution)/shard_map/project_1/pallas_call | solution.py:47
  105.7 3.9 %attention_back_next.1.own_ref = f32[2,1024,256]{2,1,0:T(8,128)S(1)} custom-call(s32[4]{0:T(128)S(1)} %pad_add_fusion.meta_ref, f32[4,10,256]{2,1,0:T(8,128)S(1)} %get-tuple-element.102.bias_ref, f32[4,4,256]{2,1,0:T(4,128)S(1)} %collective-permute-done.15.stats_ref, f32[2,1024,128]{2,1,0:T(8,128)S(1)} %get-tuple-element.103.refs_0_, ...), custom_call_target="tpu_custom_call" | custom-call | flops 1 | bytes 1 | tf_op jit(solution)/shard_map/attention_back_next/pallas_call | solution.py:47
  109.6 1.7 %collective-permute-done.20.refs_2_ = bf16[2,128,256]{2,1,0:T(8,128)(2,1)S(1)} collective-permute-done((bf16[2,128,256]{2,1,0:T(8,128)(2,1)S(1)}, bf16[2,128,256]{2,1,0:T(8,128)(2,1)S(1)}, u32[]{:S(2)}, u32[]{:S(2)}) %collective-permute-start.20) | collective-permute-done | bytes 131104 | tf_op jit(solution)/shard_map/ppermute | solution.py:701
  112.3 1.6 %collective-permute-start.22 = (bf16[3,256,256]{2,1,0:T(8,128)(2,1)S(1)}, bf16[3,256,256]{2,1,0:T(8,128)(2,1)S(1)}, u32[]{:S(2)}, u32[]{:S(2)}) collective-permute-start(bf16[3,256,256]{2,1,0:T(8,128)(2,1)S(1)} %get-tuple-element.108), channel_id=1, source_target_pairs={{0,2},{2,0},{4,6},{6,4},{8,10},{10,8},{12,14},{14,12},{16,18},{18,... | collective-permute-start | bytes 1179656 | tf_op jit(solution)/shard_map/ppermute | solution.py:617
  113.8 1.5 %collective-permute-start.23 = (bf16[3,256,256]{2,1,0:T(8,128)(2,1)S(1)}, bf16[3,256,256]{2,1,0:T(8,128)(2,1)S(1)}, u32[]{:S(2)}, u32[]{:S(2)}) collective-permute-start(bf16[3,256,256]{2,1,0:T(8,128)(2,1)S(1)} %get-tuple-element.109), channel_id=1, source_target_pairs={{0,4},{2,6},{4,0},{6,2},{8,12},{10,14},{12,8},{14,10},{16,20},{18,... | collective-permute-start | bytes 1179656 | tf_op jit(solution)/shard_map/ppermute | solution.py:617
  117.2 7.1 %collective-permute-done.22.refs_1_ = bf16[3,256,256]{2,1,0:T(8,128)(2,1)S(1)} collective-permute-done((bf16[3,256,256]{2,1,0:T(8,128)(2,1)S(1)}, bf16[3,256,256]{2,1,0:T(8,128)(2,1)S(1)}, u32[]{:S(2)}, u32[]{:S(2)}) %collective-permute-start.22) | collective-permute-done | bytes 393248 | tf_op jit(solution)/shard_map/ppermute | solution.py:617
  124.3 8.6 %collective-permute-done.23.refs_2_ = bf16[3,256,256]{2,1,0:T(8,128)(2,1)S(1)} collective-permute-done((bf16[3,256,256]{2,1,0:T(8,128)(2,1)S(1)}, bf16[3,256,256]{2,1,0:T(8,128)(2,1)S(1)}, u32[]{:S(2)}, u32[]{:S(2)}) %collective-permute-start.23) | collective-permute-done | bytes 393248 | tf_op jit(solution)/shard_map/ppermute | solution.py:617
  133.0 1.8 %unpack.1 = (bf16[256,1024]{1,0:T(8,128)(2,1)}, bf16[256,1024]{1,0:T(8,128)(2,1)}, bf16[256,1024]{1,0:T(8,128)(2,1)}) custom-call(s32[4]{0:T(128)S(1)} %pad_add_fusion.meta_ref, bf16[3,256,256]{2,1,0:T(8,128)(2,1)S(1)} %get-tuple-element.107.refs_0_, bf16[3,256,256]{2,1,0:T(8,128)(2,1)S(1)} %collective-permute-done.22.refs_1_, ...), custom_call_target="tpu_custom_call" | custom-call | flops 1 | bytes 1 | tf_op jit(solution)/shard_map/unpack/pallas_call | solution.py:584
  (53 shorter events, 24.1 us)
Async XLA Ops:
  4.3 10.3 %collective-permute-start = (bf16[2,256,256]{2,1,0:T(8,128)(2,1)}, bf16[2,256,256]{2,1,0:T(8,128)(2,1)S(1)}, u32[]{:S(2)}, u32[]{:S(2)}) collective-permute-start(bf16[2,256,256]{2,1,0:T(8,128)(2,1)} %get-tuple-element.62), channel_id=1, source_target_pairs={{0,2},{2,0},{4,6},{6,4},{8,10},{10,8},{12,14},{14,12},{16,18},{18,... | collective-permute-start | bytes 786440 | tf_op jit(solution)/shard_map/ppermute | solution.py:617
  7.3 16.1 %collective-permute-start.1 = (bf16[2,256,256]{2,1,0:T(8,128)(2,1)}, bf16[2,256,256]{2,1,0:T(8,128)(2,1)S(1)}, u32[]{:S(2)}, u32[]{:S(2)}) collective-permute-start(bf16[2,256,256]{2,1,0:T(8,128)(2,1)} %get-tuple-element.67), channel_id=1, source_target_pairs={{0,4},{2,6},{4,0},{6,2},{8,12},{10,14},{12,8},{14,10},{16,20},{18,... | collective-permute-start | bytes 786440 | tf_op jit(solution)/shard_map/ppermute | solution.py:617
  8.8 14.6 %collective-permute-start.2 = (bf16[2,256,256]{2,1,0:T(8,128)(2,1)}, bf16[2,256,256]{2,1,0:T(8,128)(2,1)S(1)}, u32[]{:S(2)}, u32[]{:S(2)}) collective-permute-start(bf16[2,256,256]{2,1,0:T(8,128)(2,1)} %get-tuple-element.68), channel_id=1, source_target_pairs={{0,6},{2,4},{4,2},{6,0},{8,14},{10,12},{12,10},{14,8},{16,22},{18,... | collective-permute-start | bytes 786440 | tf_op jit(solution)/shard_map/ppermute | solution.py:617
  12.1 11.3 %copy-start.1 = (bf16[2,256,256]{2,1,0:T(8,128)(2,1)S(1)}, bf16[2,256,256]{2,1,0:T(8,128)(2,1)}, u32[]{:S(2)}) copy-start(bf16[2,256,256]{2,1,0:T(8,128)(2,1)} %get-tuple-element.66.refs_0_) | copy-start | bytes 786436
  12.1 35.1 %copy-start.2 = (s32[32,10]{0,1:T(8,128)S(1)}, s32[32,10]{0,1:T(8,128)}, u32[]{:S(2)}) copy-start(s32[32,10]{0,1:T(8,128)} %param.11) | copy-start | bytes 3844
  24.7 30.2 %collective-permute-start.3 = (bf16[2,1024,256]{2,1,0:T(8,128)(2,1)S(1)}, bf16[2,1024,256]{2,1,0:T(8,128)(2,1)S(1)}, u32[]{:S(2)}, u32[]{:S(2)}) collective-permute-start(bf16[2,1024,256]{2,1,0:T(8,128)(2,1)S(1)} %get-tuple-element.72.refs_1_.refs_3_), channel_id=1, source_target_pairs={{0,8},{2,10},{4,12},{6,14},{8,16},{10,18},{12,20},{14,22},{16,24},... | collective-permute-start | bytes 3145736 | tf_op jit(solution)/shard_map/ppermute | solution.py:625
  28.8 15.1 %collective-permute-start.5 = (bf16[1024,256]{1,0:T(8,128)(2,1)}, bf16[1024,256]{1,0:T(8,128)(2,1)S(1)}, u32[]{:S(2)}, u32[]{:S(2)}) collective-permute-start(bf16[1024,256]{1,0:T(8,128)(2,1)} %get-tuple-element.73), channel_id=1, source_target_pairs={{0,2},{2,0},{4,6},{6,4},{8,10},{10,8},{12,14},{14,12},{16,18},{18,... | collective-permute-start | bytes 1572872 | tf_op jit(solution)/shard_map/ppermute | solution.py:617
  30.4 24.5 %collective-permute-start.7 = (bf16[1024,256]{1,0:T(8,128)(2,1)}, bf16[1024,256]{1,0:T(8,128)(2,1)S(1)}, u32[]{:S(2)}, u32[]{:S(2)}) collective-permute-start(bf16[1024,256]{1,0:T(8,128)(2,1)} %get-tuple-element.76), channel_id=1, source_target_pairs={{0,4},{2,6},{4,0},{6,2},{8,12},{10,14},{12,8},{14,10},{16,20},{18,... | collective-permute-start | bytes 1572872 | tf_op jit(solution)/shard_map/ppermute | solution.py:617
  31.9 23.0 %collective-permute-start.8 = (bf16[1024,256]{1,0:T(8,128)(2,1)}, bf16[1024,256]{1,0:T(8,128)(2,1)}, u32[]{:S(2)}, u32[]{:S(2)}) collective-permute-start(bf16[1024,256]{1,0:T(8,128)(2,1)} %get-tuple-element.77), channel_id=1, source_target_pairs={{0,6},{2,4},{4,2},{6,0},{8,14},{10,12},{12,10},{14,8},{16,22},{18,... | collective-permute-start | bytes 1572872 | tf_op jit(solution)/shard_map/ppermute | solution.py:617
  32.4 21.1 %collective-permute-start.4 = (bf16[2,128,256]{2,1,0:T(8,128)(2,1)}, bf16[2,128,256]{2,1,0:T(8,128)(2,1)S(1)}, u32[]{:S(2)}, u32[]{:S(2)}) collective-permute-start(bf16[2,128,256]{2,1,0:T(8,128)(2,1)} %get-tuple-element.74), channel_id=1, source_target_pairs={{0,16},{2,18},{4,20},{6,22},{1,17},{3,19},{5,21},{7,23}} | collective-permute-start | bytes 393224 | tf_op jit(solution)/shard_map/ppermute | solution.py:664
  44.0 10.9 %collective-permute-start.6 = (bf16[2,128,256]{2,1,0:T(8,128)(2,1)}, bf16[2,128,256]{2,1,0:T(8,128)(2,1)S(1)}, u32[]{:S(2)}, u32[]{:S(2)}) collective-permute-start(bf16[2,128,256]{2,1,0:T(8,128)(2,1)} %get-tuple-element.74), channel_id=1, source_target_pairs={{0,24},{2,26},{4,28},{6,30},{1,25},{3,27},{5,29},{7,31}} | collective-permute-start | bytes 393224 | tf_op jit(solution)/shard_map/ppermute | solution.py:664
  54.9 1.0 copy-start
  57.2 9.5 %collective-permute-start.9 = (bf16[512,1024]{1,0:T(8,128)(2,1)S(1)}, bf16[512,1024]{1,0:T(8,128)(2,1)S(1)}, u32[]{:S(2)}, u32[]{:S(2)}) collective-permute-start(bf16[512,1024]{1,0:T(8,128)(2,1)S(1)} %get-tuple-element.80.mine_ref), channel_id=1, source_target_pairs={{0,1},{1,0},{2,3},{3,2},{4,5},{5,4},{6,7},{7,6},{8,9},{9,8},{10,11... | collective-permute-start | bytes 3145736 | tf_op jit(solution)/shard_map/ppermute | solution.py:671
  57.3 27.8 %collective-permute-start.14 = (bf16[2,1024,256]{2,1,0:T(8,128)(2,1)S(1)}, bf16[2,1024,256]{2,1,0:T(8,128)(2,1)S(1)}, u32[]{:S(2)}, u32[]{:S(2)}) collective-permute-start(bf16[2,1024,256]{2,1,0:T(8,128)(2,1)S(1)} %get-tuple-element.78.refs_0_), channel_id=1, source_target_pairs={{8,0},{10,2},{12,4},{14,6},{16,8},{18,10},{20,12},{22,14},{24,16},... | collective-permute-start | bytes 3145736 | tf_op jit(solution)/shard_map/ppermute | solution.py:625
  63.1 12.6 %collective-permute-start.10 = (bf16[1024,128]{1,0:T(8,128)(2,1)S(1)}, bf16[1024,128]{1,0:T(8,128)(2,1)S(1)}, u32[]{:S(2)}, u32[]{:S(2)}) collective-permute-start(bf16[1024,128]{1,0:T(8,128)(2,1)S(1)} %get-tuple-element.79.refs_0_), channel_id=1, source_target_pairs={{0,2},{2,0},{4,6},{6,4},{8,10},{10,8},{12,14},{14,12},{16,18},{18,... | collective-permute-start | bytes 786440 | tf_op jit(solution)/shard_map/ppermute | solution.py:617
  64.7 14.0 %collective-permute-start.11 = (bf16[1024,128]{1,0:T(8,128)(2,1)S(1)}, bf16[1024,128]{1,0:T(8,128)(2,1)S(1)}, u32[]{:S(2)}, u32[]{:S(2)}) collective-permute-start(bf16[1024,128]{1,0:T(8,128)(2,1)S(1)} %get-tuple-element.79.refs_0_), channel_id=1, source_target_pairs={{0,4},{2,6},{4,0},{6,2},{8,12},{10,14},{12,8},{14,10},{16,20},{18,... | collective-permute-start | bytes 786440 | tf_op jit(solution)/shard_map/ppermute | solution.py:617
  66.2 12.5 %collective-permute-start.12 = (bf16[1024,128]{1,0:T(8,128)(2,1)S(1)}, bf16[1024,128]{1,0:T(8,128)(2,1)S(1)}, u32[]{:S(2)}, u32[]{:S(2)}) collective-permute-start(bf16[1024,128]{1,0:T(8,128)(2,1)S(1)} %get-tuple-element.79.refs_0_), channel_id=1, source_target_pairs={{0,6},{2,4},{4,2},{6,0},{8,14},{10,12},{12,10},{14,8},{16,22},{18,... | collective-permute-start | bytes 786440 | tf_op jit(solution)/shard_map/ppermute | solution.py:617
  80.9 9.9 %collective-permute-start.13 = (bf16[1,256,512]{2,1,0:T(8,128)(2,1)S(1)}, bf16[1,256,512]{2,1,0:T(8,128)(2,1)S(1)}, u32[]{:S(2)}, u32[]{:S(2)}) collective-permute-start(bf16[1,256,512]{2,1,0:T(8,128)(2,1)S(1)} %get-tuple-element.90), channel_id=1, source_target_pairs={{0,8},{2,10},{4,12},{6,14},{8,0},{10,2},{12,4},{14,6},{16,24},{18,... | collective-permute-start | bytes 786440 | tf_op jit(solution)/shard_map/ppermute | solution.py:629
  83.3 16.7 %collective-permute-start.16 = (bf16[1024,128]{1,0:T(8,128)(2,1)S(1)}, bf16[1024,128]{1,0:T(8,128)(2,1)S(1)}, u32[]{:S(2)}, u32[]{:S(2)}) collective-permute-start(bf16[1024,128]{1,0:T(8,128)(2,1)S(1)} %get-tuple-element.98.refs_0_), channel_id=1, source_target_pairs={{0,2},{2,0},{4,6},{6,4},{8,10},{10,8},{12,14},{14,12},{16,18},{18,... | collective-permute-start | bytes 786440 | tf_op jit(solution)/shard_map/ppermute | solution.py:617
  85.1 5.6 %collective-permute-start.15 = (f32[4,4,256]{2,1,0:T(4,128)S(1)}, f32[4,4,256]{2,1,0:T(4,128)S(1)}, u32[]{:S(2)}, u32[]{:S(2)}) collective-permute-start(f32[4,4,256]{2,1,0:T(4,128)S(1)} %get-tuple-element.91.stats_ref), channel_id=1, source_target_pairs={{8,0},{10,2},{12,4},{14,6},{16,8},{18,10},{20,12},{22,14},{24,16},... | collective-permute-start | bytes 49160 | tf_op jit(solution)/shard_map/ppermute | solution.py:625
  86.4 14.9 %collective-permute-start.17 = (bf16[1024,128]{1,0:T(8,128)(2,1)S(1)}, bf16[1024,128]{1,0:T(8,128)(2,1)S(1)}, u32[]{:S(2)}, u32[]{:S(2)}) collective-permute-start(bf16[1024,128]{1,0:T(8,128)(2,1)S(1)} %get-tuple-element.98.refs_0_), channel_id=1, source_target_pairs={{0,4},{2,6},{4,0},{6,2},{8,12},{10,14},{12,8},{14,10},{16,20},{18,... | collective-permute-start | bytes 786440 | tf_op jit(solution)/shard_map/ppermute | solution.py:617
  88.0 13.4 %collective-permute-start.18 = (bf16[1024,128]{1,0:T(8,128)(2,1)S(1)}, bf16[1024,128]{1,0:T(8,128)(2,1)S(1)}, u32[]{:S(2)}, u32[]{:S(2)}) collective-permute-start(bf16[1024,128]{1,0:T(8,128)(2,1)S(1)} %get-tuple-element.98.refs_0_), channel_id=1, source_target_pairs={{0,6},{2,4},{4,2},{6,0},{8,14},{10,12},{12,10},{14,8},{16,22},{18,... | collective-permute-start | bytes 786440 | tf_op jit(solution)/shard_map/ppermute | solution.py:617
  90.8 14.9 %collective-permute-start.19 = (bf16[256,512]{1,0:T(8,128)(2,1)S(1)}, bf16[256,512]{1,0:T(8,128)(2,1)S(1)}, u32[]{:S(2)}, u32[]{:S(2)}) collective-permute-start(bf16[256,512]{1,0:T(8,128)(2,1)S(1)} %halve_0.1), channel_id=1, source_target_pairs={{0,16},{2,18},{4,20},{6,22},{8,24},{10,26},{12,28},{14,30},{16,0},... | collective-permute-start | bytes 786440 | tf_op jit(solution)/shard_map/ppermute | solution.py:629
  98.8 12.5 %collective-permute-start.20 = (bf16[2,128,256]{2,1,0:T(8,128)(2,1)S(1)}, bf16[2,128,256]{2,1,0:T(8,128)(2,1)S(1)}, u32[]{:S(2)}, u32[]{:S(2)}) collective-permute-start(bf16[2,128,256]{2,1,0:T(8,128)(2,1)S(1)} %get-tuple-element.105), channel_id=1, source_target_pairs={{16,0},{18,2},{20,4},{22,6},{17,1},{19,3},{21,5},{23,7}} | collective-permute-start | bytes 393224 | tf_op jit(solution)/shard_map/ppermute | solution.py:701
  100.1 11.2 %collective-permute-start.21 = (bf16[2,128,256]{2,1,0:T(8,128)(2,1)S(1)}, bf16[2,128,256]{2,1,0:T(8,128)(2,1)S(1)}, u32[]{:S(2)}, u32[]{:S(2)}) collective-permute-start(bf16[2,128,256]{2,1,0:T(8,128)(2,1)S(1)} %get-tuple-element.106), channel_id=1, source_target_pairs={{24,0},{26,2},{28,4},{30,6},{25,1},{27,3},{29,5},{31,7}} | collective-permute-start | bytes 393224 | tf_op jit(solution)/shard_map/ppermute | solution.py:701
  103.5 13.4 %collective-permute-start.25 = (bf16[1,256,512]{2,1,0:T(8,128)(2,1)S(1)}, bf16[1,256,512]{2,1,0:T(8,128)(2,1)S(1)}, u32[]{:S(2)}, u32[]{:S(2)}) collective-permute-start(bf16[1,256,512]{2,1,0:T(8,128)(2,1)S(1)} %get-tuple-element.117), channel_id=1, source_target_pairs={{0,8},{2,10},{4,12},{6,14},{8,0},{10,2},{12,4},{14,6},{16,24},{18,... | collective-permute-start | bytes 786440 | tf_op jit(solution)/shard_map/ppermute | solution.py:629
  112.2 22.6 %collective-permute-start.27 = (bf16[2,256,512]{2,1,0:T(8,128)(2,1)S(1)}, bf16[2,256,512]{2,1,0:T(8,128)(2,1)S(1)}, u32[]{:S(2)}, u32[]{:S(2)}) collective-permute-start(bf16[2,256,512]{2,1,0:T(8,128)(2,1)S(1)} %get-tuple-element.119), channel_id=1, source_target_pairs={{0,8},{2,10},{4,12},{6,14},{8,0},{10,2},{12,4},{14,6},{16,24},{18,... | collective-permute-start | bytes 1572872 | tf_op jit(solution)/shard_map/ppermute | solution.py:629
  112.3 12.1 %collective-permute-start.22 = (bf16[3,256,256]{2,1,0:T(8,128)(2,1)S(1)}, bf16[3,256,256]{2,1,0:T(8,128)(2,1)S(1)}, u32[]{:S(2)}, u32[]{:S(2)}) collective-permute-start(bf16[3,256,256]{2,1,0:T(8,128)(2,1)S(1)} %get-tuple-element.108), channel_id=1, source_target_pairs={{0,2},{2,0},{4,6},{6,4},{8,10},{10,8},{12,14},{14,12},{16,18},{18,... | collective-permute-start | bytes 1179656 | tf_op jit(solution)/shard_map/ppermute | solution.py:617
  113.8 19.1 %collective-permute-start.23 = (bf16[3,256,256]{2,1,0:T(8,128)(2,1)S(1)}, bf16[3,256,256]{2,1,0:T(8,128)(2,1)S(1)}, u32[]{:S(2)}, u32[]{:S(2)}) collective-permute-start(bf16[3,256,256]{2,1,0:T(8,128)(2,1)S(1)} %get-tuple-element.109), channel_id=1, source_target_pairs={{0,4},{2,6},{4,0},{6,2},{8,12},{10,14},{12,8},{14,10},{16,20},{18,... | collective-permute-start | bytes 1179656 | tf_op jit(solution)/shard_map/ppermute | solution.py:617
  115.4 17.6 %collective-permute-start.24 = (bf16[3,256,256]{2,1,0:T(8,128)(2,1)S(1)}, bf16[3,256,256]{2,1,0:T(8,128)(2,1)S(1)}, u32[]{:S(2)}, u32[]{:S(2)}) collective-permute-start(bf16[3,256,256]{2,1,0:T(8,128)(2,1)S(1)} %get-tuple-element.110), channel_id=1, source_target_pairs={{0,6},{2,4},{4,2},{6,0},{8,14},{10,12},{12,10},{14,8},{16,22},{18,... | collective-permute-start | bytes 1179656 | tf_op jit(solution)/shard_map/ppermute | solution.py:617
  116.9 17.8 %collective-permute-start.26 = (bf16[256,512]{1,0:T(8,128)(2,1)S(1)}, bf16[256,512]{1,0:T(8,128)(2,1)S(1)}, u32[]{:S(2)}, u32[]{:S(2)}) collective-permute-start(bf16[256,512]{1,0:T(8,128)(2,1)S(1)} %halve_1.1), channel_id=1, source_target_pairs={{0,16},{2,18},{4,20},{6,22},{8,24},{10,26},{12,28},{14,30},{16,0},... | collective-permute-start | bytes 786440 | tf_op jit(solution)/shard_map/ppermute | solution.py:629

commit v10 on v9

--- a/solution.py
+++ b/solution.py
@@ -354,18 +354,20 @@
     )
 
 
-def backward(head, qd, own, prev, far, before, bias, stats, meta, group, slots):
+def backward(head, qd, own, prev, far, before, carry, bias, stats, meta, group, slots):
     whole, width = qd.shape[1:]
     pairs = whole // PAIR
-    counts = (3, len(far), len(before))
+    counts = (3, len(far), len(before), len(carry))
+    rows = whole // group
+    cut = group if carry else 1
     everything = 2 * whole + slots * BLK
 
     def body(meta_ref, bias_ref, stats_ref, *refs):
-        (around, far_refs, before_refs), refs = split_refs(refs, counts)
+        (around, far_refs, before_refs, carry_refs), refs = split_refs(refs, counts)
         qd_ref, *around = one_head(around, head)
         far_refs = one_head(far_refs, head)
-        ((dq_ref, grad_ref), far_outs), refs = split_refs(refs, (2, len(far)))
-        k_pool, v_pool, far_sum = refs
+        ((grad_ref,), far_outs, dq_outs), refs = split_refs(refs, (1, len(far), cut))
+        k_pool, v_pool, far_sum, dq_ref = refs
         at_group = meta_ref[1]
         fill_pools(meta_ref, *around, far_refs, k_pool, v_pool, slots)
         masks = causal_masks()
@@ -390,6 +392,13 @@
             grad_ref[1, mine, :] += dot(low[others:end], grad, NN)
             far_sum[0] += dot(ds[end:], query, NN)
             far_sum[1] += dot(low[end:], grad, NN)
+        if carry:
+            for k in range(group):
+                piece = pl.ds(pl.multiple_of((meta_ref[0] ^ k) * rows, rows), rows)
+                dq_outs[k][whole:, :] = dq_ref[piece, :]
+                dq_outs[k][:whole, :] = carry_refs[0][...]
+        else:
+            dq_outs[0][...] = dq_ref[...]
         for index, ref in enumerate(far_outs):
             slot = jnp.maximum(at_group - index - 2, 0) // 2
             start = pl.multiple_of(slot * BLK, BLK)
@@ -400,18 +409,20 @@
 
     span = (SPAN + slots) * BLK
     outs = call(
-        body, (meta,), (bias, stats, qd, own, prev, *far, *before),
-        [shape((whole, HD)), shape((2, whole, HD), jnp.float32)]
-        + [shape((2, BLK, width))] * len(far),
+        body, (meta,), (bias, stats, qd, own, prev, *far, *before, *carry),
+        [shape((2, whole, HD), jnp.float32)]
+        + [shape((2, BLK, width))] * len(far)
+        + [shape((whole + rows if carry else whole, HD))] * cut,
         [
             pltpu.VMEM((everything, HD), jnp.bfloat16),
             pltpu.VMEM((everything, HD), jnp.bfloat16),
             pltpu.VMEM((2, slots * BLK, HD), jnp.float32),
+            pltpu.VMEM((whole, HD), jnp.bfloat16),
         ],
         cost(8 * whole * span * HD * 2, 4 * 1024 * 1024, whole * span),
         f"attention_back_{head}", 24,
     )
-    return outs[0], outs[1], outs[2:]
+    return outs[0], outs[1 : 1 + len(far)], outs[1 + len(far) :]
 
 
 def backward_next(grads, qd, own, bias, stats, meta):
@@ -456,9 +467,10 @@
 
 def combine(dq, own, far, meta, group, rows):
     whole, width = own.shape[1:]
-
-    def body(meta_ref, own_ref, *refs):
-        (dq_refs, far_refs, outs, (acc,)), refs = split_refs(refs, (len(dq), len(far), group, 1))
+    heads = width // HD
+
+    def body(meta_ref, dq_ref, own_ref, *refs):
+        (far_refs, outs, (acc,)), refs = split_refs(refs, (len(far), group, 1))
         me, offset = meta_ref[0], meta_ref[2]
         acc[...] = own_ref[...]
         at = pl.multiple_of(offset * BLK, BLK)
@@ -466,13 +478,14 @@
             acc[:, pl.ds(at, BLK), :] += ref[...].astype(jnp.float32)
         for k in range(group):
             here = pl.ds(pl.multiple_of((me ^ k) * rows, rows), rows)
-            for h in range(len(dq)):
-                outs[k][0, :, h * HD : (h + 1) * HD] = dq_refs[h][here, :]
-            outs[k][1] = acc[0, here, :].astype(jnp.bfloat16)
-            outs[k][2] = acc[1, here, :].astype(jnp.bfloat16)
+            outs[k][0] = dq_ref[here, :]
+            for which in range(2):
+                for h in range(heads):
+                    lanes = slice(h * HD, (h + 1) * HD)
+                    outs[k][1 + which * heads + h] = acc[which, here, lanes].astype(jnp.bfloat16)
 
     return call(
-        body, (meta,), (own, *dq, *far), [shape((3, rows, width))] * group,
+        body, (meta,), (dq, own, *far), [shape((1 + 2 * heads, rows, HD))] * group,
         [pltpu.VMEM((2, whole, width), jnp.float32)],
         cost(0, 4 * 1024 * 1024), "combine",
     )
@@ -492,7 +505,7 @@
         me, at_group, core = meta_ref[0], meta_ref[1], meta_ref[3]
         for k in range(group):
             at = pl.multiple_of((me ^ k) * HD, HD)
-            pool[:, pl.ds(at, HD)] = attn_refs[k][...]
+            pool[:, pl.ds(at, HD)] = attn_refs[k][:whole, :]
         upper = pl.ds(pl.multiple_of(core * height, height), height)
         lower = pl.ds(pl.multiple_of((1 - core) * height, height), height)
         total[upper, :] = dot(mine_ref[...], pool[...], NN)
@@ -565,32 +578,34 @@
     )[0]
 
 
-def unpack(pieces, meta, group):
-    rows, width = pieces[0].shape[1:]
+def unpack(early, pieces, meta, group):
+    count, rows, _ = pieces[0].shape
+    heads = (count - 1) // 2
+    whole = early[0].shape[0] - rows
 
     def body(meta_ref, *refs):
+        (early_refs, piece_refs, outs, (sems,)), refs = split_refs(refs, (group, group, 3, 1))
         me = meta_ref[0]
-        outs, sems = refs[group:-1], refs[-1]
         copies = []
         for k in range(group):
-            at = pl.ds(pl.multiple_of((me ^ k) * width, width), width)
-            for which in range(3):
-                target = outs[which].at[:, at]
-                copies.append(
-                    pltpu.make_async_copy(refs[k].at[which], target, sems.at[k, which])
-                )
+            sources = [early_refs[k].at[pl.ds(whole, rows), :]]
+            sources += [piece_refs[k].at[which] for which in range(count)]
+            for which, source in enumerate(sources):
+                at = (me ^ k) * heads * HD + (which % heads) * HD
+                target = outs[which // heads].at[:, pl.ds(pl.multiple_of(at, HD), HD)]
+                copies.append(pltpu.make_async_copy(source, target, sems.at[k, which]))
         copied(*copies)
 
     return pl.pallas_call(
         body,
-        out_shape=[shape((rows, group * width))] * 3,
-        in_specs=[SMEM] + [ANY] * group,
+        out_shape=[shape((rows, group * heads * HD))] * 3,
+        in_specs=[SMEM] + [ANY] * (2 * group),
         out_specs=[ANY] * 3,
-        scratch_shapes=[pltpu.SemaphoreType.DMA((group, 3))],
+        scratch_shapes=[pltpu.SemaphoreType.DMA((group, count + 1))],
         compiler_params=params(16),
         cost_estimate=cost(0, 3 * MIB),
         name="unpack",
-    )(meta, *pieces)
+    )(meta, *early, *pieces)
 
 
 def after(value, *others):
@@ -676,17 +691,26 @@
     attn = []
     for h in range(heads):
         got, stats = forward(h, qd, pool, prev, far, bias, stats, order, group, slots)
-        attn.append([got] + [swap(got, k) for k in range(1, group)])
+        attn.append(got)
+        if h == 0:
+            attn[0] = [got] + [swap(got, k) for k in range(1, group)]
         order = after(meta, got, theirs)
 
-    dq, grads, keep, finals = [], [], [], []
+    assert heads == 2
+    grads, keep, finals = [], [], []
     far_grads = [jnp.zeros((2, BLK, width), jnp.bfloat16) for _ in far]
     order, first = after(meta, stats, theirs), []
     for h in range(heads):
-        got = backward(h, qd, pool, prev, far, far_grads, bias, stats, order, group, slots)
-        dq.append(got[0])
-        grads.append(got[1])
-        far_grads = got[2]
+        carry = attn[1:] if h == 0 else []
+        got = backward(
+            h, qd, pool, prev, far, far_grads, carry, bias, stats, order, group, slots
+        )
+        grads.append(got[0])
+        far_grads = got[1]
+        if h == 0:
+            attn[1] = early_dq = exchange(got[2])
+        else:
+            dq = got[2][0]
         order = after(meta, got[0])
         kept, first, odds, evens = project(h, mine, theirs, attn[h], first, order, group, parts)
         keep.append(kept)
@@ -709,7 +733,7 @@
     finals.append(sums)
     neighbour = swap_groups(after(first[0], final_cut[0]), 1)
     proj_grad = finish(keep, neighbour, finals, group)
-    query_grad, key_grad, value_grad = unpack(final, meta, group)
+    query_grad, key_grad, value_grad = unpack(early_dq, final, meta, group)
     return (query_grad, key_grad, value_grad, proj_grad)
 
 

time: 136 us -> 136 us (level)
    ppermute x15, waiting for transfers between devices: 28.4 us -> 23.8 us  [swap(): return lax.ppermute(piece, 'seq', route)]
    ppermute x5, waiting for transfers between devices: 1.92 us -> 5.83 us  [swap_groups(): return lax.ppermute(piece, 'seq', route)]
    ppermute x3, waiting for transfers between devices: 1.89 us -> 4.34 us  [shifted(): return lax.ppermute(piece, 'seq', route)]
    ppermute x2, waiting for transfers between devices: 1.73 us -> 0.01 us  [local(): lax.ppermute(piece, 'seq', summary_route(index + 2, True))]
  transfers between devices with their start and end apart: 28 -> 28, of which waited for: 12 -> 13; matrix products, arithmetic and copies ran while one was open for 1% -> 1% of each run, Pallas kernels for 29% -> 29%
where the time goes in v10:
time: 136 us; the launch traced here: 135 us
  Pallas kernels  46.5 us (34%)
  starting transfers between devices  43.1 us (32%)
  waiting for transfers between devices  39.6 us (29%)
  between operations  2.93 us (2%)
  local copies, waits for them, and re-layouts  2.41 us (2%)
    pallas_call x13, Pallas kernels, call(): pl.pallas_call(body, out_shape=outs, in_specs=[SMEM] * len(scalars) + [VM...  31.7 us
    ppermute x15, waiting for transfers between devices, swap(): return lax.ppermute(piece, 'seq', route)  23.8 us
    ppermute x15, starting transfers between devices, swap(): return lax.ppermute(piece, 'seq', route)  18.7 us
    pallas_call x1, Pallas kernels, grads_packed(): pl.pallas_call(body, out_shape=[shape((2 * rows + half * each, rows))] *...  8.73 us
    ppermute x2, starting transfers between devices, local(): lax.ppermute(strided if distance == 2 else later, 'seq', summary_route(di...  7.67 us
    ppermute x5, starting transfers between devices, swap_groups(): return lax.ppermute(piece, 'seq', route)  7.37 us
    ppermute x3, starting transfers between devices, shifted(): return lax.ppermute(piece, 'seq', route)  6.69 us
    ppermute x5, waiting for transfers between devices, swap_groups(): return lax.ppermute(piece, 'seq', route)  5.83 us
  transfers between devices with their start and end apart: 28, of which 13 were waited for; matrix products, arithmetic and copies ran while one was open for 1% of the time, Pallas kernels for 29%

profile of v10, /device:TPU:0, one launch (start us, length us, event | category | flops | bytes accessed | tf_op | source)
XLA Modules:
  0.0 135.3 jit_solution(5311112124192565823)
XLA Ops:
  1.3 3.0 %pack_kv.1 = (bf16[2,256,256]{2,1,0:T(8,128)(2,1)}, bf16[2,256,256]{2,1,0:T(8,128)(2,1)}, bf16[2,256,256]{2,1,0:T(8,128)(2,1)}, bf16[2,256,256]{2,1,0:T(8,128)(2,1)}) custom-call(s32[3]{0:T(128)} %pad_add_fusion.1.meta_ref, bf16[256,1024]{1,0:T(8,128)(2,1)} %k_ref.1, bf16[256,1024]{1,0:T(8,128)(2,1)} %v_ref.1), custom_call_target="tpu_custom_call" | custom-call | flops 1 | bytes 1 | tf_op jit(solution)/shard_map/pack_kv/pallas_call | solution.py:93
  4.3 3.0 %collective-permute-start = (bf16[2,256,256]{2,1,0:T(8,128)(2,1)}, bf16[2,256,256]{2,1,0:T(8,128)(2,1)S(1)}, u32[]{:S(2)}, u32[]{:S(2)}) collective-permute-start(bf16[2,256,256]{2,1,0:T(8,128)(2,1)} %get-tuple-element.65), channel_id=1, source_target_pairs={{0,2},{2,0},{4,6},{6,4},{8,10},{10,8},{12,14},{14,12},{16,18},{18,... | collective-permute-start | bytes 786440 | tf_op jit(solution)/shard_map/ppermute | solution.py:632
  7.3 1.5 %collective-permute-start.1 = (bf16[2,256,256]{2,1,0:T(8,128)(2,1)}, bf16[2,256,256]{2,1,0:T(8,128)(2,1)S(1)}, u32[]{:S(2)}, u32[]{:S(2)}) collective-permute-start(bf16[2,256,256]{2,1,0:T(8,128)(2,1)} %get-tuple-element.70), channel_id=1, source_target_pairs={{0,4},{2,6},{4,0},{6,2},{8,12},{10,14},{12,8},{14,10},{16,20},{18,... | collective-permute-start | bytes 786440 | tf_op jit(solution)/shard_map/ppermute | solution.py:632
  12.1 2.5 %collective-permute-done.refs_1_ = bf16[2,256,256]{2,1,0:T(8,128)(2,1)S(1)} collective-permute-done((bf16[2,256,256]{2,1,0:T(8,128)(2,1)}, bf16[2,256,256]{2,1,0:T(8,128)(2,1)S(1)}, u32[]{:S(2)}, u32[]{:S(2)}) %collective-permute-start) | collective-permute-done | bytes 262176 | tf_op jit(solution)/shard_map/ppermute | solution.py:632
  14.6 8.7 %attn_grad.1 = (bf16[1024,256]{1,0:T(8,128)(2,1)}, bf16[1024,256]{1,0:T(8,128)(2,1)}, bf16[1024,256]{1,0:T(8,128)(2,1)}, bf16[1024,256]{1,0:T(8,128)(2,1)}) custom-call(s32[3]{0:T(128)} %pad_add_fusion.1.meta_ref, bf16[256,1024]{1,0:T(8,128)(2,1)} %q_ref.1, bf16[256,4096]{1,0:T(8,128)(2,1)} %og_ref.1, bf16[4096,1024]{1,0:T(8,128)(2,1)} %w_ref.1), custom_call_target="tpu_custom_call" | custom-call | flops 1 | bytes 1 | tf_op jit(solution)/shard_map/attn_grad/pallas_call | solution.py:152
  24.7 4.1 %collective-permute-start.3 = (bf16[2,1024,256]{2,1,0:T(8,128)(2,1)S(1)}, bf16[2,1024,256]{2,1,0:T(8,128)(2,1)S(1)}, u32[]{:S(2)}, u32[]{:S(2)}) collective-permute-start(bf16[2,1024,256]{2,1,0:T(8,128)(2,1)S(1)} %get-tuple-element.75.refs_1_.refs_3_), channel_id=1, source_target_pairs={{0,8},{2,10},{4,12},{6,14},{8,16},{10,18},{12,20},{14,22},{16,24},... | collective-permute-start | bytes 3145736 | tf_op jit(solution)/shard_map/ppermute | solution.py:640
  28.8 1.6 %collective-permute-start.5 = (bf16[1024,256]{1,0:T(8,128)(2,1)}, bf16[1024,256]{1,0:T(8,128)(2,1)S(1)}, u32[]{:S(2)}, u32[]{:S(2)}) collective-permute-start(bf16[1024,256]{1,0:T(8,128)(2,1)} %get-tuple-element.76), channel_id=1, source_target_pairs={{0,2},{2,0},{4,6},{6,4},{8,10},{10,8},{12,14},{14,12},{16,18},{18,... | collective-permute-start | bytes 1572872 | tf_op jit(solution)/shard_map/ppermute | solution.py:632
  30.4 1.5 %collective-permute-start.7 = (bf16[1024,256]{1,0:T(8,128)(2,1)}, bf16[1024,256]{1,0:T(8,128)(2,1)S(1)}, u32[]{:S(2)}, u32[]{:S(2)}) collective-permute-start(bf16[1024,256]{1,0:T(8,128)(2,1)} %get-tuple-element.79), channel_id=1, source_target_pairs={{0,4},{2,6},{4,0},{6,2},{8,12},{10,14},{12,8},{14,10},{16,20},{18,... | collective-permute-start | bytes 1572872 | tf_op jit(solution)/shard_map/ppermute | solution.py:632
  32.4 4.4 %collective-permute-start.4 = (bf16[2,128,256]{2,1,0:T(8,128)(2,1)}, bf16[2,128,256]{2,1,0:T(8,128)(2,1)S(1)}, u32[]{:S(2)}, u32[]{:S(2)}) collective-permute-start(bf16[2,128,256]{2,1,0:T(8,128)(2,1)} %get-tuple-element.77), channel_id=1, source_target_pairs={{0,16},{2,18},{4,20},{6,22},{1,17},{3,19},{5,21},{7,23}} | collective-permute-start | bytes 393224 | tf_op jit(solution)/shard_map/ppermute | solution.py:679
  36.8 7.2 %collective-permute-done.5.refs_1_ = bf16[1024,256]{1,0:T(8,128)(2,1)S(1)} collective-permute-done((bf16[1024,256]{1,0:T(8,128)(2,1)}, bf16[1024,256]{1,0:T(8,128)(2,1)S(1)}, u32[]{:S(2)}, u32[]{:S(2)}) %collective-permute-start.5) | collective-permute-done | bytes 524320 | tf_op jit(solution)/shard_map/ppermute | solution.py:632
  44.0 3.2 %collective-permute-start.6 = (bf16[2,128,256]{2,1,0:T(8,128)(2,1)}, bf16[2,128,256]{2,1,0:T(8,128)(2,1)S(1)}, u32[]{:S(2)}, u32[]{:S(2)}) collective-permute-start(bf16[2,128,256]{2,1,0:T(8,128)(2,1)} %get-tuple-element.77), channel_id=1, source_target_pairs={{0,24},{2,26},{4,28},{6,30},{1,25},{3,27},{5,29},{7,31}} | collective-permute-start | bytes 393224 | tf_op jit(solution)/shard_map/ppermute | solution.py:679
  47.3 1.9 %masks.1 = (f32[4,11,256]{2,1,0:T(8,128)S(1)}, f32[4,10,256]{2,1,0:T(8,128)S(1)}) custom-call(s32[4]{0:T(128)S(1)} %pad_add_fusion.meta_ref, s32[32,10]{1,0:T(8,128)S(1)} %copy.10.table), custom_call_target="tpu_custom_call" | custom-call | flops 1 | bytes 1 | tf_op jit(solution)/shard_map/masks/pallas_call | solution.py:47
  49.2 4.3 %collective-permute-done.4.refs_3_ = bf16[2,128,256]{2,1,0:T(8,128)(2,1)S(1)} collective-permute-done((bf16[2,128,256]{2,1,0:T(8,128)(2,1)}, bf16[2,128,256]{2,1,0:T(8,128)(2,1)S(1)}, u32[]{:S(2)}, u32[]{:S(2)}) %collective-permute-start.4) | collective-permute-done | bytes 131104 | tf_op jit(solution)/shard_map/ppermute | solution.py:679
  58.6 4.5 %attention_0.1 = (bf16[1024,128]{1,0:T(8,128)(2,1)S(1)}, f32[4,4,256]{2,1,0:T(4,128)S(1)}) custom-call(s32[4]{0:T(128)S(1)} %pad_add_fusion.meta_ref, f32[4,11,256]{2,1,0:T(8,128)S(1)} %get-tuple-element.74.bias_ref, f32[4,4,256]{2,1,0:T(4,128)S(1)} %broadcast_in_dim.3.before_ref, bf16[2,1024,256]{2,1,0:T(8,128)(2,1)S(1)} %get-tuple-element.81.refs_0_, ...), custom_call_target="tpu_custom_call" | custom-call | flops 1 | bytes 1 | tf_op jit(solution)/shard_map/attention_0/pallas_call | solution.py:47
  63.1 2.5 %collective-permute-start.15 = (bf16[1024,128]{1,0:T(8,128)(2,1)S(1)}, bf16[1024,128]{1,0:T(8,128)(2,1)S(1)}, u32[]{:S(2)}, u32[]{:S(2)}) collective-permute-start(bf16[1024,128]{1,0:T(8,128)(2,1)S(1)} %get-tuple-element.82.refs_0_), channel_id=1, source_target_pairs={{0,6},{2,4},{4,2},{6,0},{8,14},{10,12},{12,10},{14,8},{16,22},{18,... | collective-permute-start | bytes 786440 | tf_op jit(solution)/shard_map/ppermute | solution.py:632
  66.7 4.7 %attention_1.1 = (bf16[1024,128]{1,0:T(8,128)(2,1)S(1)}, f32[4,4,256]{2,1,0:T(4,128)S(1)}) custom-call(s32[4]{0:T(128)S(1)} %pad_add_fusion.meta_ref, f32[4,11,256]{2,1,0:T(8,128)S(1)} %get-tuple-element.74.bias_ref, f32[4,4,256]{2,1,0:T(4,128)S(1)} %get-tuple-element.85.before_ref, bf16[2,1024,256]{2,1,0:T(8,128)(2,1)S(1)} %get-tuple-element.81.refs_0_, ...), custom_call_target="tpu_custom_call" | custom-call | flops 1 | bytes 1 | tf_op jit(solution)/shard_map/attention_1/pallas_call | solution.py:47
  71.4 4.4 %attention_back_0.1 = (f32[2,1024,128]{2,1,0:T(8,128)S(1)}, bf16[2,128,256]{2,1,0:T(8,128)(2,1)S(1)}, bf16[2,128,256]{2,1,0:T(8,128)(2,1)S(1)}, bf16[1280,128]{1...) custom-call(s32[4]{0:T(128)S(1)} %pad_add_fusion.meta_ref, ...), custom_call_target="tpu_custom_call" | custom-call | flops 1 | bytes 1 | tf_op jit(solution)/shard_map/attention_back_0/pallas_call | solution.py:47
  75.8 2.6 %collective-permute-done.14.refs_2_ = bf16[1024,128]{1,0:T(8,128)(2,1)S(1)} collective-permute-done((bf16[1024,128]{1,0:T(8,128)(2,1)S(1)}, bf16[1024,128]{1,0:T(8,128)(2,1)S(1)}, u32[]{:S(2)}, u32[]{:S(2)}) %collective-permute-start.14) | collective-permute-done | bytes 262176 | tf_op jit(solution)/shard_map/ppermute | solution.py:632
  78.5 2.2 %project_0.1 = (f32[256,512]{1,0:T(8,128)S(1)}, bf16[1,256,512]{2,1,0:T(8,128)(2,1)S(1)}, bf16[1,256,512]{2,1,0:T(8,128)(2,1)S(1)}, f32[1,256,512]{2,1,0:T(8,128)S(1)}) custom-call(s32[4]{0:T(128)S(1)} %pad_add_fusion.meta_ref, bf16[512,1024]{1,0:T(8,128)(2,1)S(1)} %get-tuple-element.83.mine_ref, bf16[512,1024]{1,0:T(8,128)(2,1)S(1)} %collective-permute-done.9.theirs_ref, ...), custom_call_target="tpu_custom_call" | custom-call | flops 1 | bytes 1 | tf_op jit(solution)/shard_map/project_0/pallas_call | solution.py:47
  80.7 2.4 %collective-permute-start.16 = (bf16[1,256,512]{2,1,0:T(8,128)(2,1)S(1)}, bf16[1,256,512]{2,1,0:T(8,128)(2,1)S(1)}, u32[]{:S(2)}, u32[]{:S(2)}) collective-permute-start(bf16[1,256,512]{2,1,0:T(8,128)(2,1)S(1)} %get-tuple-element.98), channel_id=1, source_target_pairs={{0,8},{2,10},{4,12},{6,14},{8,0},{10,2},{12,4},{14,6},{16,24},{18,... | collective-permute-start | bytes 786440 | tf_op jit(solution)/shard_map/ppermute | solution.py:644
  83.1 1.5 %collective-permute-start.10 = (bf16[1280,128]{1,0:T(8,128)(2,1)S(1)}, bf16[1280,128]{1,0:T(8,128)(2,1)S(1)}, u32[]{:S(2)}, u32[]{:S(2)}) collective-permute-start(bf16[1280,128]{1,0:T(8,128)(2,1)S(1)} %get-tuple-element.90), channel_id=1, source_target_pairs={{0,2},{2,0},{4,6},{6,4},{8,10},{10,8},{12,14},{14,12},{16,18},{18,... | collective-permute-start | bytes 983048 | tf_op jit(solution)/shard_map/ppermute | solution.py:632
  87.9 4.3 %collective-permute-done.18.stats_ref = f32[4,4,256]{2,1,0:T(4,128)S(1)} collective-permute-done((f32[4,4,256]{2,1,0:T(4,128)S(1)}, f32[4,4,256]{2,1,0:T(4,128)S(1)}, u32[]{:S(2)}, u32[]{:S(2)}) %collective-permute-start.18) | collective-permute-done | bytes 16416 | tf_op jit(solution)/shard_map/ppermute | solution.py:640
  92.3 3.5 %collective-permute-start.19 = (bf16[256,512]{1,0:T(8,128)(2,1)S(1)}, bf16[256,512]{1,0:T(8,128)(2,1)S(1)}, u32[]{:S(2)}, u32[]{:S(2)}) collective-permute-start(bf16[256,512]{1,0:T(8,128)(2,1)S(1)} %halve_0.1), channel_id=1, source_target_pairs={{0,16},{2,18},{4,20},{6,22},{8,24},{10,26},{12,28},{14,30},{16,0},... | collective-permute-start | bytes 786440 | tf_op jit(solution)/shard_map/ppermute | solution.py:644
  95.8 4.6 %attention_back_1.1 = (f32[2,1024,128]{2,1,0:T(8,128)S(1)}, bf16[2,128,256]{2,1,0:T(8,128)(2,1)S(1)}, bf16[2,128,256]{2,1,0:T(8,128)(2,1)S(1)}, bf16[1024,128]{1,0:T(8,128)(2,1)S(1)}) custom-call(s32[4]{0:T(128)S(1)} %pad_add_fusion.meta_ref, f32[4,11,256]{2,1,0:T(8,128)S(1)} %get-tuple-element.74.bias_ref, f32[4,4,256]{2,1,0:T(4,128)S(1)} %get-tuple-element.99.stats_ref, ...), custom_call_target="tpu_custom_call" | custom-call | flops 1 | bytes 1 | tf_op jit(solution)/shard_map/attention_back_1/pallas_call | solution.py:47
  103.0 2.1 %project_1.1 = (f32[256,512]{1,0:T(8,128)S(1)}, bf16[2,256,512]{2,1,0:T(8,128)(2,1)S(1)}, bf16[1,256,512]{2,1,0:T(8,128)(2,1)S(1)}, f32[1,256,512]{2,1,0:T(8,128)S(1)}) custom-call(s32[4]{0:T(128)S(1)} %pad_add_fusion.meta_ref, bf16[512,1024]{1,0:T(8,128)(2,1)S(1)} %get-tuple-element.83.mine_ref, bf16[512,1024]{1,0:T(8,128)(2,1)S(1)} %collective-permute-done.9.theirs_ref, ...), custom_call_target="tpu_custom_call" | custom-call | flops 1 | bytes 1 | tf_op jit(solution)/shard_map/project_1/pallas_call | solution.py:47
  105.2 3.1 %collective-permute-done.19.refs_2_ = bf16[256,512]{1,0:T(8,128)(2,1)S(1)} collective-permute-done((bf16[256,512]{1,0:T(8,128)(2,1)S(1)}, bf16[256,512]{1,0:T(8,128)(2,1)S(1)}, u32[]{:S(2)}, u32[]{:S(2)}) %collective-permute-start.19) | collective-permute-done | bytes 262176 | tf_op jit(solution)/shard_map/ppermute | solution.py:644
  108.4 3.9 %attention_back_next.1.own_ref = f32[2,1024,256]{2,1,0:T(8,128)S(1)} custom-call(s32[4]{0:T(128)S(1)} %pad_add_fusion.meta_ref, f32[4,10,256]{2,1,0:T(8,128)S(1)} %get-tuple-element.110.bias_ref, f32[4,4,256]{2,1,0:T(4,128)S(1)} %collective-permute-done.18.stats_ref, f32[2,1024,128]{2,1,0:T(8,128)S(1)} %get-tuple-element.93.refs_0_, ...), custom_call_target="tpu_custom_call" | custom-call | flops 1 | bytes 1 | tf_op jit(solution)/shard_map/attention_back_next/pallas_call | solution.py:47
  113.2 1.6 %collective-permute-start.22 = (bf16[5,256,128]{2,1,0:T(8,128)(2,1)S(1)}, bf16[5,256,128]{2,1,0:T(8,128)(2,1)S(1)}, u32[]{:S(2)}, u32[]{:S(2)}) collective-permute-start(bf16[5,256,128]{2,1,0:T(8,128)(2,1)S(1)} %get-tuple-element.114), channel_id=1, source_target_pairs={{0,2},{2,0},{4,6},{6,4},{8,10},{10,8},{12,14},{14,12},{16,18},{18,... | collective-permute-start | bytes 983048 | tf_op jit(solution)/shard_map/ppermute | solution.py:632
  118.7 5.2 %collective-permute-done.22.refs_5_ = bf16[5,256,128]{2,1,0:T(8,128)(2,1)S(1)} collective-permute-done((bf16[5,256,128]{2,1,0:T(8,128)(2,1)S(1)}, bf16[5,256,128]{2,1,0:T(8,128)(2,1)S(1)}, u32[]{:S(2)}, u32[]{:S(2)}) %collective-permute-start.22) | collective-permute-done | bytes 327712 | tf_op jit(solution)/shard_map/ppermute | solution.py:632
  123.9 6.2 %collective-permute-done.23.refs_6_ = bf16[5,256,128]{2,1,0:T(8,128)(2,1)S(1)} collective-permute-done((bf16[5,256,128]{2,1,0:T(8,128)(2,1)S(1)}, bf16[5,256,128]{2,1,0:T(8,128)(2,1)S(1)}, u32[]{:S(2)}, u32[]{:S(2)}) %collective-permute-start.23) | collective-permute-done | bytes 327712 | tf_op jit(solution)/shard_map/ppermute | solution.py:632
  130.2 1.9 %unpack.1 = (bf16[256,1024]{1,0:T(8,128)(2,1)}, bf16[256,1024]{1,0:T(8,128)(2,1)}, bf16[256,1024]{1,0:T(8,128)(2,1)}) custom-call(s32[4]{0:T(128)S(1)} %pad_add_fusion.meta_ref, bf16[1280,128]{1,0:T(8,128)(2,1)S(1)} %get-tuple-element.89.refs_0_, bf16[1280,128]{1,0:T(8,128)(2,1)S(1)} %collective-permute-done.10.refs_1_, ...), custom_call_target="tpu_custom_call" | custom-call | flops 1 | bytes 1 | tf_op jit(solution)/shard_map/unpack/pallas_call | solution.py:599
  132.3 1.8 %collective-permute-done.27.refs_4_ = bf16[2,256,512]{2,1,0:T(8,128)(2,1)S(1)} collective-permute-done((bf16[2,256,512]{2,1,0:T(8,128)(2,1)S(1)}, bf16[2,256,512]{2,1,0:T(8,128)(2,1)S(1)}, u32[]{:S(2)}, u32[]{:S(2)}) %collective-permute-start.27) | collective-permute-done | bytes 524320 | tf_op jit(solution)/shard_map/ppermute | solution.py:644
  (53 shorter events, 22.4 us)
Async XLA Ops:
  4.3 10.3 %collective-permute-start = (bf16[2,256,256]{2,1,0:T(8,128)(2,1)}, bf16[2,256,256]{2,1,0:T(8,128)(2,1)S(1)}, u32[]{:S(2)}, u32[]{:S(2)}) collective-permute-start(bf16[2,256,256]{2,1,0:T(8,128)(2,1)} %get-tuple-element.65), channel_id=1, source_target_pairs={{0,2},{2,0},{4,6},{6,4},{8,10},{10,8},{12,14},{14,12},{16,18},{18,... | collective-permute-start | bytes 786440 | tf_op jit(solution)/shard_map/ppermute | solution.py:632
  7.3 16.1 %collective-permute-start.1 = (bf16[2,256,256]{2,1,0:T(8,128)(2,1)}, bf16[2,256,256]{2,1,0:T(8,128)(2,1)S(1)}, u32[]{:S(2)}, u32[]{:S(2)}) collective-permute-start(bf16[2,256,256]{2,1,0:T(8,128)(2,1)} %get-tuple-element.70), channel_id=1, source_target_pairs={{0,4},{2,6},{4,0},{6,2},{8,12},{10,14},{12,8},{14,10},{16,20},{18,... | collective-permute-start | bytes 786440 | tf_op jit(solution)/shard_map/ppermute | solution.py:632
  8.8 14.6 %collective-permute-start.2 = (bf16[2,256,256]{2,1,0:T(8,128)(2,1)}, bf16[2,256,256]{2,1,0:T(8,128)(2,1)S(1)}, u32[]{:S(2)}, u32[]{:S(2)}) collective-permute-start(bf16[2,256,256]{2,1,0:T(8,128)(2,1)} %get-tuple-element.71), channel_id=1, source_target_pairs={{0,6},{2,4},{4,2},{6,0},{8,14},{10,12},{12,10},{14,8},{16,22},{18,... | collective-permute-start | bytes 786440 | tf_op jit(solution)/shard_map/ppermute | solution.py:632
  12.1 11.3 %copy-start.1 = (bf16[2,256,256]{2,1,0:T(8,128)(2,1)S(1)}, bf16[2,256,256]{2,1,0:T(8,128)(2,1)}, u32[]{:S(2)}) copy-start(bf16[2,256,256]{2,1,0:T(8,128)(2,1)} %get-tuple-element.69.refs_0_) | copy-start | bytes 786436
  12.1 35.1 %copy-start.2 = (s32[32,10]{0,1:T(8,128)S(1)}, s32[32,10]{0,1:T(8,128)}, u32[]{:S(2)}) copy-start(s32[32,10]{0,1:T(8,128)} %param.11) | copy-start | bytes 3844
  24.7 30.2 %collective-permute-start.3 = (bf16[2,1024,256]{2,1,0:T(8,128)(2,1)S(1)}, bf16[2,1024,256]{2,1,0:T(8,128)(2,1)S(1)}, u32[]{:S(2)}, u32[]{:S(2)}) collective-permute-start(bf16[2,1024,256]{2,1,0:T(8,128)(2,1)S(1)} %get-tuple-element.75.refs_1_.refs_3_), channel_id=1, source_target_pairs={{0,8},{2,10},{4,12},{6,14},{8,16},{10,18},{12,20},{14,22},{16,24},... | collective-permute-start | bytes 3145736 | tf_op jit(solution)/shard_map/ppermute | solution.py:640
  28.8 15.1 %collective-permute-start.5 = (bf16[1024,256]{1,0:T(8,128)(2,1)}, bf16[1024,256]{1,0:T(8,128)(2,1)S(1)}, u32[]{:S(2)}, u32[]{:S(2)}) collective-permute-start(bf16[1024,256]{1,0:T(8,128)(2,1)} %get-tuple-element.76), channel_id=1, source_target_pairs={{0,2},{2,0},{4,6},{6,4},{8,10},{10,8},{12,14},{14,12},{16,18},{18,... | collective-permute-start | bytes 1572872 | tf_op jit(solution)/shard_map/ppermute | solution.py:632
  30.4 24.5 %collective-permute-start.7 = (bf16[1024,256]{1,0:T(8,128)(2,1)}, bf16[1024,256]{1,0:T(8,128)(2,1)S(1)}, u32[]{:S(2)}, u32[]{:S(2)}) collective-permute-start(bf16[1024,256]{1,0:T(8,128)(2,1)} %get-tuple-element.79), channel_id=1, source_target_pairs={{0,4},{2,6},{4,0},{6,2},{8,12},{10,14},{12,8},{14,10},{16,20},{18,... | collective-permute-start | bytes 1572872 | tf_op jit(solution)/shard_map/ppermute | solution.py:632
  31.9 23.0 %collective-permute-start.8 = (bf16[1024,256]{1,0:T(8,128)(2,1)}, bf16[1024,256]{1,0:T(8,128)(2,1)}, u32[]{:S(2)}, u32[]{:S(2)}) collective-permute-start(bf16[1024,256]{1,0:T(8,128)(2,1)} %get-tuple-element.80), channel_id=1, source_target_pairs={{0,6},{2,4},{4,2},{6,0},{8,14},{10,12},{12,10},{14,8},{16,22},{18,... | collective-permute-start | bytes 1572872 | tf_op jit(solution)/shard_map/ppermute | solution.py:632
  32.4 21.1 %collective-permute-start.4 = (bf16[2,128,256]{2,1,0:T(8,128)(2,1)}, bf16[2,128,256]{2,1,0:T(8,128)(2,1)S(1)}, u32[]{:S(2)}, u32[]{:S(2)}) collective-permute-start(bf16[2,128,256]{2,1,0:T(8,128)(2,1)} %get-tuple-element.77), channel_id=1, source_target_pairs={{0,16},{2,18},{4,20},{6,22},{1,17},{3,19},{5,21},{7,23}} | collective-permute-start | bytes 393224 | tf_op jit(solution)/shard_map/ppermute | solution.py:679
  44.0 10.9 %collective-permute-start.6 = (bf16[2,128,256]{2,1,0:T(8,128)(2,1)}, bf16[2,128,256]{2,1,0:T(8,128)(2,1)S(1)}, u32[]{:S(2)}, u32[]{:S(2)}) collective-permute-start(bf16[2,128,256]{2,1,0:T(8,128)(2,1)} %get-tuple-element.77), channel_id=1, source_target_pairs={{0,24},{2,26},{4,28},{6,30},{1,25},{3,27},{5,29},{7,31}} | collective-permute-start | bytes 393224 | tf_op jit(solution)/shard_map/ppermute | solution.py:679
  54.9 1.0 copy-start
  57.2 9.5 %collective-permute-start.9 = (bf16[512,1024]{1,0:T(8,128)(2,1)S(1)}, bf16[512,1024]{1,0:T(8,128)(2,1)S(1)}, u32[]{:S(2)}, u32[]{:S(2)}) collective-permute-start(bf16[512,1024]{1,0:T(8,128)(2,1)S(1)} %get-tuple-element.83.mine_ref), channel_id=1, source_target_pairs={{0,1},{1,0},{2,3},{3,2},{4,5},{5,4},{6,7},{7,6},{8,9},{9,8},{10,11... | collective-permute-start | bytes 3145736 | tf_op jit(solution)/shard_map/ppermute | solution.py:686
  57.3 29.3 %collective-permute-start.17 = (bf16[2,1024,256]{2,1,0:T(8,128)(2,1)S(1)}, bf16[2,1024,256]{2,1,0:T(8,128)(2,1)S(1)}, u32[]{:S(2)}, u32[]{:S(2)}) collective-permute-start(bf16[2,1024,256]{2,1,0:T(8,128)(2,1)S(1)} %get-tuple-element.81.refs_0_), channel_id=1, source_target_pairs={{8,0},{10,2},{12,4},{14,6},{16,8},{18,10},{20,12},{22,14},{24,16},... | collective-permute-start | bytes 3145736 | tf_op jit(solution)/shard_map/ppermute | solution.py:640
  63.1 12.7 %collective-permute-start.15 = (bf16[1024,128]{1,0:T(8,128)(2,1)S(1)}, bf16[1024,128]{1,0:T(8,128)(2,1)S(1)}, u32[]{:S(2)}, u32[]{:S(2)}) collective-permute-start(bf16[1024,128]{1,0:T(8,128)(2,1)S(1)} %get-tuple-element.82.refs_0_), channel_id=1, source_target_pairs={{0,6},{2,4},{4,2},{6,0},{8,14},{10,12},{12,10},{14,8},{16,22},{18,... | collective-permute-start | bytes 786440 | tf_op jit(solution)/shard_map/ppermute | solution.py:632
  65.6 12.8 %collective-permute-start.14 = (bf16[1024,128]{1,0:T(8,128)(2,1)S(1)}, bf16[1024,128]{1,0:T(8,128)(2,1)S(1)}, u32[]{:S(2)}, u32[]{:S(2)}) collective-permute-start(bf16[1024,128]{1,0:T(8,128)(2,1)S(1)} %get-tuple-element.82.refs_0_), channel_id=1, source_target_pairs={{0,4},{2,6},{4,0},{6,2},{8,12},{10,14},{12,8},{14,10},{16,20},{18,... | collective-permute-start | bytes 786440 | tf_op jit(solution)/shard_map/ppermute | solution.py:632
  66.1 12.4 %collective-permute-start.13 = (bf16[1024,128]{1,0:T(8,128)(2,1)S(1)}, bf16[1024,128]{1,0:T(8,128)(2,1)S(1)}, u32[]{:S(2)}, u32[]{:S(2)}) collective-permute-start(bf16[1024,128]{1,0:T(8,128)(2,1)S(1)} %get-tuple-element.82.refs_0_), channel_id=1, source_target_pairs={{0,2},{2,0},{4,6},{6,4},{8,10},{10,8},{12,14},{14,12},{16,18},{18,... | collective-permute-start | bytes 786440 | tf_op jit(solution)/shard_map/ppermute | solution.py:632
  80.7 11.6 %collective-permute-start.16 = (bf16[1,256,512]{2,1,0:T(8,128)(2,1)S(1)}, bf16[1,256,512]{2,1,0:T(8,128)(2,1)S(1)}, u32[]{:S(2)}, u32[]{:S(2)}) collective-permute-start(bf16[1,256,512]{2,1,0:T(8,128)(2,1)S(1)} %get-tuple-element.98), channel_id=1, source_target_pairs={{0,8},{2,10},{4,12},{6,14},{8,0},{10,2},{12,4},{14,6},{16,24},{18,... | collective-permute-start | bytes 786440 | tf_op jit(solution)/shard_map/ppermute | solution.py:644
  83.1 18.6 %collective-permute-start.10 = (bf16[1280,128]{1,0:T(8,128)(2,1)S(1)}, bf16[1280,128]{1,0:T(8,128)(2,1)S(1)}, u32[]{:S(2)}, u32[]{:S(2)}) collective-permute-start(bf16[1280,128]{1,0:T(8,128)(2,1)S(1)} %get-tuple-element.90), channel_id=1, source_target_pairs={{0,2},{2,0},{4,6},{6,4},{8,10},{10,8},{12,14},{14,12},{16,18},{18,... | collective-permute-start | bytes 983048 | tf_op jit(solution)/shard_map/ppermute | solution.py:632
  84.6 18.4 %collective-permute-start.11 = (bf16[1280,128]{1,0:T(8,128)(2,1)S(1)}, bf16[1280,128]{1,0:T(8,128)(2,1)S(1)}, u32[]{:S(2)}, u32[]{:S(2)}) collective-permute-start(bf16[1280,128]{1,0:T(8,128)(2,1)S(1)} %get-tuple-element.91), channel_id=1, source_target_pairs={{0,4},{2,6},{4,0},{6,2},{8,12},{10,14},{12,8},{14,10},{16,20},{18,... | collective-permute-start | bytes 983048 | tf_op jit(solution)/shard_map/ppermute | solution.py:632
  85.3 17.7 %collective-permute-start.12 = (bf16[1280,128]{1,0:T(8,128)(2,1)S(1)}, bf16[1280,128]{1,0:T(8,128)(2,1)S(1)}, u32[]{:S(2)}, u32[]{:S(2)}) collective-permute-start(bf16[1280,128]{1,0:T(8,128)(2,1)S(1)} %get-tuple-element.92), channel_id=1, source_target_pairs={{0,6},{2,4},{4,2},{6,0},{8,14},{10,12},{12,10},{14,8},{16,22},{18,... | collective-permute-start | bytes 983048 | tf_op jit(solution)/shard_map/ppermute | solution.py:632
  86.6 5.6 %collective-permute-start.18 = (f32[4,4,256]{2,1,0:T(4,128)S(1)}, f32[4,4,256]{2,1,0:T(4,128)S(1)}, u32[]{:S(2)}, u32[]{:S(2)}) collective-permute-start(f32[4,4,256]{2,1,0:T(4,128)S(1)} %get-tuple-element.99.stats_ref), channel_id=1, source_target_pairs={{8,0},{10,2},{12,4},{14,6},{16,8},{18,10},{20,12},{22,14},{24,16},... | collective-permute-start | bytes 49160 | tf_op jit(solution)/shard_map/ppermute | solution.py:640
  92.3 16.1 %collective-permute-start.19 = (bf16[256,512]{1,0:T(8,128)(2,1)S(1)}, bf16[256,512]{1,0:T(8,128)(2,1)S(1)}, u32[]{:S(2)}, u32[]{:S(2)}) collective-permute-start(bf16[256,512]{1,0:T(8,128)(2,1)S(1)} %halve_0.1), channel_id=1, source_target_pairs={{0,16},{2,18},{4,20},{6,22},{8,24},{10,26},{12,28},{14,30},{16,0},... | collective-permute-start | bytes 786440 | tf_op jit(solution)/shard_map/ppermute | solution.py:644
  100.4 11.9 %collective-permute-start.20 = (bf16[2,128,256]{2,1,0:T(8,128)(2,1)S(1)}, bf16[2,128,256]{2,1,0:T(8,128)(2,1)S(1)}, u32[]{:S(2)}, u32[]{:S(2)}) collective-permute-start(bf16[2,128,256]{2,1,0:T(8,128)(2,1)S(1)} %get-tuple-element.111), channel_id=1, source_target_pairs={{16,0},{18,2},{20,4},{22,6},{17,1},{19,3},{21,5},{23,7}} | collective-permute-start | bytes 393224 | tf_op jit(solution)/shard_map/ppermute | solution.py:725
  101.7 10.6 %collective-permute-start.21 = (bf16[2,128,256]{2,1,0:T(8,128)(2,1)S(1)}, bf16[2,128,256]{2,1,0:T(8,128)(2,1)S(1)}, u32[]{:S(2)}, u32[]{:S(2)}) collective-permute-start(bf16[2,128,256]{2,1,0:T(8,128)(2,1)S(1)} %get-tuple-element.112), channel_id=1, source_target_pairs={{24,0},{26,2},{28,4},{30,6},{25,1},{27,3},{29,5},{31,7}} | collective-permute-start | bytes 393224 | tf_op jit(solution)/shard_map/ppermute | solution.py:725
  105.1 12.2 %collective-permute-start.25 = (bf16[1,256,512]{2,1,0:T(8,128)(2,1)S(1)}, bf16[1,256,512]{2,1,0:T(8,128)(2,1)S(1)}, u32[]{:S(2)}, u32[]{:S(2)}) collective-permute-start(bf16[1,256,512]{2,1,0:T(8,128)(2,1)S(1)} %get-tuple-element.123), channel_id=1, source_target_pairs={{0,8},{2,10},{4,12},{6,14},{8,0},{10,2},{12,4},{14,6},{16,24},{18,... | collective-permute-start | bytes 786440 | tf_op jit(solution)/shard_map/ppermute | solution.py:644
  113.1 21.0 %collective-permute-start.27 = (bf16[2,256,512]{2,1,0:T(8,128)(2,1)S(1)}, bf16[2,256,512]{2,1,0:T(8,128)(2,1)S(1)}, u32[]{:S(2)}, u32[]{:S(2)}) collective-permute-start(bf16[2,256,512]{2,1,0:T(8,128)(2,1)S(1)} %get-tuple-element.125), channel_id=1, source_target_pairs={{0,8},{2,10},{4,12},{6,14},{8,0},{10,2},{12,4},{14,6},{16,24},{18,... | collective-permute-start | bytes 1572872 | tf_op jit(solution)/shard_map/ppermute | solution.py:644
  113.2 10.7 %collective-permute-start.22 = (bf16[5,256,128]{2,1,0:T(8,128)(2,1)S(1)}, bf16[5,256,128]{2,1,0:T(8,128)(2,1)S(1)}, u32[]{:S(2)}, u32[]{:S(2)}) collective-permute-start(bf16[5,256,128]{2,1,0:T(8,128)(2,1)S(1)} %get-tuple-element.114), channel_id=1, source_target_pairs={{0,2},{2,0},{4,6},{6,4},{8,10},{10,8},{12,14},{14,12},{16,18},{18,... | collective-permute-start | bytes 983048 | tf_op jit(solution)/shard_map/ppermute | solution.py:632
  114.7 15.4 %collective-permute-start.23 = (bf16[5,256,128]{2,1,0:T(8,128)(2,1)S(1)}, bf16[5,256,128]{2,1,0:T(8,128)(2,1)S(1)}, u32[]{:S(2)}, u32[]{:S(2)}) collective-permute-start(bf16[5,256,128]{2,1,0:T(8,128)(2,1)S(1)} %get-tuple-element.115), channel_id=1, source_target_pairs={{0,4},{2,6},{4,0},{6,2},{8,12},{10,14},{12,8},{14,10},{16,20},{18,... | collective-permute-start | bytes 983048 | tf_op jit(solution)/shard_map/ppermute | solution.py:632
  115.6 14.6 %collective-permute-start.24 = (bf16[5,256,128]{2,1,0:T(8,128)(2,1)S(1)}, bf16[5,256,128]{2,1,0:T(8,128)(2,1)S(1)}, u32[]{:S(2)}, u32[]{:S(2)}) collective-permute-start(bf16[5,256,128]{2,1,0:T(8,128)(2,1)S(1)} %get-tuple-element.116), channel_id=1, source_target_pairs={{0,6},{2,4},{4,2},{6,0},{8,14},{10,12},{12,10},{14,8},{16,22},{18,... | collective-permute-start | bytes 983048 | tf_op jit(solution)/shard_map/ppermute | solution.py:632
  117.4 14.9 %collective-permute-start.26 = (bf16[256,512]{1,0:T(8,128)(2,1)S(1)}, bf16[256,512]{1,0:T(8,128)(2,1)S(1)}, u32[]{:S(2)}, u32[]{:S(2)}) collective-permute-start(bf16[256,512]{1,0:T(8,128)(2,1)S(1)} %halve_1.1), channel_id=1, source_target_pairs={{0,16},{2,18},{4,20},{6,22},{8,24},{10,26},{12,28},{14,30},{16,0},... | collective-permute-start | bytes 786440 | tf_op jit(solution)/shard_map/ppermute | solution.py:644

commit v11 on v10

--- a/solution.py
+++ b/solution.py
@@ -725,9 +725,8 @@
         lax.ppermute(piece, "seq", summary_route(index + 2, True))
         for index, piece in enumerate(far_grads)
     ]
-    order = after(order, finals[0])
     own_grad = backward_next(grads, next_qd, pool, bias_next, next_stats, order)
-    final_cut = combine(dq, own_grad, far_back, meta, group, rows)
+    final_cut = combine(dq, own_grad, far_back, after(meta, finals[0]), group, rows)
     final = exchange(final_cut)
     sums, _, _ = add_up(heads - 1, odds, evens, final_cut, meta)
     finals.append(sums)

time: 136 us -> 136 us (level)
    ppermute x2, waiting for transfers between devices: 0.01 us -> 2.63 us  [local(): lax.ppermute(piece, 'seq', summary_route(index + 2, True))]
    ppermute x5, waiting for transfers between devices: 5.83 us -> 3.21 us  [swap_groups(): return lax.ppermute(piece, 'seq', route)]
where the time goes in v11:
time: 136 us; the launch traced here: 135 us
  Pallas kernels  46.5 us (34%)
  starting transfers between devices  43.1 us (32%)
  waiting for transfers between devices  39.6 us (29%)
  between operations  2.92 us (2%)
  local copies, waits for them, and re-layouts  2.41 us (2%)
    pallas_call x13, Pallas kernels, call(): pl.pallas_call(body, out_shape=outs, in_specs=[SMEM] * len(scalars) + [VM...  31.7 us
    ppermute x15, waiting for transfers between devices, swap(): return lax.ppermute(piece, 'seq', route)  23.8 us
    ppermute x15, starting transfers between devices, swap(): return lax.ppermute(piece, 'seq', route)  18.7 us
    pallas_call x1, Pallas kernels, grads_packed(): pl.pallas_call(body, out_shape=[shape((2 * rows + half * each, rows))] *...  8.73 us
    ppermute x2, starting transfers between devices, local(): lax.ppermute(strided if distance == 2 else later, 'seq', summary_route(di...  7.67 us
    ppermute x5, starting transfers between devices, swap_groups(): return lax.ppermute(piece, 'seq', route)  7.38 us
    ppermute x3, starting transfers between devices, shifted(): return lax.ppermute(piece, 'seq', route)  6.69 us
    ppermute x2, waiting for transfers between devices, local(): lax.ppermute(strided if distance == 2 else later, 'seq', summary_route(di...  5.68 us
  transfers between devices with their start and end apart: 28, of which 13 were waited for; matrix products, arithmetic and copies ran while one was open for 1% of the time, Pallas kernels for 29%

profile of v11, /device:TPU:0, one launch (start us, length us, event | category | flops | bytes accessed | tf_op | source)
XLA Modules:
  0.0 135.3 jit_solution(9523471076277521326)
XLA Ops:
  1.3 3.0 %pack_kv.1 = (bf16[2,256,256]{2,1,0:T(8,128)(2,1)}, bf16[2,256,256]{2,1,0:T(8,128)(2,1)}, bf16[2,256,256]{2,1,0:T(8,128)(2,1)}, bf16[2,256,256]{2,1,0:T(8,128)(2,1)}) custom-call(s32[3]{0:T(128)} %pad_add_fusion.1.meta_ref, bf16[256,1024]{1,0:T(8,128)(2,1)} %k_ref.1, bf16[256,1024]{1,0:T(8,128)(2,1)} %v_ref.1), custom_call_target="tpu_custom_call" | custom-call | flops 1 | bytes 1 | tf_op jit(solution)/shard_map/pack_kv/pallas_call | solution.py:93
  4.3 3.0 %collective-permute-start = (bf16[2,256,256]{2,1,0:T(8,128)(2,1)}, bf16[2,256,256]{2,1,0:T(8,128)(2,1)S(1)}, u32[]{:S(2)}, u32[]{:S(2)}) collective-permute-start(bf16[2,256,256]{2,1,0:T(8,128)(2,1)} %get-tuple-element.65), channel_id=1, source_target_pairs={{0,2},{2,0},{4,6},{6,4},{8,10},{10,8},{12,14},{14,12},{16,18},{18,... | collective-permute-start | bytes 786440 | tf_op jit(solution)/shard_map/ppermute | solution.py:632
  7.3 1.5 %collective-permute-start.1 = (bf16[2,256,256]{2,1,0:T(8,128)(2,1)}, bf16[2,256,256]{2,1,0:T(8,128)(2,1)S(1)}, u32[]{:S(2)}, u32[]{:S(2)}) collective-permute-start(bf16[2,256,256]{2,1,0:T(8,128)(2,1)} %get-tuple-element.70), channel_id=1, source_target_pairs={{0,4},{2,6},{4,0},{6,2},{8,12},{10,14},{12,8},{14,10},{16,20},{18,... | collective-permute-start | bytes 786440 | tf_op jit(solution)/shard_map/ppermute | solution.py:632
  12.1 2.5 %collective-permute-done.refs_1_ = bf16[2,256,256]{2,1,0:T(8,128)(2,1)S(1)} collective-permute-done((bf16[2,256,256]{2,1,0:T(8,128)(2,1)}, bf16[2,256,256]{2,1,0:T(8,128)(2,1)S(1)}, u32[]{:S(2)}, u32[]{:S(2)}) %collective-permute-start) | collective-permute-done | bytes 262176 | tf_op jit(solution)/shard_map/ppermute | solution.py:632
  14.6 8.7 %attn_grad.1 = (bf16[1024,256]{1,0:T(8,128)(2,1)}, bf16[1024,256]{1,0:T(8,128)(2,1)}, bf16[1024,256]{1,0:T(8,128)(2,1)}, bf16[1024,256]{1,0:T(8,128)(2,1)}) custom-call(s32[3]{0:T(128)} %pad_add_fusion.1.meta_ref, bf16[256,1024]{1,0:T(8,128)(2,1)} %q_ref.1, bf16[256,4096]{1,0:T(8,128)(2,1)} %og_ref.1, bf16[4096,1024]{1,0:T(8,128)(2,1)} %w_ref.1), custom_call_target="tpu_custom_call" | custom-call | flops 1 | bytes 1 | tf_op jit(solution)/shard_map/attn_grad/pallas_call | solution.py:152
  24.7 4.1 %collective-permute-start.3 = (bf16[2,1024,256]{2,1,0:T(8,128)(2,1)S(1)}, bf16[2,1024,256]{2,1,0:T(8,128)(2,1)S(1)}, u32[]{:S(2)}, u32[]{:S(2)}) collective-permute-start(bf16[2,1024,256]{2,1,0:T(8,128)(2,1)S(1)} %get-tuple-element.75.refs_1_.refs_3_), channel_id=1, source_target_pairs={{0,8},{2,10},{4,12},{6,14},{8,16},{10,18},{12,20},{14,22},{16,24},... | collective-permute-start | bytes 3145736 | tf_op jit(solution)/shard_map/ppermute | solution.py:640
  28.8 1.6 %collective-permute-start.5 = (bf16[1024,256]{1,0:T(8,128)(2,1)}, bf16[1024,256]{1,0:T(8,128)(2,1)S(1)}, u32[]{:S(2)}, u32[]{:S(2)}) collective-permute-start(bf16[1024,256]{1,0:T(8,128)(2,1)} %get-tuple-element.76), channel_id=1, source_target_pairs={{0,2},{2,0},{4,6},{6,4},{8,10},{10,8},{12,14},{14,12},{16,18},{18,... | collective-permute-start | bytes 1572872 | tf_op jit(solution)/shard_map/ppermute | solution.py:632
  30.4 1.5 %collective-permute-start.7 = (bf16[1024,256]{1,0:T(8,128)(2,1)}, bf16[1024,256]{1,0:T(8,128)(2,1)S(1)}, u32[]{:S(2)}, u32[]{:S(2)}) collective-permute-start(bf16[1024,256]{1,0:T(8,128)(2,1)} %get-tuple-element.79), channel_id=1, source_target_pairs={{0,4},{2,6},{4,0},{6,2},{8,12},{10,14},{12,8},{14,10},{16,20},{18,... | collective-permute-start | bytes 1572872 | tf_op jit(solution)/shard_map/ppermute | solution.py:632
  32.4 4.4 %collective-permute-start.4 = (bf16[2,128,256]{2,1,0:T(8,128)(2,1)}, bf16[2,128,256]{2,1,0:T(8,128)(2,1)S(1)}, u32[]{:S(2)}, u32[]{:S(2)}) collective-permute-start(bf16[2,128,256]{2,1,0:T(8,128)(2,1)} %get-tuple-element.77), channel_id=1, source_target_pairs={{0,16},{2,18},{4,20},{6,22},{1,17},{3,19},{5,21},{7,23}} | collective-permute-start | bytes 393224 | tf_op jit(solution)/shard_map/ppermute | solution.py:679
  36.8 7.2 %collective-permute-done.5.refs_1_ = bf16[1024,256]{1,0:T(8,128)(2,1)S(1)} collective-permute-done((bf16[1024,256]{1,0:T(8,128)(2,1)}, bf16[1024,256]{1,0:T(8,128)(2,1)S(1)}, u32[]{:S(2)}, u32[]{:S(2)}) %collective-permute-start.5) | collective-permute-done | bytes 524320 | tf_op jit(solution)/shard_map/ppermute | solution.py:632
  44.0 3.2 %collective-permute-start.6 = (bf16[2,128,256]{2,1,0:T(8,128)(2,1)}, bf16[2,128,256]{2,1,0:T(8,128)(2,1)S(1)}, u32[]{:S(2)}, u32[]{:S(2)}) collective-permute-start(bf16[2,128,256]{2,1,0:T(8,128)(2,1)} %get-tuple-element.77), channel_id=1, source_target_pairs={{0,24},{2,26},{4,28},{6,30},{1,25},{3,27},{5,29},{7,31}} | collective-permute-start | bytes 393224 | tf_op jit(solution)/shard_map/ppermute | solution.py:679
  47.3 1.9 %masks.1 = (f32[4,11,256]{2,1,0:T(8,128)S(1)}, f32[4,10,256]{2,1,0:T(8,128)S(1)}) custom-call(s32[4]{0:T(128)S(1)} %pad_add_fusion.meta_ref, s32[32,10]{1,0:T(8,128)S(1)} %copy.10.table), custom_call_target="tpu_custom_call" | custom-call | flops 1 | bytes 1 | tf_op jit(solution)/shard_map/masks/pallas_call | solution.py:47
  49.2 4.3 %collective-permute-done.4.refs_3_ = bf16[2,128,256]{2,1,0:T(8,128)(2,1)S(1)} collective-permute-done((bf16[2,128,256]{2,1,0:T(8,128)(2,1)}, bf16[2,128,256]{2,1,0:T(8,128)(2,1)S(1)}, u32[]{:S(2)}, u32[]{:S(2)}) %collective-permute-start.4) | collective-permute-done | bytes 131104 | tf_op jit(solution)/shard_map/ppermute | solution.py:679
  58.6 4.5 %attention_0.1 = (bf16[1024,128]{1,0:T(8,128)(2,1)S(1)}, f32[4,4,256]{2,1,0:T(4,128)S(1)}) custom-call(s32[4]{0:T(128)S(1)} %pad_add_fusion.meta_ref, f32[4,11,256]{2,1,0:T(8,128)S(1)} %get-tuple-element.74.bias_ref, f32[4,4,256]{2,1,0:T(4,128)S(1)} %broadcast_in_dim.3.before_ref, bf16[2,1024,256]{2,1,0:T(8,128)(2,1)S(1)} %get-tuple-element.81.refs_0_, ...), custom_call_target="tpu_custom_call" | custom-call | flops 1 | bytes 1 | tf_op jit(solution)/shard_map/attention_0/pallas_call | solution.py:47
  63.1 2.5 %collective-permute-start.15 = (bf16[1024,128]{1,0:T(8,128)(2,1)S(1)}, bf16[1024,128]{1,0:T(8,128)(2,1)S(1)}, u32[]{:S(2)}, u32[]{:S(2)}) collective-permute-start(bf16[1024,128]{1,0:T(8,128)(2,1)S(1)} %get-tuple-element.82.refs_0_), channel_id=1, source_target_pairs={{0,6},{2,4},{4,2},{6,0},{8,14},{10,12},{12,10},{14,8},{16,22},{18,... | collective-permute-start | bytes 786440 | tf_op jit(solution)/shard_map/ppermute | solution.py:632
  66.7 4.7 %attention_1.1 = (bf16[1024,128]{1,0:T(8,128)(2,1)S(1)}, f32[4,4,256]{2,1,0:T(4,128)S(1)}) custom-call(s32[4]{0:T(128)S(1)} %pad_add_fusion.meta_ref, f32[4,11,256]{2,1,0:T(8,128)S(1)} %get-tuple-element.74.bias_ref, f32[4,4,256]{2,1,0:T(4,128)S(1)} %get-tuple-element.85.before_ref, bf16[2,1024,256]{2,1,0:T(8,128)(2,1)S(1)} %get-tuple-element.81.refs_0_, ...), custom_call_target="tpu_custom_call" | custom-call | flops 1 | bytes 1 | tf_op jit(solution)/shard_map/attention_1/pallas_call | solution.py:47
  71.4 4.4 %attention_back_0.1 = (f32[2,1024,128]{2,1,0:T(8,128)S(1)}, bf16[2,128,256]{2,1,0:T(8,128)(2,1)S(1)}, bf16[2,128,256]{2,1,0:T(8,128)(2,1)S(1)}, bf16[1280,128]{1...) custom-call(s32[4]{0:T(128)S(1)} %pad_add_fusion.meta_ref, ...), custom_call_target="tpu_custom_call" | custom-call | flops 1 | bytes 1 | tf_op jit(solution)/shard_map/attention_back_0/pallas_call | solution.py:47
  75.8 2.6 %collective-permute-done.14.refs_2_ = bf16[1024,128]{1,0:T(8,128)(2,1)S(1)} collective-permute-done((bf16[1024,128]{1,0:T(8,128)(2,1)S(1)}, bf16[1024,128]{1,0:T(8,128)(2,1)S(1)}, u32[]{:S(2)}, u32[]{:S(2)}) %collective-permute-start.14) | collective-permute-done | bytes 262176 | tf_op jit(solution)/shard_map/ppermute | solution.py:632
  78.5 2.2 %project_0.1 = (f32[256,512]{1,0:T(8,128)S(1)}, bf16[1,256,512]{2,1,0:T(8,128)(2,1)S(1)}, bf16[1,256,512]{2,1,0:T(8,128)(2,1)S(1)}, f32[1,256,512]{2,1,0:T(8,128)S(1)}) custom-call(s32[4]{0:T(128)S(1)} %pad_add_fusion.meta_ref, bf16[512,1024]{1,0:T(8,128)(2,1)S(1)} %get-tuple-element.83.mine_ref, bf16[512,1024]{1,0:T(8,128)(2,1)S(1)} %collective-permute-done.9.theirs_ref, ...), custom_call_target="tpu_custom_call" | custom-call | flops 1 | bytes 1 | tf_op jit(solution)/shard_map/project_0/pallas_call | solution.py:47
  80.7 2.4 %collective-permute-start.16 = (bf16[1,256,512]{2,1,0:T(8,128)(2,1)S(1)}, bf16[1,256,512]{2,1,0:T(8,128)(2,1)S(1)}, u32[]{:S(2)}, u32[]{:S(2)}) collective-permute-start(bf16[1,256,512]{2,1,0:T(8,128)(2,1)S(1)} %get-tuple-element.96), channel_id=1, source_target_pairs={{0,8},{2,10},{4,12},{6,14},{8,0},{10,2},{12,4},{14,6},{16,24},{18,... | collective-permute-start | bytes 786440 | tf_op jit(solution)/shard_map/ppermute | solution.py:644
  83.1 1.5 %collective-permute-start.10 = (bf16[1280,128]{1,0:T(8,128)(2,1)S(1)}, bf16[1280,128]{1,0:T(8,128)(2,1)S(1)}, u32[]{:S(2)}, u32[]{:S(2)}) collective-permute-start(bf16[1280,128]{1,0:T(8,128)(2,1)S(1)} %get-tuple-element.90), channel_id=1, source_target_pairs={{0,2},{2,0},{4,6},{6,4},{8,10},{10,8},{12,14},{14,12},{16,18},{18,... | collective-permute-start | bytes 983048 | tf_op jit(solution)/shard_map/ppermute | solution.py:632
  87.9 4.3 %collective-permute-done.18.stats_ref = f32[4,4,256]{2,1,0:T(4,128)S(1)} collective-permute-done((f32[4,4,256]{2,1,0:T(4,128)S(1)}, f32[4,4,256]{2,1,0:T(4,128)S(1)}, u32[]{:S(2)}, u32[]{:S(2)}) %collective-permute-start.18) | collective-permute-done | bytes 16416 | tf_op jit(solution)/shard_map/ppermute | solution.py:640
  92.3 3.5 %collective-permute-start.19 = (bf16[256,512]{1,0:T(8,128)(2,1)S(1)}, bf16[256,512]{1,0:T(8,128)(2,1)S(1)}, u32[]{:S(2)}, u32[]{:S(2)}) collective-permute-start(bf16[256,512]{1,0:T(8,128)(2,1)S(1)} %halve_0.1), channel_id=1, source_target_pairs={{0,16},{2,18},{4,20},{6,22},{8,24},{10,26},{12,28},{14,30},{16,0},... | collective-permute-start | bytes 786440 | tf_op jit(solution)/shard_map/ppermute | solution.py:644
  95.8 4.6 %attention_back_1.1 = (f32[2,1024,128]{2,1,0:T(8,128)S(1)}, bf16[2,128,256]{2,1,0:T(8,128)(2,1)S(1)}, bf16[2,128,256]{2,1,0:T(8,128)(2,1)S(1)}, bf16[1024,128]{1,0:T(8,128)(2,1)S(1)}) custom-call(s32[4]{0:T(128)S(1)} %pad_add_fusion.meta_ref, f32[4,11,256]{2,1,0:T(8,128)S(1)} %get-tuple-element.74.bias_ref, f32[4,4,256]{2,1,0:T(4,128)S(1)} %get-tuple-element.98.stats_ref, ...), custom_call_target="tpu_custom_call" | custom-call | flops 1 | bytes 1 | tf_op jit(solution)/shard_map/attention_back_1/pallas_call | solution.py:47
  103.0 2.1 %project_1.1 = (f32[256,512]{1,0:T(8,128)S(1)}, bf16[2,256,512]{2,1,0:T(8,128)(2,1)S(1)}, bf16[1,256,512]{2,1,0:T(8,128)(2,1)S(1)}, f32[1,256,512]{2,1,0:T(8,128)S(1)}) custom-call(s32[4]{0:T(128)S(1)} %pad_add_fusion.meta_ref, bf16[512,1024]{1,0:T(8,128)(2,1)S(1)} %get-tuple-element.83.mine_ref, bf16[512,1024]{1,0:T(8,128)(2,1)S(1)} %collective-permute-done.9.theirs_ref, ...), custom_call_target="tpu_custom_call" | custom-call | flops 1 | bytes 1 | tf_op jit(solution)/shard_map/project_1/pallas_call | solution.py:47
  105.2 3.9 %attention_back_next.1.own_ref = f32[2,1024,256]{2,1,0:T(8,128)S(1)} custom-call(s32[4]{0:T(128)S(1)} %pad_add_fusion.meta_ref, f32[4,10,256]{2,1,0:T(8,128)S(1)} %get-tuple-element.110.bias_ref, f32[4,4,256]{2,1,0:T(4,128)S(1)} %collective-permute-done.18.stats_ref, f32[2,1024,128]{2,1,0:T(8,128)S(1)} %get-tuple-element.93.refs_0_, ...), custom_call_target="tpu_custom_call" | custom-call | flops 1 | bytes 1 | tf_op jit(solution)/shard_map/attention_back_next/pallas_call | solution.py:47
  109.1 2.6 %collective-permute-done.20.refs_0_ = bf16[2,128,256]{2,1,0:T(8,128)(2,1)S(1)} collective-permute-done((bf16[2,128,256]{2,1,0:T(8,128)(2,1)S(1)}, bf16[2,128,256]{2,1,0:T(8,128)(2,1)S(1)}, u32[]{:S(2)}, u32[]{:S(2)}) %collective-permute-start.20) | collective-permute-done | bytes 131104 | tf_op jit(solution)/shard_map/ppermute | solution.py:725
  112.7 1.6 %collective-permute-start.22 = (bf16[5,256,128]{2,1,0:T(8,128)(2,1)S(1)}, bf16[5,256,128]{2,1,0:T(8,128)(2,1)S(1)}, u32[]{:S(2)}, u32[]{:S(2)}) collective-permute-start(bf16[5,256,128]{2,1,0:T(8,128)(2,1)S(1)} %get-tuple-element.114), channel_id=1, source_target_pairs={{0,2},{2,0},{4,6},{6,4},{8,10},{10,8},{12,14},{14,12},{16,18},{18,... | collective-permute-start | bytes 983048 | tf_op jit(solution)/shard_map/ppermute | solution.py:632
  118.7 4.7 %collective-permute-done.22.refs_5_ = bf16[5,256,128]{2,1,0:T(8,128)(2,1)S(1)} collective-permute-done((bf16[5,256,128]{2,1,0:T(8,128)(2,1)S(1)}, bf16[5,256,128]{2,1,0:T(8,128)(2,1)S(1)}, u32[]{:S(2)}, u32[]{:S(2)}) %collective-permute-start.22) | collective-permute-done | bytes 327712 | tf_op jit(solution)/shard_map/ppermute | solution.py:632
  123.4 6.8 %collective-permute-done.23.refs_6_ = bf16[5,256,128]{2,1,0:T(8,128)(2,1)S(1)} collective-permute-done((bf16[5,256,128]{2,1,0:T(8,128)(2,1)S(1)}, bf16[5,256,128]{2,1,0:T(8,128)(2,1)S(1)}, u32[]{:S(2)}, u32[]{:S(2)}) %collective-permute-start.23) | collective-permute-done | bytes 327712 | tf_op jit(solution)/shard_map/ppermute | solution.py:632
  130.2 1.9 %unpack.1 = (bf16[256,1024]{1,0:T(8,128)(2,1)}, bf16[256,1024]{1,0:T(8,128)(2,1)}, bf16[256,1024]{1,0:T(8,128)(2,1)}) custom-call(s32[4]{0:T(128)S(1)} %pad_add_fusion.meta_ref, bf16[1280,128]{1,0:T(8,128)(2,1)S(1)} %get-tuple-element.89.refs_0_, bf16[1280,128]{1,0:T(8,128)(2,1)S(1)} %collective-permute-done.10.refs_1_, ...), custom_call_target="tpu_custom_call" | custom-call | flops 1 | bytes 1 | tf_op jit(solution)/shard_map/unpack/pallas_call | solution.py:599
  132.3 1.8 %collective-permute-done.27.refs_4_ = bf16[2,256,512]{2,1,0:T(8,128)(2,1)S(1)} collective-permute-done((bf16[2,256,512]{2,1,0:T(8,128)(2,1)S(1)}, bf16[2,256,512]{2,1,0:T(8,128)(2,1)S(1)}, u32[]{:S(2)}, u32[]{:S(2)}) %collective-permute-start.27) | collective-permute-done | bytes 524320 | tf_op jit(solution)/shard_map/ppermute | solution.py:644
  (53 shorter events, 22.9 us)
Async XLA Ops:
  4.3 10.3 %collective-permute-start = (bf16[2,256,256]{2,1,0:T(8,128)(2,1)}, bf16[2,256,256]{2,1,0:T(8,128)(2,1)S(1)}, u32[]{:S(2)}, u32[]{:S(2)}) collective-permute-start(bf16[2,256,256]{2,1,0:T(8,128)(2,1)} %get-tuple-element.65), channel_id=1, source_target_pairs={{0,2},{2,0},{4,6},{6,4},{8,10},{10,8},{12,14},{14,12},{16,18},{18,... | collective-permute-start | bytes 786440 | tf_op jit(solution)/shard_map/ppermute | solution.py:632
  7.3 16.1 %collective-permute-start.1 = (bf16[2,256,256]{2,1,0:T(8,128)(2,1)}, bf16[2,256,256]{2,1,0:T(8,128)(2,1)S(1)}, u32[]{:S(2)}, u32[]{:S(2)}) collective-permute-start(bf16[2,256,256]{2,1,0:T(8,128)(2,1)} %get-tuple-element.70), channel_id=1, source_target_pairs={{0,4},{2,6},{4,0},{6,2},{8,12},{10,14},{12,8},{14,10},{16,20},{18,... | collective-permute-start | bytes 786440 | tf_op jit(solution)/shard_map/ppermute | solution.py:632
  8.8 14.6 %collective-permute-start.2 = (bf16[2,256,256]{2,1,0:T(8,128)(2,1)}, bf16[2,256,256]{2,1,0:T(8,128)(2,1)S(1)}, u32[]{:S(2)}, u32[]{:S(2)}) collective-permute-start(bf16[2,256,256]{2,1,0:T(8,128)(2,1)} %get-tuple-element.71), channel_id=1, source_target_pairs={{0,6},{2,4},{4,2},{6,0},{8,14},{10,12},{12,10},{14,8},{16,22},{18,... | collective-permute-start | bytes 786440 | tf_op jit(solution)/shard_map/ppermute | solution.py:632
  12.1 11.3 %copy-start.1 = (bf16[2,256,256]{2,1,0:T(8,128)(2,1)S(1)}, bf16[2,256,256]{2,1,0:T(8,128)(2,1)}, u32[]{:S(2)}) copy-start(bf16[2,256,256]{2,1,0:T(8,128)(2,1)} %get-tuple-element.69.refs_0_) | copy-start | bytes 786436
  12.1 35.1 %copy-start.2 = (s32[32,10]{0,1:T(8,128)S(1)}, s32[32,10]{0,1:T(8,128)}, u32[]{:S(2)}) copy-start(s32[32,10]{0,1:T(8,128)} %param.11) | copy-start | bytes 3844
  24.7 30.2 %collective-permute-start.3 = (bf16[2,1024,256]{2,1,0:T(8,128)(2,1)S(1)}, bf16[2,1024,256]{2,1,0:T(8,128)(2,1)S(1)}, u32[]{:S(2)}, u32[]{:S(2)}) collective-permute-start(bf16[2,1024,256]{2,1,0:T(8,128)(2,1)S(1)} %get-tuple-element.75.refs_1_.refs_3_), channel_id=1, source_target_pairs={{0,8},{2,10},{4,12},{6,14},{8,16},{10,18},{12,20},{14,22},{16,24},... | collective-permute-start | bytes 3145736 | tf_op jit(solution)/shard_map/ppermute | solution.py:640
  28.8 15.1 %collective-permute-start.5 = (bf16[1024,256]{1,0:T(8,128)(2,1)}, bf16[1024,256]{1,0:T(8,128)(2,1)S(1)}, u32[]{:S(2)}, u32[]{:S(2)}) collective-permute-start(bf16[1024,256]{1,0:T(8,128)(2,1)} %get-tuple-element.76), channel_id=1, source_target_pairs={{0,2},{2,0},{4,6},{6,4},{8,10},{10,8},{12,14},{14,12},{16,18},{18,... | collective-permute-start | bytes 1572872 | tf_op jit(solution)/shard_map/ppermute | solution.py:632
  30.4 24.5 %collective-permute-start.7 = (bf16[1024,256]{1,0:T(8,128)(2,1)}, bf16[1024,256]{1,0:T(8,128)(2,1)S(1)}, u32[]{:S(2)}, u32[]{:S(2)}) collective-permute-start(bf16[1024,256]{1,0:T(8,128)(2,1)} %get-tuple-element.79), channel_id=1, source_target_pairs={{0,4},{2,6},{4,0},{6,2},{8,12},{10,14},{12,8},{14,10},{16,20},{18,... | collective-permute-start | bytes 1572872 | tf_op jit(solution)/shard_map/ppermute | solution.py:632
  31.9 23.0 %collective-permute-start.8 = (bf16[1024,256]{1,0:T(8,128)(2,1)}, bf16[1024,256]{1,0:T(8,128)(2,1)}, u32[]{:S(2)}, u32[]{:S(2)}) collective-permute-start(bf16[1024,256]{1,0:T(8,128)(2,1)} %get-tuple-element.80), channel_id=1, source_target_pairs={{0,6},{2,4},{4,2},{6,0},{8,14},{10,12},{12,10},{14,8},{16,22},{18,... | collective-permute-start | bytes 1572872 | tf_op jit(solution)/shard_map/ppermute | solution.py:632
  32.4 21.1 %collective-permute-start.4 = (bf16[2,128,256]{2,1,0:T(8,128)(2,1)}, bf16[2,128,256]{2,1,0:T(8,128)(2,1)S(1)}, u32[]{:S(2)}, u32[]{:S(2)}) collective-permute-start(bf16[2,128,256]{2,1,0:T(8,128)(2,1)} %get-tuple-element.77), channel_id=1, source_target_pairs={{0,16},{2,18},{4,20},{6,22},{1,17},{3,19},{5,21},{7,23}} | collective-permute-start | bytes 393224 | tf_op jit(solution)/shard_map/ppermute | solution.py:679
  44.0 10.9 %collective-permute-start.6 = (bf16[2,128,256]{2,1,0:T(8,128)(2,1)}, bf16[2,128,256]{2,1,0:T(8,128)(2,1)S(1)}, u32[]{:S(2)}, u32[]{:S(2)}) collective-permute-start(bf16[2,128,256]{2,1,0:T(8,128)(2,1)} %get-tuple-element.77), channel_id=1, source_target_pairs={{0,24},{2,26},{4,28},{6,30},{1,25},{3,27},{5,29},{7,31}} | collective-permute-start | bytes 393224 | tf_op jit(solution)/shard_map/ppermute | solution.py:679
  54.9 1.0 copy-start
  57.2 9.5 %collective-permute-start.9 = (bf16[512,1024]{1,0:T(8,128)(2,1)S(1)}, bf16[512,1024]{1,0:T(8,128)(2,1)S(1)}, u32[]{:S(2)}, u32[]{:S(2)}) collective-permute-start(bf16[512,1024]{1,0:T(8,128)(2,1)S(1)} %get-tuple-element.83.mine_ref), channel_id=1, source_target_pairs={{0,1},{1,0},{2,3},{3,2},{4,5},{5,4},{6,7},{7,6},{8,9},{9,8},{10,11... | collective-permute-start | bytes 3145736 | tf_op jit(solution)/shard_map/ppermute | solution.py:686
  57.3 29.3 %collective-permute-start.17 = (bf16[2,1024,256]{2,1,0:T(8,128)(2,1)S(1)}, bf16[2,1024,256]{2,1,0:T(8,128)(2,1)S(1)}, u32[]{:S(2)}, u32[]{:S(2)}) collective-permute-start(bf16[2,1024,256]{2,1,0:T(8,128)(2,1)S(1)} %get-tuple-element.81.refs_0_), channel_id=1, source_target_pairs={{8,0},{10,2},{12,4},{14,6},{16,8},{18,10},{20,12},{22,14},{24,16},... | collective-permute-start | bytes 3145736 | tf_op jit(solution)/shard_map/ppermute | solution.py:640
  63.1 12.7 %collective-permute-start.15 = (bf16[1024,128]{1,0:T(8,128)(2,1)S(1)}, bf16[1024,128]{1,0:T(8,128)(2,1)S(1)}, u32[]{:S(2)}, u32[]{:S(2)}) collective-permute-start(bf16[1024,128]{1,0:T(8,128)(2,1)S(1)} %get-tuple-element.82.refs_0_), channel_id=1, source_target_pairs={{0,6},{2,4},{4,2},{6,0},{8,14},{10,12},{12,10},{14,8},{16,22},{18,... | collective-permute-start | bytes 786440 | tf_op jit(solution)/shard_map/ppermute | solution.py:632
  65.6 12.8 %collective-permute-start.14 = (bf16[1024,128]{1,0:T(8,128)(2,1)S(1)}, bf16[1024,128]{1,0:T(8,128)(2,1)S(1)}, u32[]{:S(2)}, u32[]{:S(2)}) collective-permute-start(bf16[1024,128]{1,0:T(8,128)(2,1)S(1)} %get-tuple-element.82.refs_0_), channel_id=1, source_target_pairs={{0,4},{2,6},{4,0},{6,2},{8,12},{10,14},{12,8},{14,10},{16,20},{18,... | collective-permute-start | bytes 786440 | tf_op jit(solution)/shard_map/ppermute | solution.py:632
  66.1 12.4 %collective-permute-start.13 = (bf16[1024,128]{1,0:T(8,128)(2,1)S(1)}, bf16[1024,128]{1,0:T(8,128)(2,1)S(1)}, u32[]{:S(2)}, u32[]{:S(2)}) collective-permute-start(bf16[1024,128]{1,0:T(8,128)(2,1)S(1)} %get-tuple-element.82.refs_0_), channel_id=1, source_target_pairs={{0,2},{2,0},{4,6},{6,4},{8,10},{10,8},{12,14},{14,12},{16,18},{18,... | collective-permute-start | bytes 786440 | tf_op jit(solution)/shard_map/ppermute | solution.py:632
  80.7 11.6 %collective-permute-start.16 = (bf16[1,256,512]{2,1,0:T(8,128)(2,1)S(1)}, bf16[1,256,512]{2,1,0:T(8,128)(2,1)S(1)}, u32[]{:S(2)}, u32[]{:S(2)}) collective-permute-start(bf16[1,256,512]{2,1,0:T(8,128)(2,1)S(1)} %get-tuple-element.96), channel_id=1, source_target_pairs={{0,8},{2,10},{4,12},{6,14},{8,0},{10,2},{12,4},{14,6},{16,24},{18,... | collective-permute-start | bytes 786440 | tf_op jit(solution)/shard_map/ppermute | solution.py:644
  83.1 18.6 %collective-permute-start.10 = (bf16[1280,128]{1,0:T(8,128)(2,1)S(1)}, bf16[1280,128]{1,0:T(8,128)(2,1)S(1)}, u32[]{:S(2)}, u32[]{:S(2)}) collective-permute-start(bf16[1280,128]{1,0:T(8,128)(2,1)S(1)} %get-tuple-element.90), channel_id=1, source_target_pairs={{0,2},{2,0},{4,6},{6,4},{8,10},{10,8},{12,14},{14,12},{16,18},{18,... | collective-permute-start | bytes 983048 | tf_op jit(solution)/shard_map/ppermute | solution.py:632
  84.6 18.4 %collective-permute-start.11 = (bf16[1280,128]{1,0:T(8,128)(2,1)S(1)}, bf16[1280,128]{1,0:T(8,128)(2,1)S(1)}, u32[]{:S(2)}, u32[]{:S(2)}) collective-permute-start(bf16[1280,128]{1,0:T(8,128)(2,1)S(1)} %get-tuple-element.91), channel_id=1, source_target_pairs={{0,4},{2,6},{4,0},{6,2},{8,12},{10,14},{12,8},{14,10},{16,20},{18,... | collective-permute-start | bytes 983048 | tf_op jit(solution)/shard_map/ppermute | solution.py:632
  85.3 17.7 %collective-permute-start.12 = (bf16[1280,128]{1,0:T(8,128)(2,1)S(1)}, bf16[1280,128]{1,0:T(8,128)(2,1)S(1)}, u32[]{:S(2)}, u32[]{:S(2)}) collective-permute-start(bf16[1280,128]{1,0:T(8,128)(2,1)S(1)} %get-tuple-element.92), channel_id=1, source_target_pairs={{0,6},{2,4},{4,2},{6,0},{8,14},{10,12},{12,10},{14,8},{16,22},{18,... | collective-permute-start | bytes 983048 | tf_op jit(solution)/shard_map/ppermute | solution.py:632
  86.6 5.6 %collective-permute-start.18 = (f32[4,4,256]{2,1,0:T(4,128)S(1)}, f32[4,4,256]{2,1,0:T(4,128)S(1)}, u32[]{:S(2)}, u32[]{:S(2)}) collective-permute-start(f32[4,4,256]{2,1,0:T(4,128)S(1)} %get-tuple-element.98.stats_ref), channel_id=1, source_target_pairs={{8,0},{10,2},{12,4},{14,6},{16,8},{18,10},{20,12},{22,14},{24,16},... | collective-permute-start | bytes 49160 | tf_op jit(solution)/shard_map/ppermute | solution.py:640
  92.3 16.8 %collective-permute-start.19 = (bf16[256,512]{1,0:T(8,128)(2,1)S(1)}, bf16[256,512]{1,0:T(8,128)(2,1)S(1)}, u32[]{:S(2)}, u32[]{:S(2)}) collective-permute-start(bf16[256,512]{1,0:T(8,128)(2,1)S(1)} %halve_0.1), channel_id=1, source_target_pairs={{0,16},{2,18},{4,20},{6,22},{8,24},{10,26},{12,28},{14,30},{16,0},... | collective-permute-start | bytes 786440 | tf_op jit(solution)/shard_map/ppermute | solution.py:644
  100.4 11.3 %collective-permute-start.20 = (bf16[2,128,256]{2,1,0:T(8,128)(2,1)S(1)}, bf16[2,128,256]{2,1,0:T(8,128)(2,1)S(1)}, u32[]{:S(2)}, u32[]{:S(2)}) collective-permute-start(bf16[2,128,256]{2,1,0:T(8,128)(2,1)S(1)} %get-tuple-element.111), channel_id=1, source_target_pairs={{16,0},{18,2},{20,4},{22,6},{17,1},{19,3},{21,5},{23,7}} | collective-permute-start | bytes 393224 | tf_op jit(solution)/shard_map/ppermute | solution.py:725
  101.7 10.1 %collective-permute-start.21 = (bf16[2,128,256]{2,1,0:T(8,128)(2,1)S(1)}, bf16[2,128,256]{2,1,0:T(8,128)(2,1)S(1)}, u32[]{:S(2)}, u32[]{:S(2)}) collective-permute-start(bf16[2,128,256]{2,1,0:T(8,128)(2,1)S(1)} %get-tuple-element.112), channel_id=1, source_target_pairs={{24,0},{26,2},{28,4},{30,6},{25,1},{27,3},{29,5},{31,7}} | collective-permute-start | bytes 393224 | tf_op jit(solution)/shard_map/ppermute | solution.py:725
  105.1 12.2 %collective-permute-start.25 = (bf16[1,256,512]{2,1,0:T(8,128)(2,1)S(1)}, bf16[1,256,512]{2,1,0:T(8,128)(2,1)S(1)}, u32[]{:S(2)}, u32[]{:S(2)}) collective-permute-start(bf16[1,256,512]{2,1,0:T(8,128)(2,1)S(1)} %get-tuple-element.123), channel_id=1, source_target_pairs={{0,8},{2,10},{4,12},{6,14},{8,0},{10,2},{12,4},{14,6},{16,24},{18,... | collective-permute-start | bytes 786440 | tf_op jit(solution)/shard_map/ppermute | solution.py:644
  112.6 21.5 %collective-permute-start.27 = (bf16[2,256,512]{2,1,0:T(8,128)(2,1)S(1)}, bf16[2,256,512]{2,1,0:T(8,128)(2,1)S(1)}, u32[]{:S(2)}, u32[]{:S(2)}) collective-permute-start(bf16[2,256,512]{2,1,0:T(8,128)(2,1)S(1)} %get-tuple-element.125), channel_id=1, source_target_pairs={{0,8},{2,10},{4,12},{6,14},{8,0},{10,2},{12,4},{14,6},{16,24},{18,... | collective-permute-start | bytes 1572872 | tf_op jit(solution)/shard_map/ppermute | solution.py:644
  112.7 10.7 %collective-permute-start.22 = (bf16[5,256,128]{2,1,0:T(8,128)(2,1)S(1)}, bf16[5,256,128]{2,1,0:T(8,128)(2,1)S(1)}, u32[]{:S(2)}, u32[]{:S(2)}) collective-permute-start(bf16[5,256,128]{2,1,0:T(8,128)(2,1)S(1)} %get-tuple-element.114), channel_id=1, source_target_pairs={{0,2},{2,0},{4,6},{6,4},{8,10},{10,8},{12,14},{14,12},{16,18},{18,... | collective-permute-start | bytes 983048 | tf_op jit(solution)/shard_map/ppermute | solution.py:632
  114.2 15.9 %collective-permute-start.23 = (bf16[5,256,128]{2,1,0:T(8,128)(2,1)S(1)}, bf16[5,256,128]{2,1,0:T(8,128)(2,1)S(1)}, u32[]{:S(2)}, u32[]{:S(2)}) collective-permute-start(bf16[5,256,128]{2,1,0:T(8,128)(2,1)S(1)} %get-tuple-element.115), channel_id=1, source_target_pairs={{0,4},{2,6},{4,0},{6,2},{8,12},{10,14},{12,8},{14,10},{16,20},{18,... | collective-permute-start | bytes 983048 | tf_op jit(solution)/shard_map/ppermute | solution.py:632
  115.6 14.6 %collective-permute-start.24 = (bf16[5,256,128]{2,1,0:T(8,128)(2,1)S(1)}, bf16[5,256,128]{2,1,0:T(8,128)(2,1)S(1)}, u32[]{:S(2)}, u32[]{:S(2)}) collective-permute-start(bf16[5,256,128]{2,1,0:T(8,128)(2,1)S(1)} %get-tuple-element.116), channel_id=1, source_target_pairs={{0,6},{2,4},{4,2},{6,0},{8,14},{10,12},{12,10},{14,8},{16,22},{18,... | collective-permute-start | bytes 983048 | tf_op jit(solution)/shard_map/ppermute | solution.py:632
  117.4 14.9 %collective-permute-start.26 = (bf16[256,512]{1,0:T(8,128)(2,1)S(1)}, bf16[256,512]{1,0:T(8,128)(2,1)S(1)}, u32[]{:S(2)}, u32[]{:S(2)}) collective-permute-start(bf16[256,512]{1,0:T(8,128)(2,1)S(1)} %halve_1.1), channel_id=1, source_target_pairs={{0,16},{2,18},{4,20},{6,22},{8,24},{10,26},{12,28},{14,30},{16,0},... | collective-permute-start | bytes 786440 | tf_op jit(solution)/shard_map/ppermute | solution.py:644
